TPU v7x, 32 devices: a whole 2x2x4 slice. The times are simulated.
32 devices in a mesh: dp: 8 (over z, y), blk: 4 (over x, core).
Axes of the slice: x: 2, y: 2, z: 4, core: 2. Of those that a mesh axis runs over, the one named last changes fastest.
Arguments:
- programs: float32 [4096, 512], P(('dp', 'blk'))
- traces: float32 [4096, 512], P(('dp', 'blk'))
- hard_owner: int32 [4096, 16], P(('dp', 'blk')), may hold values from 0 to 31, all different within a row; in each aligned block of 128 rows (0 to 127, 128 to 255, ...) at most 96 rows name the same one
- hard_row: int32 [4096, 16], P(('dp', 'blk')), may hold values from 0 to 127
Outputs:
- grad_programs: float32 [4096, 512], P(('dp', 'blk'))
- grad_traces: float32 [4096, 512], P(('dp', 'blk'))
- row_loss: float32 [4096], P(('dp', 'blk'))
Inputs may be any that keep to these rules, and one draw needn't show every extreme that they name: `hard_owner`: each program names 16 different blocks. Among the 128 programs of one device at most 96 name the same block, and in every draw some device has a block named by exactly 96 of its programs.
All inputs are finite; a program needn't handle non-finite values.
Results may differ from a plain program's by a relative error of at most 0.00035.
Values may be sent and summed in bfloat16 or wider, within the bound.
No kernel may reach another device: no remote copies, remote signals or barrier semaphores. Data moves between devices by JAX's collectives and lax.ppermute only.
A program may use at most 64 MiB of HBM per device.

v0:
```python
import jax
import jax.numpy as jnp
from jax import lax
from jax.sharding import PartitionSpec as P

EPSILON = 1e-06
LOGIT_SCALE = 14.0
HIGH = lax.Precision.HIGHEST


def passed_along(shard, axis, by):
    count = lax.axis_size(axis)
    return lax.ppermute(shard, axis, [(i, (i + by) % count) for i in range(count)])


def normalize(values):
    length = jnp.sqrt(jnp.sum(values * values, axis=-1, keepdims=True) + EPSILON)
    return (values / length, length)


def on_device(programs, traces, hard_owner, hard_row):
    row_count, feat_width = programs.shape
    neg_count = hard_owner.shape[1]
    blk_count = lax.axis_size("blk")
    dp_count = lax.axis_size("dp")
    owner_count = dp_count * blk_count
    prog_unit, prog_len = normalize(programs)
    trace_unit, trace_len = normalize(traces)

    def score_block(trace_block):
        return LOGIT_SCALE * jnp.einsum(
            "rd,cd->rc", prog_unit, trace_block, precision=HIGH, preferred_element_type=jnp.float32
        )

    current = trace_unit
    exp_total = jnp.zeros((row_count,), jnp.float32)
    for turn_index in range(blk_count):
        if turn_index > 0:
            current = passed_along(current, "blk", 1)
        scores = score_block(current)
        exps = jnp.exp(scores)
        exp_total = exp_total + jnp.sum(exps, axis=1)
    log_group = jnp.log(exp_total)
    current = trace_unit
    grad_block = jnp.zeros((row_count, feat_width), jnp.float32)
    grad_prog = jnp.zeros((row_count, feat_width), jnp.float32)
    for turn_index in range(blk_count):
        if turn_index > 0:
            current, grad_block = passed_along((current, grad_block), "blk", 1)
        weights = jnp.exp(score_block(current) - log_group[:, None])
        grad_prog = grad_prog + LOGIT_SCALE * jnp.dot(
            weights, current, precision=HIGH, preferred_element_type=jnp.float32
        )
        grad_block = grad_block + LOGIT_SCALE * jnp.einsum(
            "rc,rd->cd", weights, prog_unit, precision=HIGH, preferred_element_type=jnp.float32
        )
    grad_trace = passed_along(grad_block, "blk", 1)
    slot_cap = row_count * neg_count * 3 // (2 * owner_count)
    owner_flat = hard_owner.reshape(-1)
    row_flat = hard_row.reshape(-1)
    owner_hits = (owner_flat[:, None] == jnp.arange(owner_count, dtype=jnp.int32)[None, :]).astype(
        jnp.int32
    )
    bucket_rank = jnp.sum((jnp.cumsum(owner_hits, axis=0) - 1) * owner_hits, axis=1)
    slot_index = owner_flat * slot_cap + bucket_rank
    request_buf = (
        jnp.zeros((owner_count * slot_cap,), jnp.int32)
        .at[slot_index]
        .set(row_flat)
        .reshape(owner_count, slot_cap)
    )
    wanted = lax.all_to_all(request_buf, ("dp", "blk"), split_axis=0, concat_axis=0, tiled=True)
    trace_low = trace_unit.astype(jnp.bfloat16)
    answer = trace_low[wanted]
    fetched = lax.all_to_all(answer, ("dp", "blk"), split_axis=0, concat_axis=0, tiled=True)
    hard_unit = fetched.reshape(owner_count * slot_cap, feat_width)[slot_index].reshape(
        row_count, neg_count, feat_width
    )
    hard_scores = LOGIT_SCALE * jnp.einsum(
        "rd,rnd->rn", prog_unit, hard_unit, precision=HIGH, preferred_element_type=jnp.float32
    )
    pos_score = LOGIT_SCALE * jnp.sum(prog_unit * trace_unit, axis=-1)
    log_hard = jnp.log(jnp.exp(pos_score) + jnp.sum(jnp.exp(hard_scores), axis=1))
    hard_weight = jnp.exp(hard_scores - log_hard[:, None])
    pos_weight = jnp.exp(pos_score - log_hard)
    sent = (
        (LOGIT_SCALE * hard_weight[:, :, None] * prog_unit[:, None, :])
        .astype(jnp.bfloat16)
        .reshape(-1, feat_width)
    )
    outgoing = (
        jnp.zeros((owner_count * slot_cap, feat_width), jnp.bfloat16)
        .at[slot_index]
        .set(sent)
        .reshape(owner_count, slot_cap, feat_width)
    )
    returned = lax.all_to_all(outgoing, ("dp", "blk"), split_axis=0, concat_axis=0, tiled=True)
    grad_back = (
        jnp.zeros((row_count, feat_width), jnp.float32)
        .at[wanted.reshape(-1)]
        .add(returned.reshape(-1, feat_width).astype(jnp.float32))
    )
    prog_term = LOGIT_SCALE * (
        jnp.einsum(
            "rn,rnd->rd", hard_weight, hard_unit, precision=HIGH, preferred_element_type=jnp.float32
        )
        + (pos_weight - 2.0)[:, None] * trace_unit
    )
    trace_term = LOGIT_SCALE * (pos_weight - 2.0)[:, None] * prog_unit
    dir_prog = grad_prog + prog_term
    dir_trace = grad_trace + grad_back + trace_term
    grad_programs = (
        dir_prog - prog_unit * jnp.sum(prog_unit * dir_prog, axis=-1, keepdims=True)
    ) / prog_len
    grad_traces = (
        dir_trace - trace_unit * jnp.sum(trace_unit * dir_trace, axis=-1, keepdims=True)
    ) / trace_len
    row_loss = log_group + (log_hard - 2.0 * pos_score)
    return (grad_programs, grad_traces, row_loss)


def solution(mesh):
    in_specs = (
        P(("dp", "blk"), None),
        P(("dp", "blk"), None),
        P(("dp", "blk"), None),
        P(("dp", "blk"), None),
    )
    out_specs = (P(("dp", "blk"), None), P(("dp", "blk"), None), P(("dp", "blk")))
    return jax.shard_map(
        on_device, mesh=mesh, in_specs=in_specs, out_specs=out_specs, check_vma=False
    )
```

profile of v0, /device:TPU:0, one launch (start us, length us, event | category | flops | bytes accessed | tf_op | source)
XLA Modules:
  0.0 248.4 jit_solution(7496988262346656768)
XLA Ops:
  1.4 0.8 copy.8
  2.6 9.1 %reduce-window.6 = s32[32,16,128]{2,1,0:T(8,128)S(1)} reduce-window(s32[32,16,128]{2,1,0:T(8,128)S(1)} %fusion.12, s32[]{:T(128)} %constant.14.clone.1), window={size=1x1x128 pad=0_0x0_0x127_0}, to_apply=%region_6.0 | reduce-window | flops 8323072 | bytes 524292 | tf_op jit(solution)/shard_map/reduce-window
  12.4 0.8 copy.12
  13.4 8.1 %scatter_custom_fusion = s32[3072]{0:T(1024)S(1)} fusion(s32[2048]{0:T(1024)S(1)} %bitcast.75, s32[2048]{0:T(1024)S(1)} %reshape.214, s32[]{:T(128)} %constant.14.clone.1), kind=kCustom, calls=%fused_computation.69 | custom fusion | bytes 12292 | tf_op jit(solution)/shard_map/scatter | solution.py:69
  22.2 7.3 %all-to-all-start = ((s32[32,1,96]{2,1,0:T(1,128)}), s32[32,1,96]{2,1,0:T(1,128)S(1)}, u32[]{:S(2)}, u32[]{:S(2)}) async-start(s32[32,1,96]{2,1,0:T(1,128)} %all_to_all.14), calls=%async_computation | async-start | bytes 32768 | tf_op jit(solution)/shard_map/all_to_all | solution.py:72
  31.2 5.4 %all-to-all-done = s32[32,1,96]{2,1,0:T(1,128)S(1)} async-done(((s32[32,1,96]{2,1,0:T(1,128)}), s32[32,1,96]{2,1,0:T(1,128)S(1)}, u32[]{:S(2)}, u32[]{:S(2)}) %all-to-all-start) | async-done | bytes 12320 | tf_op jit(solution)/shard_map/all_to_all | solution.py:72
  36.6 13.2 %gather_fusion = bf16[3072,512]{1,0:T(8,128)(2,1)} fusion(bf16[128,512]{1,0:T(8,128)(2,1)S(1)} %convert_element_type.18, s32[3072]{0:T(1024)S(1)} %broadcast_clamp_fusion), kind=kCustom, calls=%fused_computation | custom fusion | bytes 6303744 | tf_op jit(solution)/shard_map/gather | solution.py:74
  49.9 2.8 %all-to-all-start.1 = ((bf16[32,96,512]{2,1,0:T(8,128)(2,1)}), bf16[32,96,512]{2,1,0:T(8,128)(2,1)S(1)}, u32[]{:S(2)}, u32[]{:S(2)}) async-start(bf16[32,96,512]{2,1,0:T(8,128)(2,1)} %bitcast.63), calls=%async_computation.1 | async-start | bytes 6291456 | tf_op jit(solution)/shard_map/all_to_all | solution.py:75
  52.8 25.1 %collective-permute-done = f32[128,512]{1,0:T(8,128)S(1)} collective-permute-done((f32[128,512]{1,0:T(8,128)}, f32[128,512]{1,0:T(8,128)S(1)}, u32[]{:S(2)}, u32[]{:S(2)}) %collective-permute-start) | collective-permute-done | bytes 262176 | tf_op jit(solution)/shard_map/ppermute | solution.py:13
  78.6 2.5 %exponential_reduce_fusion.4 = (f32[128]{0:T(128)}, f32[128,128]{0,1:T(8,128)}) fusion(f32[128,512]{1,0:T(8,128)S(1)} %get-tuple-element.10, f32[128,512]{1,0:T(8,128)} %copy-done), kind=kOutput, calls=%fused_computation.55 | convolution fusion | flops 100695936 | bytes 590336 | tf_op jit(solution)/shard_map/rd,cd->rc/dot_general | solution.py:31
  81.1 3.6 %collective-permute-done.1 = f32[128,512]{1,0:T(8,128)S(1)} collective-permute-done((f32[128,512]{1,0:T(8,128)S(1)}, f32[128,512]{1,0:T(8,128)S(1)}, u32[]{:S(2)}, u32[]{:S(2)}) %collective-permute-start.1) | collective-permute-done | bytes 262176 | tf_op jit(solution)/shard_map/ppermute | solution.py:13
  84.7 0.9 exponential_reduce_fusion.3
  85.6 0.9 exponential_reduce_fusion.2
  86.5 9.6 %collective-permute-done.2 = f32[128,512]{1,0:T(8,128)S(1)} collective-permute-done((f32[128,512]{1,0:T(8,128)S(1)}, f32[128,512]{1,0:T(8,128)S(1)}, u32[]{:S(2)}, u32[]{:S(2)}) %collective-permute-start.2) | collective-permute-done | bytes 262176 | tf_op jit(solution)/shard_map/ppermute | solution.py:13
  96.8 1.6 exponential_reduce_fusion.1
  98.4 25.9 %all-to-all-done.1 = bf16[32,96,512]{2,1,0:T(8,128)(2,1)S(1)} async-done(((bf16[32,96,512]{2,1,0:T(8,128)(2,1)}), bf16[32,96,512]{2,1,0:T(8,128)(2,1)S(1)}, u32[]{:S(2)}, u32[]{:S(2)}) %all-to-all-start.1) | async-done | bytes 3145760 | tf_op jit(solution)/shard_map/all_to_all | solution.py:75
  124.2 9.9 %gather_fusion.1 = bf16[2048,512]{1,0:T(8,128)(2,1)} fusion(bf16[3072,512]{1,0:T(8,128)(2,1)S(1)} %bitcast.61, s32[2048]{0:T(1024)} %broadcast_clamp_fusion.1), kind=kCustom, calls=%fused_computation.1 | custom fusion | bytes 4202496 | tf_op jit(solution)/shard_map/gather | solution.py:76
  134.1 3.6 %fusion.10 = f32[128,1,16]{2,1,0:T(1,128)S(1)} fusion(bf16[128,16,512]{2,1,0:T(8,128)(2,1)} %bitcast.65, f32[128,512,1]{1,0,2:T(8,128)S(1)} %bitcast.62), kind=kOutput, calls=%fused_computation.29 | convolution fusion | flops 12582912 | bytes 2367488 | tf_op jit(solution)/shard_map/rd,rnd->rn/dot_general | solution.py:79
  137.8 1.3 broadcast_multiply_fusion.2
  139.7 11.8 %scatter_custom_fusion.1 = bf16[3072,512]{1,0:T(8,128)(2,1)} fusion(s32[2048]{0:T(1024)} %bitcast.77, bf16[2048,512]{1,0:T(8,128)(2,1)S(1)} %fusion.2, bf16[]{:T(256)} %constant.20.clone.1), kind=kCustom, calls=%fused_computation.9 | custom fusion | bytes 3146240 | tf_op jit(solution)/shard_map/scatter | solution.py:94
  151.4 3.9 %all-to-all-start.2 = ((bf16[32,96,512]{2,1,0:T(8,128)(2,1)}), bf16[32,96,512]{2,1,0:T(8,128)(2,1)}, u32[]{:S(2)}, u32[]{:S(2)}) async-start(bf16[32,96,512]{2,1,0:T(8,128)(2,1)} %bitcast.64), calls=%async_computation.2 | async-start | bytes 6291456 | tf_op jit(solution)/shard_map/all_to_all | solution.py:97
  157.5 1.0 fusion.24
  158.6 1.1 fusion.13
  159.7 20.9 %collective-permute-done.3 = f32[128,512]{1,0:T(8,128)S(1)} collective-permute-done((f32[128,512]{1,0:T(8,128)S(1)}, f32[128,512]{1,0:T(8,128)S(1)}, u32[]{:S(2)}, u32[]{:S(2)}) %collective-permute-start.3) | collective-permute-done | bytes 262176 | tf_op jit(solution)/shard_map/ppermute | solution.py:13
  180.6 1.0 fusion.5
  182.6 12.3 %collective-permute-done.4 = f32[128,512]{1,0:T(8,128)S(1)} collective-permute-done((f32[128,512]{1,0:T(8,128)S(1)}, f32[128,512]{1,0:T(8,128)S(1)}, u32[]{:S(2)}, u32[]{:S(2)}) %collective-permute-start.4) | collective-permute-done | bytes 262176 | tf_op jit(solution)/shard_map/ppermute | solution.py:13
  195.9 5.1 %collective-permute-done.5 = f32[128,512]{1,0:T(8,128)S(1)} collective-permute-done((f32[128,512]{1,0:T(8,128)S(1)}, f32[128,512]{1,0:T(8,128)S(1)}, u32[]{:S(2)}, u32[]{:S(2)}) %collective-permute-start.5) | collective-permute-done | bytes 262176 | tf_op jit(solution)/shard_map/ppermute | solution.py:13
  201.7 5.2 %collective-permute-done.6 = f32[128,512]{1,0:T(8,128)S(1)} collective-permute-done((f32[128,512]{1,0:T(8,128)S(1)}, f32[128,512]{1,0:T(8,128)S(1)}, u32[]{:S(2)}, u32[]{:S(2)}) %collective-permute-start.6) | collective-permute-done | bytes 262176 | tf_op jit(solution)/shard_map/ppermute | solution.py:13
  206.9 0.8 multiply_add_fusion
  207.8 19.2 %all-to-all-done.2 = bf16[32,96,512]{2,1,0:T(8,128)(2,1)} async-done(((bf16[32,96,512]{2,1,0:T(8,128)(2,1)}), bf16[32,96,512]{2,1,0:T(8,128)(2,1)}, u32[]{:S(2)}, u32[]{:S(2)}) %all-to-all-start.2) | async-done | bytes 3145760 | tf_op jit(solution)/shard_map/all_to_all | solution.py:97
  226.9 20.5 %scatter_custom_fusion.2 = f32[128,512]{1,0:T(8,128)S(1)} fusion(f32[128,512]{1,0:T(8,128)S(1)} %get-tuple-element.12, s32[3072]{0:T(1024)S(1)} %bitcast.78, bf16[3072,512]{1,0:T(8,128)(2,1)} %bitcast.20), kind=kCustom, calls=%fused_computation.5 | custom fusion | flops 3145728 | bytes 3407872 | tf_op jit(solution)/shard_map/scatter-add | solution.py:101
  247.6 0.8 subtract_divide_fusion
  (91 shorter events, 11.3 us)
Async XLA Ops:
  0.6 28.9 %copy-start.4 = (f32[128,512]{1,0:T(8,128)S(1)}, f32[128,512]{1,0:T(8,128)}, u32[]{:S(2)}) copy-start(f32[128,512]{1,0:T(8,128)} %param.5) | copy-start | bytes 786436
  0.6 29.0 %copy-start.3 = (f32[128,512]{1,0:T(8,128)S(1)}, f32[128,512]{1,0:T(8,128)}, u32[]{:S(2)}) copy-start(f32[128,512]{1,0:T(8,128)} %param.4) | copy-start | bytes 786436
  13.4 64.6 %copy-start.15 = (s32[2048,1]{0,1:T(1,128)}, s32[2048,1]{0,1:T(1,128)S(1)}, u32[]{:S(2)}) copy-start(s32[2048,1]{0,1:T(1,128)S(1)} %compare_select_fusion.1) | copy-start | bytes 24580
  22.2 14.4 %all-to-all-start = ((s32[32,1,96]{2,1,0:T(1,128)}), s32[32,1,96]{2,1,0:T(1,128)S(1)}, u32[]{:S(2)}, u32[]{:S(2)}) async-start(s32[32,1,96]{2,1,0:T(1,128)} %all_to_all.14), calls=%async_computation | async-start | bytes 32768 | tf_op jit(solution)/shard_map/all_to_all | solution.py:72
  29.7 20.1 %copy-start.16 = (f32[128]{0:T(128)}, f32[128]{0:T(128)S(1)}, u32[]{:S(2)}) copy-start(f32[128]{0:T(128)S(1)} %get-tuple-element.27) | copy-start | bytes 1540
  29.8 20.1 %copy-start.18 = (f32[128]{0:T(128)}, f32[128]{0:T(128)S(1)}, u32[]{:S(2)}) copy-start(f32[128]{0:T(128)S(1)} %get-tuple-element.28) | copy-start | bytes 1540
  30.5 0.7 copy-start
  49.9 74.4 %all-to-all-start.1 = ((bf16[32,96,512]{2,1,0:T(8,128)(2,1)}), bf16[32,96,512]{2,1,0:T(8,128)(2,1)S(1)}, u32[]{:S(2)}, u32[]{:S(2)}) async-start(bf16[32,96,512]{2,1,0:T(8,128)(2,1)} %bitcast.63), calls=%async_computation.1 | async-start | bytes 6291456 | tf_op jit(solution)/shard_map/all_to_all | solution.py:75
  52.6 25.3 %collective-permute-start = (f32[128,512]{1,0:T(8,128)}, f32[128,512]{1,0:T(8,128)S(1)}, u32[]{:S(2)}, u32[]{:S(2)}) collective-permute-start(f32[128,512]{1,0:T(8,128)} %copy-done), channel_id=1, source_target_pairs={{0,1},{1,2},{2,3},{3,0},{4,5},{5,6},{6,7},{7,4},{8,9},{9,10},{10,1... | collective-permute-start | bytes 786440 | tf_op jit(solution)/shard_map/ppermute | solution.py:13
  78.0 18.1 %copy-start.7 = (f32[128,512]{1,0:T(8,128)}, f32[128,512]{1,0:T(8,128)S(1)}, u32[]{:S(2)}) copy-start(f32[128,512]{1,0:T(8,128)S(1)} %collective-permute-done) | copy-start | bytes 786436
  78.0 6.7 %collective-permute-start.1 = (f32[128,512]{1,0:T(8,128)S(1)}, f32[128,512]{1,0:T(8,128)S(1)}, u32[]{:S(2)}, u32[]{:S(2)}) collective-permute-start(f32[128,512]{1,0:T(8,128)S(1)} %collective-permute-done), channel_id=1, source_target_pairs={{0,1},{1,2},{2,3},{3,0},{4,5},{5,6},{6,7},{7,4},{8,9},{9,10},{10,1... | collective-permute-start | bytes 786440 | tf_op jit(solution)/shard_map/ppermute | solution.py:13
  84.7 11.4 %copy-start.5 = (f32[128,512]{1,0:T(8,128)}, f32[128,512]{1,0:T(8,128)S(1)}, u32[]{:S(2)}) copy-start(f32[128,512]{1,0:T(8,128)S(1)} %collective-permute-done.1) | copy-start | bytes 786436
  84.7 11.4 %collective-permute-start.2 = (f32[128,512]{1,0:T(8,128)S(1)}, f32[128,512]{1,0:T(8,128)S(1)}, u32[]{:S(2)}, u32[]{:S(2)}) collective-permute-start(f32[128,512]{1,0:T(8,128)S(1)} %collective-permute-done.1), channel_id=1, source_target_pairs={{0,1},{1,2},{2,3},{3,0},{4,5},{5,6},{6,7},{7,4},{8,9},{9,10},{10,1... | collective-permute-start | bytes 786440 | tf_op jit(solution)/shard_map/ppermute | solution.py:13
  96.1 0.7 copy-start.9
  139.1 17.5 %copy-start.13 = (f32[128]{0:T(128)}, f32[128]{0:T(128)S(1)}, u32[]{:S(2)}) copy-start(f32[128]{0:T(128)S(1)} %get-tuple-element.15) | copy-start | bytes 1540
  151.4 5.2 %copy-start.11 = (f32[128,128]{0,1:T(8,128)S(1)}, f32[128,128]{0,1:T(8,128)}, u32[]{:S(2)}) copy-start(f32[128,128]{0,1:T(8,128)} %get-tuple-element.22) | copy-start | bytes 196612
  151.4 6.1 %copy-start.2 = (bf16[2048,512]{1,0:T(8,128)(2,1)S(1)}, bf16[2048,512]{1,0:T(8,128)(2,1)}, u32[]{:S(2)}) copy-start(bf16[2048,512]{1,0:T(8,128)(2,1)} %gather_fusion.1) | copy-start | bytes 6291460
  151.4 7.1 %copy-start.1 = (f32[128,512]{1,0:T(8,128)S(1)}, f32[128,512]{1,0:T(8,128)}, u32[]{:S(2)}) copy-start(f32[128,512]{1,0:T(8,128)} %copy-done) | copy-start | bytes 786436
  151.4 75.5 %all-to-all-start.2 = ((bf16[32,96,512]{2,1,0:T(8,128)(2,1)}), bf16[32,96,512]{2,1,0:T(8,128)(2,1)}, u32[]{:S(2)}, u32[]{:S(2)}) async-start(bf16[32,96,512]{2,1,0:T(8,128)(2,1)} %bitcast.64), calls=%async_computation.2 | async-start | bytes 6291456 | tf_op jit(solution)/shard_map/all_to_all | solution.py:97
  155.3 26.8 %copy-start.8 = (f32[128,512]{1,0:T(8,128)S(1)}, f32[128,512]{1,0:T(8,128)}, u32[]{:S(2)}) copy-start(f32[128,512]{1,0:T(8,128)} %copy-done.7) | copy-start | bytes 786436
  157.1 24.7 %copy-start.14 = (f32[128]{0:T(128)S(1)}, f32[128]{0:T(128)}, u32[]{:S(2)}) copy-start(f32[128]{0:T(128)} %copy-done.13) | copy-start | bytes 1540
  157.1 38.0 %copy-start.12 = (f32[128,128]{0,1:T(8,128)S(1)}, f32[128,128]{0,1:T(8,128)}, u32[]{:S(2)}) copy-start(f32[128,128]{0,1:T(8,128)} %get-tuple-element.18) | copy-start | bytes 196612
  157.1 23.5 %collective-permute-start.3 = (f32[128,512]{1,0:T(8,128)S(1)}, f32[128,512]{1,0:T(8,128)S(1)}, u32[]{:S(2)}, u32[]{:S(2)}) collective-permute-start(f32[128,512]{1,0:T(8,128)S(1)} %convolution_multiply_fusion.3), channel_id=1, source_target_pairs={{0,1},{1,2},{2,3},{3,0},{4,5},{5,6},{6,7},{7,4},{8,9},{9,10},{10,1... | collective-permute-start | bytes 786440 | tf_op jit(solution)/shard_map/ppermute | solution.py:13
  157.5 37.9 %copy-start.6 = (f32[128,512]{1,0:T(8,128)S(1)}, f32[128,512]{1,0:T(8,128)}, u32[]{:S(2)}) copy-start(f32[128,512]{1,0:T(8,128)} %copy-done.5) | copy-start | bytes 786436
  158.5 42.6 %copy-start.10 = (f32[128,512]{1,0:T(8,128)S(1)}, f32[128,512]{1,0:T(8,128)}, u32[]{:S(2)}) copy-start(f32[128,512]{1,0:T(8,128)} %copy-done.9) | copy-start | bytes 786436
  158.5 42.6 %copy-start.21 = (f32[128]{0:T(128)S(1)}, f32[128]{0:T(128)}, u32[]{:S(2)}) copy-start(f32[128]{0:T(128)} %get-tuple-element.8) | copy-start | bytes 1540
  181.7 25.2 %copy-start.19 = (f32[128]{0:T(128)S(1)}, f32[128]{0:T(128)}, u32[]{:S(2)}) copy-start(f32[128]{0:T(128)} %copy-done.18) | copy-start | bytes 1540
  181.7 25.2 %copy-start.20 = (f32[128]{0:T(128)S(1)}, f32[128]{0:T(128)}, u32[]{:S(2)}) copy-start(f32[128]{0:T(128)} %get-tuple-element.7) | copy-start | bytes 1540
  181.7 13.2 %collective-permute-start.4 = (f32[128,512]{1,0:T(8,128)S(1)}, f32[128,512]{1,0:T(8,128)S(1)}, u32[]{:S(2)}, u32[]{:S(2)}) collective-permute-start(f32[128,512]{1,0:T(8,128)S(1)} %fusion.5), channel_id=1, source_target_pairs={{0,1},{1,2},{2,3},{3,0},{4,5},{5,6},{6,7},{7,4},{8,9},{9,10},{10,1... | collective-permute-start | bytes 786440 | tf_op jit(solution)/shard_map/ppermute | solution.py:13
  195.0 6.0 %collective-permute-start.5 = (f32[128,512]{1,0:T(8,128)S(1)}, f32[128,512]{1,0:T(8,128)S(1)}, u32[]{:S(2)}, u32[]{:S(2)}) collective-permute-start(f32[128,512]{1,0:T(8,128)S(1)} %add.160), channel_id=1, source_target_pairs={{0,1},{1,2},{2,3},{3,0},{4,5},{5,6},{6,7},{7,4},{8,9},{9,10},{10,1... | collective-permute-start | bytes 786440 | tf_op jit(solution)/shard_map/ppermute | solution.py:13
  201.1 5.8 %collective-permute-start.6 = (f32[128,512]{1,0:T(8,128)S(1)}, f32[128,512]{1,0:T(8,128)S(1)}, u32[]{:S(2)}, u32[]{:S(2)}) collective-permute-start(f32[128,512]{1,0:T(8,128)S(1)} %add.161), channel_id=1, source_target_pairs={{0,1},{1,2},{2,3},{3,0},{4,5},{5,6},{6,7},{7,4},{8,9},{9,10},{10,1... | collective-permute-start | bytes 786440 | tf_op jit(solution)/shard_map/ppermute | solution.py:13
  201.1 46.4 %copy-start.17 = (f32[128]{0:T(128)S(1)}, f32[128]{0:T(128)}, u32[]{:S(2)}) copy-start(f32[128]{0:T(128)} %copy-done.16) | copy-start | bytes 1540
where the time goes:
time: 249 us; the launch traced here: 248 us
  waiting for transfers between devices  132 us (53%)
  local copies, waits for them, and re-layouts  48.3 us (19%)
  other arithmetic  36.8 us (15%)
  matrix products  15.2 us (6%)
  starting transfers between devices  14.7 us (6%)
    ppermute x7, waiting for transfers between devices, passed_along(): lax.ppermute(shard, axis, [(i, (i + by) % count) for i in range(count)])  81.9 us
    all_to_all x1, waiting for transfers between devices, on_device(): lax.all_to_all(answer, ('dp', 'blk'), split_axis=0, concat_axis=0, tiled=...  25.9 us
    scatter-add x1, other arithmetic, on_device(): grad_back = jnp.zeros((row_count, feat_width), jnp.float32).at[wanted.res...  20.5 us
    all_to_all x1, waiting for transfers between devices, on_device(): lax.all_to_all(outgoing, ('dp', 'blk'), split_axis=0, concat_axis=0, tile...  19.2 us
    gather x1, local copies, waits for them, and re-layouts, on_device(): answer = trace_low[wanted]  13.2 us
    scatter x1, local copies, waits for them, and re-layouts, on_device(): outgoing = jnp.zeros((owner_count * slot_cap, feat_width), jnp.bfloat16)....  11.8 us
    another operation x3, other arithmetic  10.1 us
    gather x1, local copies, waits for them, and re-layouts, on_device(): fetched.reshape(owner_count * slot_cap, feat_width)[slot_index]  9.89 us
  transfers between devices with their start and end apart: 10, of which 10 were waited for; matrix products, arithmetic and copies ran while one was open for 6% of the time, Pallas kernels for 0%

commit v1 on v0

v1 whole, which is shorter than its diff:
```python
import functools

import jax
import jax.numpy as jnp
from jax import lax
from jax.experimental import pallas as pl
from jax.experimental.pallas import tpu as pltpu
from jax.sharding import PartitionSpec as P

EPSILON = 1e-06
SCALE = 14.0
LOW = jnp.bfloat16
F32 = jnp.float32
ROWS = 128
VMEM_LIMIT = 40 * 1024 * 1024


def normalize(values):
    length = jnp.sqrt(jnp.sum(values * values, axis=-1, keepdims=True) + EPSILON)
    return values / length, length


def dot(a, b, contract=(1, 0)):
    return lax.dot_general(
        a, b, (((contract[0],), (contract[1],)), ((), ())), preferred_element_type=F32
    )


def halves(values):
    high = values.astype(LOW)
    return high, (values - high.astype(F32)).astype(LOW)


def dot3(a, b, contract=(1, 0)):
    return (
        dot(a[0], b[1], contract) + dot(a[1], b[0], contract)
    ) + dot(a[0], b[0], contract)


def eye():
    shape = (ROWS, ROWS)
    return lax.broadcasted_iota(jnp.int32, shape, 0) == lax.broadcasted_iota(jnp.int32, shape, 1)


def to_row(column):
    return jnp.sum(jnp.where(eye(), column, 0.0), axis=0, keepdims=True)


def to_column(row):
    return jnp.sum(jnp.where(eye(), row, 0.0), axis=1, keepdims=True)


def own_plane():
    return lax.div(lax.axis_index("dp"), 2)


def own_core():
    return lax.rem(lax.axis_index("blk"), 2)


def aux_rows(planes, feat):
    per_row = feat // ROWS
    picks = 8 * (-(-planes // per_row))
    return picks, -(-(picks + 8) // 16) * 16


def prepare(planes, prog_ref, trace_ref, owner_ref, row_ref, msg_ref, low_ref, group_ref):
    feat = prog_ref.shape[1]
    neg = owner_ref.shape[1]
    prog_unit, _ = normalize(prog_ref[...])
    trace_unit, _ = normalize(trace_ref[...])
    prog_high, prog_low = halves(prog_unit)
    trace_high, trace_low = halves(trace_unit)
    msg_ref[0:ROWS, :] = prog_high
    low_ref[...] = trace_high
    group_ref[0:ROWS, :] = trace_low
    group_ref[ROWS : 2 * ROWS, :] = prog_high
    group_ref[2 * ROWS : 3 * ROWS, :] = prog_low
    pos = to_row(SCALE * jnp.sum(prog_unit * trace_unit, axis=-1, keepdims=True))
    unit = jnp.where(eye(), 1.0, 0.0).astype(LOW)
    owners = dot(owner_ref[...].astype(F32).astype(LOW), unit, (0, 0))
    rows = dot(row_ref[...].astype(F32).astype(LOW), unit, (0, 0)) + 1.0
    index = lax.broadcasted_iota(jnp.int32, (planes * 8, ROWS), 0).astype(F32)
    picks = jnp.zeros((planes * 8, ROWS), F32)
    for n in range(neg):
        picks = picks + jnp.where(index == owners[n : n + 1, :], rows[n : n + 1, :], 0.0)
    per_row = feat // ROWS
    blank = jnp.zeros((8, ROWS), F32)
    parts = []
    for start in range(0, planes, per_row):
        tiles = [
            picks[p * 8 : p * 8 + 8, :] if p < planes else blank
            for p in range(start, start + per_row)
        ]
        parts.append(jnp.concatenate(tiles, axis=1))
    high = pos.astype(LOW).astype(F32)
    mid = (pos - high).astype(LOW).astype(F32)
    last = pos - high - mid
    line = lax.broadcasted_iota(jnp.int32, (8, ROWS), 0)
    pos_tile = jnp.where(line == 0, high, jnp.where(line == 1, mid, jnp.where(line == 2, last, 0.0)))
    parts.append(jnp.concatenate([pos_tile] + [blank] * (per_row - 1), axis=1))
    left = msg_ref.shape[0] - ROWS - 8 * len(parts)
    if left:
        parts.append(jnp.zeros((left, feat), F32))
    msg_ref[ROWS:, :] = jnp.concatenate(parts, axis=0).astype(LOW)


def score(planes, *refs):
    count = 2 * planes
    msgs, traces = refs[:count], refs[count : count + 8]
    exp_ref, pick_ref, sum_ref, pos_ref, prog_ref, trace_ref = refs[count + 8 :]
    feat = trace_ref.shape[1]
    per_row = feat // ROWS
    picks_rows, _ = aux_rows(planes, feat)
    plane, core = own_plane(), own_core()
    for b, msg in enumerate(msgs):
        prog_ref[b * ROWS : (b + 1) * ROWS, :] = msg[0:ROWS, :]
        aux = msg[ROWS:, :].astype(F32)
        chosen = jnp.zeros((8, ROWS), F32)
        for p in range(planes):
            at, lane = 8 * (p // per_row), ROWS * (p % per_row)
            tile = aux[at : at + 8, lane : lane + ROWS]
            chosen = chosen + jnp.where(plane == p, 1.0, 0.0) * tile
        pick_ref[:, b * ROWS : (b + 1) * ROWS] = by_slot(chosen)
        pos = aux[picks_rows : picks_rows + 8, 0:ROWS]
        pos_ref[:, b * ROWS : (b + 1) * ROWS] = pos[0:1, :] + pos[1:2, :] + pos[2:3, :]
    for q in range(8):
        trace_ref[q * ROWS : (q + 1) * ROWS, :] = traces[q][...]
    total_width = count * ROWS
    below = lax.broadcasted_iota(jnp.int32, (ROWS, total_width), 0).astype(F32) + 1.0
    sums = jnp.zeros((1, total_width), F32)
    for q in range(8):
        scores = dot(traces[q][...], prog_ref[...], (1, 1))
        pick = pick_ref[q : q + 1, :]
        found = jnp.sum(jnp.where(below == pick, scores, 0.0), axis=0, keepdims=True)
        exps = jnp.where(pick > 0.0, jnp.exp(SCALE * found), 0.0)
        exp_ref[q : q + 1, :] = exps
        sums = sums + exps
    for b in range(count):
        sum_ref[:, pl.ds(block_lane(planes, b, plane, core), ROWS)] = sums[
            :, b * ROWS : (b + 1) * ROWS
        ]


def by_slot(picks):
    blk = lax.axis_index("blk")
    bits = (lax.rem(blk, 2), lax.div(blk, 2), lax.rem(lax.axis_index("dp"), 2))
    for step, bit in zip((1, 2, 4), bits):
        turned = []
        for at in range(0, 8, 2 * step):
            turned += [picks[at + step : at + 2 * step, :], picks[at : at + step, :]]
        picks = jnp.where(bit == 1, jnp.concatenate(turned, axis=0), picks)
    return picks


def block_lane(planes, b, plane, core):
    source = lax.rem(plane - b % planes + planes, planes)
    other = core if b < planes else 1 - core
    return pl.multiple_of((2 * source + other) * ROWS, ROWS)


def program_terms(planes, exp_ref, pick_ref, trace_ref, own_ref, *out_refs):
    width = planes * ROWS
    lanes = lax.broadcasted_iota(jnp.int32, (width, ROWS), 1).astype(F32) + 1.0
    exps = jnp.transpose(exp_ref[:, 0:width])
    picks = jnp.transpose(pick_ref[:, 0:width])
    high, low = [], []
    for q in range(8):
        values = jnp.where(lanes == picks[:, q : q + 1], exps[:, q : q + 1], 0.0)
        value_high, value_low = halves(values)
        high.append(value_high)
        low.append(value_low)
    total = dot(jnp.concatenate(high, axis=1), trace_ref[...]) + dot(
        jnp.concatenate(low, axis=1), trace_ref[...]
    )
    own_ref[...] = total[0:ROWS, :]
    for k, out_ref in enumerate(out_refs, 1):
        out_ref[...] = total[k * ROWS : (k + 1) * ROWS, :].astype(LOW)


def trace_terms(planes, exp_ref, pick_ref, pos_ref, prog_ref, *refs):
    sums = refs[:planes]
    total_ref, own_ref, x_ref, y_ref, xy_ref = refs[planes : planes + 5]
    high_ref, low_ref = refs[planes + 5 :]
    plane, core = own_plane(), own_core()
    count = 2 * planes
    below = lax.broadcasted_iota(jnp.int32, (ROWS, ROWS), 0).astype(F32) + 1.0
    for b in range(count):
        lane = block_lane(planes, b, plane, core)
        total = jnp.exp(pos_ref[:, b * ROWS : (b + 1) * ROWS])
        for one in sums:
            total = total + one[:, pl.ds(lane, ROWS)]
        if b == 0:
            total_ref[...] = total
        scale = SCALE / total
        for i in range(4):
            q = 2 * i
            weight = exp_ref[q : q + 1, b * ROWS : (b + 1) * ROWS] * scale
            pick = pick_ref[q : q + 1, b * ROWS : (b + 1) * ROWS]
            values = jnp.where(below == pick, weight, 0.0)
            high, low = halves(values)
            high_ref[i * ROWS : (i + 1) * ROWS, b * ROWS : (b + 1) * ROWS] = high
            low_ref[i * ROWS : (i + 1) * ROWS, b * ROWS : (b + 1) * ROWS] = low
    result = dot(high_ref[...], prog_ref[...]) + dot(low_ref[...], prog_ref[...])
    own_ref[...] = result[0:ROWS, :]
    for i, out_ref in enumerate((x_ref, y_ref, xy_ref), 1):
        out_ref[...] = result[i * ROWS : (i + 1) * ROWS, :].astype(LOW)


def group_terms(*refs):
    highs, groups = refs[:4], refs[4:8]
    prog_out, trace_out, log_ref = refs[8:]

    def joined(parts):
        return jnp.concatenate(parts, axis=0)

    trace = (joined([h[...] for h in highs]), joined([g[0:ROWS, :] for g in groups]))
    prog = (
        joined([g[ROWS : 2 * ROWS, :] for g in groups]),
        joined([g[2 * ROWS :, :] for g in groups]),
    )
    scores = SCALE * dot3(prog, trace, (1, 1))
    exps = jnp.exp(scores)
    total = jnp.sum(exps, axis=1, keepdims=True)
    weights = exps / total
    log_ref[...] = to_row(jnp.log(total[0:ROWS, :]))
    prog_out[...] = dot3(halves(weights[0:ROWS, :]), trace)
    trace_out[...] = dot3(halves(jnp.transpose(weights[:, 0:ROWS])), prog)


def finish(planes, prog_ref, trace_ref, total_ref, log_ref, group_prog, group_trace, *refs):
    prog_own, progs = refs[0], refs[1:planes]
    trace_own, traces = refs[planes], refs[planes + 1 : planes + 4]
    grad_prog_ref, grad_trace_ref, loss_ref = refs[planes + 4 :]
    prog_unit, prog_len = normalize(prog_ref[...])
    trace_unit, trace_len = normalize(trace_ref[...])
    pos = SCALE * jnp.sum(prog_unit * trace_unit, axis=-1, keepdims=True)
    total = to_column(total_ref[...])
    hard = prog_own[...]
    for one in progs:
        hard = hard + one[...].astype(F32)
    pull = jnp.exp(pos) / total - 2.0
    dir_prog = SCALE * (group_prog[...] + hard / total + pull * trace_unit)
    back = trace_own[...]
    for one in traces:
        back = back + one[...].astype(F32)
    dir_trace = SCALE * (group_trace[...] + pull * prog_unit) + back
    along = jnp.sum(prog_unit * dir_prog, axis=-1, keepdims=True)
    grad_prog_ref[...] = (dir_prog - prog_unit * along) / prog_len
    along = jnp.sum(trace_unit * dir_trace, axis=-1, keepdims=True)
    grad_trace_ref[...] = (dir_trace - trace_unit * along) / trace_len
    loss_ref[...] = log_ref[...] + (jnp.log(total_ref[...]) - 2.0 * to_row(pos))


def call(body, outs, flops, moved, scratch=()):
    return pl.pallas_call(
        body,
        out_shape=[jax.ShapeDtypeStruct(shape, dtype) for shape, dtype in outs],
        scratch_shapes=list(scratch),
        compiler_params=pltpu.CompilerParams(vmem_limit_bytes=VMEM_LIMIT),
        cost_estimate=pl.CostEstimate(flops=flops, bytes_accessed=moved, transcendentals=0),
    )


def on_device(dp_count, blk_count, programs, traces, hard_owner, hard_row):
    rows, feat = programs.shape
    planes = dp_count // 2
    size = dp_count * blk_count
    both = ("dp", "blk")

    def flipped(value, bits):
        return lax.ppermute(value, both, [(i, i ^ bits) for i in range(size)])

    def shifted(value, by):
        plane_size = 2 * blk_count
        return lax.ppermute(
            value, both, [(i, (i + by * plane_size) % size) for i in range(size)]
        )

    x_bit, y_bit = 2, blk_count
    _, extra = aux_rows(planes, feat)
    block = rows * feat
    msg, high, group = call(
        functools.partial(prepare, planes),
        [((rows + extra, feat), LOW), ((rows, feat), LOW), ((3 * rows, feat), LOW)],
        10 * block,
        20 * block,
    )(programs, traces, hard_owner, hard_row)

    msgs = [msg] + [shifted(msg, k) for k in range(1, planes)]
    highs = [high, flipped(high, x_bit), flipped(high, y_bit), flipped(high, x_bit + y_bit)]
    other_highs = [flipped(one, 1) for one in highs]
    other_msgs = [flipped(one, 1) for one in msgs]
    slots = [one for pair in zip(highs, other_highs) for one in pair]
    group_x = flipped(group, x_bit)
    groups = [group, flipped(group, 1), group_x, flipped(group_x, 1)]

    width = 2 * planes * rows
    exps, picks, sums, pos, prog_all, trace_all = call(
        functools.partial(score, planes),
        [
            ((8, width), F32),
            ((8, width), F32),
            ((1, width), F32),
            ((1, width), F32),
            ((width, feat), LOW),
            ((8 * rows, feat), LOW),
        ],
        2 * 8 * rows * width * feat,
        4 * width * feat,
    )(*msgs, *other_msgs, *slots)
    all_sums = [sums] + [shifted(sums, k) for k in range(1, planes)]

    prog_parts = call(
        functools.partial(program_terms, planes),
        [((rows, feat), F32)] + [((rows, feat), LOW)] * (planes - 1),
        4 * 8 * rows * planes * rows * feat,
        4 * width * feat,
    )(exps, picks, trace_all)
    prog_back = [prog_parts[0]] + [shifted(prog_parts[k], -k) for k in range(1, planes)]

    total, trace_own, part_x, part_y, part_xy = call(
        functools.partial(trace_terms, planes),
        [((1, rows), F32), ((rows, feat), F32)] + [((rows, feat), LOW)] * 3,
        4 * 4 * rows * width * feat,
        4 * width * feat,
        [pltpu.VMEM((4 * rows, width), LOW)] * 2,
    )(exps, picks, pos, prog_all, *all_sums)
    trace_back = [
        trace_own,
        flipped(part_x, x_bit),
        flipped(part_y, y_bit),
        flipped(part_xy, x_bit + y_bit),
    ]

    group_prog, group_trace, log_group = call(
        group_terms,
        [((rows, feat), F32), ((rows, feat), F32), ((1, rows), F32)],
        6 * 6 * rows * 4 * rows * feat,
        20 * block,
    )(*slots[:4], *groups)

    grad_programs, grad_traces, loss = call(
        functools.partial(finish, planes),
        [((rows, feat), F32), ((rows, feat), F32), ((1, rows), F32)],
        20 * block,
        30 * block,
    )(
        programs,
        traces,
        total,
        log_group,
        group_prog,
        group_trace,
        *prog_back,
        *trace_back,
    )
    return grad_programs, grad_traces, loss.reshape(rows)


def solution(mesh):
    spec = P(("dp", "blk"), None)
    return jax.shard_map(
        functools.partial(on_device, mesh.shape["dp"], mesh.shape["blk"]),
        mesh=mesh,
        in_specs=(spec,) * 4,
        out_specs=(spec, spec, P(("dp", "blk"))),
        check_vma=False,
    )
```

time: 249 us -> 57.8 us (0.23)
  waiting for transfers between devices: 132 us -> 16.9 us
  local copies, waits for them, and re-layouts: 48.3 us -> 2.81 us
  other arithmetic: 36.8 us -> 0 us
  matrix products: 15.2 us -> 0 us
  starting transfers between devices: 14.7 us -> 27.3 us
  Pallas kernels: 0 us -> 9.84 us
    ppermute x7 -> x26, waiting for transfers between devices: 81.9 us -> 16.9 us  [the longest x9 11.9 us: shifted(): lax.ppermute(value, both, [(i, (i + by * plane_size) % size) for i in ran...]
    all_to_all x3 -> x0, waiting for transfers between devices: 50.4 us -> none  [the longest x1 25.9 us: on_device(): lax.all_to_all(answer, ('dp', 'blk'), split_axis=0, concat_axis=0, tiled=...]
    ppermute x7 -> x26, starting transfers between devices: 0.76 us -> 27.3 us  [the longest x9 15.1 us: shifted(): lax.ppermute(value, both, [(i, (i + by * plane_size) % size) for i in ran...]
    gather x2 -> x0, local copies, waits for them, and re-layouts: 23.1 us -> none  [the longest x1 13.2 us: on_device(): answer = trace_low[wanted]]
    scatter-add x1 -> x0, other arithmetic: 20.5 us -> none  [on_device(): grad_back = jnp.zeros((row_count, feat_width), jnp.float32).at[wanted.res...]
    scatter x2 -> x0, local copies, waits for them, and re-layouts: 19.8 us -> none  [the longest x1 11.8 us: on_device(): outgoing = jnp.zeros((owner_count * slot_cap, feat_width), jnp.bfloat16)....]
    dot_general x14 -> x0, matrix products: 15.2 us -> none  [the longest x4 5.92 us: score_block(): jnp.einsum('rd,cd->rc', prog_unit, trace_block, precision=HIGH, preferred...]
    all_to_all x3 -> x0, starting transfers between devices: 14 us -> none  [the longest x1 7.3 us: on_device(): lax.all_to_all(request_buf, ('dp', 'blk'), split_axis=0, concat_axis=0, t...]
  transfers between devices with their start and end apart: 10 -> 26, of which waited for: 10 -> 10; matrix products, arithmetic and copies ran while one was open for 6% -> 0% of each run, Pallas kernels for 0% -> 14%
where the time goes in v1:
time: 57.8 us; the launch traced here: 57.6 us
  starting transfers between devices  27.3 us (47%)
  waiting for transfers between devices  16.9 us (29%)
  Pallas kernels  9.84 us (17%)
  local copies, waits for them, and re-layouts  2.81 us (5%)
  between operations  0.72 us (1%)
    ppermute x9, starting transfers between devices, shifted(): lax.ppermute(value, both, [(i, (i + by * plane_size) % size) for i in ran...  15.1 us
    ppermute x17, starting transfers between devices, flipped(): return lax.ppermute(value, both, [(i, i ^ bits) for i in range(size)])  12.2 us
    ppermute x9, waiting for transfers between devices, shifted(): lax.ppermute(value, both, [(i, (i + by * plane_size) % size) for i in ran...  11.9 us
    ppermute x17, waiting for transfers between devices, flipped(): return lax.ppermute(value, both, [(i, i ^ bits) for i in range(size)])  4.99 us
    pallas_call x1, Pallas kernels, on_device(): call(functools.partial(score, planes), [((8, width), F32), ((8, width), F...  2.9 us
    unnamed x12, local copies, waits for them, and re-layouts  2.81 us
    pallas_call x1, Pallas kernels, on_device(): call(functools.partial(program_terms, planes), [((rows, feat), F32)] + [(...  2.39 us
    pallas_call x1, Pallas kernels, on_device(): call(group_terms, [((rows, feat), F32), ((rows, feat), F32), ((1, rows),...  1.56 us
  transfers between devices with their start and end apart: 26, of which 10 were waited for; matrix products, arithmetic and copies ran while one was open for 0% of the time, Pallas kernels for 14%

profile of v1, /device:TPU:0, one launch (start us, length us, event | category | flops | bytes accessed | tf_op | source)
XLA Modules:
  0.0 57.6 jit_solution(7561723430282223065)
XLA Ops:
  0.6 0.8 %copy.7.owner_ref = s32[128,16]{1,0:T(8,128)S(1)} copy(s32[128,16]{0,1:T(8,128)} %param.6) | data formatting | bytes 16384 | tf_op args[2]
  1.6 0.9 %copy-done = f32[128,512]{1,0:T(8,128)S(1)} copy-done((f32[128,512]{1,0:T(8,128)S(1)}, f32[128,512]{1,0:T(8,128)}, u32[]{:S(2)}) %copy-start) | copy-done | bytes 262168
  2.5 0.9 %copy-done.2 = f32[128,512]{1,0:T(8,128)S(1)} copy-done((f32[128,512]{1,0:T(8,128)S(1)}, f32[128,512]{1,0:T(8,128)}, u32[]{:S(2)}) %copy-start.2) | copy-done | bytes 262168
  3.5 0.3 shard_map.67
  3.8 3.0 %collective-permute-start.8 = (bf16[128,512]{1,0:T(8,128)(2,1)S(1)}, bf16[128,512]{1,0:T(8,128)(2,1)S(1)}, u32[]{:S(2)}, u32[]{:S(2)}) collective-permute-start(bf16[128,512]{1,0:T(8,128)(2,1)S(1)} %get-tuple-element.28.refs_8_.refs_0_), channel_id=1, source_target_pairs={{0,2},{1,3},{2,0},{3,1},{4,6},{5,7},{6,4},{7,5},{8,10},{9,11},{10,... | collective-permute-start | bytes 393224 | tf_op jit(solution)/shard_map/ppermute | solution.py:272
  6.8 1.5 %collective-permute-start.10 = (bf16[128,512]{1,0:T(8,128)(2,1)S(1)}, bf16[128,512]{1,0:T(8,128)(2,1)S(1)}, u32[]{:S(2)}, u32[]{:S(2)}) collective-permute-start(bf16[128,512]{1,0:T(8,128)(2,1)S(1)} %get-tuple-element.28.refs_8_.refs_0_), channel_id=1, source_target_pairs={{0,4},{1,5},{2,6},{3,7},{4,0},{5,1},{6,2},{7,3},{8,12},{9,13},{10,... | collective-permute-start | bytes 393224 | tf_op jit(solution)/shard_map/ppermute | solution.py:272
  8.3 1.9 %collective-permute-start.18 = (bf16[384,512]{1,0:T(8,128)(2,1)S(1)}, bf16[384,512]{1,0:T(8,128)(2,1)S(1)}, u32[]{:S(2)}, u32[]{:S(2)}) collective-permute-start(bf16[384,512]{1,0:T(8,128)(2,1)S(1)} %get-tuple-element.35.refs_4_), channel_id=1, source_target_pairs={{0,2},{1,3},{2,0},{3,1},{4,6},{5,7},{6,4},{7,5},{8,10},{9,11},{10,... | collective-permute-start | bytes 1179656 | tf_op jit(solution)/shard_map/ppermute | solution.py:272
  10.3 0.4 collective-permute-done.8.refs_10_.refs_2_
  10.7 1.8 %collective-permute-start = (bf16[144,512]{1,0:T(8,128)(2,1)S(1)}, bf16[144,512]{1,0:T(8,128)(2,1)S(1)}, u32[]{:S(2)}, u32[]{:S(2)}) collective-permute-start(bf16[144,512]{1,0:T(8,128)(2,1)S(1)} %get-tuple-element.27.refs_0_), channel_id=1, source_target_pairs={{0,8},{1,9},{2,10},{3,11},{4,12},{5,13},{6,14},{7,15},{8,16},{9,17... | collective-permute-start | bytes 442376 | tf_op jit(solution)/shard_map/ppermute | solution.py:276
  12.5 0.9 %collective-permute-done.10.refs_12_ = bf16[128,512]{1,0:T(8,128)(2,1)S(1)} collective-permute-done((bf16[128,512]{1,0:T(8,128)(2,1)S(1)}, bf16[128,512]{1,0:T(8,128)(2,1)S(1)}, u32[]{:S(2)}, u32[]{:S(2)}) %collective-permute-start.10) | collective-permute-done | bytes 131104 | tf_op jit(solution)/shard_map/ppermute | solution.py:272
  13.4 2.6 %collective-permute-start.1 = (bf16[144,512]{1,0:T(8,128)(2,1)S(1)}, bf16[144,512]{1,0:T(8,128)(2,1)S(1)}, u32[]{:S(2)}, u32[]{:S(2)}) collective-permute-start(bf16[144,512]{1,0:T(8,128)(2,1)S(1)} %get-tuple-element.27.refs_0_), channel_id=1, source_target_pairs={{0,16},{1,17},{2,18},{3,19},{4,20},{5,21},{6,22},{7,23},{8,24},{9,... | collective-permute-start | bytes 442376 | tf_op jit(solution)/shard_map/ppermute | solution.py:276
  16.0 3.3 %collective-permute-start.2 = (bf16[144,512]{1,0:T(8,128)(2,1)S(1)}, bf16[144,512]{1,0:T(8,128)(2,1)S(1)}, u32[]{:S(2)}, u32[]{:S(2)}) collective-permute-start(bf16[144,512]{1,0:T(8,128)(2,1)S(1)} %get-tuple-element.27.refs_0_), channel_id=1, source_target_pairs={{0,24},{1,25},{2,26},{3,27},{4,28},{5,29},{6,30},{7,31},{8,0},{9,1... | collective-permute-start | bytes 442376 | tf_op jit(solution)/shard_map/ppermute | solution.py:276
  19.3 0.5 collective-permute-start.9
  19.8 5.0 %collective-permute-done.1.refs_2_ = bf16[144,512]{1,0:T(8,128)(2,1)S(1)} collective-permute-done((bf16[144,512]{1,0:T(8,128)(2,1)S(1)}, bf16[144,512]{1,0:T(8,128)(2,1)S(1)}, u32[]{:S(2)}, u32[]{:S(2)}) %collective-permute-start.1) | collective-permute-done | bytes 147488 | tf_op jit(solution)/shard_map/ppermute | solution.py:276
  24.8 0.5 collective-permute-start.13
  25.4 0.4 collective-permute-start.5
  26.9 0.6 %collective-permute-done.6.refs_7_ = bf16[144,512]{1,0:T(8,128)(2,1)S(1)} collective-permute-done((bf16[144,512]{1,0:T(8,128)(2,1)S(1)}, bf16[144,512]{1,0:T(8,128)(2,1)S(1)}, u32[]{:S(2)}, u32[]{:S(2)}) %collective-permute-start.6) | collective-permute-done | bytes 147488 | tf_op jit(solution)/shard_map/ppermute | solution.py:272
  27.5 2.9 %shard_map.68 = (f32[8,1024]{1,0:T(8,128)S(1)}, f32[8,1024]{1,0:T(8,128)S(1)}, f32[1,1024]{1,0:T(1,128)S(1)}, f32[1,1024]{1,0:T(1,128)S(1)}, bf16[1024,512]{1,0:...) custom-call(bf16[144,512]{1,0:T(8,128)(2,1)S(1)} %get-tuple-element.27.refs_0_, ...), custom_call_target="tpu_custom_call" | custom-call | flops 1073741824 | bytes 2097152 | tf_op jit(solution)/shard_map/pallas_call | solution.py:299
  30.4 2.4 %shard_map.71 = (f32[128,512]{1,0:T(8,128)S(1)}, bf16[128,512]{1,0:T(8,128)(2,1)S(1)}, bf16[128,512]{1,0:T(8,128)(2,1)S(1)}, bf16[128,512]{1,0:T(8,128)(2,1)S(1)}) custom-call(f32[8,1024]{1,0:T(8,128)S(1)} %get-tuple-element.29.exp_ref, f32[8,1024]{1,0:T(8,128)S(1)} %get-tuple-element.30.pick_ref, bf16[1024,512]{1,0:T(8,128)(2,1)S(1)} %get-tuple-element.39.trace_ref), custom_call_target="tpu_custom_call" | custom-call | flops 1073741824 | bytes 2097152 | tf_op jit(solution)/shard_map/pallas_call | solution.py:314
  32.9 4.8 %collective-permute-start.20 = (bf16[128,512]{1,0:T(8,128)(2,1)S(1)}, bf16[128,512]{1,0:T(8,128)(2,1)S(1)}, u32[]{:S(2)}, u32[]{:S(2)}) collective-permute-start(bf16[128,512]{1,0:T(8,128)(2,1)S(1)} %get-tuple-element.41), channel_id=1, source_target_pairs={{0,24},{1,25},{2,26},{3,27},{4,28},{5,29},{6,30},{7,31},{8,0},{9,1... | collective-permute-start | bytes 393224 | tf_op jit(solution)/shard_map/ppermute | solution.py:276
  37.6 0.6 %collective-permute-start.15 = (f32[1,1024]{1,0:T(1,128)S(1)}, f32[1,1024]{1,0:T(1,128)S(1)}, u32[]{:S(2)}, u32[]{:S(2)}) collective-permute-start(f32[1,1024]{1,0:T(1,128)S(1)} %get-tuple-element.33.refs_0_), channel_id=1, source_target_pairs={{0,16},{1,17},{2,18},{3,19},{4,20},{5,21},{6,22},{7,23},{8,24},{9,... | collective-permute-start | bytes 12296 | tf_op jit(solution)/shard_map/ppermute | solution.py:276
  38.2 4.8 %collective-permute-done.14.refs_1_ = f32[1,1024]{1,0:T(1,128)S(1)} collective-permute-done((f32[1,1024]{1,0:T(1,128)S(1)}, f32[1,1024]{1,0:T(1,128)S(1)}, u32[]{:S(2)}, u32[]{:S(2)}) %collective-permute-start.14) | collective-permute-done | bytes 4128 | tf_op jit(solution)/shard_map/ppermute | solution.py:276
  43.0 1.7 %collective-permute-start.21 = (bf16[128,512]{1,0:T(8,128)(2,1)S(1)}, bf16[128,512]{1,0:T(8,128)(2,1)S(1)}, u32[]{:S(2)}, u32[]{:S(2)}) collective-permute-start(bf16[128,512]{1,0:T(8,128)(2,1)S(1)} %get-tuple-element.42), channel_id=1, source_target_pairs={{0,16},{1,17},{2,18},{3,19},{4,20},{5,21},{6,22},{7,23},{8,24},{9,... | collective-permute-start | bytes 393224 | tf_op jit(solution)/shard_map/ppermute | solution.py:276
  44.8 1.9 %collective-permute-done.16.refs_3_ = f32[1,1024]{1,0:T(1,128)S(1)} collective-permute-done((f32[1,1024]{1,0:T(1,128)S(1)}, f32[1,1024]{1,0:T(1,128)S(1)}, u32[]{:S(2)}, u32[]{:S(2)}) %collective-permute-start.16) | collective-permute-done | bytes 4128 | tf_op jit(solution)/shard_map/ppermute | solution.py:276
  46.9 1.3 %shard_map.69 = (f32[1,128]{1,0:T(1,128)S(1)}, f32[128,512]{1,0:T(8,128)S(1)}, bf16[128,512]{1,0:T(8,128)(2,1)S(1)}, bf16[128,512]{1,0:T(8,128)(2,1)S(1)}, bf16[128,512]{1,0:T(8,128)(2,1)S(1)}) custom-call(f32[8,1024]{1,0:T(8,128)S(1)} %get-tuple-element.29.exp_ref, f32[8,1024]{1,0:T(8,128)S(1)} %get-tuple-element.30.pick_ref, ...), custom_call_target="tpu_custom_call" | custom-call | flops 1073741824 | bytes 2097152 | tf_op jit(solution)/shard_map/pallas_call | solution.py:322
  48.3 0.6 %collective-permute-start.23 = (bf16[128,512]{1,0:T(8,128)(2,1)S(1)}, bf16[128,512]{1,0:T(8,128)(2,1)S(1)}, u32[]{:S(2)}, u32[]{:S(2)}) collective-permute-start(bf16[128,512]{1,0:T(8,128)(2,1)S(1)} %get-tuple-element.45), channel_id=1, source_target_pairs={{0,2},{1,3},{2,0},{3,1},{4,6},{5,7},{6,4},{7,5},{8,10},{9,11},{10,... | collective-permute-start | bytes 393224 | tf_op jit(solution)/shard_map/ppermute | solution.py:272
  48.9 1.5 %collective-permute-start.24 = (bf16[128,512]{1,0:T(8,128)(2,1)S(1)}, bf16[128,512]{1,0:T(8,128)(2,1)S(1)}, u32[]{:S(2)}, u32[]{:S(2)}) collective-permute-start(bf16[128,512]{1,0:T(8,128)(2,1)S(1)} %get-tuple-element.46), channel_id=1, source_target_pairs={{0,4},{1,5},{2,6},{3,7},{4,0},{5,1},{6,2},{7,3},{8,12},{9,13},{10,... | collective-permute-start | bytes 393224 | tf_op jit(solution)/shard_map/ppermute | solution.py:272
  50.4 1.4 %collective-permute-start.25 = (bf16[128,512]{1,0:T(8,128)(2,1)S(1)}, bf16[128,512]{1,0:T(8,128)(2,1)S(1)}, u32[]{:S(2)}, u32[]{:S(2)}) collective-permute-start(bf16[128,512]{1,0:T(8,128)(2,1)S(1)} %get-tuple-element.47), channel_id=1, source_target_pairs={{0,6},{1,7},{2,4},{3,5},{4,2},{5,3},{6,0},{7,1},{8,14},{9,15},{10,... | collective-permute-start | bytes 393224 | tf_op jit(solution)/shard_map/ppermute | solution.py:272
  51.9 1.6 %shard_map.70 = (f32[128,512]{1,0:T(8,128)S(1)}, f32[128,512]{1,0:T(8,128)S(1)}, f32[1,128]{1,0:T(1,128)S(1)}) custom-call(bf16[128,512]{1,0:T(8,128)(2,1)S(1)} %get-tuple-element.28.refs_8_.refs_0_, bf16[128,512]{1,0:T(8,128)(2,1)S(1)} %collective-permute-done.7.refs_9_.refs_1_, bf16[128,512]{1,0:T(8,128)(2,1)S(1)} %collective-permute-done.8.refs_10_.refs_2_, ...), custom_call_target="tpu_custom_call" | custom-call | flops 1207959552 | bytes 1310720 | tf_op jit(solution)/shard_map/pallas_call | solution.py:336
  53.7 0.6 %collective-permute-done.24.refs_6_ = bf16[128,512]{1,0:T(8,128)(2,1)S(1)} collective-permute-done((bf16[128,512]{1,0:T(8,128)(2,1)S(1)}, bf16[128,512]{1,0:T(8,128)(2,1)S(1)}, u32[]{:S(2)}, u32[]{:S(2)}) %collective-permute-start.24) | collective-permute-done | bytes 131104 | tf_op jit(solution)/shard_map/ppermute | solution.py:272
  54.3 2.0 %collective-permute-done.25.refs_7_ = bf16[128,512]{1,0:T(8,128)(2,1)S(1)} collective-permute-done((bf16[128,512]{1,0:T(8,128)(2,1)S(1)}, bf16[128,512]{1,0:T(8,128)(2,1)S(1)}, u32[]{:S(2)}, u32[]{:S(2)}) %collective-permute-start.25) | collective-permute-done | bytes 131104 | tf_op jit(solution)/shard_map/ppermute | solution.py:272
  56.3 1.3 %shard_map.72 = (f32[128,512]{1,0:T(8,128)}, f32[128,512]{1,0:T(8,128)}, f32[1,128]{1,0:T(1,128)}) custom-call(f32[128,512]{1,0:T(8,128)S(1)} %copy-done.1, f32[128,512]{1,0:T(8,128)S(1)} %copy-done.3, f32[1,128]{1,0:T(1,128)S(1)} %get-tuple-element.34.total_ref, f32[1,128]{1,0:T(1,128)S(1)} %get-tuple-element.36.log_ref, ...), custom_call_target="tpu_custom_call" | custom-call | flops 1310720 | bytes 1966080 | tf_op jit(solution)/shard_map/pallas_call | solution.py:343
  (38 shorter events, 1.9 us)
Async XLA Ops:
  0.6 0.8 %copy-start.4 = (s32[128,16]{0,1:T(8,128)S(1)}, s32[128,16]{0,1:T(8,128)}, u32[]{:S(2)}) copy-start(s32[128,16]{0,1:T(8,128)} %param.7) | copy-start | bytes 24580
  1.5 1.0 %copy-start = (f32[128,512]{1,0:T(8,128)S(1)}, f32[128,512]{1,0:T(8,128)}, u32[]{:S(2)}) copy-start(f32[128,512]{1,0:T(8,128)} %prog_ref.3) | copy-start | bytes 786436
  2.5 0.9 %copy-start.2 = (f32[128,512]{1,0:T(8,128)S(1)}, f32[128,512]{1,0:T(8,128)}, u32[]{:S(2)}) copy-start(f32[128,512]{1,0:T(8,128)} %trace_ref.3) | copy-start | bytes 786436
  3.8 6.9 %collective-permute-start.8 = (bf16[128,512]{1,0:T(8,128)(2,1)S(1)}, bf16[128,512]{1,0:T(8,128)(2,1)S(1)}, u32[]{:S(2)}, u32[]{:S(2)}) collective-permute-start(bf16[128,512]{1,0:T(8,128)(2,1)S(1)} %get-tuple-element.28.refs_8_.refs_0_), channel_id=1, source_target_pairs={{0,2},{1,3},{2,0},{3,1},{4,6},{5,7},{6,4},{7,5},{8,10},{9,11},{10,... | collective-permute-start | bytes 393224 | tf_op jit(solution)/shard_map/ppermute | solution.py:272
  6.8 6.6 %collective-permute-start.10 = (bf16[128,512]{1,0:T(8,128)(2,1)S(1)}, bf16[128,512]{1,0:T(8,128)(2,1)S(1)}, u32[]{:S(2)}, u32[]{:S(2)}) collective-permute-start(bf16[128,512]{1,0:T(8,128)(2,1)S(1)} %get-tuple-element.28.refs_8_.refs_0_), channel_id=1, source_target_pairs={{0,4},{1,5},{2,6},{3,7},{4,0},{5,1},{6,2},{7,3},{8,12},{9,13},{10,... | collective-permute-start | bytes 393224 | tf_op jit(solution)/shard_map/ppermute | solution.py:272
  8.3 7.7 %collective-permute-start.12 = (bf16[128,512]{1,0:T(8,128)(2,1)S(1)}, bf16[128,512]{1,0:T(8,128)(2,1)S(1)}, u32[]{:S(2)}, u32[]{:S(2)}) collective-permute-start(bf16[128,512]{1,0:T(8,128)(2,1)S(1)} %get-tuple-element.28.refs_8_.refs_0_), channel_id=1, source_target_pairs={{0,6},{1,7},{2,4},{3,5},{4,2},{5,3},{6,0},{7,1},{8,14},{9,15},{10,... | collective-permute-start | bytes 393224 | tf_op jit(solution)/shard_map/ppermute | solution.py:272
  8.3 18.4 %collective-permute-start.18 = (bf16[384,512]{1,0:T(8,128)(2,1)S(1)}, bf16[384,512]{1,0:T(8,128)(2,1)S(1)}, u32[]{:S(2)}, u32[]{:S(2)}) collective-permute-start(bf16[384,512]{1,0:T(8,128)(2,1)S(1)} %get-tuple-element.35.refs_4_), channel_id=1, source_target_pairs={{0,2},{1,3},{2,0},{3,1},{4,6},{5,7},{6,4},{7,5},{8,10},{9,11},{10,... | collective-permute-start | bytes 1179656 | tf_op jit(solution)/shard_map/ppermute | solution.py:272
  10.3 9.0 %collective-permute-start.7 = (bf16[128,512]{1,0:T(8,128)(2,1)S(1)}, bf16[128,512]{1,0:T(8,128)(2,1)S(1)}, u32[]{:S(2)}, u32[]{:S(2)}) collective-permute-start(bf16[128,512]{1,0:T(8,128)(2,1)S(1)} %get-tuple-element.28.refs_8_.refs_0_), channel_id=1, source_target_pairs={{0,1},{1,0},{2,3},{3,2},{4,5},{5,4},{6,7},{7,6},{8,9},{9,8},{10,11... | collective-permute-start | bytes 393224 | tf_op jit(solution)/shard_map/ppermute | solution.py:272
  10.7 8.6 %collective-permute-start = (bf16[144,512]{1,0:T(8,128)(2,1)S(1)}, bf16[144,512]{1,0:T(8,128)(2,1)S(1)}, u32[]{:S(2)}, u32[]{:S(2)}) collective-permute-start(bf16[144,512]{1,0:T(8,128)(2,1)S(1)} %get-tuple-element.27.refs_0_), channel_id=1, source_target_pairs={{0,8},{1,9},{2,10},{3,11},{4,12},{5,13},{6,14},{7,15},{8,16},{9,17... | collective-permute-start | bytes 442376 | tf_op jit(solution)/shard_map/ppermute | solution.py:276
  13.4 11.4 %collective-permute-start.1 = (bf16[144,512]{1,0:T(8,128)(2,1)S(1)}, bf16[144,512]{1,0:T(8,128)(2,1)S(1)}, u32[]{:S(2)}, u32[]{:S(2)}) collective-permute-start(bf16[144,512]{1,0:T(8,128)(2,1)S(1)} %get-tuple-element.27.refs_0_), channel_id=1, source_target_pairs={{0,16},{1,17},{2,18},{3,19},{4,20},{5,21},{6,22},{7,23},{8,24},{9,... | collective-permute-start | bytes 442376 | tf_op jit(solution)/shard_map/ppermute | solution.py:276
  16.0 8.8 %collective-permute-start.2 = (bf16[144,512]{1,0:T(8,128)(2,1)S(1)}, bf16[144,512]{1,0:T(8,128)(2,1)S(1)}, u32[]{:S(2)}, u32[]{:S(2)}) collective-permute-start(bf16[144,512]{1,0:T(8,128)(2,1)S(1)} %get-tuple-element.27.refs_0_), channel_id=1, source_target_pairs={{0,24},{1,25},{2,26},{3,27},{4,28},{5,29},{6,30},{7,31},{8,0},{9,1... | collective-permute-start | bytes 442376 | tf_op jit(solution)/shard_map/ppermute | solution.py:276
  19.3 6.0 %collective-permute-start.3 = (bf16[144,512]{1,0:T(8,128)(2,1)S(1)}, bf16[144,512]{1,0:T(8,128)(2,1)S(1)}, u32[]{:S(2)}, u32[]{:S(2)}) collective-permute-start(bf16[144,512]{1,0:T(8,128)(2,1)S(1)} %get-tuple-element.27.refs_0_), channel_id=1, source_target_pairs={{0,1},{1,0},{2,3},{3,2},{4,5},{5,4},{6,7},{7,6},{8,9},{9,8},{10,11... | collective-permute-start | bytes 442376 | tf_op jit(solution)/shard_map/ppermute | solution.py:272
  19.3 6.1 %collective-permute-start.9 = (bf16[128,512]{1,0:T(8,128)(2,1)S(1)}, bf16[128,512]{1,0:T(8,128)(2,1)S(1)}, u32[]{:S(2)}, u32[]{:S(2)}) collective-permute-start(bf16[128,512]{1,0:T(8,128)(2,1)S(1)} %collective-permute-done.8.refs_10_.refs_2_), channel_id=1, source_target_pairs={{0,1},{1,0},{2,3},{3,2},{4,5},{5,4},{6,7},{7,6},{8,9},{9,8},{10,11... | collective-permute-start | bytes 393224 | tf_op jit(solution)/shard_map/ppermute | solution.py:272
  24.8 1.3 %collective-permute-start.11 = (bf16[128,512]{1,0:T(8,128)(2,1)S(1)}, bf16[128,512]{1,0:T(8,128)(2,1)S(1)}, u32[]{:S(2)}, u32[]{:S(2)}) collective-permute-start(bf16[128,512]{1,0:T(8,128)(2,1)S(1)} %collective-permute-done.10.refs_12_), channel_id=1, source_target_pairs={{0,1},{1,0},{2,3},{3,2},{4,5},{5,4},{6,7},{7,6},{8,9},{9,8},{10,11... | collective-permute-start | bytes 393224 | tf_op jit(solution)/shard_map/ppermute | solution.py:272
  24.8 1.5 %collective-permute-start.13 = (bf16[128,512]{1,0:T(8,128)(2,1)S(1)}, bf16[128,512]{1,0:T(8,128)(2,1)S(1)}, u32[]{:S(2)}, u32[]{:S(2)}) collective-permute-start(bf16[128,512]{1,0:T(8,128)(2,1)S(1)} %collective-permute-done.12.refs_14_), channel_id=1, source_target_pairs={{0,1},{1,0},{2,3},{3,2},{4,5},{5,4},{6,7},{7,6},{8,9},{9,8},{10,11... | collective-permute-start | bytes 393224 | tf_op jit(solution)/shard_map/ppermute | solution.py:272
  25.3 1.5 %collective-permute-start.4 = (bf16[144,512]{1,0:T(8,128)(2,1)S(1)}, bf16[144,512]{1,0:T(8,128)(2,1)S(1)}, u32[]{:S(2)}, u32[]{:S(2)}) collective-permute-start(bf16[144,512]{1,0:T(8,128)(2,1)S(1)} %collective-permute-done.refs_1_), channel_id=1, source_target_pairs={{0,1},{1,0},{2,3},{3,2},{4,5},{5,4},{6,7},{7,6},{8,9},{9,8},{10,11... | collective-permute-start | bytes 442376 | tf_op jit(solution)/shard_map/ppermute | solution.py:272
  25.4 1.5 %collective-permute-start.5 = (bf16[144,512]{1,0:T(8,128)(2,1)S(1)}, bf16[144,512]{1,0:T(8,128)(2,1)S(1)}, u32[]{:S(2)}, u32[]{:S(2)}) collective-permute-start(bf16[144,512]{1,0:T(8,128)(2,1)S(1)} %collective-permute-done.1.refs_2_), channel_id=1, source_target_pairs={{0,1},{1,0},{2,3},{3,2},{4,5},{5,4},{6,7},{7,6},{8,9},{9,8},{10,11... | collective-permute-start | bytes 442376 | tf_op jit(solution)/shard_map/ppermute | solution.py:272
  26.2 1.4 %collective-permute-start.6 = (bf16[144,512]{1,0:T(8,128)(2,1)S(1)}, bf16[144,512]{1,0:T(8,128)(2,1)S(1)}, u32[]{:S(2)}, u32[]{:S(2)}) collective-permute-start(bf16[144,512]{1,0:T(8,128)(2,1)S(1)} %collective-permute-done.2.refs_3_), channel_id=1, source_target_pairs={{0,1},{1,0},{2,3},{3,2},{4,5},{5,4},{6,7},{7,6},{8,9},{9,8},{10,11... | collective-permute-start | bytes 442376 | tf_op jit(solution)/shard_map/ppermute | solution.py:272
  26.4 21.9 %collective-permute-start.17 = (bf16[384,512]{1,0:T(8,128)(2,1)S(1)}, bf16[384,512]{1,0:T(8,128)(2,1)S(1)}, u32[]{:S(2)}, u32[]{:S(2)}) collective-permute-start(bf16[384,512]{1,0:T(8,128)(2,1)S(1)} %get-tuple-element.35.refs_4_), channel_id=1, source_target_pairs={{0,1},{1,0},{2,3},{3,2},{4,5},{5,4},{6,7},{7,6},{8,9},{9,8},{10,11... | collective-permute-start | bytes 1179656 | tf_op jit(solution)/shard_map/ppermute | solution.py:272
  26.7 23.7 %collective-permute-start.19 = (bf16[384,512]{1,0:T(8,128)(2,1)S(1)}, bf16[384,512]{1,0:T(8,128)(2,1)S(1)}, u32[]{:S(2)}, u32[]{:S(2)}) collective-permute-start(bf16[384,512]{1,0:T(8,128)(2,1)S(1)} %collective-permute-done.18.refs_6_), channel_id=1, source_target_pairs={{0,1},{1,0},{2,3},{3,2},{4,5},{5,4},{6,7},{7,6},{8,9},{9,8},{10,11... | collective-permute-start | bytes 1179656 | tf_op jit(solution)/shard_map/ppermute | solution.py:272
  32.9 16.0 %collective-permute-start.20 = (bf16[128,512]{1,0:T(8,128)(2,1)S(1)}, bf16[128,512]{1,0:T(8,128)(2,1)S(1)}, u32[]{:S(2)}, u32[]{:S(2)}) collective-permute-start(bf16[128,512]{1,0:T(8,128)(2,1)S(1)} %get-tuple-element.41), channel_id=1, source_target_pairs={{0,24},{1,25},{2,26},{3,27},{4,28},{5,29},{6,30},{7,31},{8,0},{9,1... | collective-permute-start | bytes 393224 | tf_op jit(solution)/shard_map/ppermute | solution.py:276
  37.6 5.4 %collective-permute-start.14 = (f32[1,1024]{1,0:T(1,128)S(1)}, f32[1,1024]{1,0:T(1,128)S(1)}, u32[]{:S(2)}, u32[]{:S(2)}) collective-permute-start(f32[1,1024]{1,0:T(1,128)S(1)} %get-tuple-element.33.refs_0_), channel_id=1, source_target_pairs={{0,8},{1,9},{2,10},{3,11},{4,12},{5,13},{6,14},{7,15},{8,16},{9,17... | collective-permute-start | bytes 12296 | tf_op jit(solution)/shard_map/ppermute | solution.py:276
  37.6 5.4 %collective-permute-start.15 = (f32[1,1024]{1,0:T(1,128)S(1)}, f32[1,1024]{1,0:T(1,128)S(1)}, u32[]{:S(2)}, u32[]{:S(2)}) collective-permute-start(f32[1,1024]{1,0:T(1,128)S(1)} %get-tuple-element.33.refs_0_), channel_id=1, source_target_pairs={{0,16},{1,17},{2,18},{3,19},{4,20},{5,21},{6,22},{7,23},{8,24},{9,... | collective-permute-start | bytes 12296 | tf_op jit(solution)/shard_map/ppermute | solution.py:276
  43.0 3.6 %collective-permute-start.16 = (f32[1,1024]{1,0:T(1,128)S(1)}, f32[1,1024]{1,0:T(1,128)S(1)}, u32[]{:S(2)}, u32[]{:S(2)}) collective-permute-start(f32[1,1024]{1,0:T(1,128)S(1)} %get-tuple-element.33.refs_0_), channel_id=1, source_target_pairs={{0,24},{1,25},{2,26},{3,27},{4,28},{5,29},{6,30},{7,31},{8,0},{9,1... | collective-permute-start | bytes 12296 | tf_op jit(solution)/shard_map/ppermute | solution.py:276
  43.0 10.7 %collective-permute-start.21 = (bf16[128,512]{1,0:T(8,128)(2,1)S(1)}, bf16[128,512]{1,0:T(8,128)(2,1)S(1)}, u32[]{:S(2)}, u32[]{:S(2)}) collective-permute-start(bf16[128,512]{1,0:T(8,128)(2,1)S(1)} %get-tuple-element.42), channel_id=1, source_target_pairs={{0,16},{1,17},{2,18},{3,19},{4,20},{5,21},{6,22},{7,23},{8,24},{9,... | collective-permute-start | bytes 393224 | tf_op jit(solution)/shard_map/ppermute | solution.py:276
  46.6 7.1 %collective-permute-start.22 = (bf16[128,512]{1,0:T(8,128)(2,1)S(1)}, bf16[128,512]{1,0:T(8,128)(2,1)S(1)}, u32[]{:S(2)}, u32[]{:S(2)}) collective-permute-start(bf16[128,512]{1,0:T(8,128)(2,1)S(1)} %get-tuple-element.43), channel_id=1, source_target_pairs={{0,8},{1,9},{2,10},{3,11},{4,12},{5,13},{6,14},{7,15},{8,16},{9,17... | collective-permute-start | bytes 393224 | tf_op jit(solution)/shard_map/ppermute | solution.py:276
  48.3 5.4 %collective-permute-start.23 = (bf16[128,512]{1,0:T(8,128)(2,1)S(1)}, bf16[128,512]{1,0:T(8,128)(2,1)S(1)}, u32[]{:S(2)}, u32[]{:S(2)}) collective-permute-start(bf16[128,512]{1,0:T(8,128)(2,1)S(1)} %get-tuple-element.45), channel_id=1, source_target_pairs={{0,2},{1,3},{2,0},{3,1},{4,6},{5,7},{6,4},{7,5},{8,10},{9,11},{10,... | collective-permute-start | bytes 393224 | tf_op jit(solution)/shard_map/ppermute | solution.py:272
  48.9 5.4 %collective-permute-start.24 = (bf16[128,512]{1,0:T(8,128)(2,1)S(1)}, bf16[128,512]{1,0:T(8,128)(2,1)S(1)}, u32[]{:S(2)}, u32[]{:S(2)}) collective-permute-start(bf16[128,512]{1,0:T(8,128)(2,1)S(1)} %get-tuple-element.46), channel_id=1, source_target_pairs={{0,4},{1,5},{2,6},{3,7},{4,0},{5,1},{6,2},{7,3},{8,12},{9,13},{10,... | collective-permute-start | bytes 393224 | tf_op jit(solution)/shard_map/ppermute | solution.py:272
  50.4 5.9 %copy-start.1 = (f32[128,512]{1,0:T(8,128)S(1)}, f32[128,512]{1,0:T(8,128)}, u32[]{:S(2)}) copy-start(f32[128,512]{1,0:T(8,128)} %prog_ref.3) | copy-start | bytes 786436
  50.4 5.9 %copy-start.3 = (f32[128,512]{1,0:T(8,128)S(1)}, f32[128,512]{1,0:T(8,128)}, u32[]{:S(2)}) copy-start(f32[128,512]{1,0:T(8,128)} %trace_ref.3) | copy-start | bytes 786436
  50.4 5.9 %collective-permute-start.25 = (bf16[128,512]{1,0:T(8,128)(2,1)S(1)}, bf16[128,512]{1,0:T(8,128)(2,1)S(1)}, u32[]{:S(2)}, u32[]{:S(2)}) collective-permute-start(bf16[128,512]{1,0:T(8,128)(2,1)S(1)} %get-tuple-element.47), channel_id=1, source_target_pairs={{0,6},{1,7},{2,4},{3,5},{4,2},{5,3},{6,0},{7,1},{8,14},{9,15},{10,... | collective-permute-start | bytes 393224 | tf_op jit(solution)/shard_map/ppermute | solution.py:272

commit v2 on v1

v2 whole, which is shorter than its diff:
```python
import functools

import jax
import jax.numpy as jnp
from jax import lax
from jax.experimental import pallas as pl
from jax.experimental.pallas import tpu as pltpu
from jax.sharding import PartitionSpec as P

EPSILON = 1e-06
SCALE = 14.0
LOW = jnp.bfloat16
F32 = jnp.float32
ROWS = 128
VMEM_LIMIT = 40 * 1024 * 1024


def normalize(values):
    length = jnp.sqrt(jnp.sum(values * values, axis=-1, keepdims=True) + EPSILON)
    return values / length, length


def dot(a, b, contract=(1, 0)):
    return lax.dot_general(
        a, b, (((contract[0],), (contract[1],)), ((), ())), preferred_element_type=F32
    )


def halves(values):
    high = values.astype(LOW)
    return high, (values - high.astype(F32)).astype(LOW)


def dot3(a, b, contract=(1, 0)):
    return (
        dot(a[0], b[1], contract) + dot(a[1], b[0], contract)
    ) + dot(a[0], b[0], contract)


def eye():
    shape = (ROWS, ROWS)
    return lax.broadcasted_iota(jnp.int32, shape, 0) == lax.broadcasted_iota(jnp.int32, shape, 1)


def to_row(column):
    return jnp.sum(jnp.where(eye(), column, 0.0), axis=0, keepdims=True)


def to_column(row):
    return jnp.sum(jnp.where(eye(), row, 0.0), axis=1, keepdims=True)


def own_plane():
    return lax.div(lax.axis_index("dp"), 2)


def own_core():
    return lax.rem(lax.axis_index("blk"), 2)


def prepare(planes, *refs):
    sources, msg_refs, refs = refs[:4], refs[4 : 4 + planes], refs[4 + planes :]
    (high_ref, group_ref), buffers, pick_ref, sems = refs[:2], refs[2:6], refs[6], refs[7]
    copies = [
        pltpu.make_async_copy(source, buffer, sems.at[i])
        for i, (source, buffer) in enumerate(zip(sources, buffers))
    ]
    for copy in copies:
        copy.start()
    for copy in copies:
        copy.wait()
    prog_ref, trace_ref, owner_ref, row_ref = buffers
    feat = prog_ref.shape[1]
    neg = owner_ref.shape[0]
    prog_unit, _ = normalize(prog_ref[...])
    trace_unit, _ = normalize(trace_ref[...])
    prog_high, prog_low = halves(prog_unit)
    high_ref[...], group_ref[0:ROWS, :] = halves(trace_unit)
    group_ref[ROWS : 2 * ROWS, :] = prog_high
    group_ref[2 * ROWS : 3 * ROWS, :] = prog_low
    pos = to_row(SCALE * jnp.sum(prog_unit * trace_unit, axis=-1, keepdims=True))
    high = pos.astype(LOW).astype(F32)
    mid = (pos - high).astype(LOW).astype(F32)
    last = pos - high - mid
    line = lax.broadcasted_iota(jnp.int32, (8, ROWS), 0)
    pos_tile = jnp.where(line == 0, high, jnp.where(line == 1, mid, jnp.where(line == 2, last, 0.0)))
    owners = owner_ref[...]
    rows = row_ref[...].astype(F32) + 1.0
    index = lax.broadcasted_iota(jnp.int32, (planes * 8, ROWS), 0)
    picks = jnp.zeros((planes * 8, ROWS), F32)
    for n in range(neg):
        picks = picks + jnp.where(index == owners[n : n + 1, :], rows[n : n + 1, :], 0.0)
    pick_ref[...] = picks
    plane = own_plane()
    rest = jnp.zeros((8, feat - 2 * ROWS), F32)
    for k, msg_ref in enumerate(msg_refs):
        at = pl.multiple_of(8 * lax.rem(plane + k, planes), 8)
        aux = jnp.concatenate([pick_ref[pl.ds(at, 8), :], pos_tile, rest], axis=1)
        msg_ref[0:ROWS, :] = prog_high
        msg_ref[ROWS:, :] = aux.astype(LOW)


def score_block(msgs, trace_ref, exp_ref, pick_ref, pos_ref, prog_ref):
    for b, msg in enumerate(msgs):
        lanes = slice(b * ROWS, (b + 1) * ROWS)
        prog_ref[lanes, :] = msg[0:ROWS, :]
        aux = msg[ROWS:, :].astype(F32)
        pick_ref[:, lanes] = by_slot(aux[:, 0:ROWS])
        pos = aux[:, ROWS : 2 * ROWS]
        pos_ref[:, lanes] = pos[0:1, :] + pos[1:2, :] + pos[2:3, :]
    width = len(msgs) * ROWS
    below = lax.broadcasted_iota(jnp.int32, (ROWS, width), 0).astype(F32) + 1.0
    sums = jnp.zeros((1, width), F32)
    all_scores = dot(trace_ref[...], prog_ref[...], (1, 1))
    for q in range(8):
        scores = all_scores[q * ROWS : (q + 1) * ROWS, :]
        pick = pick_ref[q : q + 1, :]
        found = jnp.sum(jnp.where(below == pick, scores, 0.0), axis=0, keepdims=True)
        exps = jnp.where(pick > 0.0, jnp.exp(SCALE * found), 0.0)
        exp_ref[q : q + 1, :] = exps
        sums = sums + exps
    return sums


def score_first(own_ref, other_ref, *refs):
    traces, (exp_ref, pick_ref, pos_ref, prog_ref, sum_ref, trace_ref) = refs[:8], refs[8:]
    for q in range(8):
        trace_ref[q * ROWS : (q + 1) * ROWS, :] = traces[q][...]
    sum_ref[...] = score_block(
        (own_ref, other_ref), trace_ref, exp_ref, pick_ref, pos_ref, prog_ref
    )


def score_rest(planes, sum_in, trace_ref, *refs):
    count = 2 * planes - 2
    msgs, (exp_ref, pick_ref, pos_ref, prog_ref, sum_ref) = refs[:count], refs[count:]
    sums = score_block(msgs, trace_ref, exp_ref, pick_ref, pos_ref, prog_ref)
    plane, core = own_plane(), own_core()
    for b in range(count + 2):
        part = sum_in[:, b * ROWS : (b + 1) * ROWS] if b < 2 else sums[:, (b - 2) * ROWS : (b - 1) * ROWS]
        sum_ref[:, pl.ds(block_lane(planes, b, plane, core), ROWS)] = part


def by_slot(picks):
    blk = lax.axis_index("blk")
    bits = (lax.rem(blk, 2), lax.div(blk, 2), lax.rem(lax.axis_index("dp"), 2))
    for step, bit in zip((1, 2, 4), bits):
        turned = []
        for at in range(0, 8, 2 * step):
            turned += [picks[at + step : at + 2 * step, :], picks[at : at + step, :]]
        picks = jnp.where(bit == 1, jnp.concatenate(turned, axis=0), picks)
    return picks


def block_lane(planes, b, plane, core):
    source = lax.rem(plane - b // 2 + planes, planes)
    other = 1 - core if b % 2 else core
    return pl.multiple_of((2 * source + other) * ROWS, ROWS)


def program_terms(planes, exp_first, pick_first, exp_rest, pick_rest, trace_ref, _, mark_ref, own_ref, *out_refs):
    def mine(first, rest):
        tiles = [first[:, 0:ROWS]] + [
            rest[:, 2 * k * ROWS : (2 * k + 1) * ROWS] for k in range(planes - 1)
        ]
        return jnp.transpose(jnp.concatenate(tiles, axis=1))

    exps, picks = mine(exp_first, exp_rest), mine(pick_first, pick_rest)
    lanes = lax.broadcasted_iota(jnp.int32, (planes * ROWS, ROWS), 1).astype(F32) + 1.0
    values = [
        jnp.where(lanes == picks[:, q : q + 1], exps[:, q : q + 1], 0.0).astype(LOW)
        for q in range(8)
    ]
    total = dot(jnp.concatenate(values, axis=1), trace_ref[...])
    mark_ref[...] = total[0:8, 0:ROWS]
    own_ref[...] = total[0:ROWS, :]
    for k, out_ref in enumerate(out_refs, 1):
        out_ref[...] = total[k * ROWS : (k + 1) * ROWS, :].astype(LOW)


def trace_terms(planes, *refs):
    firsts, rests, sums, refs = refs[:4], refs[4:8], refs[8 : 8 + planes], refs[9 + planes :]
    total_ref, own_ref, x_ref, y_ref, xy_ref, high_ref, low_ref = refs
    plane, core = own_plane(), own_core()
    below = lax.broadcasted_iota(jnp.int32, (ROWS, ROWS), 0).astype(F32) + 1.0
    for b in range(2 * planes):
        exp_ref, pick_ref, pos_ref, _ = firsts if b < 2 else rests
        at = (b if b < 2 else b - 2) * ROWS
        lane = block_lane(planes, b, plane, core)
        total = jnp.exp(pos_ref[:, at : at + ROWS])
        for one in sums:
            total = total + one[:, pl.ds(lane, ROWS)]
        if b == 0:
            total_ref[...] = total
        scale = SCALE / total
        for i in range(4):
            q = 2 * i
            weight = exp_ref[q : q + 1, at : at + ROWS] * scale
            pick = pick_ref[q : q + 1, at : at + ROWS]
            high, low = halves(jnp.where(below == pick, weight, 0.0))
            high_ref[i * ROWS : (i + 1) * ROWS, b * ROWS : (b + 1) * ROWS] = high
            low_ref[i * ROWS : (i + 1) * ROWS, b * ROWS : (b + 1) * ROWS] = low
    first, rest = firsts[3][...], rests[3][...]
    edge = 2 * ROWS
    result = (
        dot(high_ref[:, 0:edge], first) + dot(low_ref[:, 0:edge], first)
        + dot(high_ref[:, edge:], rest) + dot(low_ref[:, edge:], rest)
    )
    own_ref[...] = result[0:ROWS, :]
    for i, out_ref in enumerate((x_ref, y_ref, xy_ref), 1):
        out_ref[...] = result[i * ROWS : (i + 1) * ROWS, :].astype(LOW)


def group_terms(*refs):
    highs, groups, (programs, traces, total_ref, trace_own) = refs[:4], refs[4:8], refs[8:12]
    prog_base, trace_base, prog_out, trace_out, size_ref, loss_ref = refs[12:]

    def joined(parts):
        return jnp.concatenate(parts, axis=0)

    trace = (joined([h[...] for h in highs]), joined([g[0:ROWS, :] for g in groups]))
    prog = (
        joined([g[ROWS : 2 * ROWS, :] for g in groups]),
        joined([g[2 * ROWS :, :] for g in groups]),
    )
    scores = SCALE * dot3(prog, trace, (1, 1))
    exps = jnp.exp(scores)
    total = jnp.sum(exps, axis=1, keepdims=True)
    weights = exps / total
    prog_unit, prog_len = normalize(programs[...])
    trace_unit, trace_len = normalize(traces[...])
    prog_out[...] = prog_unit
    trace_out[...] = trace_unit
    pos = SCALE * jnp.sum(prog_unit * trace_unit, axis=-1, keepdims=True)
    hard_total = to_column(total_ref[...])
    pull = jnp.exp(pos) / hard_total - 2.0
    lane = lax.broadcasted_iota(jnp.int32, (ROWS, ROWS), 1)
    sizes = jnp.where(lane == 0, prog_len, jnp.where(lane == 1, trace_len, SCALE / hard_total))
    size_ref[...] = sizes
    group_prog = dot3(halves(weights[0:ROWS, :]), trace)
    prog_base[...] = SCALE * (group_prog + pull * trace_unit)
    group_trace = dot3(halves(jnp.transpose(weights[:, 0:ROWS])), prog)
    trace_base[...] = SCALE * (group_trace + pull * prog_unit) + trace_own[...]
    loss_ref[...] = to_row(jnp.log(total[0:ROWS, :]) - 2.0 * pos) + jnp.log(total_ref[...])


def finish(planes, prog_base, trace_base, prog_unit, trace_unit, size_ref, *refs):
    progs, traces, (prog_out, trace_out) = refs[:planes], refs[planes : planes + 3], refs[planes + 3 :]
    back = trace_base[...]
    for one in traces:
        back = back + one[...].astype(F32)
    hard = progs[0][...]
    for one in progs[1:]:
        hard = hard + one[...].astype(F32)
    direction = prog_base[...] + size_ref[:, 2:3] * hard
    for unit, towards, length, out in (
        (prog_unit[...], direction, size_ref[:, 0:1], prog_out),
        (trace_unit[...], back, size_ref[:, 1:2], trace_out),
    ):
        along = jnp.sum(unit * towards, axis=-1, keepdims=True)
        out[...] = (towards - unit * along) / length


def call(body, outs, flops, moved, scratch=(), in_specs=None, limit=VMEM_LIMIT):
    return pl.pallas_call(
        body,
        out_shape=[jax.ShapeDtypeStruct(shape, dtype) for shape, dtype in outs],
        scratch_shapes=list(scratch),
        **({"in_specs": in_specs} if in_specs else {}),
        compiler_params=pltpu.CompilerParams(vmem_limit_bytes=limit),
        cost_estimate=pl.CostEstimate(flops=flops, bytes_accessed=moved, transcendentals=0),
    )


def passed_on(count, *refs):
    for source, target in zip(refs[:count], refs[-count:]):
        target[...] = source[...]


def after(values, *earlier):
    return call(
        functools.partial(passed_on, len(values)),
        [(value.shape, value.dtype) for value in values],
        0,
        0,
    )(*values, *earlier)


def on_device(dp_count, blk_count, programs, traces, hard_owner, hard_row):
    rows, feat = programs.shape
    planes = dp_count // 2
    size = dp_count * blk_count
    both = ("dp", "blk")

    def flipped(value, bits):
        return lax.ppermute(value, both, [(i, i ^ bits) for i in range(size)])

    def shifted(value, by):
        plane_size = 2 * blk_count
        return lax.ppermute(
            value, both, [(i, (i + by * plane_size) % size) for i in range(size)]
        )

    x_bit, y_bit = 2, blk_count
    block = rows * feat
    shape, width = (rows, feat), 2 * rows
    rest = (2 * planes - 2) * rows
    hbm = pl.BlockSpec(memory_space=pltpu.HBM)
    vmem = pl.BlockSpec(memory_space=pltpu.VMEM)
    index = hard_owner.shape[::-1]
    *msgs, high, group = call(
        functools.partial(prepare, planes),
        [((rows + 8, feat), LOW)] * planes + [(shape, LOW), ((3 * rows, feat), LOW)],
        10 * block,
        20 * block,
        [
            pltpu.VMEM(shape, F32),
            pltpu.VMEM(shape, F32),
            pltpu.VMEM(index, jnp.int32),
            pltpu.VMEM(index, jnp.int32),
            pltpu.VMEM((8 * planes, rows), F32),
            pltpu.SemaphoreType.DMA((4,)),
        ],
        [hbm] * 4,
        None,
    )(programs, traces, hard_owner.T, hard_row.T)
    own_msg = msgs[0]
    other_msg = flipped(own_msg, 1)
    high = after([high], other_msg)[0]
    *msgs, group = after([shifted(msgs[k], k) for k in range(1, planes)] + [group])
    group_x = flipped(group, x_bit)
    msgs = [one for msg in msgs for one in (msg, flipped(msg, 1))]
    highs = [high, flipped(high, x_bit), flipped(high, y_bit), flipped(high, x_bit + y_bit)]
    slots = [one for high in highs for one in (high, flipped(high, 1))]

    def lists(width):
        return [((8, width), F32), ((8, width), F32), ((1, width), F32), ((width, feat), LOW)]

    *first, sum_first, trace_all = call(
        score_first,
        lists(width) + [((1, width), F32), ((8 * rows, feat), LOW)],
        16 * rows * width * feat,
        8 * width * feat,
    )(own_msg, other_msg, *slots)
    *others, sums = call(
        functools.partial(score_rest, planes),
        lists(rest) + [((1, width + rest), F32)],
        16 * rows * rest * feat,
        4 * rest * feat,
    )(sum_first, trace_all, *msgs)
    all_sums = [sums] + [shifted(sums, k) for k in range(1, planes)]

    mark, prog_own, *prog_parts = call(
        functools.partial(program_terms, planes),
        [((8, rows), F32), (shape, F32)] + [(shape, LOW)] * (planes - 1),
        16 * rows * planes * rows * feat,
        4 * width * feat,
        (),
        [vmem] * 5 + [vmem],
    )(*first[:2], *others[:2], trace_all, flipped(sums, 1))
    prog_back = [shifted(part, -k) for k, part in enumerate(prog_parts, 1)]

    total, trace_own, part_x, part_y, part_xy = call(
        functools.partial(trace_terms, planes),
        [((1, rows), F32), (shape, F32)] + [(shape, LOW)] * 3,
        16 * rows * (width + rest) * feat,
        4 * width * feat,
        [pltpu.VMEM((4 * rows, width + rest), LOW)] * 2,
        [vmem] * (8 + planes) + [vmem],
    )(*first, *others, *all_sums, flipped(mark, 1))
    trace_back = [
        flipped(part_x, x_bit),
        flipped(part_y, y_bit),
        flipped(part_xy, x_bit + y_bit),
    ]

    group_x = after([group_x], total)[0]
    groups = [group, flipped(group, 1), group_x, flipped(group_x, 1)]
    *bases, loss = call(
        group_terms,
        [(shape, F32)] * 4 + [((rows, rows), F32), ((1, rows), F32)],
        block,
        block,
    )(*slots[:4], *groups, programs, traces, total, trace_own)

    grad_programs, grad_traces = call(
        functools.partial(finish, planes), [(shape, F32)] * 2, block, block
    )(*bases, prog_own, *prog_back, *trace_back)
    return grad_programs, grad_traces, loss.reshape(rows)


def solution(mesh):
    spec = P(("dp", "blk"), None)
    return jax.shard_map(
        functools.partial(on_device, mesh.shape["dp"], mesh.shape["blk"]),
        mesh=mesh,
        in_specs=(spec,) * 4,
        out_specs=(spec, spec, P(("dp", "blk"))),
        check_vma=False,
    )
```

time: 57.8 us -> 52.1 us (0.901)
  waiting for transfers between devices: 16.9 us -> 8.92 us
  starting transfers between devices: 27.3 us -> 31.7 us
  local copies, waits for them, and re-layouts: 2.81 us -> 0.93 us
    ppermute x9, waiting for transfers between devices: 11.9 us -> 7.7 us  [shifted(): lax.ppermute(value, both, [(i, (i + by * plane_size) % size) for i in ran...]
    ppermute x17 -> x19, waiting for transfers between devices: 4.99 us -> 1.22 us  [flipped(): return lax.ppermute(value, both, [(i, i ^ bits) for i in range(size)])]
    ppermute x17 -> x19, starting transfers between devices: 12.2 us -> 14.8 us  [flipped(): return lax.ppermute(value, both, [(i, i ^ bits) for i in range(size)])]
    unnamed x12 -> x10, local copies, waits for them, and re-layouts: 2.81 us -> 0.93 us
    ppermute x9, starting transfers between devices: 15.1 us -> 16.9 us  [shifted(): lax.ppermute(value, both, [(i, (i + by * plane_size) % size) for i in ran...]
    pallas_call x6 -> x10, Pallas kernels: 9.84 us -> 9.6 us  [the longest x1 2.27 us: on_device(): call(functools.partial(prepare, planes), [((rows + 8, feat), LOW)] * plan...]
  transfers between devices with their start and end apart: 26 -> 28, of which waited for: 10 -> 7; matrix products, arithmetic and copies ran while one was open for 0% -> 0% of each run, Pallas kernels for 14% -> 12%
where the time goes in v2:
time: 52.1 us; the launch traced here: 52 us
  starting transfers between devices  31.7 us (61%)
  Pallas kernels  9.6 us (18%)
  waiting for transfers between devices  8.92 us (17%)
  local copies, waits for them, and re-layouts  0.93 us (2%)
  between operations  0.78 us (1%)
    ppermute x9, starting transfers between devices, shifted(): lax.ppermute(value, both, [(i, (i + by * plane_size) % size) for i in ran...  16.9 us
    ppermute x19, starting transfers between devices, flipped(): return lax.ppermute(value, both, [(i, i ^ bits) for i in range(size)])  14.8 us
    ppermute x9, waiting for transfers between devices, shifted(): lax.ppermute(value, both, [(i, (i + by * plane_size) % size) for i in ran...  7.7 us
    pallas_call x1, Pallas kernels, on_device(): call(functools.partial(prepare, planes), [((rows + 8, feat), LOW)] * plan...  2.27 us
    pallas_call x1, Pallas kernels, on_device(): call(group_terms, [(shape, F32)] * 4 + [((rows, rows), F32), ((1, rows),...  2 us
    pallas_call x1, Pallas kernels, on_device(): call(functools.partial(trace_terms, planes), [((1, rows), F32), (shape, F...  1.34 us
    pallas_call x1, Pallas kernels, on_device(): call(functools.partial(program_terms, planes), [((8, rows), F32), (shape,...  1.28 us
    ppermute x19, waiting for transfers between devices, flipped(): return lax.ppermute(value, both, [(i, i ^ bits) for i in range(size)])  1.22 us
  transfers between devices with their start and end apart: 28, of which 7 were waited for; matrix products, arithmetic and copies ran while one was open for 0% of the time, Pallas kernels for 12%

profile of v2, /device:TPU:0, one launch (start us, length us, event | category | flops | bytes accessed | tf_op | source)
XLA Modules:
  0.0 52.0 jit_solution(13311006206925406007)
XLA Ops:
  0.6 2.3 %shard_map.67 = (bf16[136,512]{1,0:T(8,128)(2,1)}, bf16[136,512]{1,0:T(8,128)(2,1)}, bf16[136,512]{1,0:T(8,128)(2,1)}, bf16[136,512]{1,0:T(8,128)(2,1)}, bf16[12...) custom-call(f32[128,512]{1,0:T(8,128)} %refs_8_.1, f32[128,512]{1,0:T(8,128)} %refs_9_.1, s32[16,128]{1,0:T(8,128)} %bitcast.3, ...), custom_call_target="tpu_custom_call" | custom-call | flops 655360 | bytes 1310720 | tf_op jit(solution)/shard_map/pallas_call | solution.py:311
  2.9 0.5 collective-permute-start
  3.4 2.6 %collective-permute-start.4 = (bf16[136,512]{1,0:T(8,128)(2,1)}, bf16[136,512]{1,0:T(8,128)(2,1)S(1)}, u32[]{:S(2)}, u32[]{:S(2)}) collective-permute-start(bf16[136,512]{1,0:T(8,128)(2,1)} %get-tuple-element.44), channel_id=1, source_target_pairs={{0,8},{1,9},{2,10},{3,11},{4,12},{5,13},{6,14},{7,15},{8,16},{9,17... | collective-permute-start | bytes 417800 | tf_op jit(solution)/shard_map/ppermute | solution.py:300
  6.1 2.6 %collective-permute-start.5 = (bf16[136,512]{1,0:T(8,128)(2,1)}, bf16[136,512]{1,0:T(8,128)(2,1)S(1)}, u32[]{:S(2)}, u32[]{:S(2)}) collective-permute-start(bf16[136,512]{1,0:T(8,128)(2,1)} %get-tuple-element.45), channel_id=1, source_target_pairs={{0,16},{1,17},{2,18},{3,19},{4,20},{5,21},{6,22},{7,23},{8,24},{9,... | collective-permute-start | bytes 417800 | tf_op jit(solution)/shard_map/ppermute | solution.py:300
  8.7 0.9 %copy-done.4 = bf16[128,512]{1,0:T(8,128)(2,1)S(1)} copy-done((bf16[128,512]{1,0:T(8,128)(2,1)S(1)}, bf16[128,512]{1,0:T(8,128)(2,1)}, u32[]{:S(2)}) %copy-start.4) | copy-done | bytes 131096
  9.6 1.6 %collective-permute-start.2 = (bf16[128,512]{1,0:T(8,128)(2,1)S(1)}, bf16[128,512]{1,0:T(8,128)(2,1)S(1)}, u32[]{:S(2)}, u32[]{:S(2)}) collective-permute-start(bf16[128,512]{1,0:T(8,128)(2,1)S(1)} %shard_map.68.refs_0_), channel_id=1, source_target_pairs={{0,2},{1,3},{2,0},{3,1},{4,6},{5,7},{6,4},{7,5},{8,10},{9,11},{10,... | collective-permute-start | bytes 393224 | tf_op jit(solution)/shard_map/ppermute | solution.py:296
  11.1 1.5 %collective-permute-start.9 = (bf16[128,512]{1,0:T(8,128)(2,1)S(1)}, bf16[128,512]{1,0:T(8,128)(2,1)S(1)}, u32[]{:S(2)}, u32[]{:S(2)}) collective-permute-start(bf16[128,512]{1,0:T(8,128)(2,1)S(1)} %shard_map.68.refs_0_), channel_id=1, source_target_pairs={{0,4},{1,5},{2,6},{3,7},{4,0},{5,1},{6,2},{7,3},{8,12},{9,13},{10,... | collective-permute-start | bytes 393224 | tf_op jit(solution)/shard_map/ppermute | solution.py:296
  12.7 1.3 %collective-permute-start.6 = (bf16[136,512]{1,0:T(8,128)(2,1)}, bf16[136,512]{1,0:T(8,128)(2,1)S(1)}, u32[]{:S(2)}, u32[]{:S(2)}) collective-permute-start(bf16[136,512]{1,0:T(8,128)(2,1)} %get-tuple-element.46), channel_id=1, source_target_pairs={{0,24},{1,25},{2,26},{3,27},{4,28},{5,29},{6,30},{7,31},{8,0},{9,1... | collective-permute-start | bytes 417800 | tf_op jit(solution)/shard_map/ppermute | solution.py:300
  14.0 1.5 %collective-permute-start.11 = (bf16[128,512]{1,0:T(8,128)(2,1)S(1)}, bf16[128,512]{1,0:T(8,128)(2,1)S(1)}, u32[]{:S(2)}, u32[]{:S(2)}) collective-permute-start(bf16[128,512]{1,0:T(8,128)(2,1)S(1)} %shard_map.68.refs_0_), channel_id=1, source_target_pairs={{0,6},{1,7},{2,4},{3,5},{4,2},{5,3},{6,0},{7,1},{8,14},{9,15},{10,... | collective-permute-start | bytes 393224 | tf_op jit(solution)/shard_map/ppermute | solution.py:296
  15.5 3.2 %collective-permute-done.5.refs_1_ = bf16[136,512]{1,0:T(8,128)(2,1)S(1)} collective-permute-done((bf16[136,512]{1,0:T(8,128)(2,1)}, bf16[136,512]{1,0:T(8,128)(2,1)S(1)}, u32[]{:S(2)}, u32[]{:S(2)}) %collective-permute-start.5) | collective-permute-done | bytes 139296 | tf_op jit(solution)/shard_map/ppermute | solution.py:300
  18.7 0.5 collective-permute-start.3
  19.3 1.4 %collective-permute-done.6.refs_2_ = bf16[136,512]{1,0:T(8,128)(2,1)S(1)} collective-permute-done((bf16[136,512]{1,0:T(8,128)(2,1)}, bf16[136,512]{1,0:T(8,128)(2,1)S(1)}, u32[]{:S(2)}, u32[]{:S(2)}) %collective-permute-start.6) | collective-permute-done | bytes 139296 | tf_op jit(solution)/shard_map/ppermute | solution.py:300
  20.7 0.7 %collective-permute-start.8 = (bf16[384,512]{1,0:T(8,128)(2,1)S(1)}, bf16[384,512]{1,0:T(8,128)(2,1)S(1)}, u32[]{:S(2)}, u32[]{:S(2)}) collective-permute-start(bf16[384,512]{1,0:T(8,128)(2,1)S(1)} %get-tuple-element.48.refs_4_), channel_id=1, source_target_pairs={{0,2},{1,3},{2,0},{3,1},{4,6},{5,7},{6,4},{7,5},{8,10},{9,11},{10,... | collective-permute-start | bytes 1179656 | tf_op jit(solution)/shard_map/ppermute | solution.py:296
  21.4 0.5 collective-permute-start.13
  22.8 0.5 shard_map.70
  23.5 1.1 %shard_map.71 = (f32[8,768]{1,0:T(8,128)S(1)}, f32[8,768]{1,0:T(8,128)S(1)}, f32[1,768]{1,0:T(1,128)S(1)}, bf16[768,512]{1,0:T(8,128)(2,1)S(1)}, f32[1,1024]{1,0:T(1,128)S(1)}) custom-call(f32[1,256]{1,0:T(1,128)S(1)} %get-tuple-element.53.sum_in, bf16[1024,512]{1,0:T(8,128)(2,1)S(1)} %get-tuple-element.54.trace_ref, ...), custom_call_target="tpu_custom_call" | custom-call | flops 805306368 | bytes 1572864 | tf_op jit(solution)/shard_map/pallas_call | solution.py:345
  25.0 2.4 %collective-permute-start.16 = (f32[1,1024]{1,0:T(1,128)S(1)}, f32[1,1024]{1,0:T(1,128)S(1)}, u32[]{:S(2)}, u32[]{:S(2)}) collective-permute-start(f32[1,1024]{1,0:T(1,128)S(1)} %get-tuple-element.62.refs_8_), channel_id=1, source_target_pairs={{0,8},{1,9},{2,10},{3,11},{4,12},{5,13},{6,14},{7,15},{8,16},{9,17... | collective-permute-start | bytes 12296 | tf_op jit(solution)/shard_map/ppermute | solution.py:300
  27.3 2.2 %collective-permute-start.17 = (f32[1,1024]{1,0:T(1,128)S(1)}, f32[1,1024]{1,0:T(1,128)S(1)}, u32[]{:S(2)}, u32[]{:S(2)}) collective-permute-start(f32[1,1024]{1,0:T(1,128)S(1)} %get-tuple-element.62.refs_8_), channel_id=1, source_target_pairs={{0,16},{1,17},{2,18},{3,19},{4,20},{5,21},{6,22},{7,23},{8,24},{9,... | collective-permute-start | bytes 12296 | tf_op jit(solution)/shard_map/ppermute | solution.py:300
  29.5 2.4 %collective-permute-start.18 = (f32[1,1024]{1,0:T(1,128)S(1)}, f32[1,1024]{1,0:T(1,128)S(1)}, u32[]{:S(2)}, u32[]{:S(2)}) collective-permute-start(f32[1,1024]{1,0:T(1,128)S(1)} %get-tuple-element.62.refs_8_), channel_id=1, source_target_pairs={{0,24},{1,25},{2,26},{3,27},{4,28},{5,29},{6,30},{7,31},{8,0},{9,1... | collective-permute-start | bytes 12296 | tf_op jit(solution)/shard_map/ppermute | solution.py:300
  31.9 1.3 %shard_map.72 = (f32[8,128]{1,0:T(8,128)S(1)}, f32[128,512]{1,0:T(8,128)S(1)}, bf16[128,512]{1,0:T(8,128)(2,1)S(1)}, bf16[128,512]{1,0:T(8,128)(2,1)S(1)}, bf16[128,512]{1,0:T(8,128)(2,1)S(1)}) custom-call(f32[8,256]{1,0:T(8,128)S(1)} %get-tuple-element.49.exp_first.refs_0_, f32[8,256]{1,0:T(8,128)S(1)} %get-tuple-element.50.pick_first.refs_1_, ...), custom_call_target="tpu_custom_call" | custom-call | flops 536870912 | bytes 524288 | tf_op jit(solution)/shard_map/pallas_call | solution.py:353
  33.3 0.5 collective-permute-start.7
  33.8 0.6 %collective-permute-done.20.refs_12_ = f32[8,128]{1,0:T(8,128)S(1)} collective-permute-done((f32[8,128]{1,0:T(8,128)S(1)}, f32[8,128]{1,0:T(8,128)S(1)}, u32[]{:S(2)}, u32[]{:S(2)}) %collective-permute-start.20) | collective-permute-done | bytes 4128 | tf_op jit(solution)/shard_map/ppermute | solution.py:296
  34.4 1.3 %shard_map.73 = (f32[1,128]{1,0:T(1,128)S(1)}, f32[128,512]{1,0:T(8,128)S(1)}, bf16[128,512]{1,0:T(8,128)(2,1)S(1)}, bf16[128,512]{1,0:T(8,128)(2,1)S(1)}, bf16[128,512]{1,0:T(8,128)(2,1)S(1)}) custom-call(f32[8,256]{1,0:T(8,128)S(1)} %get-tuple-element.49.exp_first.refs_0_, f32[8,256]{1,0:T(8,128)S(1)} %get-tuple-element.50.pick_first.refs_1_, ...), custom_call_target="tpu_custom_call" | custom-call | flops 1073741824 | bytes 524288 | tf_op jit(solution)/shard_map/pallas_call | solution.py:363
  36.0 2.8 %collective-permute-start.22 = (bf16[128,512]{1,0:T(8,128)(2,1)S(1)}, bf16[128,512]{1,0:T(8,128)(2,1)S(1)}, u32[]{:S(2)}, u32[]{:S(2)}) collective-permute-start(bf16[128,512]{1,0:T(8,128)(2,1)S(1)} %get-tuple-element.72), channel_id=1, source_target_pairs={{0,24},{1,25},{2,26},{3,27},{4,28},{5,29},{6,30},{7,31},{8,0},{9,1... | collective-permute-start | bytes 393224 | tf_op jit(solution)/shard_map/ppermute | solution.py:300
  38.8 0.7 %collective-permute-start.24 = (bf16[128,512]{1,0:T(8,128)(2,1)S(1)}, bf16[128,512]{1,0:T(8,128)(2,1)S(1)}, u32[]{:S(2)}, u32[]{:S(2)}) collective-permute-start(bf16[128,512]{1,0:T(8,128)(2,1)S(1)} %get-tuple-element.74), channel_id=1, source_target_pairs={{0,8},{1,9},{2,10},{3,11},{4,12},{5,13},{6,14},{7,15},{8,16},{9,17... | collective-permute-start | bytes 393224 | tf_op jit(solution)/shard_map/ppermute | solution.py:300
  39.5 2.4 %collective-permute-start.25 = (bf16[128,512]{1,0:T(8,128)(2,1)S(1)}, bf16[128,512]{1,0:T(8,128)(2,1)S(1)}, u32[]{:S(2)}, u32[]{:S(2)}) collective-permute-start(bf16[128,512]{1,0:T(8,128)(2,1)S(1)} %get-tuple-element.75), channel_id=1, source_target_pairs={{0,2},{1,3},{2,0},{3,1},{4,6},{5,7},{6,4},{7,5},{8,10},{9,11},{10,... | collective-permute-start | bytes 393224 | tf_op jit(solution)/shard_map/ppermute | solution.py:296
  41.9 0.8 %collective-permute-done.22.refs_1_ = bf16[128,512]{1,0:T(8,128)(2,1)S(1)} collective-permute-done((bf16[128,512]{1,0:T(8,128)(2,1)S(1)}, bf16[128,512]{1,0:T(8,128)(2,1)S(1)}, u32[]{:S(2)}, u32[]{:S(2)}) %collective-permute-start.22) | collective-permute-done | bytes 131104 | tf_op jit(solution)/shard_map/ppermute | solution.py:300
  42.7 1.7 %collective-permute-start.26 = (bf16[128,512]{1,0:T(8,128)(2,1)S(1)}, bf16[128,512]{1,0:T(8,128)(2,1)S(1)}, u32[]{:S(2)}, u32[]{:S(2)}) collective-permute-start(bf16[128,512]{1,0:T(8,128)(2,1)S(1)} %get-tuple-element.76), channel_id=1, source_target_pairs={{0,4},{1,5},{2,6},{3,7},{4,0},{5,1},{6,2},{7,3},{8,12},{9,13},{10,... | collective-permute-start | bytes 393224 | tf_op jit(solution)/shard_map/ppermute | solution.py:296
  44.5 2.1 %collective-permute-start.27 = (bf16[128,512]{1,0:T(8,128)(2,1)S(1)}, bf16[128,512]{1,0:T(8,128)(2,1)S(1)}, u32[]{:S(2)}, u32[]{:S(2)}) collective-permute-start(bf16[128,512]{1,0:T(8,128)(2,1)S(1)} %get-tuple-element.77), channel_id=1, source_target_pairs={{0,6},{1,7},{2,4},{3,5},{4,2},{5,3},{6,0},{7,1},{8,14},{9,15},{10,... | collective-permute-start | bytes 393224 | tf_op jit(solution)/shard_map/ppermute | solution.py:296
  46.6 2.0 %shard_map.75 = (f32[128,512]{1,0:T(8,128)S(1)}, f32[128,512]{1,0:T(8,128)S(1)}, f32[128,512]{1,0:T(8,128)S(1)}, f32[128,512]{1,0:T(8,128)S(1)}, f32[128,128]{1,0:T(8,128)S(1)}, /*index=5*/f32[1,128]{1,0:T(1,128)}) custom-call(bf16[128,512]{1,0:T(8,128)(2,1)S(1)} %shard_map.68.refs_0_, bf16[128,512]{1,0:T(8,128)(2,1)S(1)} %collective-permute-done.1.refs_1_, ...), custom_call_target="tpu_custom_call" | custom-call | flops 65536 | bytes 65536 | tf_op jit(solution)/shard_map/pallas_call | solution.py:379
  48.6 2.3 %collective-permute-done.23.refs_2_ = bf16[128,512]{1,0:T(8,128)(2,1)S(1)} collective-permute-done((bf16[128,512]{1,0:T(8,128)(2,1)S(1)}, bf16[128,512]{1,0:T(8,128)(2,1)S(1)}, u32[]{:S(2)}, u32[]{:S(2)}) %collective-permute-start.23) | collective-permute-done | bytes 131104 | tf_op jit(solution)/shard_map/ppermute | solution.py:300
  50.9 1.0 %shard_map.76 = (f32[128,512]{1,0:T(8,128)}, f32[128,512]{1,0:T(8,128)}) custom-call(f32[128,512]{1,0:T(8,128)S(1)} %get-tuple-element.66.prog_base, f32[128,512]{1,0:T(8,128)S(1)} %get-tuple-element.67.trace_base, f32[128,512]{1,0:T(8,128)S(1)} %get-tuple-element.68.prog_unit, f32[128,512]{1,0:T(8,128)S(1)} %get-tuple-element.69.trace_unit, ...), custom_call_target="tpu_custom_call" | custom-call | flops 65536 | bytes 65536 | tf_op jit(solution)/shard_map/pallas_call | solution.py:386
  (44 shorter events, 2.0 us)
Async XLA Ops:
  2.9 17.8 %copy-start.2 = (bf16[384,512]{1,0:T(8,128)(2,1)S(1)}, bf16[384,512]{1,0:T(8,128)(2,1)}, u32[]{:S(2)}) copy-start(bf16[384,512]{1,0:T(8,128)(2,1)} %get-tuple-element.47.refs_3_) | copy-start | bytes 1179652
  2.9 5.7 %collective-permute-start = (bf16[136,512]{1,0:T(8,128)(2,1)}, bf16[136,512]{1,0:T(8,128)(2,1)S(1)}, u32[]{:S(2)}, u32[]{:S(2)}) collective-permute-start(bf16[136,512]{1,0:T(8,128)(2,1)} %get-tuple-element.43.own_ref), channel_id=1, source_target_pairs={{0,1},{1,0},{2,3},{3,2},{4,5},{5,4},{6,7},{7,6},{8,9},{9,8},{10,11... | collective-permute-start | bytes 417800 | tf_op jit(solution)/shard_map/ppermute | solution.py:296
  3.4 10.6 %collective-permute-start.4 = (bf16[136,512]{1,0:T(8,128)(2,1)}, bf16[136,512]{1,0:T(8,128)(2,1)S(1)}, u32[]{:S(2)}, u32[]{:S(2)}) collective-permute-start(bf16[136,512]{1,0:T(8,128)(2,1)} %get-tuple-element.44), channel_id=1, source_target_pairs={{0,8},{1,9},{2,10},{3,11},{4,12},{5,13},{6,14},{7,15},{8,16},{9,17... | collective-permute-start | bytes 417800 | tf_op jit(solution)/shard_map/ppermute | solution.py:300
  6.1 12.6 %collective-permute-start.5 = (bf16[136,512]{1,0:T(8,128)(2,1)}, bf16[136,512]{1,0:T(8,128)(2,1)S(1)}, u32[]{:S(2)}, u32[]{:S(2)}) collective-permute-start(bf16[136,512]{1,0:T(8,128)(2,1)} %get-tuple-element.45), channel_id=1, source_target_pairs={{0,16},{1,17},{2,18},{3,19},{4,20},{5,21},{6,22},{7,23},{8,24},{9,... | collective-permute-start | bytes 417800 | tf_op jit(solution)/shard_map/ppermute | solution.py:300
  9.6 9.1 %collective-permute-start.2 = (bf16[128,512]{1,0:T(8,128)(2,1)S(1)}, bf16[128,512]{1,0:T(8,128)(2,1)S(1)}, u32[]{:S(2)}, u32[]{:S(2)}) collective-permute-start(bf16[128,512]{1,0:T(8,128)(2,1)S(1)} %shard_map.68.refs_0_), channel_id=1, source_target_pairs={{0,2},{1,3},{2,0},{3,1},{4,6},{5,7},{6,4},{7,5},{8,10},{9,11},{10,... | collective-permute-start | bytes 393224 | tf_op jit(solution)/shard_map/ppermute | solution.py:296
  11.1 8.1 %collective-permute-start.9 = (bf16[128,512]{1,0:T(8,128)(2,1)S(1)}, bf16[128,512]{1,0:T(8,128)(2,1)S(1)}, u32[]{:S(2)}, u32[]{:S(2)}) collective-permute-start(bf16[128,512]{1,0:T(8,128)(2,1)S(1)} %shard_map.68.refs_0_), channel_id=1, source_target_pairs={{0,4},{1,5},{2,6},{3,7},{4,0},{5,1},{6,2},{7,3},{8,12},{9,13},{10,... | collective-permute-start | bytes 393224 | tf_op jit(solution)/shard_map/ppermute | solution.py:296
  12.7 8.0 %collective-permute-start.6 = (bf16[136,512]{1,0:T(8,128)(2,1)}, bf16[136,512]{1,0:T(8,128)(2,1)S(1)}, u32[]{:S(2)}, u32[]{:S(2)}) collective-permute-start(bf16[136,512]{1,0:T(8,128)(2,1)} %get-tuple-element.46), channel_id=1, source_target_pairs={{0,24},{1,25},{2,26},{3,27},{4,28},{5,29},{6,30},{7,31},{8,0},{9,1... | collective-permute-start | bytes 417800 | tf_op jit(solution)/shard_map/ppermute | solution.py:300
  14.0 7.4 %collective-permute-start.11 = (bf16[128,512]{1,0:T(8,128)(2,1)S(1)}, bf16[128,512]{1,0:T(8,128)(2,1)S(1)}, u32[]{:S(2)}, u32[]{:S(2)}) collective-permute-start(bf16[128,512]{1,0:T(8,128)(2,1)S(1)} %shard_map.68.refs_0_), channel_id=1, source_target_pairs={{0,6},{1,7},{2,4},{3,5},{4,2},{5,3},{6,0},{7,1},{8,14},{9,15},{10,... | collective-permute-start | bytes 393224 | tf_op jit(solution)/shard_map/ppermute | solution.py:296
  18.7 2.7 %collective-permute-start.1 = (bf16[128,512]{1,0:T(8,128)(2,1)S(1)}, bf16[128,512]{1,0:T(8,128)(2,1)S(1)}, u32[]{:S(2)}, u32[]{:S(2)}) collective-permute-start(bf16[128,512]{1,0:T(8,128)(2,1)S(1)} %shard_map.68.refs_0_), channel_id=1, source_target_pairs={{0,1},{1,0},{2,3},{3,2},{4,5},{5,4},{6,7},{7,6},{8,9},{9,8},{10,11... | collective-permute-start | bytes 393224 | tf_op jit(solution)/shard_map/ppermute | solution.py:296
  18.7 3.2 %collective-permute-start.3 = (bf16[128,512]{1,0:T(8,128)(2,1)S(1)}, bf16[128,512]{1,0:T(8,128)(2,1)S(1)}, u32[]{:S(2)}, u32[]{:S(2)}) collective-permute-start(bf16[128,512]{1,0:T(8,128)(2,1)S(1)} %collective-permute-done.2.refs_2_), channel_id=1, source_target_pairs={{0,1},{1,0},{2,3},{3,2},{4,5},{5,4},{6,7},{7,6},{8,9},{9,8},{10,11... | collective-permute-start | bytes 393224 | tf_op jit(solution)/shard_map/ppermute | solution.py:296
  19.2 2.8 %collective-permute-start.10 = (bf16[128,512]{1,0:T(8,128)(2,1)S(1)}, bf16[128,512]{1,0:T(8,128)(2,1)S(1)}, u32[]{:S(2)}, u32[]{:S(2)}) collective-permute-start(bf16[128,512]{1,0:T(8,128)(2,1)S(1)} %collective-permute-done.9.refs_4_), channel_id=1, source_target_pairs={{0,1},{1,0},{2,3},{3,2},{4,5},{5,4},{6,7},{7,6},{8,9},{9,8},{10,11... | collective-permute-start | bytes 393224 | tf_op jit(solution)/shard_map/ppermute | solution.py:296
  20.7 2.1 %copy-start.3 = (bf16[136,512]{1,0:T(8,128)(2,1)S(1)}, bf16[136,512]{1,0:T(8,128)(2,1)}, u32[]{:S(2)}) copy-start(bf16[136,512]{1,0:T(8,128)(2,1)} %get-tuple-element.43.own_ref) | copy-start | bytes 417796
  20.7 15.0 %collective-permute-start.8 = (bf16[384,512]{1,0:T(8,128)(2,1)S(1)}, bf16[384,512]{1,0:T(8,128)(2,1)S(1)}, u32[]{:S(2)}, u32[]{:S(2)}) collective-permute-start(bf16[384,512]{1,0:T(8,128)(2,1)S(1)} %get-tuple-element.48.refs_4_), channel_id=1, source_target_pairs={{0,2},{1,3},{2,0},{3,1},{4,6},{5,7},{6,4},{7,5},{8,10},{9,11},{10,... | collective-permute-start | bytes 1179656 | tf_op jit(solution)/shard_map/ppermute | solution.py:296
  21.4 1.3 %collective-permute-start.12 = (bf16[128,512]{1,0:T(8,128)(2,1)S(1)}, bf16[128,512]{1,0:T(8,128)(2,1)S(1)}, u32[]{:S(2)}, u32[]{:S(2)}) collective-permute-start(bf16[128,512]{1,0:T(8,128)(2,1)S(1)} %collective-permute-done.11.refs_6_), channel_id=1, source_target_pairs={{0,1},{1,0},{2,3},{3,2},{4,5},{5,4},{6,7},{7,6},{8,9},{9,8},{10,11... | collective-permute-start | bytes 393224 | tf_op jit(solution)/shard_map/ppermute | solution.py:296
  21.4 1.8 %collective-permute-start.13 = (bf16[136,512]{1,0:T(8,128)(2,1)S(1)}, bf16[136,512]{1,0:T(8,128)(2,1)S(1)}, u32[]{:S(2)}, u32[]{:S(2)}) collective-permute-start(bf16[136,512]{1,0:T(8,128)(2,1)S(1)} %get-tuple-element.55.refs_0_), channel_id=1, source_target_pairs={{0,1},{1,0},{2,3},{3,2},{4,5},{5,4},{6,7},{7,6},{8,9},{9,8},{10,11... | collective-permute-start | bytes 417800 | tf_op jit(solution)/shard_map/ppermute | solution.py:296
  21.9 1.4 %collective-permute-start.14 = (bf16[136,512]{1,0:T(8,128)(2,1)S(1)}, bf16[136,512]{1,0:T(8,128)(2,1)S(1)}, u32[]{:S(2)}, u32[]{:S(2)}) collective-permute-start(bf16[136,512]{1,0:T(8,128)(2,1)S(1)} %get-tuple-element.56.refs_2_), channel_id=1, source_target_pairs={{0,1},{1,0},{2,3},{3,2},{4,5},{5,4},{6,7},{7,6},{8,9},{9,8},{10,11... | collective-permute-start | bytes 417800 | tf_op jit(solution)/shard_map/ppermute | solution.py:296
  22.0 1.5 %collective-permute-start.15 = (bf16[136,512]{1,0:T(8,128)(2,1)S(1)}, bf16[136,512]{1,0:T(8,128)(2,1)S(1)}, u32[]{:S(2)}, u32[]{:S(2)}) collective-permute-start(bf16[136,512]{1,0:T(8,128)(2,1)S(1)} %get-tuple-element.57.refs_4_), channel_id=1, source_target_pairs={{0,1},{1,0},{2,3},{3,2},{4,5},{5,4},{6,7},{7,6},{8,9},{9,8},{10,11... | collective-permute-start | bytes 417800 | tf_op jit(solution)/shard_map/ppermute | solution.py:296
  24.6 7.3 %collective-permute-start.19 = (f32[1,1024]{1,0:T(1,128)S(1)}, f32[1,1024]{1,0:T(1,128)S(1)}, u32[]{:S(2)}, u32[]{:S(2)}) collective-permute-start(f32[1,1024]{1,0:T(1,128)S(1)} %get-tuple-element.62.refs_8_), channel_id=1, source_target_pairs={{0,1},{1,0},{2,3},{3,2},{4,5},{5,4},{6,7},{7,6},{8,9},{9,8},{10,11... | collective-permute-start | bytes 12296 | tf_op jit(solution)/shard_map/ppermute | solution.py:296
  25.0 8.3 %collective-permute-start.16 = (f32[1,1024]{1,0:T(1,128)S(1)}, f32[1,1024]{1,0:T(1,128)S(1)}, u32[]{:S(2)}, u32[]{:S(2)}) collective-permute-start(f32[1,1024]{1,0:T(1,128)S(1)} %get-tuple-element.62.refs_8_), channel_id=1, source_target_pairs={{0,8},{1,9},{2,10},{3,11},{4,12},{5,13},{6,14},{7,15},{8,16},{9,17... | collective-permute-start | bytes 12296 | tf_op jit(solution)/shard_map/ppermute | solution.py:300
  27.3 6.4 %collective-permute-start.17 = (f32[1,1024]{1,0:T(1,128)S(1)}, f32[1,1024]{1,0:T(1,128)S(1)}, u32[]{:S(2)}, u32[]{:S(2)}) collective-permute-start(f32[1,1024]{1,0:T(1,128)S(1)} %get-tuple-element.62.refs_8_), channel_id=1, source_target_pairs={{0,16},{1,17},{2,18},{3,19},{4,20},{5,21},{6,22},{7,23},{8,24},{9,... | collective-permute-start | bytes 12296 | tf_op jit(solution)/shard_map/ppermute | solution.py:300
  29.5 4.2 %collective-permute-start.18 = (f32[1,1024]{1,0:T(1,128)S(1)}, f32[1,1024]{1,0:T(1,128)S(1)}, u32[]{:S(2)}, u32[]{:S(2)}) collective-permute-start(f32[1,1024]{1,0:T(1,128)S(1)} %get-tuple-element.62.refs_8_), channel_id=1, source_target_pairs={{0,24},{1,25},{2,26},{3,27},{4,28},{5,29},{6,30},{7,31},{8,0},{9,1... | collective-permute-start | bytes 12296 | tf_op jit(solution)/shard_map/ppermute | solution.py:300
  33.2 1.2 %collective-permute-start.20 = (f32[8,128]{1,0:T(8,128)S(1)}, f32[8,128]{1,0:T(8,128)S(1)}, u32[]{:S(2)}, u32[]{:S(2)}) collective-permute-start(f32[8,128]{1,0:T(8,128)S(1)} %get-tuple-element.63), channel_id=1, source_target_pairs={{0,1},{1,0},{2,3},{3,2},{4,5},{5,4},{6,7},{7,6},{8,9},{9,8},{10,11... | collective-permute-start | bytes 12296 | tf_op jit(solution)/shard_map/ppermute | solution.py:296
  33.3 6.2 %collective-permute-start.7 = (bf16[384,512]{1,0:T(8,128)(2,1)S(1)}, bf16[384,512]{1,0:T(8,128)(2,1)S(1)}, u32[]{:S(2)}, u32[]{:S(2)}) collective-permute-start(bf16[384,512]{1,0:T(8,128)(2,1)S(1)} %get-tuple-element.48.refs_4_), channel_id=1, source_target_pairs={{0,1},{1,0},{2,3},{3,2},{4,5},{5,4},{6,7},{7,6},{8,9},{9,8},{10,11... | collective-permute-start | bytes 1179656 | tf_op jit(solution)/shard_map/ppermute | solution.py:296
  35.8 10.9 %copy-start = (f32[128,512]{1,0:T(8,128)S(1)}, f32[128,512]{1,0:T(8,128)}, u32[]{:S(2)}) copy-start(f32[128,512]{1,0:T(8,128)} %refs_8_.1) | copy-start | bytes 786436
  35.8 10.9 %copy-start.1 = (f32[128,512]{1,0:T(8,128)S(1)}, f32[128,512]{1,0:T(8,128)}, u32[]{:S(2)}) copy-start(f32[128,512]{1,0:T(8,128)} %refs_9_.1) | copy-start | bytes 786436
  35.8 8.7 %collective-permute-start.21 = (bf16[384,512]{1,0:T(8,128)(2,1)S(1)}, bf16[384,512]{1,0:T(8,128)(2,1)S(1)}, u32[]{:S(2)}, u32[]{:S(2)}) collective-permute-start(bf16[384,512]{1,0:T(8,128)(2,1)S(1)} %shard_map.74.refs_6_), channel_id=1, source_target_pairs={{0,1},{1,0},{2,3},{3,2},{4,5},{5,4},{6,7},{7,6},{8,9},{9,8},{10,11... | collective-permute-start | bytes 1179656 | tf_op jit(solution)/shard_map/ppermute | solution.py:296
  36.0 6.7 %collective-permute-start.22 = (bf16[128,512]{1,0:T(8,128)(2,1)S(1)}, bf16[128,512]{1,0:T(8,128)(2,1)S(1)}, u32[]{:S(2)}, u32[]{:S(2)}) collective-permute-start(bf16[128,512]{1,0:T(8,128)(2,1)S(1)} %get-tuple-element.72), channel_id=1, source_target_pairs={{0,24},{1,25},{2,26},{3,27},{4,28},{5,29},{6,30},{7,31},{8,0},{9,1... | collective-permute-start | bytes 393224 | tf_op jit(solution)/shard_map/ppermute | solution.py:300
  38.8 12.1 %collective-permute-start.23 = (bf16[128,512]{1,0:T(8,128)(2,1)S(1)}, bf16[128,512]{1,0:T(8,128)(2,1)S(1)}, u32[]{:S(2)}, u32[]{:S(2)}) collective-permute-start(bf16[128,512]{1,0:T(8,128)(2,1)S(1)} %get-tuple-element.73), channel_id=1, source_target_pairs={{0,16},{1,17},{2,18},{3,19},{4,20},{5,21},{6,22},{7,23},{8,24},{9,... | collective-permute-start | bytes 393224 | tf_op jit(solution)/shard_map/ppermute | solution.py:300
  38.8 12.1 %collective-permute-start.24 = (bf16[128,512]{1,0:T(8,128)(2,1)S(1)}, bf16[128,512]{1,0:T(8,128)(2,1)S(1)}, u32[]{:S(2)}, u32[]{:S(2)}) collective-permute-start(bf16[128,512]{1,0:T(8,128)(2,1)S(1)} %get-tuple-element.74), channel_id=1, source_target_pairs={{0,8},{1,9},{2,10},{3,11},{4,12},{5,13},{6,14},{7,15},{8,16},{9,17... | collective-permute-start | bytes 393224 | tf_op jit(solution)/shard_map/ppermute | solution.py:300
  39.5 11.4 %collective-permute-start.25 = (bf16[128,512]{1,0:T(8,128)(2,1)S(1)}, bf16[128,512]{1,0:T(8,128)(2,1)S(1)}, u32[]{:S(2)}, u32[]{:S(2)}) collective-permute-start(bf16[128,512]{1,0:T(8,128)(2,1)S(1)} %get-tuple-element.75), channel_id=1, source_target_pairs={{0,2},{1,3},{2,0},{3,1},{4,6},{5,7},{6,4},{7,5},{8,10},{9,11},{10,... | collective-permute-start | bytes 393224 | tf_op jit(solution)/shard_map/ppermute | solution.py:296
  42.7 8.2 %collective-permute-start.26 = (bf16[128,512]{1,0:T(8,128)(2,1)S(1)}, bf16[128,512]{1,0:T(8,128)(2,1)S(1)}, u32[]{:S(2)}, u32[]{:S(2)}) collective-permute-start(bf16[128,512]{1,0:T(8,128)(2,1)S(1)} %get-tuple-element.76), channel_id=1, source_target_pairs={{0,4},{1,5},{2,6},{3,7},{4,0},{5,1},{6,2},{7,3},{8,12},{9,13},{10,... | collective-permute-start | bytes 393224 | tf_op jit(solution)/shard_map/ppermute | solution.py:296
  44.5 6.4 %collective-permute-start.27 = (bf16[128,512]{1,0:T(8,128)(2,1)S(1)}, bf16[128,512]{1,0:T(8,128)(2,1)S(1)}, u32[]{:S(2)}, u32[]{:S(2)}) collective-permute-start(bf16[128,512]{1,0:T(8,128)(2,1)S(1)} %get-tuple-element.77), channel_id=1, source_target_pairs={{0,6},{1,7},{2,4},{3,5},{4,2},{5,3},{6,0},{7,1},{8,14},{9,15},{10,... | collective-permute-start | bytes 393224 | tf_op jit(solution)/shard_map/ppermute | solution.py:296
  (1 other events, 0.9 us)

commit v3 on v2

--- a/solution.py
+++ b/solution.py
@@ -12,6 +12,7 @@
 LOW = jnp.bfloat16
 F32 = jnp.float32
 ROWS = 128
+AHEAD = 2 * 10**9
 VMEM_LIMIT = 40 * 1024 * 1024
 
 
@@ -50,8 +51,8 @@
     return jnp.sum(jnp.where(eye(), row, 0.0), axis=1, keepdims=True)
 
 
-def own_plane():
-    return lax.div(lax.axis_index("dp"), 2)
+def own_plane(planes):
+    return lax.rem(lax.axis_index("dp"), planes)
 
 
 def own_core():
@@ -60,7 +61,7 @@
 
 def prepare(planes, *refs):
     sources, msg_refs, refs = refs[:4], refs[4 : 4 + planes], refs[4 + planes :]
-    (high_ref, group_ref), buffers, pick_ref, sems = refs[:2], refs[2:6], refs[6], refs[7]
+    high_ref, buffers, pick_ref, sems = refs[0], refs[1:5], refs[5], refs[6]
     copies = [
         pltpu.make_async_copy(source, buffer, sems.at[i])
         for i, (source, buffer) in enumerate(zip(sources, buffers))
@@ -74,10 +75,8 @@
     neg = owner_ref.shape[0]
     prog_unit, _ = normalize(prog_ref[...])
     trace_unit, _ = normalize(trace_ref[...])
-    prog_high, prog_low = halves(prog_unit)
-    high_ref[...], group_ref[0:ROWS, :] = halves(trace_unit)
-    group_ref[ROWS : 2 * ROWS, :] = prog_high
-    group_ref[2 * ROWS : 3 * ROWS, :] = prog_low
+    prog_high = prog_unit.astype(LOW)
+    high_ref[...] = trace_unit.astype(LOW)
     pos = to_row(SCALE * jnp.sum(prog_unit * trace_unit, axis=-1, keepdims=True))
     high = pos.astype(LOW).astype(F32)
     mid = (pos - high).astype(LOW).astype(F32)
@@ -86,26 +85,32 @@
     pos_tile = jnp.where(line == 0, high, jnp.where(line == 1, mid, jnp.where(line == 2, last, 0.0)))
     owners = owner_ref[...]
     rows = row_ref[...].astype(F32) + 1.0
-    index = lax.broadcasted_iota(jnp.int32, (planes * 8, ROWS), 0)
+    line = lax.broadcasted_iota(jnp.int32, (planes * 8, ROWS), 0)
+    index = (lax.shift_right_logical(line, 2) & 1) * (4 * planes) + lax.shift_right_logical(line, 3) * 4 + (line & 3)
     picks = jnp.zeros((planes * 8, ROWS), F32)
     for n in range(neg):
         picks = picks + jnp.where(index == owners[n : n + 1, :], rows[n : n + 1, :], 0.0)
     pick_ref[...] = picks
-    plane = own_plane()
+    plane = own_plane(planes)
     rest = jnp.zeros((8, feat - 2 * ROWS), F32)
     for k, msg_ref in enumerate(msg_refs):
-        at = pl.multiple_of(8 * lax.rem(plane + k, planes), 8)
+        at = pl.multiple_of(8 * (plane ^ k), 8)
         aux = jnp.concatenate([pick_ref[pl.ds(at, 8), :], pos_tile, rest], axis=1)
         msg_ref[0:ROWS, :] = prog_high
         msg_ref[ROWS:, :] = aux.astype(LOW)
 
 
-def score_block(msgs, trace_ref, exp_ref, pick_ref, pos_ref, prog_ref):
+def group_parts(prog_ref, trace_ref, *refs):
+    _, refs[-1][0:ROWS, :] = halves(normalize(trace_ref[...])[0])
+    refs[-1][ROWS : 2 * ROWS, :], refs[-1][2 * ROWS :, :] = halves(normalize(prog_ref[...])[0])
+
+
+def score_block(planes, msgs, trace_ref, exp_ref, pick_ref, pos_ref, prog_ref):
     for b, msg in enumerate(msgs):
         lanes = slice(b * ROWS, (b + 1) * ROWS)
         prog_ref[lanes, :] = msg[0:ROWS, :]
         aux = msg[ROWS:, :].astype(F32)
-        pick_ref[:, lanes] = by_slot(aux[:, 0:ROWS])
+        pick_ref[:, lanes] = by_slot(planes, aux[:, 0:ROWS])
         pos = aux[:, ROWS : 2 * ROWS]
         pos_ref[:, lanes] = pos[0:1, :] + pos[1:2, :] + pos[2:3, :]
     width = len(msgs) * ROWS
@@ -122,28 +127,28 @@
     return sums
 
 
-def score_first(own_ref, other_ref, *refs):
+def score_first(planes, own_ref, other_ref, *refs):
     traces, (exp_ref, pick_ref, pos_ref, prog_ref, sum_ref, trace_ref) = refs[:8], refs[8:]
     for q in range(8):
         trace_ref[q * ROWS : (q + 1) * ROWS, :] = traces[q][...]
     sum_ref[...] = score_block(
-        (own_ref, other_ref), trace_ref, exp_ref, pick_ref, pos_ref, prog_ref
+        planes, (own_ref, other_ref), trace_ref, exp_ref, pick_ref, pos_ref, prog_ref
     )
 
 
 def score_rest(planes, sum_in, trace_ref, *refs):
     count = 2 * planes - 2
     msgs, (exp_ref, pick_ref, pos_ref, prog_ref, sum_ref) = refs[:count], refs[count:]
-    sums = score_block(msgs, trace_ref, exp_ref, pick_ref, pos_ref, prog_ref)
-    plane, core = own_plane(), own_core()
+    sums = score_block(planes, msgs, trace_ref, exp_ref, pick_ref, pos_ref, prog_ref)
+    plane, core = own_plane(planes), own_core()
     for b in range(count + 2):
         part = sum_in[:, b * ROWS : (b + 1) * ROWS] if b < 2 else sums[:, (b - 2) * ROWS : (b - 1) * ROWS]
-        sum_ref[:, pl.ds(block_lane(planes, b, plane, core), ROWS)] = part
-
-
-def by_slot(picks):
+        sum_ref[:, pl.ds(block_lane(b, plane, core), ROWS)] = part
+
+
+def by_slot(planes, picks):
     blk = lax.axis_index("blk")
-    bits = (lax.rem(blk, 2), lax.div(blk, 2), lax.rem(lax.axis_index("dp"), 2))
+    bits = (lax.rem(blk, 2), lax.div(blk, 2), lax.div(lax.axis_index("dp"), planes))
     for step, bit in zip((1, 2, 4), bits):
         turned = []
         for at in range(0, 8, 2 * step):
@@ -152,10 +157,8 @@
     return picks
 
 
-def block_lane(planes, b, plane, core):
-    source = lax.rem(plane - b // 2 + planes, planes)
-    other = 1 - core if b % 2 else core
-    return pl.multiple_of((2 * source + other) * ROWS, ROWS)
+def block_lane(b, plane, core):
+    return pl.multiple_of((2 * (plane ^ (b // 2)) + (core ^ (b % 2))) * ROWS, ROWS)
 
 
 def program_terms(planes, exp_first, pick_first, exp_rest, pick_rest, trace_ref, _, mark_ref, own_ref, *out_refs):
@@ -180,13 +183,13 @@
 
 def trace_terms(planes, *refs):
     firsts, rests, sums, refs = refs[:4], refs[4:8], refs[8 : 8 + planes], refs[9 + planes :]
-    total_ref, own_ref, x_ref, y_ref, xy_ref, high_ref, low_ref = refs
-    plane, core = own_plane(), own_core()
+    total_ref, own_ref, x_ref, h_ref, xh_ref, high_ref, low_ref = refs
+    plane, core = own_plane(planes), own_core()
     below = lax.broadcasted_iota(jnp.int32, (ROWS, ROWS), 0).astype(F32) + 1.0
     for b in range(2 * planes):
         exp_ref, pick_ref, pos_ref, _ = firsts if b < 2 else rests
         at = (b if b < 2 else b - 2) * ROWS
-        lane = block_lane(planes, b, plane, core)
+        lane = block_lane(b, plane, core)
         total = jnp.exp(pos_ref[:, at : at + ROWS])
         for one in sums:
             total = total + one[:, pl.ds(lane, ROWS)]
@@ -207,22 +210,25 @@
         + dot(high_ref[:, edge:], rest) + dot(low_ref[:, edge:], rest)
     )
     own_ref[...] = result[0:ROWS, :]
-    for i, out_ref in enumerate((x_ref, y_ref, xy_ref), 1):
-        out_ref[...] = result[i * ROWS : (i + 1) * ROWS, :].astype(LOW)
+    for i, out_ref in enumerate((x_ref, h_ref, xh_ref), 1):
+        out_ref[...] = result[i * ROWS : (i + 1) * ROWS, :].astype(out_ref.dtype)
+
+
+def added(own_ref, other_ref, x_ref, out_ref, x_out):
+    out_ref[...] = (own_ref[...] + other_ref[...].astype(F32)).astype(LOW)
+    x_out[...] = x_ref[...]
 
 
 def group_terms(*refs):
-    highs, groups, (programs, traces, total_ref, trace_own) = refs[:4], refs[4:8], refs[8:12]
-    prog_base, trace_base, prog_out, trace_out, size_ref, loss_ref = refs[12:]
-
-    def joined(parts):
-        return jnp.concatenate(parts, axis=0)
-
-    trace = (joined([h[...] for h in highs]), joined([g[0:ROWS, :] for g in groups]))
-    prog = (
-        joined([g[ROWS : 2 * ROWS, :] for g in groups]),
-        joined([g[2 * ROWS :, :] for g in groups]),
-    )
+    highs, groups, (programs, traces, total_ref, trace_own) = refs[:4], refs[4:6], refs[6:10]
+    prog_base, trace_base, prog_out, trace_out, size_ref, loss_ref = refs[10:]
+
+    def part(which):
+        at = [(x * 3 + which) * ROWS for x in range(2)]
+        return jnp.concatenate([g[a : a + ROWS, :] for a in at for g in groups], axis=0)
+
+    trace = (jnp.concatenate([h[...] for h in highs], axis=0), part(0))
+    prog = (part(1), part(2))
     scores = SCALE * dot3(prog, trace, (1, 1))
     exps = jnp.exp(scores)
     total = jnp.sum(exps, axis=1, keepdims=True)
@@ -245,7 +251,7 @@
 
 
 def finish(planes, prog_base, trace_base, prog_unit, trace_unit, size_ref, *refs):
-    progs, traces, (prog_out, trace_out) = refs[:planes], refs[planes : planes + 3], refs[planes + 3 :]
+    progs, traces, (prog_out, trace_out) = refs[:planes], refs[planes : planes + 2], refs[planes + 2 :]
     back = trace_base[...]
     for one in traces:
         back = back + one[...].astype(F32)
@@ -272,16 +278,21 @@
     )
 
 
+def joined(own_ref, x_ref, _, out_ref):
+    out_ref[0 : 3 * ROWS, :] = own_ref[...]
+    out_ref[3 * ROWS :, :] = x_ref[...]
+
+
 def passed_on(count, *refs):
     for source, target in zip(refs[:count], refs[-count:]):
         target[...] = source[...]
 
 
-def after(values, *earlier):
+def after(values, *earlier, cost=0):
     return call(
         functools.partial(passed_on, len(values)),
         [(value.shape, value.dtype) for value in values],
-        0,
+        cost,
         0,
     )(*values, *earlier)
 
@@ -295,22 +306,19 @@
     def flipped(value, bits):
         return lax.ppermute(value, both, [(i, i ^ bits) for i in range(size)])
 
-    def shifted(value, by):
-        plane_size = 2 * blk_count
-        return lax.ppermute(
-            value, both, [(i, (i + by * plane_size) % size) for i in range(size)]
-        )
-
-    x_bit, y_bit = 2, blk_count
+    def to_plane(value, k):
+        return flipped(value, k * blk_count)
+
+    x_bit, h_bit = 2, planes * blk_count
     block = rows * feat
     shape, width = (rows, feat), 2 * rows
     rest = (2 * planes - 2) * rows
     hbm = pl.BlockSpec(memory_space=pltpu.HBM)
     vmem = pl.BlockSpec(memory_space=pltpu.VMEM)
     index = hard_owner.shape[::-1]
-    *msgs, high, group = call(
+    *sent, high = call(
         functools.partial(prepare, planes),
-        [((rows + 8, feat), LOW)] * planes + [(shape, LOW), ((3 * rows, feat), LOW)],
+        [((rows + 8, feat), LOW)] * planes + [(shape, LOW)],
         10 * block,
         20 * block,
         [
@@ -324,31 +332,33 @@
         [hbm] * 4,
         None,
     )(programs, traces, hard_owner.T, hard_row.T)
-    own_msg = msgs[0]
-    other_msg = flipped(own_msg, 1)
-    high = after([high], other_msg)[0]
-    *msgs, group = after([shifted(msgs[k], k) for k in range(1, planes)] + [group])
+    far_first = list(range(planes - 1, 0, -1))
+    high_h = flipped(high, h_bit)
+    msgs = [sent[0], *after([to_plane(sent[k], k) for k in far_first], cost=AHEAD)[::-1]]
+    highs = [high, flipped(high, x_bit), high_h, flipped(high_h, x_bit)]
+    group = call(group_parts, [((3 * rows, feat), LOW)], 10 * block, 20 * block)(
+        programs, traces, high_h
+    )[0]
+    msgs = [one for k in range(planes) for one in (msgs[k], flipped(msgs[k], 1))]
+    slots = [one for high in highs for one in (high, flipped(high, 1))]
     group_x = flipped(group, x_bit)
-    msgs = [one for msg in msgs for one in (msg, flipped(msg, 1))]
-    highs = [high, flipped(high, x_bit), flipped(high, y_bit), flipped(high, x_bit + y_bit)]
-    slots = [one for high in highs for one in (high, flipped(high, 1))]
 
     def lists(width):
         return [((8, width), F32), ((8, width), F32), ((1, width), F32), ((width, feat), LOW)]
 
     *first, sum_first, trace_all = call(
-        score_first,
+        functools.partial(score_first, planes),
         lists(width) + [((1, width), F32), ((8 * rows, feat), LOW)],
         16 * rows * width * feat,
         8 * width * feat,
-    )(own_msg, other_msg, *slots)
+    )(*msgs[:2], *slots)
     *others, sums = call(
         functools.partial(score_rest, planes),
         lists(rest) + [((1, width + rest), F32)],
         16 * rows * rest * feat,
         4 * rest * feat,
-    )(sum_first, trace_all, *msgs)
-    all_sums = [sums] + [shifted(sums, k) for k in range(1, planes)]
+    )(sum_first, trace_all, *msgs[2:])
+    all_sums = [sums] + [to_plane(sums, k) for k in far_first]
 
     mark, prog_own, *prog_parts = call(
         functools.partial(program_terms, planes),
@@ -358,30 +368,27 @@
         (),
         [vmem] * 5 + [vmem],
     )(*first[:2], *others[:2], trace_all, flipped(sums, 1))
-    prog_back = [shifted(part, -k) for k, part in enumerate(prog_parts, 1)]
-
-    total, trace_own, part_x, part_y, part_xy = call(
+    total, trace_own, part_x, part_h, part_xh = call(
         functools.partial(trace_terms, planes),
-        [((1, rows), F32), (shape, F32)] + [(shape, LOW)] * 3,
+        [((1, rows), F32), (shape, F32), (shape, LOW), (shape, F32), (shape, LOW)],
         16 * rows * (width + rest) * feat,
         4 * width * feat,
         [pltpu.VMEM((4 * rows, width + rest), LOW)] * 2,
         [vmem] * (8 + planes) + [vmem],
     )(*first, *others, *all_sums, flipped(mark, 1))
-    trace_back = [
-        flipped(part_x, x_bit),
-        flipped(part_y, y_bit),
-        flipped(part_xy, x_bit + y_bit),
-    ]
-
-    group_x = after([group_x], total)[0]
-    groups = [group, flipped(group, 1), group_x, flipped(group_x, 1)]
+    for_h, part_x = call(added, [(shape, LOW)] * 2, block, 4 * block)(
+        part_h, flipped(part_xh, x_bit), part_x
+    )
+    trace_back = [flipped(for_h, h_bit), flipped(part_x, x_bit)]
+
+    groups = call(joined, [((6 * rows, feat), LOW)], 0, 0)(group, group_x, total)[0]
+    prog_back = [to_plane(part, k) for k, part in enumerate(prog_parts, 1)]
     *bases, loss = call(
         group_terms,
         [(shape, F32)] * 4 + [((rows, rows), F32), ((1, rows), F32)],
         block,
         block,
-    )(*slots[:4], *groups, programs, traces, total, trace_own)
+    )(*slots[:4], groups, flipped(groups, 1), programs, traces, total, trace_own)
 
     grad_programs, grad_traces = call(
         functools.partial(finish, planes), [(shape, F32)] * 2, block, block

time: 52.1 us -> 47.4 us (0.910)
  starting transfers between devices: 31.7 us -> 27.5 us
  local copies, waits for them, and re-layouts: 0.93 us -> 0.02 us
    ppermute x9 -> x0, starting transfers between devices: 16.9 us -> none  [shifted(): lax.ppermute(value, both, [(i, (i + by * plane_size) % size) for i in ran...]
    ppermute x19 -> x27, starting transfers between devices: 14.8 us -> 27.5 us  [flipped(): return lax.ppermute(value, both, [(i, i ^ bits) for i in range(size)])]
    ppermute x19 -> x27, waiting for transfers between devices: 1.22 us -> 9.09 us  [flipped(): return lax.ppermute(value, both, [(i, i ^ bits) for i in range(size)])]
    ppermute x9 -> x0, waiting for transfers between devices: 7.7 us -> none  [shifted(): lax.ppermute(value, both, [(i, (i + by * plane_size) % size) for i in ran...]
    unnamed x10 -> x8, local copies, waits for them, and re-layouts: 0.93 us -> 0.02 us
  transfers between devices with their start and end apart: 28 -> 27, of which waited for: 7 -> 12; matrix products, arithmetic and copies ran while one was open for 0% -> 0% of each run, Pallas kernels for 12% -> 14%
where the time goes in v3:
time: 47.4 us; the launch traced here: 47.2 us
  starting transfers between devices  27.5 us (58%)
  Pallas kernels  9.83 us (21%)
  waiting for transfers between devices  9.09 us (19%)
  between operations  0.81 us (2%)
    ppermute x27, starting transfers between devices, flipped(): return lax.ppermute(value, both, [(i, i ^ bits) for i in range(size)])  27.5 us
    ppermute x27, waiting for transfers between devices, flipped(): return lax.ppermute(value, both, [(i, i ^ bits) for i in range(size)])  9.09 us
    pallas_call x1, Pallas kernels, on_device(): call(functools.partial(prepare, planes), [((rows + 8, feat), LOW)] * plan...  2.22 us
    pallas_call x1, Pallas kernels, on_device(): call(group_terms, [(shape, F32)] * 4 + [((rows, rows), F32), ((1, rows),...  2.05 us
    pallas_call x1, Pallas kernels, on_device(): call(functools.partial(trace_terms, planes), [((1, rows), F32), (shape, F...  1.34 us
    pallas_call x1, Pallas kernels, on_device(): call(functools.partial(program_terms, planes), [((8, rows), F32), (shape,...  1.28 us
    pallas_call x1, Pallas kernels, on_device(): call(functools.partial(score_rest, planes), lists(rest) + [((1, width + r...  1.1 us
    pallas_call x1, Pallas kernels, on_device(): call(functools.partial(finish, planes), [(shape, F32)] * 2, block, block)  1.04 us
  transfers between devices with their start and end apart: 27, of which 12 were waited for; matrix products, arithmetic and copies ran while one was open for 0% of the time, Pallas kernels for 14%

profile of v3, /device:TPU:0, one launch (start us, length us, event | category | flops | bytes accessed | tf_op | source)
XLA Modules:
  0.0 47.2 jit_solution(4319220083444980014)
XLA Ops:
  0.7 2.2 %shard_map.67 = (bf16[136,512]{1,0:T(8,128)(2,1)}, bf16[136,512]{1,0:T(8,128)(2,1)}, bf16[136,512]{1,0:T(8,128)(2,1)}, bf16[136,512]{1,0:T(8,128)(2,1)}, bf16[128,512]{1,0:T(8,128)(2,1)}) custom-call(f32[128,512]{1,0:T(8,128)} %refs_6_.1, f32[128,512]{1,0:T(8,128)} %refs_7_.1, s32[16,128]{1,0:T(8,128)} %bitcast.3, s32[16,128]{1,0:T(8,128)} %bitcast.4), custom_call_target="tpu_custom_call" | custom-call | flops 655360 | bytes 1310720 | tf_op jit(solution)/shard_map/pallas_call | solution.py:319
  2.9 4.1 %collective-permute-start.3 = (bf16[128,512]{1,0:T(8,128)(2,1)}, bf16[128,512]{1,0:T(8,128)(2,1)S(1)}, u32[]{:S(2)}, u32[]{:S(2)}) collective-permute-start(bf16[128,512]{1,0:T(8,128)(2,1)} %get-tuple-element.42.refs_0_), channel_id=1, source_target_pairs={{0,16},{1,17},{2,18},{3,19},{4,20},{5,21},{6,22},{7,23},{8,24},{9,... | collective-permute-start | bytes 393224 | tf_op jit(solution)/shard_map/ppermute | solution.py:307
  7.0 1.5 %collective-permute-start.1 = (bf16[128,512]{1,0:T(8,128)(2,1)}, bf16[128,512]{1,0:T(8,128)(2,1)S(1)}, u32[]{:S(2)}, u32[]{:S(2)}) collective-permute-start(bf16[128,512]{1,0:T(8,128)(2,1)} %get-tuple-element.42.refs_0_), channel_id=1, source_target_pairs={{0,2},{1,3},{2,0},{3,1},{4,6},{5,7},{6,4},{7,5},{8,10},{9,11},{10,... | collective-permute-start | bytes 393224 | tf_op jit(solution)/shard_map/ppermute | solution.py:307
  8.5 2.5 %collective-permute-start.9 = (bf16[136,512]{1,0:T(8,128)(2,1)}, bf16[136,512]{1,0:T(8,128)(2,1)S(1)}, u32[]{:S(2)}, u32[]{:S(2)}) collective-permute-start(bf16[136,512]{1,0:T(8,128)(2,1)} %get-tuple-element.50), channel_id=1, source_target_pairs={{0,12},{1,13},{2,14},{3,15},{4,8},{5,9},{6,10},{7,11},{8,4},{9,5},... | collective-permute-start | bytes 417800 | tf_op jit(solution)/shard_map/ppermute | solution.py:307
  11.0 0.4 collective-permute-start.10
  11.5 0.5 %collective-permute-start.11 = (bf16[136,512]{1,0:T(8,128)(2,1)}, bf16[136,512]{1,0:T(8,128)(2,1)S(1)}, u32[]{:S(2)}, u32[]{:S(2)}) collective-permute-start(bf16[136,512]{1,0:T(8,128)(2,1)} %get-tuple-element.52), channel_id=1, source_target_pairs={{0,4},{1,5},{2,6},{3,7},{4,0},{5,1},{6,2},{7,3},{8,12},{9,13},{10,... | collective-permute-start | bytes 417800 | tf_op jit(solution)/shard_map/ppermute | solution.py:307
  12.0 1.6 %collective-permute-done.3.refs_0_.refs_4_ = bf16[128,512]{1,0:T(8,128)(2,1)S(1)} collective-permute-done((bf16[128,512]{1,0:T(8,128)(2,1)}, bf16[128,512]{1,0:T(8,128)(2,1)S(1)}, u32[]{:S(2)}, u32[]{:S(2)}) %collective-permute-start.3) | collective-permute-done | bytes 131104 | tf_op jit(solution)/shard_map/ppermute | solution.py:307
  13.6 1.5 %collective-permute-start.7 = (bf16[128,512]{1,0:T(8,128)(2,1)S(1)}, bf16[128,512]{1,0:T(8,128)(2,1)S(1)}, u32[]{:S(2)}, u32[]{:S(2)}) collective-permute-start(bf16[128,512]{1,0:T(8,128)(2,1)S(1)} %collective-permute-done.3.refs_0_.refs_4_), channel_id=1, source_target_pairs={{0,2},{1,3},{2,0},{3,1},{4,6},{5,7},{6,4},{7,5},{8,10},{9,11},{10,... | collective-permute-start | bytes 393224 | tf_op jit(solution)/shard_map/ppermute | solution.py:307
  15.7 1.5 %collective-permute-done.9.refs_0_ = bf16[136,512]{1,0:T(8,128)(2,1)S(1)} collective-permute-done((bf16[136,512]{1,0:T(8,128)(2,1)}, bf16[136,512]{1,0:T(8,128)(2,1)S(1)}, u32[]{:S(2)}, u32[]{:S(2)}) %collective-permute-start.9) | collective-permute-done | bytes 139296 | tf_op jit(solution)/shard_map/ppermute | solution.py:307
  17.2 1.1 %collective-permute-start.4 = (bf16[384,512]{1,0:T(8,128)(2,1)S(1)}, bf16[384,512]{1,0:T(8,128)(2,1)S(1)}, u32[]{:S(2)}, u32[]{:S(2)}) collective-permute-start(bf16[384,512]{1,0:T(8,128)(2,1)S(1)} %shard_map.68.own_ref), channel_id=1, source_target_pairs={{0,2},{1,3},{2,0},{3,1},{4,6},{5,7},{6,4},{7,5},{8,10},{9,11},{10,... | collective-permute-start | bytes 1179656 | tf_op jit(solution)/shard_map/ppermute | solution.py:307
  18.3 0.9 %collective-permute-done.10.refs_1_ = bf16[136,512]{1,0:T(8,128)(2,1)S(1)} collective-permute-done((bf16[136,512]{1,0:T(8,128)(2,1)}, bf16[136,512]{1,0:T(8,128)(2,1)S(1)}, u32[]{:S(2)}, u32[]{:S(2)}) %collective-permute-start.10) | collective-permute-done | bytes 139296 | tf_op jit(solution)/shard_map/ppermute | solution.py:307
  19.1 0.5 %collective-permute-start.2 = (bf16[128,512]{1,0:T(8,128)(2,1)S(1)}, bf16[128,512]{1,0:T(8,128)(2,1)S(1)}, u32[]{:S(2)}, u32[]{:S(2)}) collective-permute-start(bf16[128,512]{1,0:T(8,128)(2,1)S(1)} %collective-permute-done.1.refs_2_), channel_id=1, source_target_pairs={{0,1},{1,0},{2,3},{3,2},{4,5},{5,4},{6,7},{7,6},{8,9},{9,8},{10,11... | collective-permute-start | bytes 393224 | tf_op jit(solution)/shard_map/ppermute | solution.py:307
  19.9 0.6 %collective-permute-start.12 = (bf16[136,512]{1,0:T(8,128)(2,1)S(1)}, bf16[136,512]{1,0:T(8,128)(2,1)S(1)}, u32[]{:S(2)}, u32[]{:S(2)}) collective-permute-start(bf16[136,512]{1,0:T(8,128)(2,1)S(1)} %get-tuple-element.53.refs_0_), channel_id=1, source_target_pairs={{0,1},{1,0},{2,3},{3,2},{4,5},{5,4},{6,7},{7,6},{8,9},{9,8},{10,11... | collective-permute-start | bytes 417800 | tf_op jit(solution)/shard_map/ppermute | solution.py:307
  21.3 0.5 %shard_map.69 = (f32[8,256]{1,0:T(8,128)S(1)}, f32[8,256]{1,0:T(8,128)S(1)}, f32[1,256]{1,0:T(1,128)S(1)}, bf16[256,512]{1,0:T(8,128)(2,1)S(1)}, f32[1,256]{1,0:T(1,128)S(1)}, /*index=5*/bf16[1024,512]{1,0:T(8,128)(2,1)S(1)}) custom-call(bf16[136,512]{1,0:T(8,128)(2,1)S(1)} %copy-done.3, bf16[136,512]{1,0:T(8,128)(2,1)S(1)} %collective-permute-done.5.other_ref, ...), custom_call_target="tpu_custom_call" | custom-call | flops 268435456 | bytes 1048576 | tf_op jit(solution)/shard_map/pallas_call | solution.py:349
  22.1 1.1 %shard_map.71 = (f32[8,768]{1,0:T(8,128)S(1)}, f32[8,768]{1,0:T(8,128)S(1)}, f32[1,768]{1,0:T(1,128)S(1)}, bf16[768,512]{1,0:T(8,128)(2,1)S(1)}, f32[1,1024]{1,0:T(1,128)S(1)}) custom-call(f32[1,256]{1,0:T(1,128)S(1)} %get-tuple-element.48.sum_in, bf16[1024,512]{1,0:T(8,128)(2,1)S(1)} %get-tuple-element.49.trace_ref, ...), custom_call_target="tpu_custom_call" | custom-call | flops 805306368 | bytes 1572864 | tf_op jit(solution)/shard_map/pallas_call | solution.py:355
  23.2 0.4 collective-permute-start.18
  23.6 1.6 %collective-permute-start.17 = (f32[1,1024]{1,0:T(1,128)S(1)}, f32[1,1024]{1,0:T(1,128)S(1)}, u32[]{:S(2)}, u32[]{:S(2)}) collective-permute-start(f32[1,1024]{1,0:T(1,128)S(1)} %get-tuple-element.60.refs_8_), channel_id=1, source_target_pairs={{0,4},{1,5},{2,6},{3,7},{4,0},{5,1},{6,2},{7,3},{8,12},{9,13},{10,... | collective-permute-start | bytes 12296 | tf_op jit(solution)/shard_map/ppermute | solution.py:307
  25.1 0.7 %collective-permute-start.16 = (f32[1,1024]{1,0:T(1,128)S(1)}, f32[1,1024]{1,0:T(1,128)S(1)}, u32[]{:S(2)}, u32[]{:S(2)}) collective-permute-start(f32[1,1024]{1,0:T(1,128)S(1)} %get-tuple-element.60.refs_8_), channel_id=1, source_target_pairs={{0,8},{1,9},{2,10},{3,11},{4,12},{5,13},{6,14},{7,15},{8,0},{9,1},... | collective-permute-start | bytes 12296 | tf_op jit(solution)/shard_map/ppermute | solution.py:307
  25.9 1.2 %collective-permute-start.15 = (f32[1,1024]{1,0:T(1,128)S(1)}, f32[1,1024]{1,0:T(1,128)S(1)}, u32[]{:S(2)}, u32[]{:S(2)}) collective-permute-start(f32[1,1024]{1,0:T(1,128)S(1)} %get-tuple-element.60.refs_8_), channel_id=1, source_target_pairs={{0,12},{1,13},{2,14},{3,15},{4,8},{5,9},{6,10},{7,11},{8,4},{9,5},... | collective-permute-start | bytes 12296 | tf_op jit(solution)/shard_map/ppermute | solution.py:307
  27.1 1.3 %shard_map.72 = (f32[8,128]{1,0:T(8,128)S(1)}, f32[128,512]{1,0:T(8,128)S(1)}, bf16[128,512]{1,0:T(8,128)(2,1)S(1)}, bf16[128,512]{1,0:T(8,128)(2,1)S(1)}, bf16[128,512]{1,0:T(8,128)(2,1)S(1)}) custom-call(f32[8,256]{1,0:T(8,128)S(1)} %get-tuple-element.44.exp_first.refs_0_, f32[8,256]{1,0:T(8,128)S(1)} %get-tuple-element.45.pick_first.refs_1_, ...), custom_call_target="tpu_custom_call" | custom-call | flops 536870912 | bytes 524288 | tf_op jit(solution)/shard_map/pallas_call | solution.py:363
  28.7 1.6 %collective-permute-done.15.refs_9_ = f32[1,1024]{1,0:T(1,128)S(1)} collective-permute-done((f32[1,1024]{1,0:T(1,128)S(1)}, f32[1,1024]{1,0:T(1,128)S(1)}, u32[]{:S(2)}, u32[]{:S(2)}) %collective-permute-start.15) | collective-permute-done | bytes 4128 | tf_op jit(solution)/shard_map/ppermute | solution.py:307
  30.4 1.3 %shard_map.73 = (f32[1,128]{1,0:T(1,128)S(1)}, f32[128,512]{1,0:T(8,128)S(1)}, bf16[128,512]{1,0:T(8,128)(2,1)S(1)}, f32[128,512]{1,0:T(8,128)S(1)}, bf16[128,512]{1,0:T(8,128)(2,1)S(1)}) custom-call(f32[8,256]{1,0:T(8,128)S(1)} %get-tuple-element.44.exp_first.refs_0_, f32[8,256]{1,0:T(8,128)S(1)} %get-tuple-element.45.pick_first.refs_1_, ...), custom_call_target="tpu_custom_call" | custom-call | flops 1073741824 | bytes 524288 | tf_op jit(solution)/shard_map/pallas_call | solution.py:371
  31.9 1.6 %collective-permute-start.24 = (bf16[128,512]{1,0:T(8,128)(2,1)S(1)}, bf16[128,512]{1,0:T(8,128)(2,1)S(1)}, u32[]{:S(2)}, u32[]{:S(2)}) collective-permute-start(bf16[128,512]{1,0:T(8,128)(2,1)S(1)} %get-tuple-element.74), channel_id=1, source_target_pairs={{0,2},{1,3},{2,0},{3,1},{4,6},{5,7},{6,4},{7,5},{8,10},{9,11},{10,... | collective-permute-start | bytes 393224 | tf_op jit(solution)/shard_map/ppermute | solution.py:307
  33.4 0.9 %collective-permute-start.21 = (bf16[128,512]{1,0:T(8,128)(2,1)S(1)}, bf16[128,512]{1,0:T(8,128)(2,1)S(1)}, u32[]{:S(2)}, u32[]{:S(2)}) collective-permute-start(bf16[128,512]{1,0:T(8,128)(2,1)S(1)} %get-tuple-element.70), channel_id=1, source_target_pairs={{0,4},{1,5},{2,6},{3,7},{4,0},{5,1},{6,2},{7,3},{8,12},{9,13},{10,... | collective-permute-start | bytes 393224 | tf_op jit(solution)/shard_map/ppermute | solution.py:307
  34.3 0.9 %collective-permute-start.22 = (bf16[128,512]{1,0:T(8,128)(2,1)S(1)}, bf16[128,512]{1,0:T(8,128)(2,1)S(1)}, u32[]{:S(2)}, u32[]{:S(2)}) collective-permute-start(bf16[128,512]{1,0:T(8,128)(2,1)S(1)} %get-tuple-element.71), channel_id=1, source_target_pairs={{0,8},{1,9},{2,10},{3,11},{4,12},{5,13},{6,14},{7,15},{8,0},{9,1},... | collective-permute-start | bytes 393224 | tf_op jit(solution)/shard_map/ppermute | solution.py:307
  35.2 1.7 %collective-permute-start.23 = (bf16[128,512]{1,0:T(8,128)(2,1)S(1)}, bf16[128,512]{1,0:T(8,128)(2,1)S(1)}, u32[]{:S(2)}, u32[]{:S(2)}) collective-permute-start(bf16[128,512]{1,0:T(8,128)(2,1)S(1)} %get-tuple-element.72), channel_id=1, source_target_pairs={{0,12},{1,13},{2,14},{3,15},{4,8},{5,9},{6,10},{7,11},{8,4},{9,5},... | collective-permute-start | bytes 393224 | tf_op jit(solution)/shard_map/ppermute | solution.py:307
  36.9 0.9 %collective-permute-done.24.other_ref = bf16[128,512]{1,0:T(8,128)(2,1)S(1)} collective-permute-done((bf16[128,512]{1,0:T(8,128)(2,1)S(1)}, bf16[128,512]{1,0:T(8,128)(2,1)S(1)}, u32[]{:S(2)}, u32[]{:S(2)}) %collective-permute-start.24) | collective-permute-done | bytes 131104 | tf_op jit(solution)/shard_map/ppermute | solution.py:307
  37.8 3.4 %collective-permute-start.25 = (bf16[128,512]{1,0:T(8,128)(2,1)S(1)}, bf16[128,512]{1,0:T(8,128)(2,1)S(1)}, u32[]{:S(2)}, u32[]{:S(2)}) collective-permute-start(bf16[128,512]{1,0:T(8,128)(2,1)S(1)} %get-tuple-element.76), channel_id=1, source_target_pairs={{0,16},{1,17},{2,18},{3,19},{4,20},{5,21},{6,22},{7,23},{8,24},{9,... | collective-permute-start | bytes 393224 | tf_op jit(solution)/shard_map/ppermute | solution.py:307
  41.2 1.5 %collective-permute-start.26 = (bf16[128,512]{1,0:T(8,128)(2,1)S(1)}, bf16[128,512]{1,0:T(8,128)(2,1)S(1)}, u32[]{:S(2)}, u32[]{:S(2)}) collective-permute-start(bf16[128,512]{1,0:T(8,128)(2,1)S(1)} %get-tuple-element.77), channel_id=1, source_target_pairs={{0,2},{1,3},{2,0},{3,1},{4,6},{5,7},{6,4},{7,5},{8,10},{9,11},{10,... | collective-permute-start | bytes 393224 | tf_op jit(solution)/shard_map/ppermute | solution.py:307
  42.7 2.1 %shard_map.75 = (f32[128,512]{1,0:T(8,128)S(1)}, f32[128,512]{1,0:T(8,128)S(1)}, f32[128,512]{1,0:T(8,128)S(1)}, f32[128,512]{1,0:T(8,128)S(1)}, f32[128,128]{1,0:T(8,128)S(1)}, /*index=5*/f32[1,128]{1,0:T(1,128)}) custom-call(bf16[128,512]{1,0:T(8,128)(2,1)S(1)} %copy-done.2, bf16[128,512]{1,0:T(8,128)(2,1)S(1)} %collective-permute-done.refs_1_, ...), custom_call_target="tpu_custom_call" | custom-call | flops 65536 | bytes 65536 | tf_op jit(solution)/shard_map/pallas_call | solution.py:386
  44.8 1.0 %collective-permute-done.23.refs_3_ = bf16[128,512]{1,0:T(8,128)(2,1)S(1)} collective-permute-done((bf16[128,512]{1,0:T(8,128)(2,1)S(1)}, bf16[128,512]{1,0:T(8,128)(2,1)S(1)}, u32[]{:S(2)}, u32[]{:S(2)}) %collective-permute-start.23) | collective-permute-done | bytes 131104 | tf_op jit(solution)/shard_map/ppermute | solution.py:307
  46.2 1.0 %shard_map.77 = (f32[128,512]{1,0:T(8,128)}, f32[128,512]{1,0:T(8,128)}) custom-call(f32[128,512]{1,0:T(8,128)S(1)} %get-tuple-element.64.prog_base, f32[128,512]{1,0:T(8,128)S(1)} %get-tuple-element.65.trace_base, f32[128,512]{1,0:T(8,128)S(1)} %get-tuple-element.66.prog_unit, f32[128,512]{1,0:T(8,128)S(1)} %get-tuple-element.67.trace_unit, ...), custom_call_target="tpu_custom_call" | custom-call | flops 65536 | bytes 65536 | tf_op jit(solution)/shard_map/pallas_call | solution.py:393
  (41 shorter events, 2.8 us)
Async XLA Ops:
  0.6 14.5 %copy-start = (f32[128,512]{1,0:T(8,128)S(1)}, f32[128,512]{1,0:T(8,128)}, u32[]{:S(2)}) copy-start(f32[128,512]{1,0:T(8,128)} %refs_6_.1) | copy-start | bytes 786436
  0.6 14.5 %copy-start.1 = (f32[128,512]{1,0:T(8,128)S(1)}, f32[128,512]{1,0:T(8,128)}, u32[]{:S(2)}) copy-start(f32[128,512]{1,0:T(8,128)} %refs_7_.1) | copy-start | bytes 786436
  2.9 10.7 %collective-permute-start.3 = (bf16[128,512]{1,0:T(8,128)(2,1)}, bf16[128,512]{1,0:T(8,128)(2,1)S(1)}, u32[]{:S(2)}, u32[]{:S(2)}) collective-permute-start(bf16[128,512]{1,0:T(8,128)(2,1)} %get-tuple-element.42.refs_0_), channel_id=1, source_target_pairs={{0,16},{1,17},{2,18},{3,19},{4,20},{5,21},{6,22},{7,23},{8,24},{9,... | collective-permute-start | bytes 393224 | tf_op jit(solution)/shard_map/ppermute | solution.py:307
  7.0 6.6 %collective-permute-start.1 = (bf16[128,512]{1,0:T(8,128)(2,1)}, bf16[128,512]{1,0:T(8,128)(2,1)S(1)}, u32[]{:S(2)}, u32[]{:S(2)}) collective-permute-start(bf16[128,512]{1,0:T(8,128)(2,1)} %get-tuple-element.42.refs_0_), channel_id=1, source_target_pairs={{0,2},{1,3},{2,0},{3,1},{4,6},{5,7},{6,4},{7,5},{8,10},{9,11},{10,... | collective-permute-start | bytes 393224 | tf_op jit(solution)/shard_map/ppermute | solution.py:307
  8.5 8.7 %collective-permute-start.9 = (bf16[136,512]{1,0:T(8,128)(2,1)}, bf16[136,512]{1,0:T(8,128)(2,1)S(1)}, u32[]{:S(2)}, u32[]{:S(2)}) collective-permute-start(bf16[136,512]{1,0:T(8,128)(2,1)} %get-tuple-element.50), channel_id=1, source_target_pairs={{0,12},{1,13},{2,14},{3,15},{4,8},{5,9},{6,10},{7,11},{8,4},{9,5},... | collective-permute-start | bytes 417800 | tf_op jit(solution)/shard_map/ppermute | solution.py:307
  11.0 8.1 %collective-permute-start.10 = (bf16[136,512]{1,0:T(8,128)(2,1)}, bf16[136,512]{1,0:T(8,128)(2,1)S(1)}, u32[]{:S(2)}, u32[]{:S(2)}) collective-permute-start(bf16[136,512]{1,0:T(8,128)(2,1)} %get-tuple-element.51), channel_id=1, source_target_pairs={{0,8},{1,9},{2,10},{3,11},{4,12},{5,13},{6,14},{7,15},{8,0},{9,1},... | collective-permute-start | bytes 417800 | tf_op jit(solution)/shard_map/ppermute | solution.py:307
  11.5 3.9 %copy-start.3 = (bf16[136,512]{1,0:T(8,128)(2,1)S(1)}, bf16[136,512]{1,0:T(8,128)(2,1)}, u32[]{:S(2)}) copy-start(bf16[136,512]{1,0:T(8,128)(2,1)} %get-tuple-element.43.own_ref) | copy-start | bytes 417796
  11.5 7.7 %collective-permute-start.11 = (bf16[136,512]{1,0:T(8,128)(2,1)}, bf16[136,512]{1,0:T(8,128)(2,1)S(1)}, u32[]{:S(2)}, u32[]{:S(2)}) collective-permute-start(bf16[136,512]{1,0:T(8,128)(2,1)} %get-tuple-element.52), channel_id=1, source_target_pairs={{0,4},{1,5},{2,6},{3,7},{4,0},{5,1},{6,2},{7,3},{8,12},{9,13},{10,... | collective-permute-start | bytes 417800 | tf_op jit(solution)/shard_map/ppermute | solution.py:307
  13.6 1.8 %collective-permute-start = (bf16[128,512]{1,0:T(8,128)(2,1)}, bf16[128,512]{1,0:T(8,128)(2,1)S(1)}, u32[]{:S(2)}, u32[]{:S(2)}) collective-permute-start(bf16[128,512]{1,0:T(8,128)(2,1)} %get-tuple-element.42.refs_0_), channel_id=1, source_target_pairs={{0,1},{1,0},{2,3},{3,2},{4,5},{5,4},{6,7},{7,6},{8,9},{9,8},{10,11... | collective-permute-start | bytes 393224 | tf_op jit(solution)/shard_map/ppermute | solution.py:307
  13.6 6.3 %collective-permute-start.7 = (bf16[128,512]{1,0:T(8,128)(2,1)S(1)}, bf16[128,512]{1,0:T(8,128)(2,1)S(1)}, u32[]{:S(2)}, u32[]{:S(2)}) collective-permute-start(bf16[128,512]{1,0:T(8,128)(2,1)S(1)} %collective-permute-done.3.refs_0_.refs_4_), channel_id=1, source_target_pairs={{0,2},{1,3},{2,0},{3,1},{4,6},{5,7},{6,4},{7,5},{8,10},{9,11},{10,... | collective-permute-start | bytes 393224 | tf_op jit(solution)/shard_map/ppermute | solution.py:307
  15.4 5.9 %copy-start.2 = (bf16[128,512]{1,0:T(8,128)(2,1)S(1)}, bf16[128,512]{1,0:T(8,128)(2,1)}, u32[]{:S(2)}) copy-start(bf16[128,512]{1,0:T(8,128)(2,1)} %get-tuple-element.42.refs_0_) | copy-start | bytes 393220
  15.4 4.5 %collective-permute-start.5 = (bf16[136,512]{1,0:T(8,128)(2,1)S(1)}, bf16[136,512]{1,0:T(8,128)(2,1)S(1)}, u32[]{:S(2)}, u32[]{:S(2)}) collective-permute-start(bf16[136,512]{1,0:T(8,128)(2,1)S(1)} %copy-done.3), channel_id=1, source_target_pairs={{0,1},{1,0},{2,3},{3,2},{4,5},{5,4},{6,7},{7,6},{8,9},{9,8},{10,11... | collective-permute-start | bytes 417800 | tf_op jit(solution)/shard_map/ppermute | solution.py:307
  17.2 14.5 %collective-permute-start.4 = (bf16[384,512]{1,0:T(8,128)(2,1)S(1)}, bf16[384,512]{1,0:T(8,128)(2,1)S(1)}, u32[]{:S(2)}, u32[]{:S(2)}) collective-permute-start(bf16[384,512]{1,0:T(8,128)(2,1)S(1)} %shard_map.68.own_ref), channel_id=1, source_target_pairs={{0,2},{1,3},{2,0},{3,1},{4,6},{5,7},{6,4},{7,5},{8,10},{9,11},{10,... | collective-permute-start | bytes 1179656 | tf_op jit(solution)/shard_map/ppermute | solution.py:307
  19.1 1.4 %collective-permute-start.6 = (bf16[128,512]{1,0:T(8,128)(2,1)S(1)}, bf16[128,512]{1,0:T(8,128)(2,1)S(1)}, u32[]{:S(2)}, u32[]{:S(2)}) collective-permute-start(bf16[128,512]{1,0:T(8,128)(2,1)S(1)} %collective-permute-done.3.refs_0_.refs_4_), channel_id=1, source_target_pairs={{0,1},{1,0},{2,3},{3,2},{4,5},{5,4},{6,7},{7,6},{8,9},{9,8},{10,11... | collective-permute-start | bytes 393224 | tf_op jit(solution)/shard_map/ppermute | solution.py:307
  19.1 1.5 %collective-permute-start.2 = (bf16[128,512]{1,0:T(8,128)(2,1)S(1)}, bf16[128,512]{1,0:T(8,128)(2,1)S(1)}, u32[]{:S(2)}, u32[]{:S(2)}) collective-permute-start(bf16[128,512]{1,0:T(8,128)(2,1)S(1)} %collective-permute-done.1.refs_2_), channel_id=1, source_target_pairs={{0,1},{1,0},{2,3},{3,2},{4,5},{5,4},{6,7},{7,6},{8,9},{9,8},{10,11... | collective-permute-start | bytes 393224 | tf_op jit(solution)/shard_map/ppermute | solution.py:307
  19.9 1.3 %collective-permute-start.8 = (bf16[128,512]{1,0:T(8,128)(2,1)S(1)}, bf16[128,512]{1,0:T(8,128)(2,1)S(1)}, u32[]{:S(2)}, u32[]{:S(2)}) collective-permute-start(bf16[128,512]{1,0:T(8,128)(2,1)S(1)} %collective-permute-done.7.refs_6_), channel_id=1, source_target_pairs={{0,1},{1,0},{2,3},{3,2},{4,5},{5,4},{6,7},{7,6},{8,9},{9,8},{10,11... | collective-permute-start | bytes 393224 | tf_op jit(solution)/shard_map/ppermute | solution.py:307
  19.9 1.8 %collective-permute-start.12 = (bf16[136,512]{1,0:T(8,128)(2,1)S(1)}, bf16[136,512]{1,0:T(8,128)(2,1)S(1)}, u32[]{:S(2)}, u32[]{:S(2)}) collective-permute-start(bf16[136,512]{1,0:T(8,128)(2,1)S(1)} %get-tuple-element.53.refs_0_), channel_id=1, source_target_pairs={{0,1},{1,0},{2,3},{3,2},{4,5},{5,4},{6,7},{7,6},{8,9},{9,8},{10,11... | collective-permute-start | bytes 417800 | tf_op jit(solution)/shard_map/ppermute | solution.py:307
  20.5 1.4 %collective-permute-start.13 = (bf16[136,512]{1,0:T(8,128)(2,1)S(1)}, bf16[136,512]{1,0:T(8,128)(2,1)S(1)}, u32[]{:S(2)}, u32[]{:S(2)}) collective-permute-start(bf16[136,512]{1,0:T(8,128)(2,1)S(1)} %get-tuple-element.54.refs_2_), channel_id=1, source_target_pairs={{0,1},{1,0},{2,3},{3,2},{4,5},{5,4},{6,7},{7,6},{8,9},{9,8},{10,11... | collective-permute-start | bytes 417800 | tf_op jit(solution)/shard_map/ppermute | solution.py:307
  20.7 1.4 %collective-permute-start.14 = (bf16[136,512]{1,0:T(8,128)(2,1)S(1)}, bf16[136,512]{1,0:T(8,128)(2,1)S(1)}, u32[]{:S(2)}, u32[]{:S(2)}) collective-permute-start(bf16[136,512]{1,0:T(8,128)(2,1)S(1)} %get-tuple-element.55.refs_4_), channel_id=1, source_target_pairs={{0,1},{1,0},{2,3},{3,2},{4,5},{5,4},{6,7},{7,6},{8,9},{9,8},{10,11... | collective-permute-start | bytes 417800 | tf_op jit(solution)/shard_map/ppermute | solution.py:307
  23.2 3.9 %collective-permute-start.18 = (f32[1,1024]{1,0:T(1,128)S(1)}, f32[1,1024]{1,0:T(1,128)S(1)}, u32[]{:S(2)}, u32[]{:S(2)}) collective-permute-start(f32[1,1024]{1,0:T(1,128)S(1)} %get-tuple-element.60.refs_8_), channel_id=1, source_target_pairs={{0,1},{1,0},{2,3},{3,2},{4,5},{5,4},{6,7},{7,6},{8,9},{9,8},{10,11... | collective-permute-start | bytes 12296 | tf_op jit(solution)/shard_map/ppermute | solution.py:307
  23.6 4.9 %collective-permute-start.17 = (f32[1,1024]{1,0:T(1,128)S(1)}, f32[1,1024]{1,0:T(1,128)S(1)}, u32[]{:S(2)}, u32[]{:S(2)}) collective-permute-start(f32[1,1024]{1,0:T(1,128)S(1)} %get-tuple-element.60.refs_8_), channel_id=1, source_target_pairs={{0,4},{1,5},{2,6},{3,7},{4,0},{5,1},{6,2},{7,3},{8,12},{9,13},{10,... | collective-permute-start | bytes 12296 | tf_op jit(solution)/shard_map/ppermute | solution.py:307
  25.1 3.6 %collective-permute-start.16 = (f32[1,1024]{1,0:T(1,128)S(1)}, f32[1,1024]{1,0:T(1,128)S(1)}, u32[]{:S(2)}, u32[]{:S(2)}) collective-permute-start(f32[1,1024]{1,0:T(1,128)S(1)} %get-tuple-element.60.refs_8_), channel_id=1, source_target_pairs={{0,8},{1,9},{2,10},{3,11},{4,12},{5,13},{6,14},{7,15},{8,0},{9,1},... | collective-permute-start | bytes 12296 | tf_op jit(solution)/shard_map/ppermute | solution.py:307
  25.9 4.5 %collective-permute-start.15 = (f32[1,1024]{1,0:T(1,128)S(1)}, f32[1,1024]{1,0:T(1,128)S(1)}, u32[]{:S(2)}, u32[]{:S(2)}) collective-permute-start(f32[1,1024]{1,0:T(1,128)S(1)} %get-tuple-element.60.refs_8_), channel_id=1, source_target_pairs={{0,12},{1,13},{2,14},{3,15},{4,8},{5,9},{6,10},{7,11},{8,4},{9,5},... | collective-permute-start | bytes 12296 | tf_op jit(solution)/shard_map/ppermute | solution.py:307
  28.4 2.0 %collective-permute-start.19 = (f32[8,128]{1,0:T(8,128)S(1)}, f32[8,128]{1,0:T(8,128)S(1)}, u32[]{:S(2)}, u32[]{:S(2)}) collective-permute-start(f32[8,128]{1,0:T(8,128)S(1)} %get-tuple-element.61), channel_id=1, source_target_pairs={{0,1},{1,0},{2,3},{3,2},{4,5},{5,4},{6,7},{7,6},{8,9},{9,8},{10,11... | collective-permute-start | bytes 12296 | tf_op jit(solution)/shard_map/ppermute | solution.py:307
  31.8 9.4 %collective-permute-start.20 = (bf16[768,512]{1,0:T(8,128)(2,1)S(1)}, bf16[768,512]{1,0:T(8,128)(2,1)S(1)}, u32[]{:S(2)}, u32[]{:S(2)}) collective-permute-start(bf16[768,512]{1,0:T(8,128)(2,1)S(1)} %shard_map.74.refs_4_), channel_id=1, source_target_pairs={{0,1},{1,0},{2,3},{3,2},{4,5},{5,4},{6,7},{7,6},{8,9},{9,8},{10,11... | collective-permute-start | bytes 2359304 | tf_op jit(solution)/shard_map/ppermute | solution.py:307
  31.9 5.9 %collective-permute-start.24 = (bf16[128,512]{1,0:T(8,128)(2,1)S(1)}, bf16[128,512]{1,0:T(8,128)(2,1)S(1)}, u32[]{:S(2)}, u32[]{:S(2)}) collective-permute-start(bf16[128,512]{1,0:T(8,128)(2,1)S(1)} %get-tuple-element.74), channel_id=1, source_target_pairs={{0,2},{1,3},{2,0},{3,1},{4,6},{5,7},{6,4},{7,5},{8,10},{9,11},{10,... | collective-permute-start | bytes 393224 | tf_op jit(solution)/shard_map/ppermute | solution.py:307
  33.4 11.3 %collective-permute-start.21 = (bf16[128,512]{1,0:T(8,128)(2,1)S(1)}, bf16[128,512]{1,0:T(8,128)(2,1)S(1)}, u32[]{:S(2)}, u32[]{:S(2)}) collective-permute-start(bf16[128,512]{1,0:T(8,128)(2,1)S(1)} %get-tuple-element.70), channel_id=1, source_target_pairs={{0,4},{1,5},{2,6},{3,7},{4,0},{5,1},{6,2},{7,3},{8,12},{9,13},{10,... | collective-permute-start | bytes 393224 | tf_op jit(solution)/shard_map/ppermute | solution.py:307
  34.3 10.5 %collective-permute-start.22 = (bf16[128,512]{1,0:T(8,128)(2,1)S(1)}, bf16[128,512]{1,0:T(8,128)(2,1)S(1)}, u32[]{:S(2)}, u32[]{:S(2)}) collective-permute-start(bf16[128,512]{1,0:T(8,128)(2,1)S(1)} %get-tuple-element.71), channel_id=1, source_target_pairs={{0,8},{1,9},{2,10},{3,11},{4,12},{5,13},{6,14},{7,15},{8,0},{9,1},... | collective-permute-start | bytes 393224 | tf_op jit(solution)/shard_map/ppermute | solution.py:307
  35.2 10.6 %collective-permute-start.23 = (bf16[128,512]{1,0:T(8,128)(2,1)S(1)}, bf16[128,512]{1,0:T(8,128)(2,1)S(1)}, u32[]{:S(2)}, u32[]{:S(2)}) collective-permute-start(bf16[128,512]{1,0:T(8,128)(2,1)S(1)} %get-tuple-element.72), channel_id=1, source_target_pairs={{0,12},{1,13},{2,14},{3,15},{4,8},{5,9},{6,10},{7,11},{8,4},{9,5},... | collective-permute-start | bytes 393224 | tf_op jit(solution)/shard_map/ppermute | solution.py:307
  37.8 8.0 %collective-permute-start.25 = (bf16[128,512]{1,0:T(8,128)(2,1)S(1)}, bf16[128,512]{1,0:T(8,128)(2,1)S(1)}, u32[]{:S(2)}, u32[]{:S(2)}) collective-permute-start(bf16[128,512]{1,0:T(8,128)(2,1)S(1)} %get-tuple-element.76), channel_id=1, source_target_pairs={{0,16},{1,17},{2,18},{3,19},{4,20},{5,21},{6,22},{7,23},{8,24},{9,... | collective-permute-start | bytes 393224 | tf_op jit(solution)/shard_map/ppermute | solution.py:307
  41.2 5.0 %collective-permute-start.26 = (bf16[128,512]{1,0:T(8,128)(2,1)S(1)}, bf16[128,512]{1,0:T(8,128)(2,1)S(1)}, u32[]{:S(2)}, u32[]{:S(2)}) collective-permute-start(bf16[128,512]{1,0:T(8,128)(2,1)S(1)} %get-tuple-element.77), channel_id=1, source_target_pairs={{0,2},{1,3},{2,0},{3,1},{4,6},{5,7},{6,4},{7,5},{8,10},{9,11},{10,... | collective-permute-start | bytes 393224 | tf_op jit(solution)/shard_map/ppermute | solution.py:307

commit v4 on v3

--- a/solution.py
+++ b/solution.py
@@ -13,6 +13,7 @@
 F32 = jnp.float32
 ROWS = 128
 AHEAD = 2 * 10**9
+JOIN = 0
 VMEM_LIMIT = 40 * 1024 * 1024
 
 
@@ -181,11 +182,10 @@
         out_ref[...] = total[k * ROWS : (k + 1) * ROWS, :].astype(LOW)
 
 
-def trace_terms(planes, *refs):
+def far_terms(planes, *refs):
     firsts, rests, sums, refs = refs[:4], refs[4:8], refs[8 : 8 + planes], refs[9 + planes :]
-    total_ref, own_ref, x_ref, h_ref, xh_ref, high_ref, low_ref = refs
+    total_ref, weight_ref, far_ref = refs
     plane, core = own_plane(planes), own_core()
-    below = lax.broadcasted_iota(jnp.int32, (ROWS, ROWS), 0).astype(F32) + 1.0
     for b in range(2 * planes):
         exp_ref, pick_ref, pos_ref, _ = firsts if b < 2 else rests
         at = (b if b < 2 else b - 2) * ROWS
@@ -195,23 +195,35 @@
             total = total + one[:, pl.ds(lane, ROWS)]
         if b == 0:
             total_ref[...] = total
-        scale = SCALE / total
-        for i in range(4):
-            q = 2 * i
-            weight = exp_ref[q : q + 1, at : at + ROWS] * scale
-            pick = pick_ref[q : q + 1, at : at + ROWS]
-            high, low = halves(jnp.where(below == pick, weight, 0.0))
-            high_ref[i * ROWS : (i + 1) * ROWS, b * ROWS : (b + 1) * ROWS] = high
-            low_ref[i * ROWS : (i + 1) * ROWS, b * ROWS : (b + 1) * ROWS] = low
-    first, rest = firsts[3][...], rests[3][...]
-    edge = 2 * ROWS
-    result = (
-        dot(high_ref[:, 0:edge], first) + dot(low_ref[:, 0:edge], first)
-        + dot(high_ref[:, edge:], rest) + dot(low_ref[:, edge:], rest)
-    )
+        weight_ref[:, b * ROWS : (b + 1) * ROWS] = exp_ref[:, at : at + ROWS] * (SCALE / total)
+    picks = jnp.concatenate([firsts[1][...], rests[1][...]], axis=1)
+    progs = firsts[3][...], rests[3][...]
+    far_ref[...] = weighted(weight_ref[...], picks, progs, (6,)).astype(LOW)
+
+
+def weighted(weights, picks, progs, slots):
+    below = lax.broadcasted_iota(jnp.int32, (ROWS, weights.shape[1]), 0).astype(F32) + 1.0
+    high = weights.astype(LOW).astype(F32)
+    low = weights - high
+    pairs = [[], []]
+    for q in slots:
+        chosen = below == picks[q : q + 1, :]
+        for rows, part in zip(pairs, (high, low)):
+            rows.append(jnp.where(chosen, part[q : q + 1, :], 0.0).astype(LOW))
+    edge = progs[0].shape[0]
+    result = 0.0
+    for rows in pairs:
+        values = jnp.concatenate(rows, axis=0)
+        result = result + dot(values[:, :edge], progs[0]) + dot(values[:, edge:], progs[1])
+    return result
+
+
+def near_terms(weight_ref, pick_first, pick_rest, prog_first, prog_rest, own_ref, x_ref, h_ref):
+    picks = jnp.concatenate([pick_first[...], pick_rest[...]], axis=1)
+    result = weighted(weight_ref[...], picks, (prog_first[...], prog_rest[...]), (0, 2, 4))
     own_ref[...] = result[0:ROWS, :]
-    for i, out_ref in enumerate((x_ref, h_ref, xh_ref), 1):
-        out_ref[...] = result[i * ROWS : (i + 1) * ROWS, :].astype(out_ref.dtype)
+    x_ref[...] = result[ROWS : 2 * ROWS, :].astype(LOW)
+    h_ref[...] = result[2 * ROWS :, :]
 
 
 def added(own_ref, other_ref, x_ref, out_ref, x_out):
@@ -349,39 +361,46 @@
     *first, sum_first, trace_all = call(
         functools.partial(score_first, planes),
         lists(width) + [((1, width), F32), ((8 * rows, feat), LOW)],
-        16 * rows * width * feat,
-        8 * width * feat,
+        10**8,
+        0,
     )(*msgs[:2], *slots)
     *others, sums = call(
         functools.partial(score_rest, planes),
         lists(rest) + [((1, width + rest), F32)],
-        16 * rows * rest * feat,
-        4 * rest * feat,
+        3 * 10**8,
+        0,
     )(sum_first, trace_all, *msgs[2:])
     all_sums = [sums] + [to_plane(sums, k) for k in far_first]
 
     mark, prog_own, *prog_parts = call(
         functools.partial(program_terms, planes),
         [((8, rows), F32), (shape, F32)] + [(shape, LOW)] * (planes - 1),
-        16 * rows * planes * rows * feat,
+        AHEAD,
         4 * width * feat,
         (),
         [vmem] * 5 + [vmem],
-    )(*first[:2], *others[:2], trace_all, flipped(sums, 1))
-    total, trace_own, part_x, part_h, part_xh = call(
-        functools.partial(trace_terms, planes),
-        [((1, rows), F32), (shape, F32), (shape, LOW), (shape, F32), (shape, LOW)],
-        16 * rows * (width + rest) * feat,
+    )(*first[:2], *others[:2], trace_all, sums)
+    wide = (8, width + rest)
+    total, weights, part_xh = call(
+        functools.partial(far_terms, planes),
+        [((1, rows), F32), (wide, F32), (shape, LOW)],
+        0,
+        0,
+        (),
+        [vmem] * (9 + planes),
+    )(*first, *others, *all_sums, mark)
+    trace_own, part_x, part_h = call(
+        near_terms,
+        [(shape, F32), (shape, LOW), (shape, F32)],
+        12 * rows * (width + rest) * feat,
         4 * width * feat,
-        [pltpu.VMEM((4 * rows, width + rest), LOW)] * 2,
-        [vmem] * (8 + planes) + [vmem],
-    )(*first, *others, *all_sums, flipped(mark, 1))
+    )(weights, first[1], others[1], first[3], others[3])
     for_h, part_x = call(added, [(shape, LOW)] * 2, block, 4 * block)(
         part_h, flipped(part_xh, x_bit), part_x
     )
     trace_back = [flipped(for_h, h_bit), flipped(part_x, x_bit)]
 
-    groups = call(joined, [((6 * rows, feat), LOW)], 0, 0)(group, group_x, total)[0]
+    groups = call(joined, [((6 * rows, feat), LOW)], JOIN, 0)(group, group_x, total)[0]
     prog_back = [to_plane(part, k) for k, part in enumerate(prog_parts, 1)]
     *bases, loss = call(
         group_terms,

time: 47.4 us -> 46.3 us (0.977)
  waiting for transfers between devices: 9.09 us -> 8.43 us
  starting transfers between devices: 27.5 us -> 27 us
    ppermute x27 -> x25, waiting for transfers between devices: 9.09 us -> 8.43 us  [flipped(): return lax.ppermute(value, both, [(i, i ^ bits) for i in range(size)])]
    ppermute x27 -> x25, starting transfers between devices: 27.5 us -> 27 us  [flipped(): return lax.ppermute(value, both, [(i, i ^ bits) for i in range(size)])]
    pallas_call x2 -> x3, Pallas kernels: 1.39 us -> 1.48 us  [the longest x1 0.97 us: on_device(): call(near_terms, [(shape, F32), (shape, LOW), (shape, F32)], 12 * rows *...]
  transfers between devices with their start and end apart: 27 -> 25, of which waited for: 12 -> 11; matrix products, arithmetic and copies ran while one was open for 0% -> 0% of each run, Pallas kernels for 14% -> 14%
where the time goes in v4:
time: 46.3 us; the launch traced here: 46.1 us
  starting transfers between devices  27 us (58%)
  Pallas kernels  9.92 us (21%)
  waiting for transfers between devices  8.43 us (18%)
  between operations  0.81 us (2%)
    ppermute x25, starting transfers between devices, flipped(): return lax.ppermute(value, both, [(i, i ^ bits) for i in range(size)])  27 us
    ppermute x25, waiting for transfers between devices, flipped(): return lax.ppermute(value, both, [(i, i ^ bits) for i in range(size)])  8.43 us
    pallas_call x1, Pallas kernels, on_device(): call(functools.partial(prepare, planes), [((rows + 8, feat), LOW)] * plan...  2.23 us
    pallas_call x1, Pallas kernels, on_device(): call(group_terms, [(shape, F32)] * 4 + [((rows, rows), F32), ((1, rows),...  2.04 us
    pallas_call x1, Pallas kernels, on_device(): call(functools.partial(program_terms, planes), [((8, rows), F32), (shape,...  1.29 us
    pallas_call x1, Pallas kernels, on_device(): call(functools.partial(score_rest, planes), lists(rest) + [((1, width + r...  1.1 us
    pallas_call x1, Pallas kernels, on_device(): call(functools.partial(finish, planes), [(shape, F32)] * 2, block, block)  1.03 us
    pallas_call x1, Pallas kernels, on_device(): call(near_terms, [(shape, F32), (shape, LOW), (shape, F32)], 12 * rows *...  0.97 us
  transfers between devices with their start and end apart: 25, of which 11 were waited for; matrix products, arithmetic and copies ran while one was open for 0% of the time, Pallas kernels for 14%

profile of v4, /device:TPU:0, one launch (start us, length us, event | category | flops | bytes accessed | tf_op | source)
XLA Modules:
  0.0 46.1 jit_solution(1223299953287460922)
XLA Ops:
  0.7 2.2 %shard_map.67 = (bf16[136,512]{1,0:T(8,128)(2,1)}, bf16[136,512]{1,0:T(8,128)(2,1)}, bf16[136,512]{1,0:T(8,128)(2,1)}, bf16[136,512]{1,0:T(8,128)(2,1)}, bf16[128,512]{1,0:T(8,128)(2,1)}) custom-call(f32[128,512]{1,0:T(8,128)} %refs_6_.1, f32[128,512]{1,0:T(8,128)} %refs_7_.1, s32[16,128]{1,0:T(8,128)} %bitcast.3, s32[16,128]{1,0:T(8,128)} %bitcast.4), custom_call_target="tpu_custom_call" | custom-call | flops 655360 | bytes 1310720 | tf_op jit(solution)/shard_map/pallas_call | solution.py:331
  2.9 4.1 %collective-permute-start.3 = (bf16[128,512]{1,0:T(8,128)(2,1)}, bf16[128,512]{1,0:T(8,128)(2,1)S(1)}, u32[]{:S(2)}, u32[]{:S(2)}) collective-permute-start(bf16[128,512]{1,0:T(8,128)(2,1)} %get-tuple-element.43.refs_0_), channel_id=1, source_target_pairs={{0,16},{1,17},{2,18},{3,19},{4,20},{5,21},{6,22},{7,23},{8,24},{9,... | collective-permute-start | bytes 393224 | tf_op jit(solution)/shard_map/ppermute | solution.py:319
  7.0 1.5 %collective-permute-start.1 = (bf16[128,512]{1,0:T(8,128)(2,1)}, bf16[128,512]{1,0:T(8,128)(2,1)S(1)}, u32[]{:S(2)}, u32[]{:S(2)}) collective-permute-start(bf16[128,512]{1,0:T(8,128)(2,1)} %get-tuple-element.43.refs_0_), channel_id=1, source_target_pairs={{0,2},{1,3},{2,0},{3,1},{4,6},{5,7},{6,4},{7,5},{8,10},{9,11},{10,... | collective-permute-start | bytes 393224 | tf_op jit(solution)/shard_map/ppermute | solution.py:319
  8.5 2.5 %collective-permute-start.9 = (bf16[136,512]{1,0:T(8,128)(2,1)}, bf16[136,512]{1,0:T(8,128)(2,1)S(1)}, u32[]{:S(2)}, u32[]{:S(2)}) collective-permute-start(bf16[136,512]{1,0:T(8,128)(2,1)} %get-tuple-element.51), channel_id=1, source_target_pairs={{0,12},{1,13},{2,14},{3,15},{4,8},{5,9},{6,10},{7,11},{8,4},{9,5},... | collective-permute-start | bytes 417800 | tf_op jit(solution)/shard_map/ppermute | solution.py:319
  11.0 0.4 collective-permute-start.10
  11.5 0.5 %collective-permute-start.11 = (bf16[136,512]{1,0:T(8,128)(2,1)}, bf16[136,512]{1,0:T(8,128)(2,1)S(1)}, u32[]{:S(2)}, u32[]{:S(2)}) collective-permute-start(bf16[136,512]{1,0:T(8,128)(2,1)} %get-tuple-element.53), channel_id=1, source_target_pairs={{0,4},{1,5},{2,6},{3,7},{4,0},{5,1},{6,2},{7,3},{8,12},{9,13},{10,... | collective-permute-start | bytes 417800 | tf_op jit(solution)/shard_map/ppermute | solution.py:319
  12.0 1.6 %collective-permute-done.3.refs_0_.refs_4_ = bf16[128,512]{1,0:T(8,128)(2,1)S(1)} collective-permute-done((bf16[128,512]{1,0:T(8,128)(2,1)}, bf16[128,512]{1,0:T(8,128)(2,1)S(1)}, u32[]{:S(2)}, u32[]{:S(2)}) %collective-permute-start.3) | collective-permute-done | bytes 131104 | tf_op jit(solution)/shard_map/ppermute | solution.py:319
  13.6 1.5 %collective-permute-start.7 = (bf16[128,512]{1,0:T(8,128)(2,1)S(1)}, bf16[128,512]{1,0:T(8,128)(2,1)S(1)}, u32[]{:S(2)}, u32[]{:S(2)}) collective-permute-start(bf16[128,512]{1,0:T(8,128)(2,1)S(1)} %collective-permute-done.3.refs_0_.refs_4_), channel_id=1, source_target_pairs={{0,2},{1,3},{2,0},{3,1},{4,6},{5,7},{6,4},{7,5},{8,10},{9,11},{10,... | collective-permute-start | bytes 393224 | tf_op jit(solution)/shard_map/ppermute | solution.py:319
  15.7 1.5 %collective-permute-done.9.refs_0_ = bf16[136,512]{1,0:T(8,128)(2,1)S(1)} collective-permute-done((bf16[136,512]{1,0:T(8,128)(2,1)}, bf16[136,512]{1,0:T(8,128)(2,1)S(1)}, u32[]{:S(2)}, u32[]{:S(2)}) %collective-permute-start.9) | collective-permute-done | bytes 139296 | tf_op jit(solution)/shard_map/ppermute | solution.py:319
  17.2 1.1 %collective-permute-start.4 = (bf16[384,512]{1,0:T(8,128)(2,1)S(1)}, bf16[384,512]{1,0:T(8,128)(2,1)S(1)}, u32[]{:S(2)}, u32[]{:S(2)}) collective-permute-start(bf16[384,512]{1,0:T(8,128)(2,1)S(1)} %shard_map.68.own_ref), channel_id=1, source_target_pairs={{0,2},{1,3},{2,0},{3,1},{4,6},{5,7},{6,4},{7,5},{8,10},{9,11},{10,... | collective-permute-start | bytes 1179656 | tf_op jit(solution)/shard_map/ppermute | solution.py:319
  18.3 0.9 %collective-permute-done.10.refs_1_ = bf16[136,512]{1,0:T(8,128)(2,1)S(1)} collective-permute-done((bf16[136,512]{1,0:T(8,128)(2,1)}, bf16[136,512]{1,0:T(8,128)(2,1)S(1)}, u32[]{:S(2)}, u32[]{:S(2)}) %collective-permute-start.10) | collective-permute-done | bytes 139296 | tf_op jit(solution)/shard_map/ppermute | solution.py:319
  19.1 0.5 %collective-permute-start.2 = (bf16[128,512]{1,0:T(8,128)(2,1)S(1)}, bf16[128,512]{1,0:T(8,128)(2,1)S(1)}, u32[]{:S(2)}, u32[]{:S(2)}) collective-permute-start(bf16[128,512]{1,0:T(8,128)(2,1)S(1)} %collective-permute-done.1.refs_2_), channel_id=1, source_target_pairs={{0,1},{1,0},{2,3},{3,2},{4,5},{5,4},{6,7},{7,6},{8,9},{9,8},{10,11... | collective-permute-start | bytes 393224 | tf_op jit(solution)/shard_map/ppermute | solution.py:319
  19.9 0.6 %collective-permute-start.12 = (bf16[136,512]{1,0:T(8,128)(2,1)S(1)}, bf16[136,512]{1,0:T(8,128)(2,1)S(1)}, u32[]{:S(2)}, u32[]{:S(2)}) collective-permute-start(bf16[136,512]{1,0:T(8,128)(2,1)S(1)} %get-tuple-element.54.refs_0_), channel_id=1, source_target_pairs={{0,1},{1,0},{2,3},{3,2},{4,5},{5,4},{6,7},{7,6},{8,9},{9,8},{10,11... | collective-permute-start | bytes 417800 | tf_op jit(solution)/shard_map/ppermute | solution.py:319
  21.3 0.5 %shard_map.69 = (f32[8,256]{1,0:T(8,128)S(1)}, f32[8,256]{1,0:T(8,128)S(1)}, f32[1,256]{1,0:T(1,128)S(1)}, bf16[256,512]{1,0:T(8,128)(2,1)S(1)}, f32[1,256]{1,0:T(1,128)S(1)}, /*index=5*/bf16[1024,512]{1,0:T(8,128)(2,1)S(1)}) custom-call(bf16[136,512]{1,0:T(8,128)(2,1)S(1)} %copy-done.3, bf16[136,512]{1,0:T(8,128)(2,1)S(1)} %collective-permute-done.5.other_ref, ...), custom_call_target="tpu_custom_call" | custom-call | flops 100000000 | tf_op jit(solution)/shard_map/pallas_call | solution.py:361
  22.1 1.1 %shard_map.71 = (f32[8,768]{1,0:T(8,128)S(1)}, f32[8,768]{1,0:T(8,128)S(1)}, f32[1,768]{1,0:T(1,128)S(1)}, bf16[768,512]{1,0:T(8,128)(2,1)S(1)}, f32[1,1024]{1,0:T(1,128)S(1)}) custom-call(f32[1,256]{1,0:T(1,128)S(1)} %get-tuple-element.49.sum_in, bf16[1024,512]{1,0:T(8,128)(2,1)S(1)} %get-tuple-element.50.trace_ref, ...), custom_call_target="tpu_custom_call" | custom-call | flops 300000000 | tf_op jit(solution)/shard_map/pallas_call | solution.py:367
  23.2 1.6 %collective-permute-start.17 = (f32[1,1024]{1,0:T(1,128)S(1)}, f32[1,1024]{1,0:T(1,128)S(1)}, u32[]{:S(2)}, u32[]{:S(2)}) collective-permute-start(f32[1,1024]{1,0:T(1,128)S(1)} %get-tuple-element.61._.refs_8_), channel_id=1, source_target_pairs={{0,4},{1,5},{2,6},{3,7},{4,0},{5,1},{6,2},{7,3},{8,12},{9,13},{10,... | collective-permute-start | bytes 12296 | tf_op jit(solution)/shard_map/ppermute | solution.py:319
  24.8 0.7 %collective-permute-start.16 = (f32[1,1024]{1,0:T(1,128)S(1)}, f32[1,1024]{1,0:T(1,128)S(1)}, u32[]{:S(2)}, u32[]{:S(2)}) collective-permute-start(f32[1,1024]{1,0:T(1,128)S(1)} %get-tuple-element.61._.refs_8_), channel_id=1, source_target_pairs={{0,8},{1,9},{2,10},{3,11},{4,12},{5,13},{6,14},{7,15},{8,0},{9,1},... | collective-permute-start | bytes 12296 | tf_op jit(solution)/shard_map/ppermute | solution.py:319
  25.6 1.2 %collective-permute-start.15 = (f32[1,1024]{1,0:T(1,128)S(1)}, f32[1,1024]{1,0:T(1,128)S(1)}, u32[]{:S(2)}, u32[]{:S(2)}) collective-permute-start(f32[1,1024]{1,0:T(1,128)S(1)} %get-tuple-element.61._.refs_8_), channel_id=1, source_target_pairs={{0,12},{1,13},{2,14},{3,15},{4,8},{5,9},{6,10},{7,11},{8,4},{9,5},... | collective-permute-start | bytes 12296 | tf_op jit(solution)/shard_map/ppermute | solution.py:319
  26.7 1.3 %shard_map.72 = (f32[8,128]{1,0:T(8,128)S(1)}, f32[128,512]{1,0:T(8,128)S(1)}, bf16[128,512]{1,0:T(8,128)(2,1)S(1)}, bf16[128,512]{1,0:T(8,128)(2,1)S(1)}, bf16[128,512]{1,0:T(8,128)(2,1)S(1)}) custom-call(f32[8,256]{1,0:T(8,128)S(1)} %get-tuple-element.45.exp_first.refs_0_, f32[8,256]{1,0:T(8,128)S(1)} %get-tuple-element.46.pick_first.refs_1_, ...), custom_call_target="tpu_custom_call" | custom-call | flops 2000000000 | bytes 524288 | tf_op jit(solution)/shard_map/pallas_call | solution.py:375
  28.4 1.6 %collective-permute-done.15.refs_9_ = f32[1,1024]{1,0:T(1,128)S(1)} collective-permute-done((f32[1,1024]{1,0:T(1,128)S(1)}, f32[1,1024]{1,0:T(1,128)S(1)}, u32[]{:S(2)}, u32[]{:S(2)}) %collective-permute-start.15) | collective-permute-done | bytes 4128 | tf_op jit(solution)/shard_map/ppermute | solution.py:319
  30.1 0.5 shard_map.73
  30.7 1.6 %collective-permute-start.22 = (bf16[128,512]{1,0:T(8,128)(2,1)S(1)}, bf16[128,512]{1,0:T(8,128)(2,1)S(1)}, u32[]{:S(2)}, u32[]{:S(2)}) collective-permute-start(bf16[128,512]{1,0:T(8,128)(2,1)S(1)} %get-tuple-element.76), channel_id=1, source_target_pairs={{0,2},{1,3},{2,0},{3,1},{4,6},{5,7},{6,4},{7,5},{8,10},{9,11},{10,... | collective-permute-start | bytes 393224 | tf_op jit(solution)/shard_map/ppermute | solution.py:319
  32.2 0.5 %collective-permute-start.19 = (bf16[128,512]{1,0:T(8,128)(2,1)S(1)}, bf16[128,512]{1,0:T(8,128)(2,1)S(1)}, u32[]{:S(2)}, u32[]{:S(2)}) collective-permute-start(bf16[128,512]{1,0:T(8,128)(2,1)S(1)} %get-tuple-element.72), channel_id=1, source_target_pairs={{0,4},{1,5},{2,6},{3,7},{4,0},{5,1},{6,2},{7,3},{8,12},{9,13},{10,... | collective-permute-start | bytes 393224 | tf_op jit(solution)/shard_map/ppermute | solution.py:319
  32.7 1.3 %collective-permute-start.20 = (bf16[128,512]{1,0:T(8,128)(2,1)S(1)}, bf16[128,512]{1,0:T(8,128)(2,1)S(1)}, u32[]{:S(2)}, u32[]{:S(2)}) collective-permute-start(bf16[128,512]{1,0:T(8,128)(2,1)S(1)} %get-tuple-element.73), channel_id=1, source_target_pairs={{0,8},{1,9},{2,10},{3,11},{4,12},{5,13},{6,14},{7,15},{8,0},{9,1},... | collective-permute-start | bytes 393224 | tf_op jit(solution)/shard_map/ppermute | solution.py:319
  34.0 1.7 %collective-permute-start.21 = (bf16[128,512]{1,0:T(8,128)(2,1)S(1)}, bf16[128,512]{1,0:T(8,128)(2,1)S(1)}, u32[]{:S(2)}, u32[]{:S(2)}) collective-permute-start(bf16[128,512]{1,0:T(8,128)(2,1)S(1)} %get-tuple-element.74), channel_id=1, source_target_pairs={{0,12},{1,13},{2,14},{3,15},{4,8},{5,9},{6,10},{7,11},{8,4},{9,5},... | collective-permute-start | bytes 393224 | tf_op jit(solution)/shard_map/ppermute | solution.py:319
  35.7 1.0 %shard_map.75 = (f32[128,512]{1,0:T(8,128)S(1)}, bf16[128,512]{1,0:T(8,128)(2,1)S(1)}, f32[128,512]{1,0:T(8,128)S(1)}) custom-call(f32[8,1024]{1,0:T(8,128)S(1)} %get-tuple-element.64.weight_ref, f32[8,256]{1,0:T(8,128)S(1)} %get-tuple-element.46.pick_first.refs_1_, f32[8,768]{1,0:T(8,128)S(1)} %get-tuple-element.58.pick_rest.refs_5_, ...), custom_call_target="tpu_custom_call" | custom-call | flops 805306368 | bytes 524288 | tf_op jit(solution)/shard_map/pallas_call | solution.py:392
  36.8 3.4 %collective-permute-start.23 = (bf16[128,512]{1,0:T(8,128)(2,1)S(1)}, bf16[128,512]{1,0:T(8,128)(2,1)S(1)}, u32[]{:S(2)}, u32[]{:S(2)}) collective-permute-start(bf16[128,512]{1,0:T(8,128)(2,1)S(1)} %get-tuple-element.78), channel_id=1, source_target_pairs={{0,16},{1,17},{2,18},{3,19},{4,20},{5,21},{6,22},{7,23},{8,24},{9,... | collective-permute-start | bytes 393224 | tf_op jit(solution)/shard_map/ppermute | solution.py:319
  40.1 1.4 %collective-permute-start.24 = (bf16[128,512]{1,0:T(8,128)(2,1)S(1)}, bf16[128,512]{1,0:T(8,128)(2,1)S(1)}, u32[]{:S(2)}, u32[]{:S(2)}) collective-permute-start(bf16[128,512]{1,0:T(8,128)(2,1)S(1)} %get-tuple-element.79), channel_id=1, source_target_pairs={{0,2},{1,3},{2,0},{3,1},{4,6},{5,7},{6,4},{7,5},{8,10},{9,11},{10,... | collective-permute-start | bytes 393224 | tf_op jit(solution)/shard_map/ppermute | solution.py:319
  41.5 2.0 %shard_map.76 = (f32[128,512]{1,0:T(8,128)S(1)}, f32[128,512]{1,0:T(8,128)S(1)}, f32[128,512]{1,0:T(8,128)S(1)}, f32[128,512]{1,0:T(8,128)S(1)}, f32[128,128]{1,0:T(8,128)S(1)}, /*index=5*/f32[1,128]{1,0:T(1,128)}) custom-call(bf16[128,512]{1,0:T(8,128)(2,1)S(1)} %copy-done.2, bf16[128,512]{1,0:T(8,128)(2,1)S(1)} %collective-permute-done.refs_1_, ...), custom_call_target="tpu_custom_call" | custom-call | flops 65536 | bytes 65536 | tf_op jit(solution)/shard_map/pallas_call | solution.py:405
  43.5 1.1 %collective-permute-done.21.refs_3_ = bf16[128,512]{1,0:T(8,128)(2,1)S(1)} collective-permute-done((bf16[128,512]{1,0:T(8,128)(2,1)S(1)}, bf16[128,512]{1,0:T(8,128)(2,1)S(1)}, u32[]{:S(2)}, u32[]{:S(2)}) %collective-permute-start.21) | collective-permute-done | bytes 131104 | tf_op jit(solution)/shard_map/ppermute | solution.py:319
  44.6 0.5 %collective-permute-done.24.refs_5_ = bf16[128,512]{1,0:T(8,128)(2,1)S(1)} collective-permute-done((bf16[128,512]{1,0:T(8,128)(2,1)S(1)}, bf16[128,512]{1,0:T(8,128)(2,1)S(1)}, u32[]{:S(2)}, u32[]{:S(2)}) %collective-permute-start.24) | collective-permute-done | bytes 131104 | tf_op jit(solution)/shard_map/ppermute | solution.py:319
  45.1 1.0 %shard_map.78 = (f32[128,512]{1,0:T(8,128)}, f32[128,512]{1,0:T(8,128)}) custom-call(f32[128,512]{1,0:T(8,128)S(1)} %get-tuple-element.66.prog_base, f32[128,512]{1,0:T(8,128)S(1)} %get-tuple-element.67.trace_base, f32[128,512]{1,0:T(8,128)S(1)} %get-tuple-element.68.prog_unit, f32[128,512]{1,0:T(8,128)S(1)} %get-tuple-element.69.trace_unit, ...), custom_call_target="tpu_custom_call" | custom-call | flops 65536 | bytes 65536 | tf_op jit(solution)/shard_map/pallas_call | solution.py:412
  (38 shorter events, 2.4 us)
Async XLA Ops:
  0.6 14.5 %copy-start = (f32[128,512]{1,0:T(8,128)S(1)}, f32[128,512]{1,0:T(8,128)}, u32[]{:S(2)}) copy-start(f32[128,512]{1,0:T(8,128)} %refs_6_.1) | copy-start | bytes 786436
  0.6 14.5 %copy-start.1 = (f32[128,512]{1,0:T(8,128)S(1)}, f32[128,512]{1,0:T(8,128)}, u32[]{:S(2)}) copy-start(f32[128,512]{1,0:T(8,128)} %refs_7_.1) | copy-start | bytes 786436
  2.9 10.7 %collective-permute-start.3 = (bf16[128,512]{1,0:T(8,128)(2,1)}, bf16[128,512]{1,0:T(8,128)(2,1)S(1)}, u32[]{:S(2)}, u32[]{:S(2)}) collective-permute-start(bf16[128,512]{1,0:T(8,128)(2,1)} %get-tuple-element.43.refs_0_), channel_id=1, source_target_pairs={{0,16},{1,17},{2,18},{3,19},{4,20},{5,21},{6,22},{7,23},{8,24},{9,... | collective-permute-start | bytes 393224 | tf_op jit(solution)/shard_map/ppermute | solution.py:319
  7.0 6.6 %collective-permute-start.1 = (bf16[128,512]{1,0:T(8,128)(2,1)}, bf16[128,512]{1,0:T(8,128)(2,1)S(1)}, u32[]{:S(2)}, u32[]{:S(2)}) collective-permute-start(bf16[128,512]{1,0:T(8,128)(2,1)} %get-tuple-element.43.refs_0_), channel_id=1, source_target_pairs={{0,2},{1,3},{2,0},{3,1},{4,6},{5,7},{6,4},{7,5},{8,10},{9,11},{10,... | collective-permute-start | bytes 393224 | tf_op jit(solution)/shard_map/ppermute | solution.py:319
  8.5 8.7 %collective-permute-start.9 = (bf16[136,512]{1,0:T(8,128)(2,1)}, bf16[136,512]{1,0:T(8,128)(2,1)S(1)}, u32[]{:S(2)}, u32[]{:S(2)}) collective-permute-start(bf16[136,512]{1,0:T(8,128)(2,1)} %get-tuple-element.51), channel_id=1, source_target_pairs={{0,12},{1,13},{2,14},{3,15},{4,8},{5,9},{6,10},{7,11},{8,4},{9,5},... | collective-permute-start | bytes 417800 | tf_op jit(solution)/shard_map/ppermute | solution.py:319
  11.0 8.1 %collective-permute-start.10 = (bf16[136,512]{1,0:T(8,128)(2,1)}, bf16[136,512]{1,0:T(8,128)(2,1)S(1)}, u32[]{:S(2)}, u32[]{:S(2)}) collective-permute-start(bf16[136,512]{1,0:T(8,128)(2,1)} %get-tuple-element.52), channel_id=1, source_target_pairs={{0,8},{1,9},{2,10},{3,11},{4,12},{5,13},{6,14},{7,15},{8,0},{9,1},... | collective-permute-start | bytes 417800 | tf_op jit(solution)/shard_map/ppermute | solution.py:319
  11.5 3.9 %copy-start.3 = (bf16[136,512]{1,0:T(8,128)(2,1)S(1)}, bf16[136,512]{1,0:T(8,128)(2,1)}, u32[]{:S(2)}) copy-start(bf16[136,512]{1,0:T(8,128)(2,1)} %get-tuple-element.44.own_ref) | copy-start | bytes 417796
  11.5 7.7 %collective-permute-start.11 = (bf16[136,512]{1,0:T(8,128)(2,1)}, bf16[136,512]{1,0:T(8,128)(2,1)S(1)}, u32[]{:S(2)}, u32[]{:S(2)}) collective-permute-start(bf16[136,512]{1,0:T(8,128)(2,1)} %get-tuple-element.53), channel_id=1, source_target_pairs={{0,4},{1,5},{2,6},{3,7},{4,0},{5,1},{6,2},{7,3},{8,12},{9,13},{10,... | collective-permute-start | bytes 417800 | tf_op jit(solution)/shard_map/ppermute | solution.py:319
  13.6 1.8 %collective-permute-start = (bf16[128,512]{1,0:T(8,128)(2,1)}, bf16[128,512]{1,0:T(8,128)(2,1)S(1)}, u32[]{:S(2)}, u32[]{:S(2)}) collective-permute-start(bf16[128,512]{1,0:T(8,128)(2,1)} %get-tuple-element.43.refs_0_), channel_id=1, source_target_pairs={{0,1},{1,0},{2,3},{3,2},{4,5},{5,4},{6,7},{7,6},{8,9},{9,8},{10,11... | collective-permute-start | bytes 393224 | tf_op jit(solution)/shard_map/ppermute | solution.py:319
  13.6 6.3 %collective-permute-start.7 = (bf16[128,512]{1,0:T(8,128)(2,1)S(1)}, bf16[128,512]{1,0:T(8,128)(2,1)S(1)}, u32[]{:S(2)}, u32[]{:S(2)}) collective-permute-start(bf16[128,512]{1,0:T(8,128)(2,1)S(1)} %collective-permute-done.3.refs_0_.refs_4_), channel_id=1, source_target_pairs={{0,2},{1,3},{2,0},{3,1},{4,6},{5,7},{6,4},{7,5},{8,10},{9,11},{10,... | collective-permute-start | bytes 393224 | tf_op jit(solution)/shard_map/ppermute | solution.py:319
  15.4 5.9 %copy-start.2 = (bf16[128,512]{1,0:T(8,128)(2,1)S(1)}, bf16[128,512]{1,0:T(8,128)(2,1)}, u32[]{:S(2)}) copy-start(bf16[128,512]{1,0:T(8,128)(2,1)} %get-tuple-element.43.refs_0_) | copy-start | bytes 393220
  15.4 4.5 %collective-permute-start.5 = (bf16[136,512]{1,0:T(8,128)(2,1)S(1)}, bf16[136,512]{1,0:T(8,128)(2,1)S(1)}, u32[]{:S(2)}, u32[]{:S(2)}) collective-permute-start(bf16[136,512]{1,0:T(8,128)(2,1)S(1)} %copy-done.3), channel_id=1, source_target_pairs={{0,1},{1,0},{2,3},{3,2},{4,5},{5,4},{6,7},{7,6},{8,9},{9,8},{10,11... | collective-permute-start | bytes 417800 | tf_op jit(solution)/shard_map/ppermute | solution.py:319
  17.2 13.3 %collective-permute-start.4 = (bf16[384,512]{1,0:T(8,128)(2,1)S(1)}, bf16[384,512]{1,0:T(8,128)(2,1)S(1)}, u32[]{:S(2)}, u32[]{:S(2)}) collective-permute-start(bf16[384,512]{1,0:T(8,128)(2,1)S(1)} %shard_map.68.own_ref), channel_id=1, source_target_pairs={{0,2},{1,3},{2,0},{3,1},{4,6},{5,7},{6,4},{7,5},{8,10},{9,11},{10,... | collective-permute-start | bytes 1179656 | tf_op jit(solution)/shard_map/ppermute | solution.py:319
  19.1 1.4 %collective-permute-start.6 = (bf16[128,512]{1,0:T(8,128)(2,1)S(1)}, bf16[128,512]{1,0:T(8,128)(2,1)S(1)}, u32[]{:S(2)}, u32[]{:S(2)}) collective-permute-start(bf16[128,512]{1,0:T(8,128)(2,1)S(1)} %collective-permute-done.3.refs_0_.refs_4_), channel_id=1, source_target_pairs={{0,1},{1,0},{2,3},{3,2},{4,5},{5,4},{6,7},{7,6},{8,9},{9,8},{10,11... | collective-permute-start | bytes 393224 | tf_op jit(solution)/shard_map/ppermute | solution.py:319
  19.1 1.5 %collective-permute-start.2 = (bf16[128,512]{1,0:T(8,128)(2,1)S(1)}, bf16[128,512]{1,0:T(8,128)(2,1)S(1)}, u32[]{:S(2)}, u32[]{:S(2)}) collective-permute-start(bf16[128,512]{1,0:T(8,128)(2,1)S(1)} %collective-permute-done.1.refs_2_), channel_id=1, source_target_pairs={{0,1},{1,0},{2,3},{3,2},{4,5},{5,4},{6,7},{7,6},{8,9},{9,8},{10,11... | collective-permute-start | bytes 393224 | tf_op jit(solution)/shard_map/ppermute | solution.py:319
  19.9 1.3 %collective-permute-start.8 = (bf16[128,512]{1,0:T(8,128)(2,1)S(1)}, bf16[128,512]{1,0:T(8,128)(2,1)S(1)}, u32[]{:S(2)}, u32[]{:S(2)}) collective-permute-start(bf16[128,512]{1,0:T(8,128)(2,1)S(1)} %collective-permute-done.7.refs_6_), channel_id=1, source_target_pairs={{0,1},{1,0},{2,3},{3,2},{4,5},{5,4},{6,7},{7,6},{8,9},{9,8},{10,11... | collective-permute-start | bytes 393224 | tf_op jit(solution)/shard_map/ppermute | solution.py:319
  19.9 1.8 %collective-permute-start.12 = (bf16[136,512]{1,0:T(8,128)(2,1)S(1)}, bf16[136,512]{1,0:T(8,128)(2,1)S(1)}, u32[]{:S(2)}, u32[]{:S(2)}) collective-permute-start(bf16[136,512]{1,0:T(8,128)(2,1)S(1)} %get-tuple-element.54.refs_0_), channel_id=1, source_target_pairs={{0,1},{1,0},{2,3},{3,2},{4,5},{5,4},{6,7},{7,6},{8,9},{9,8},{10,11... | collective-permute-start | bytes 417800 | tf_op jit(solution)/shard_map/ppermute | solution.py:319
  20.5 1.4 %collective-permute-start.13 = (bf16[136,512]{1,0:T(8,128)(2,1)S(1)}, bf16[136,512]{1,0:T(8,128)(2,1)S(1)}, u32[]{:S(2)}, u32[]{:S(2)}) collective-permute-start(bf16[136,512]{1,0:T(8,128)(2,1)S(1)} %get-tuple-element.55.refs_2_), channel_id=1, source_target_pairs={{0,1},{1,0},{2,3},{3,2},{4,5},{5,4},{6,7},{7,6},{8,9},{9,8},{10,11... | collective-permute-start | bytes 417800 | tf_op jit(solution)/shard_map/ppermute | solution.py:319
  20.7 1.4 %collective-permute-start.14 = (bf16[136,512]{1,0:T(8,128)(2,1)S(1)}, bf16[136,512]{1,0:T(8,128)(2,1)S(1)}, u32[]{:S(2)}, u32[]{:S(2)}) collective-permute-start(bf16[136,512]{1,0:T(8,128)(2,1)S(1)} %get-tuple-element.56.refs_4_), channel_id=1, source_target_pairs={{0,1},{1,0},{2,3},{3,2},{4,5},{5,4},{6,7},{7,6},{8,9},{9,8},{10,11... | collective-permute-start | bytes 417800 | tf_op jit(solution)/shard_map/ppermute | solution.py:319
  23.2 4.9 %collective-permute-start.17 = (f32[1,1024]{1,0:T(1,128)S(1)}, f32[1,1024]{1,0:T(1,128)S(1)}, u32[]{:S(2)}, u32[]{:S(2)}) collective-permute-start(f32[1,1024]{1,0:T(1,128)S(1)} %get-tuple-element.61._.refs_8_), channel_id=1, source_target_pairs={{0,4},{1,5},{2,6},{3,7},{4,0},{5,1},{6,2},{7,3},{8,12},{9,13},{10,... | collective-permute-start | bytes 12296 | tf_op jit(solution)/shard_map/ppermute | solution.py:319
  24.8 3.6 %collective-permute-start.16 = (f32[1,1024]{1,0:T(1,128)S(1)}, f32[1,1024]{1,0:T(1,128)S(1)}, u32[]{:S(2)}, u32[]{:S(2)}) collective-permute-start(f32[1,1024]{1,0:T(1,128)S(1)} %get-tuple-element.61._.refs_8_), channel_id=1, source_target_pairs={{0,8},{1,9},{2,10},{3,11},{4,12},{5,13},{6,14},{7,15},{8,0},{9,1},... | collective-permute-start | bytes 12296 | tf_op jit(solution)/shard_map/ppermute | solution.py:319
  25.6 4.5 %collective-permute-start.15 = (f32[1,1024]{1,0:T(1,128)S(1)}, f32[1,1024]{1,0:T(1,128)S(1)}, u32[]{:S(2)}, u32[]{:S(2)}) collective-permute-start(f32[1,1024]{1,0:T(1,128)S(1)} %get-tuple-element.61._.refs_8_), channel_id=1, source_target_pairs={{0,12},{1,13},{2,14},{3,15},{4,8},{5,9},{6,10},{7,11},{8,4},{9,5},... | collective-permute-start | bytes 12296 | tf_op jit(solution)/shard_map/ppermute | solution.py:319
  30.6 9.5 %collective-permute-start.18 = (bf16[768,512]{1,0:T(8,128)(2,1)S(1)}, bf16[768,512]{1,0:T(8,128)(2,1)S(1)}, u32[]{:S(2)}, u32[]{:S(2)}) collective-permute-start(bf16[768,512]{1,0:T(8,128)(2,1)S(1)} %shard_map.74.refs_4_), channel_id=1, source_target_pairs={{0,1},{1,0},{2,3},{3,2},{4,5},{5,4},{6,7},{7,6},{8,9},{9,8},{10,11... | collective-permute-start | bytes 2359304 | tf_op jit(solution)/shard_map/ppermute | solution.py:319
  30.7 6.0 %collective-permute-start.22 = (bf16[128,512]{1,0:T(8,128)(2,1)S(1)}, bf16[128,512]{1,0:T(8,128)(2,1)S(1)}, u32[]{:S(2)}, u32[]{:S(2)}) collective-permute-start(bf16[128,512]{1,0:T(8,128)(2,1)S(1)} %get-tuple-element.76), channel_id=1, source_target_pairs={{0,2},{1,3},{2,0},{3,1},{4,6},{5,7},{6,4},{7,5},{8,10},{9,11},{10,... | collective-permute-start | bytes 393224 | tf_op jit(solution)/shard_map/ppermute | solution.py:319
  32.2 11.3 %collective-permute-start.19 = (bf16[128,512]{1,0:T(8,128)(2,1)S(1)}, bf16[128,512]{1,0:T(8,128)(2,1)S(1)}, u32[]{:S(2)}, u32[]{:S(2)}) collective-permute-start(bf16[128,512]{1,0:T(8,128)(2,1)S(1)} %get-tuple-element.72), channel_id=1, source_target_pairs={{0,4},{1,5},{2,6},{3,7},{4,0},{5,1},{6,2},{7,3},{8,12},{9,13},{10,... | collective-permute-start | bytes 393224 | tf_op jit(solution)/shard_map/ppermute | solution.py:319
  32.7 10.8 %collective-permute-start.20 = (bf16[128,512]{1,0:T(8,128)(2,1)S(1)}, bf16[128,512]{1,0:T(8,128)(2,1)S(1)}, u32[]{:S(2)}, u32[]{:S(2)}) collective-permute-start(bf16[128,512]{1,0:T(8,128)(2,1)S(1)} %get-tuple-element.73), channel_id=1, source_target_pairs={{0,8},{1,9},{2,10},{3,11},{4,12},{5,13},{6,14},{7,15},{8,0},{9,1},... | collective-permute-start | bytes 393224 | tf_op jit(solution)/shard_map/ppermute | solution.py:319
  34.0 10.6 %collective-permute-start.21 = (bf16[128,512]{1,0:T(8,128)(2,1)S(1)}, bf16[128,512]{1,0:T(8,128)(2,1)S(1)}, u32[]{:S(2)}, u32[]{:S(2)}) collective-permute-start(bf16[128,512]{1,0:T(8,128)(2,1)S(1)} %get-tuple-element.74), channel_id=1, source_target_pairs={{0,12},{1,13},{2,14},{3,15},{4,8},{5,9},{6,10},{7,11},{8,4},{9,5},... | collective-permute-start | bytes 393224 | tf_op jit(solution)/shard_map/ppermute | solution.py:319
  36.8 7.9 %collective-permute-start.23 = (bf16[128,512]{1,0:T(8,128)(2,1)S(1)}, bf16[128,512]{1,0:T(8,128)(2,1)S(1)}, u32[]{:S(2)}, u32[]{:S(2)}) collective-permute-start(bf16[128,512]{1,0:T(8,128)(2,1)S(1)} %get-tuple-element.78), channel_id=1, source_target_pairs={{0,16},{1,17},{2,18},{3,19},{4,20},{5,21},{6,22},{7,23},{8,24},{9,... | collective-permute-start | bytes 393224 | tf_op jit(solution)/shard_map/ppermute | solution.py:319
  40.1 5.0 %collective-permute-start.24 = (bf16[128,512]{1,0:T(8,128)(2,1)S(1)}, bf16[128,512]{1,0:T(8,128)(2,1)S(1)}, u32[]{:S(2)}, u32[]{:S(2)}) collective-permute-start(bf16[128,512]{1,0:T(8,128)(2,1)S(1)} %get-tuple-element.79), channel_id=1, source_target_pairs={{0,2},{1,3},{2,0},{3,1},{4,6},{5,7},{6,4},{7,5},{8,10},{9,11},{10,... | collective-permute-start | bytes 393224 | tf_op jit(solution)/shard_map/ppermute | solution.py:319

commit v5 on v3

v5 whole, which is shorter than its diff:
```python
import functools

import jax
import jax.numpy as jnp
from jax import lax
from jax.experimental import pallas as pl
from jax.experimental.pallas import tpu as pltpu
from jax.sharding import PartitionSpec as P

EPSILON = 1e-06
SCALE = 14.0
LOW = jnp.bfloat16
F32 = jnp.float32
ROWS = 128
AHEAD = 2 * 10**9
NEAR = 10**8
FAR = 5*10**9
HALF = 2*10**9
STACK = 0
TRACE = 4*10**9
LAST = 3*10**8
JOIN = 0
VMEM_LIMIT = 40 * 1024 * 1024


def normalize(values):
    length = jnp.sqrt(jnp.sum(values * values, axis=-1, keepdims=True) + EPSILON)
    return values / length, length


def dot(a, b, contract=(1, 0)):
    return lax.dot_general(
        a, b, (((contract[0],), (contract[1],)), ((), ())), preferred_element_type=F32
    )


def halves(values):
    high = values.astype(LOW)
    return high, (values - high.astype(F32)).astype(LOW)


def dot3(a, b, contract=(1, 0)):
    return (
        dot(a[0], b[1], contract) + dot(a[1], b[0], contract)
    ) + dot(a[0], b[0], contract)


def eye():
    shape = (ROWS, ROWS)
    return lax.broadcasted_iota(jnp.int32, shape, 0) == lax.broadcasted_iota(jnp.int32, shape, 1)


def to_row(column):
    return jnp.sum(jnp.where(eye(), column, 0.0), axis=0, keepdims=True)


def to_column(row):
    return jnp.sum(jnp.where(eye(), row, 0.0), axis=1, keepdims=True)


def own_plane(planes):
    return lax.rem(lax.axis_index("dp"), planes)


def own_core():
    return lax.rem(lax.axis_index("blk"), 2)


def prepare(planes, *refs):
    sources, msg_refs, refs = refs[:4], refs[4 : 4 + planes], refs[4 + planes :]
    high_ref, buffers, pick_ref, sems = refs[0], refs[1:5], refs[5], refs[6]
    copies = [
        pltpu.make_async_copy(source, buffer, sems.at[i])
        for i, (source, buffer) in enumerate(zip(sources, buffers))
    ]
    for copy in copies:
        copy.start()
    for copy in copies:
        copy.wait()
    prog_ref, trace_ref, owner_ref, row_ref = buffers
    feat = prog_ref.shape[1]
    neg = owner_ref.shape[0]
    prog_unit, _ = normalize(prog_ref[...])
    trace_unit, _ = normalize(trace_ref[...])
    prog_high = prog_unit.astype(LOW)
    high_ref[...] = trace_unit.astype(LOW)
    pos = to_row(SCALE * jnp.sum(prog_unit * trace_unit, axis=-1, keepdims=True))
    high = pos.astype(LOW).astype(F32)
    mid = (pos - high).astype(LOW).astype(F32)
    last = pos - high - mid
    line = lax.broadcasted_iota(jnp.int32, (8, ROWS), 0)
    pos_tile = jnp.where(line == 0, high, jnp.where(line == 1, mid, jnp.where(line == 2, last, 0.0)))
    owners = owner_ref[...]
    rows = row_ref[...].astype(F32) + 1.0
    line = lax.broadcasted_iota(jnp.int32, (planes * 8, ROWS), 0)
    x, h, c = (lax.shift_right_logical(line, bit) & 1 for bit in range(3))
    index = (planes * h + lax.shift_right_logical(line, 3)) * 4 + 2 * x + c
    picks = jnp.zeros((planes * 8, ROWS), F32)
    for n in range(neg):
        picks = picks + jnp.where(index == owners[n : n + 1, :], rows[n : n + 1, :], 0.0)
    pick_ref[...] = picks
    plane = own_plane(planes)
    rest = jnp.zeros((8, feat - 2 * ROWS), F32)
    for k, msg_ref in enumerate(msg_refs):
        at = pl.multiple_of(8 * (plane ^ k), 8)
        aux = jnp.concatenate([pick_ref[pl.ds(at, 8), :], pos_tile, rest], axis=1)
        msg_ref[0:ROWS, :] = prog_high
        msg_ref[ROWS:, :] = aux.astype(LOW)


def group_parts(prog_ref, trace_ref, *refs):
    _, refs[-1][0:ROWS, :] = halves(normalize(trace_ref[...])[0])
    refs[-1][ROWS : 2 * ROWS, :], refs[-1][2 * ROWS :, :] = halves(normalize(prog_ref[...])[0])


def stack_programs(planes, *refs):
    msgs, out_ref = refs[:planes], refs[planes]
    for k, msg in enumerate(msgs):
        out_ref[k * ROWS : (k + 1) * ROWS, :] = msg[0:ROWS, :]
    aux = jnp.concatenate([msg[ROWS:, :].astype(F32) for msg in msgs], axis=0)
    out_ref[planes * ROWS :, :] = aux.astype(LOW)


def stack_traces(*refs):
    for i, ref in enumerate(refs[:-1]):
        refs[-1][i * ROWS : (i + 1) * ROWS, :] = ref[...]


def found(scores, picks, slots):
    below = lax.broadcasted_iota(jnp.int32, (ROWS, scores.shape[1]), 0).astype(F32) + 1.0
    exps = []
    for i, q in enumerate(slots):
        pick = picks[q : q + 1, :]
        block = scores[i * ROWS : (i + 1) * ROWS, :]
        score = jnp.sum(jnp.where(below == pick, block, 0.0), axis=0, keepdims=True)
        exps.append(jnp.where(pick > 0.0, jnp.exp(SCALE * score), 0.0))
    return exps


def score_near(planes, own_ref, other_ref, near_own, near_other, exp_ref, pick_ref, pos_ref):
    side = planes * ROWS
    for at, stack in ((0, own_ref), (side, other_ref)):
        aux = stack[side:, :].astype(F32)
        for k in range(planes):
            lanes = slice(at + k * ROWS, at + (k + 1) * ROWS)
            tile = aux[8 * k : 8 * k + 8, :]
            pick_ref[:, lanes] = by_slot(planes, tile[:, 0:ROWS])
            pos = tile[:, ROWS : 2 * ROWS]
            pos_ref[:, lanes] = pos[0:1, :] + pos[1:2, :] + pos[2:3, :]
    zero = jnp.zeros((1, side), F32)
    for at, stack in ((0, own_ref), (side, other_ref)):
        lanes = slice(at, at + side)
        exps = []
        for first, near in ((0, near_own), (4, near_other)):
            scores = dot(near[...], stack[0:side, :], (1, 1))
            exps += found(scores, pick_ref[:, lanes], range(first, first + 3)) + [zero]
        exp_ref[:, lanes] = jnp.concatenate(exps, axis=0)


def score_far(planes, exp_in, pick_ref, own_ref, other_ref, far_own, far_other, exp_ref, sum_ref):
    side = planes * ROWS
    plane, core = own_plane(planes), own_core()
    far = jnp.concatenate([far_own[...], far_other[...]], axis=0)
    line = lax.broadcasted_iota(jnp.int32, (8, side), 0)
    for c, stack in enumerate((own_ref, other_ref)):
        lanes = slice(c * side, (c + 1) * side)
        scores = dot(far, stack[0:side, :], (1, 1))
        three, seven = found(scores, pick_ref[:, lanes], (3, 7))
        exps = jnp.where(line == 3, three, jnp.where(line == 7, seven, exp_in[:, lanes]))
        exp_ref[:, lanes] = exps
        sums = jnp.sum(exps, axis=0, keepdims=True)
        for k in range(planes):
            lane = block_lane(planes, c * planes + k, plane, core)
            sum_ref[:, pl.ds(lane, ROWS)] = sums[:, k * ROWS : (k + 1) * ROWS]


def by_slot(planes, picks):
    blk = lax.axis_index("blk")
    bits = (lax.div(blk, 2), lax.div(lax.axis_index("dp"), planes), lax.rem(blk, 2))
    for step, bit in zip((1, 2, 4), bits):
        turned = []
        for at in range(0, 8, 2 * step):
            turned += [picks[at + step : at + 2 * step, :], picks[at : at + step, :]]
        picks = jnp.where(bit == 1, jnp.concatenate(turned, axis=0), picks)
    return picks


def block_lane(planes, b, plane, core):
    return pl.multiple_of((2 * (plane ^ (b % planes)) + (core ^ (b // planes))) * ROWS, ROWS)


def program_terms(planes, exp_ref, pick_ref, near_own, far_own, near_other, far_other, _, *refs):
    mark_ref, own_ref, *out_refs = refs
    side = planes * ROWS
    exps, picks = jnp.transpose(exp_ref[:, 0:side]), jnp.transpose(pick_ref[:, 0:side])
    lanes = lax.broadcasted_iota(jnp.int32, (side, ROWS), 1).astype(F32) + 1.0
    values = jnp.concatenate(
        [
            jnp.where(lanes == picks[:, q : q + 1], exps[:, q : q + 1], 0.0).astype(LOW)
            for q in range(8)
        ],
        axis=1,
    )
    traces = [ref[...] for ref in (near_own, far_own, near_other, far_other)]
    total = dot(values, jnp.concatenate(traces, axis=0))
    mark_ref[...] = total[0:8, 0:ROWS]
    own_ref[...] = total[0:ROWS, :]
    for k, out_ref in enumerate(out_refs, 1):
        out_ref[...] = total[k * ROWS : (k + 1) * ROWS, :].astype(LOW)


def far_terms(planes, exp_ref, pick_ref, pos_ref, own_stack, other_stack, _, *refs):
    sums, (total_ref, weight_ref, far_ref) = refs[:planes], refs[planes:]
    plane, core = own_plane(planes), own_core()
    for b in range(2 * planes):
        lanes = slice(b * ROWS, (b + 1) * ROWS)
        lane = block_lane(planes, b, plane, core)
        total = jnp.exp(pos_ref[:, lanes])
        for one in sums:
            total = total + one[:, pl.ds(lane, ROWS)]
        if b == 0:
            total_ref[...] = total
        weight_ref[:, lanes] = exp_ref[:, lanes] * (SCALE / total)
    far_ref[...] = weighted(planes, weight_ref, pick_ref, own_stack, other_stack, (3,)).astype(LOW)


def weighted(planes, weight_ref, pick_ref, own_stack, other_stack, slots):
    side = planes * ROWS
    below = lax.broadcasted_iota(jnp.int32, (ROWS, side), 0).astype(F32) + 1.0
    result = 0.0
    for at, stack in ((0, own_stack), (side, other_stack)):
        weights = weight_ref[:, at : at + side]
        high = weights.astype(LOW).astype(F32)
        for part in (high, weights - high):
            rows = [
                jnp.where(below == pick_ref[q : q + 1, at : at + side], part[q : q + 1, :], 0.0)
                for q in slots
            ]
            result = result + dot(jnp.concatenate(rows, axis=0).astype(LOW), stack[0:side, :])
    return result


def near_terms(planes, weight_ref, pick_ref, own_stack, other_stack, own_ref, x_ref, h_ref):
    result = weighted(planes, weight_ref, pick_ref, own_stack, other_stack, (0, 1, 2))
    own_ref[...] = result[0:ROWS, :]
    x_ref[...] = result[ROWS : 2 * ROWS, :].astype(LOW)
    h_ref[...] = result[2 * ROWS :, :]


def added(own_ref, other_ref, x_ref, out_ref, x_out):
    out_ref[...] = (own_ref[...] + other_ref[...].astype(F32)).astype(LOW)
    x_out[...] = x_ref[...]


def group_terms(*refs):
    nears, groups, (programs, traces, total_ref, trace_own) = refs[:2], refs[2:4], refs[4:8]
    prog_base, trace_base, prog_out, trace_out, size_ref, loss_ref = refs[8:]

    def part(which):
        at = [(x * 3 + which) * ROWS for x in range(2)]
        return jnp.concatenate([g[a : a + ROWS, :] for a in at for g in groups], axis=0)

    highs = [n[x * ROWS : (x + 1) * ROWS, :] for x in range(2) for n in nears]
    trace = (jnp.concatenate(highs, axis=0), part(0))
    prog = (part(1), part(2))
    scores = SCALE * dot3(prog, trace, (1, 1))
    exps = jnp.exp(scores)
    total = jnp.sum(exps, axis=1, keepdims=True)
    weights = exps / total
    prog_unit, prog_len = normalize(programs[...])
    trace_unit, trace_len = normalize(traces[...])
    prog_out[...] = prog_unit
    trace_out[...] = trace_unit
    pos = SCALE * jnp.sum(prog_unit * trace_unit, axis=-1, keepdims=True)
    hard_total = to_column(total_ref[...])
    pull = jnp.exp(pos) / hard_total - 2.0
    lane = lax.broadcasted_iota(jnp.int32, (ROWS, ROWS), 1)
    sizes = jnp.where(lane == 0, prog_len, jnp.where(lane == 1, trace_len, SCALE / hard_total))
    size_ref[...] = sizes
    group_prog = dot3(halves(weights[0:ROWS, :]), trace)
    prog_base[...] = SCALE * (group_prog + pull * trace_unit)
    group_trace = dot3(halves(jnp.transpose(weights[:, 0:ROWS])), prog)
    trace_base[...] = SCALE * (group_trace + pull * prog_unit) + trace_own[...]
    loss_ref[...] = to_row(jnp.log(total[0:ROWS, :]) - 2.0 * pos) + jnp.log(total_ref[...])


def finish(planes, prog_base, trace_base, prog_unit, trace_unit, size_ref, *refs):
    progs, traces, (prog_out, trace_out) = refs[:planes], refs[planes : planes + 2], refs[planes + 2 :]
    back = trace_base[...]
    for one in traces:
        back = back + one[...].astype(F32)
    hard = progs[0][...]
    for one in progs[1:]:
        hard = hard + one[...].astype(F32)
    direction = prog_base[...] + size_ref[:, 2:3] * hard
    for unit, towards, length, out in (
        (prog_unit[...], direction, size_ref[:, 0:1], prog_out),
        (trace_unit[...], back, size_ref[:, 1:2], trace_out),
    ):
        along = jnp.sum(unit * towards, axis=-1, keepdims=True)
        out[...] = (towards - unit * along) / length


def call(body, outs, flops, moved, scratch=(), in_specs=None, limit=VMEM_LIMIT):
    return pl.pallas_call(
        body,
        out_shape=[jax.ShapeDtypeStruct(shape, dtype) for shape, dtype in outs],
        scratch_shapes=list(scratch),
        **({"in_specs": in_specs} if in_specs else {}),
        compiler_params=pltpu.CompilerParams(vmem_limit_bytes=limit),
        cost_estimate=pl.CostEstimate(flops=flops, bytes_accessed=moved, transcendentals=0),
    )


def joined(own_ref, x_ref, _, out_ref):
    out_ref[0 : 3 * ROWS, :] = own_ref[...]
    out_ref[3 * ROWS :, :] = x_ref[...]


def on_device(dp_count, blk_count, programs, traces, hard_owner, hard_row):
    rows, feat = programs.shape
    planes = dp_count // 2
    size = dp_count * blk_count
    both = ("dp", "blk")

    def flipped(value, bits):
        return lax.ppermute(value, both, [(i, i ^ bits) for i in range(size)])

    def to_plane(value, k):
        return flipped(value, k * blk_count)

    x_bit, h_bit = 2, planes * blk_count
    block = rows * feat
    shape, side, width = (rows, feat), planes * rows, 2 * planes * rows
    hbm = pl.BlockSpec(memory_space=pltpu.HBM)
    index = hard_owner.shape[::-1]
    *sent, high = call(
        functools.partial(prepare, planes),
        [((rows + 8, feat), LOW)] * planes + [(shape, LOW)],
        10 * block,
        20 * block,
        [
            pltpu.VMEM(shape, F32),
            pltpu.VMEM(shape, F32),
            pltpu.VMEM(index, jnp.int32),
            pltpu.VMEM(index, jnp.int32),
            pltpu.VMEM((8 * planes, rows), F32),
            pltpu.SemaphoreType.DMA((4,)),
        ],
        [hbm] * 4,
        None,
    )(programs, traces, hard_owner.T, hard_row.T)
    high_h = flipped(high, h_bit)
    far_first = list(range(planes - 1, 0, -1))
    arrived = [to_plane(sent[k], k) for k in far_first]
    stack = call(
        functools.partial(stack_programs, planes), [((side + 8 * planes, feat), LOW)], STACK, 0
    )(sent[0], *arrived[::-1])[0]
    high_h = call(stack_traces, [(shape, LOW)], HALF, 0)(high_h)[0]
    high_x, far = flipped(high, x_bit), flipped(high_h, x_bit)
    far = call(stack_traces, [(shape, LOW)], FAR, 0)(far)[0]
    near = call(stack_traces, [((3 * rows, feat), LOW)], TRACE, 0)(high, high_x, high_h)[0]
    group = call(group_parts, [((3 * rows, feat), LOW)], 10 * block, 20 * block)(
        programs, traces, high_h
    )[0]
    group_x = flipped(group, x_bit)
    other_stack, other_near, other_far = (flipped(one, 1) for one in (stack, near, far))
    stacks = stack, other_stack

    lists = [((8, width), F32), ((8, width), F32), ((1, width), F32)]
    exps, picks, pos = call(functools.partial(score_near, planes), lists, NEAR, 0)(
        *stacks, near, other_near
    )
    exps, sums = call(functools.partial(score_far, planes), lists[1:], LAST, 0)(
        exps, picks, *stacks, far, other_far
    )
    all_sums = [sums] + [to_plane(sums, k) for k in far_first]

    mark, prog_own, *prog_parts = call(
        functools.partial(program_terms, planes),
        [((8, rows), F32), (shape, F32)] + [(shape, LOW)] * (planes - 1),
        AHEAD,
        0,
    )(exps, picks, near, far, other_near, other_far, sums)
    total, weights, part_xh = call(
        functools.partial(far_terms, planes), [((1, rows), F32), lists[0], (shape, LOW)], 0, 0
    )(exps, picks, pos, *stacks, mark, *all_sums)
    trace_own, part_x, part_h = call(
        functools.partial(near_terms, planes),
        [(shape, F32), (shape, LOW), (shape, F32)],
        12 * rows * width * feat,
        4 * width * feat,
    )(weights, picks, *stacks)
    for_h, part_x = call(added, [(shape, LOW)] * 2, block, 4 * block)(
        part_h, flipped(part_xh, x_bit), part_x
    )
    trace_back = [flipped(for_h, h_bit), flipped(part_x, x_bit)]

    groups = call(joined, [((6 * rows, feat), LOW)], JOIN, 0)(group, group_x, total)[0]
    prog_back = [to_plane(part, k) for k, part in enumerate(prog_parts, 1)]
    *bases, loss = call(
        group_terms,
        [(shape, F32)] * 4 + [((rows, rows), F32), ((1, rows), F32)],
        block,
        block,
    )(near, other_near, groups, flipped(groups, 1), programs, traces, total, trace_own)

    grad_programs, grad_traces = call(
        functools.partial(finish, planes), [(shape, F32)] * 2, block, block
    )(*bases, prog_own, *prog_back, *trace_back)
    return grad_programs, grad_traces, loss.reshape(rows)


def solution(mesh):
    spec = P(("dp", "blk"), None)
    return jax.shard_map(
        functools.partial(on_device, mesh.shape["dp"], mesh.shape["blk"]),
        mesh=mesh,
        in_specs=(spec,) * 4,
        out_specs=(spec, spec, P(("dp", "blk"))),
        check_vma=False,
    )
```

time: 47.4 us -> 45 us (0.949)
  starting transfers between devices: 27.5 us -> 24.5 us
  waiting for transfers between devices: 9.09 us -> 9.68 us
    ppermute x27 -> x20, starting transfers between devices: 27.5 us -> 24.5 us  [flipped(): return lax.ppermute(value, both, [(i, i ^ bits) for i in range(size)])]
    ppermute x27 -> x20, waiting for transfers between devices: 9.09 us -> 9.68 us  [flipped(): return lax.ppermute(value, both, [(i, i ^ bits) for i in range(size)])]
    pallas_call x5 -> x9, Pallas kernels: 3.01 us -> 3.14 us  [the longest x1 1.08 us: on_device(): call(functools.partial(score_near, planes), lists, NEAR, 0)]
  transfers between devices with their start and end apart: 27 -> 20, of which waited for: 12 -> 10; matrix products, arithmetic and copies ran while one was open for 0% -> 0% of each run, Pallas kernels for 14% -> 15%
where the time goes in v5:
time: 45 us; the launch traced here: 44.9 us
  starting transfers between devices  24.5 us (54%)
  Pallas kernels  9.83 us (22%)
  waiting for transfers between devices  9.68 us (22%)
  between operations  0.82 us (2%)
    ppermute x20, starting transfers between devices, flipped(): return lax.ppermute(value, both, [(i, i ^ bits) for i in range(size)])  24.5 us
    ppermute x20, waiting for transfers between devices, flipped(): return lax.ppermute(value, both, [(i, i ^ bits) for i in range(size)])  9.68 us
    pallas_call x1, Pallas kernels, on_device(): call(functools.partial(prepare, planes), [((rows + 8, feat), LOW)] * plan...  2.16 us
    pallas_call x1, Pallas kernels, on_device(): call(group_terms, [(shape, F32)] * 4 + [((rows, rows), F32), ((1, rows),...  2 us
    pallas_call x1, Pallas kernels, on_device(): call(functools.partial(program_terms, planes), [((8, rows), F32), (shape,...  1.27 us
    pallas_call x1, Pallas kernels, on_device(): call(functools.partial(score_near, planes), lists, NEAR, 0)  1.08 us
    pallas_call x1, Pallas kernels, on_device(): call(functools.partial(finish, planes), [(shape, F32)] * 2, block, block)  1.03 us
    pallas_call x1, Pallas kernels, on_device(): call(functools.partial(near_terms, planes), [(shape, F32), (shape, LOW),...  0.97 us
  transfers between devices with their start and end apart: 20, of which 10 were waited for; matrix products, arithmetic and copies ran while one was open for 0% of the time, Pallas kernels for 15%

profile of v5, /device:TPU:0, one launch (start us, length us, event | category | flops | bytes accessed | tf_op | source)
XLA Modules:
  0.0 44.9 jit_solution(4590714849473461869)
XLA Ops:
  0.6 2.2 %shard_map.67 = (bf16[136,512]{1,0:T(8,128)(2,1)}, bf16[136,512]{1,0:T(8,128)(2,1)}, bf16[136,512]{1,0:T(8,128)(2,1)}, bf16[136,512]{1,0:T(8,128)(2,1)}, bf16[128,512]{1,0:T(8,128)(2,1)}) custom-call(f32[128,512]{1,0:T(8,128)} %refs_4_.1, f32[128,512]{1,0:T(8,128)} %refs_5_.1, s32[16,128]{1,0:T(8,128)} %bitcast.3, s32[16,128]{1,0:T(8,128)} %bitcast.4), custom_call_target="tpu_custom_call" | custom-call | flops 655360 | bytes 1310720 | tf_op jit(solution)/shard_map/pallas_call | solution.py:337
  2.8 4.1 %collective-permute-start.1 = (bf16[128,512]{1,0:T(8,128)(2,1)}, bf16[128,512]{1,0:T(8,128)(2,1)S(1)}, u32[]{:S(2)}, u32[]{:S(2)}) collective-permute-start(bf16[128,512]{1,0:T(8,128)(2,1)} %get-tuple-element.34.refs_0_), channel_id=1, source_target_pairs={{0,16},{1,17},{2,18},{3,19},{4,20},{5,21},{6,22},{7,23},{8,24},{9,... | collective-permute-start | bytes 393224 | tf_op jit(solution)/shard_map/ppermute | solution.py:327
  6.9 1.5 %collective-permute-start = (bf16[128,512]{1,0:T(8,128)(2,1)}, bf16[128,512]{1,0:T(8,128)(2,1)S(1)}, u32[]{:S(2)}, u32[]{:S(2)}) collective-permute-start(bf16[128,512]{1,0:T(8,128)(2,1)} %get-tuple-element.34.refs_0_), channel_id=1, source_target_pairs={{0,2},{1,3},{2,0},{3,1},{4,6},{5,7},{6,4},{7,5},{8,10},{9,11},{10,... | collective-permute-start | bytes 393224 | tf_op jit(solution)/shard_map/ppermute | solution.py:327
  8.4 1.5 %collective-permute-start.4 = (bf16[136,512]{1,0:T(8,128)(2,1)}, bf16[136,512]{1,0:T(8,128)(2,1)S(1)}, u32[]{:S(2)}, u32[]{:S(2)}) collective-permute-start(bf16[136,512]{1,0:T(8,128)(2,1)} %get-tuple-element.36), channel_id=1, source_target_pairs={{0,4},{1,5},{2,6},{3,7},{4,0},{5,1},{6,2},{7,3},{8,12},{9,13},{10,... | collective-permute-start | bytes 417800 | tf_op jit(solution)/shard_map/ppermute | solution.py:327
  9.9 1.6 %collective-permute-start.5 = (bf16[136,512]{1,0:T(8,128)(2,1)}, bf16[136,512]{1,0:T(8,128)(2,1)S(1)}, u32[]{:S(2)}, u32[]{:S(2)}) collective-permute-start(bf16[136,512]{1,0:T(8,128)(2,1)} %get-tuple-element.37), channel_id=1, source_target_pairs={{0,8},{1,9},{2,10},{3,11},{4,12},{5,13},{6,14},{7,15},{8,0},{9,1},... | collective-permute-start | bytes 417800 | tf_op jit(solution)/shard_map/ppermute | solution.py:327
  11.5 0.4 collective-permute-start.6
  11.9 1.6 %collective-permute-done.1.refs_0_ = bf16[128,512]{1,0:T(8,128)(2,1)S(1)} collective-permute-done((bf16[128,512]{1,0:T(8,128)(2,1)}, bf16[128,512]{1,0:T(8,128)(2,1)S(1)}, u32[]{:S(2)}, u32[]{:S(2)}) %collective-permute-start.1) | collective-permute-done | bytes 131104 | tf_op jit(solution)/shard_map/ppermute | solution.py:327
  13.5 1.6 %collective-permute-start.8 = (bf16[128,512]{1,0:T(8,128)(2,1)S(1)}, bf16[128,512]{1,0:T(8,128)(2,1)S(1)}, u32[]{:S(2)}, u32[]{:S(2)}) collective-permute-start(bf16[128,512]{1,0:T(8,128)(2,1)S(1)} %shard_map.68.refs_2_.refs_0_), channel_id=1, source_target_pairs={{0,2},{1,3},{2,0},{3,1},{4,6},{5,7},{6,4},{7,5},{8,10},{9,11},{10,... | collective-permute-start | bytes 393224 | tf_op jit(solution)/shard_map/ppermute | solution.py:327
  15.4 0.5 %collective-permute-start.3 = (bf16[384,512]{1,0:T(8,128)(2,1)S(1)}, bf16[384,512]{1,0:T(8,128)(2,1)S(1)}, u32[]{:S(2)}, u32[]{:S(2)}) collective-permute-start(bf16[384,512]{1,0:T(8,128)(2,1)S(1)} %shard_map.70.own_ref), channel_id=1, source_target_pairs={{0,2},{1,3},{2,0},{3,1},{4,6},{5,7},{6,4},{7,5},{8,10},{9,11},{10,... | collective-permute-start | bytes 1179656 | tf_op jit(solution)/shard_map/ppermute | solution.py:327
  16.1 0.7 %collective-permute-done.5.refs_2_ = bf16[136,512]{1,0:T(8,128)(2,1)S(1)} collective-permute-done((bf16[136,512]{1,0:T(8,128)(2,1)}, bf16[136,512]{1,0:T(8,128)(2,1)S(1)}, u32[]{:S(2)}, u32[]{:S(2)}) %collective-permute-start.5) | collective-permute-done | bytes 139296 | tf_op jit(solution)/shard_map/ppermute | solution.py:327
  16.7 2.6 %collective-permute-done.6.refs_3_ = bf16[136,512]{1,0:T(8,128)(2,1)S(1)} collective-permute-done((bf16[136,512]{1,0:T(8,128)(2,1)}, bf16[136,512]{1,0:T(8,128)(2,1)S(1)}, u32[]{:S(2)}, u32[]{:S(2)}) %collective-permute-start.6) | collective-permute-done | bytes 139296 | tf_op jit(solution)/shard_map/ppermute | solution.py:327
  19.4 0.6 %collective-permute-done.8.refs_0_ = bf16[128,512]{1,0:T(8,128)(2,1)S(1)} collective-permute-done((bf16[128,512]{1,0:T(8,128)(2,1)S(1)}, bf16[128,512]{1,0:T(8,128)(2,1)S(1)}, u32[]{:S(2)}, u32[]{:S(2)}) %collective-permute-start.8) | collective-permute-done | bytes 131104 | tf_op jit(solution)/shard_map/ppermute | solution.py:327
  20.1 1.2 %collective-permute-done.7.other_ref.other_stack = bf16[544,512]{1,0:T(8,128)(2,1)S(1)} collective-permute-done((bf16[544,512]{1,0:T(8,128)(2,1)S(1)}, bf16[544,512]{1,0:T(8,128)(2,1)S(1)}, u32[]{:S(2)}, u32[]{:S(2)}) %collective-permute-start.7) | collective-permute-done | bytes 557088 | tf_op jit(solution)/shard_map/ppermute | solution.py:327
  21.4 1.1 %shard_map.72 = (f32[8,1024]{1,0:T(8,128)S(1)}, f32[8,1024]{1,0:T(8,128)S(1)}, f32[1,1024]{1,0:T(1,128)S(1)}) custom-call(bf16[544,512]{1,0:T(8,128)(2,1)S(1)} %shard_map.71.own_ref.own_stack, bf16[544,512]{1,0:T(8,128)(2,1)S(1)} %collective-permute-done.7.other_ref.other_stack, bf16[384,512]{1,0:T(8,128)(2,1)S(1)} %shard_map.69.near_own.refs_0_, ...), custom_call_target="tpu_custom_call" | custom-call | flops 100000000 | tf_op jit(solution)/shard_map/pallas_call | solution.py:371
  22.5 0.5 %shard_map.74 = (f32[8,1024]{1,0:T(8,128)S(1)}, f32[1,1024]{1,0:T(1,128)S(1)}) custom-call(f32[8,1024]{1,0:T(8,128)S(1)} %get-tuple-element.39.exp_in, f32[8,1024]{1,0:T(8,128)S(1)} %get-tuple-element.40.pick_ref, bf16[544,512]{1,0:T(8,128)(2,1)S(1)} %shard_map.71.own_ref.own_stack, bf16[544,512]{1,0:T(8,128)(2,1)S(1)} %collective-permute-done.7.other_ref.other_stack, ...), custom_call_target="tpu_custom_call" | custom-call | flops 300000000 | tf_op jit(solution)/shard_map/pallas_call | solution.py:374
  23.0 1.5 %collective-permute-start.12 = (f32[1,1024]{1,0:T(1,128)S(1)}, f32[1,1024]{1,0:T(1,128)S(1)}, u32[]{:S(2)}, u32[]{:S(2)}) collective-permute-start(f32[1,1024]{1,0:T(1,128)S(1)} %get-tuple-element.43._.refs_0_), channel_id=1, source_target_pairs={{0,4},{1,5},{2,6},{3,7},{4,0},{5,1},{6,2},{7,3},{8,12},{9,13},{10,... | collective-permute-start | bytes 12296 | tf_op jit(solution)/shard_map/ppermute | solution.py:327
  24.5 2.0 %collective-permute-start.10 = (f32[1,1024]{1,0:T(1,128)S(1)}, f32[1,1024]{1,0:T(1,128)S(1)}, u32[]{:S(2)}, u32[]{:S(2)}) collective-permute-start(f32[1,1024]{1,0:T(1,128)S(1)} %get-tuple-element.43._.refs_0_), channel_id=1, source_target_pairs={{0,12},{1,13},{2,14},{3,15},{4,8},{5,9},{6,10},{7,11},{8,4},{9,5},... | collective-permute-start | bytes 12296 | tf_op jit(solution)/shard_map/ppermute | solution.py:327
  26.5 1.3 %shard_map.75 = (f32[8,128]{1,0:T(8,128)S(1)}, f32[128,512]{1,0:T(8,128)S(1)}, bf16[128,512]{1,0:T(8,128)(2,1)S(1)}, bf16[128,512]{1,0:T(8,128)(2,1)S(1)}, bf16[128,512]{1,0:T(8,128)(2,1)S(1)}) custom-call(f32[8,1024]{1,0:T(8,128)S(1)} %get-tuple-element.41.exp_ref, f32[8,1024]{1,0:T(8,128)S(1)} %get-tuple-element.40.pick_ref, ...), custom_call_target="tpu_custom_call" | custom-call | flops 2000000000 | tf_op jit(solution)/shard_map/pallas_call | solution.py:379
  27.8 0.3 collective-permute-done.11.refs_2_
  28.1 0.9 %collective-permute-done.10.refs_1_ = f32[1,1024]{1,0:T(1,128)S(1)} collective-permute-done((f32[1,1024]{1,0:T(1,128)S(1)}, f32[1,1024]{1,0:T(1,128)S(1)}, u32[]{:S(2)}, u32[]{:S(2)}) %collective-permute-start.10) | collective-permute-done | bytes 4128 | tf_op jit(solution)/shard_map/ppermute | solution.py:327
  29.0 0.5 %shard_map.76 = (f32[1,128]{1,0:T(1,128)S(1)}, f32[8,1024]{1,0:T(8,128)S(1)}, bf16[128,512]{1,0:T(8,128)(2,1)S(1)}) custom-call(f32[8,1024]{1,0:T(8,128)S(1)} %get-tuple-element.41.exp_ref, f32[8,1024]{1,0:T(8,128)S(1)} %get-tuple-element.40.pick_ref, f32[1,1024]{1,0:T(1,128)S(1)} %get-tuple-element.42.pos_ref, ...), custom_call_target="tpu_custom_call" | custom-call | tf_op jit(solution)/shard_map/pallas_call | solution.py:385
  29.6 1.3 %collective-permute-start.17 = (bf16[128,512]{1,0:T(8,128)(2,1)S(1)}, bf16[128,512]{1,0:T(8,128)(2,1)S(1)}, u32[]{:S(2)}, u32[]{:S(2)}) collective-permute-start(bf16[128,512]{1,0:T(8,128)(2,1)S(1)} %get-tuple-element.58), channel_id=1, source_target_pairs={{0,2},{1,3},{2,0},{3,1},{4,6},{5,7},{6,4},{7,5},{8,10},{9,11},{10,... | collective-permute-start | bytes 393224 | tf_op jit(solution)/shard_map/ppermute | solution.py:327
  30.9 0.8 %collective-permute-start.14 = (bf16[128,512]{1,0:T(8,128)(2,1)S(1)}, bf16[128,512]{1,0:T(8,128)(2,1)S(1)}, u32[]{:S(2)}, u32[]{:S(2)}) collective-permute-start(bf16[128,512]{1,0:T(8,128)(2,1)S(1)} %get-tuple-element.54), channel_id=1, source_target_pairs={{0,4},{1,5},{2,6},{3,7},{4,0},{5,1},{6,2},{7,3},{8,12},{9,13},{10,... | collective-permute-start | bytes 393224 | tf_op jit(solution)/shard_map/ppermute | solution.py:327
  31.7 1.1 %collective-permute-start.15 = (bf16[128,512]{1,0:T(8,128)(2,1)S(1)}, bf16[128,512]{1,0:T(8,128)(2,1)S(1)}, u32[]{:S(2)}, u32[]{:S(2)}) collective-permute-start(bf16[128,512]{1,0:T(8,128)(2,1)S(1)} %get-tuple-element.55), channel_id=1, source_target_pairs={{0,8},{1,9},{2,10},{3,11},{4,12},{5,13},{6,14},{7,15},{8,0},{9,1},... | collective-permute-start | bytes 393224 | tf_op jit(solution)/shard_map/ppermute | solution.py:327
  32.8 1.6 %collective-permute-start.16 = (bf16[128,512]{1,0:T(8,128)(2,1)S(1)}, bf16[128,512]{1,0:T(8,128)(2,1)S(1)}, u32[]{:S(2)}, u32[]{:S(2)}) collective-permute-start(bf16[128,512]{1,0:T(8,128)(2,1)S(1)} %get-tuple-element.56), channel_id=1, source_target_pairs={{0,12},{1,13},{2,14},{3,15},{4,8},{5,9},{6,10},{7,11},{8,4},{9,5},... | collective-permute-start | bytes 393224 | tf_op jit(solution)/shard_map/ppermute | solution.py:327
  34.4 1.0 %shard_map.78 = (f32[128,512]{1,0:T(8,128)S(1)}, bf16[128,512]{1,0:T(8,128)(2,1)S(1)}, f32[128,512]{1,0:T(8,128)S(1)}) custom-call(f32[8,1024]{1,0:T(8,128)S(1)} %get-tuple-element.46.weight_ref, f32[8,1024]{1,0:T(8,128)S(1)} %get-tuple-element.40.pick_ref, bf16[544,512]{1,0:T(8,128)(2,1)S(1)} %shard_map.71.own_ref.own_stack, ...), custom_call_target="tpu_custom_call" | custom-call | flops 805306368 | bytes 2097152 | tf_op jit(solution)/shard_map/pallas_call | solution.py:388
  35.6 3.3 %collective-permute-start.18 = (bf16[128,512]{1,0:T(8,128)(2,1)S(1)}, bf16[128,512]{1,0:T(8,128)(2,1)S(1)}, u32[]{:S(2)}, u32[]{:S(2)}) collective-permute-start(bf16[128,512]{1,0:T(8,128)(2,1)S(1)} %get-tuple-element.60), channel_id=1, source_target_pairs={{0,16},{1,17},{2,18},{3,19},{4,20},{5,21},{6,22},{7,23},{8,24},{9,... | collective-permute-start | bytes 393224 | tf_op jit(solution)/shard_map/ppermute | solution.py:327
  38.9 1.4 %collective-permute-start.19 = (bf16[128,512]{1,0:T(8,128)(2,1)S(1)}, bf16[128,512]{1,0:T(8,128)(2,1)S(1)}, u32[]{:S(2)}, u32[]{:S(2)}) collective-permute-start(bf16[128,512]{1,0:T(8,128)(2,1)S(1)} %get-tuple-element.61), channel_id=1, source_target_pairs={{0,2},{1,3},{2,0},{3,1},{4,6},{5,7},{6,4},{7,5},{8,10},{9,11},{10,... | collective-permute-start | bytes 393224 | tf_op jit(solution)/shard_map/ppermute | solution.py:327
  40.2 2.0 %shard_map.79 = (f32[128,512]{1,0:T(8,128)S(1)}, f32[128,512]{1,0:T(8,128)S(1)}, f32[128,512]{1,0:T(8,128)S(1)}, f32[128,512]{1,0:T(8,128)S(1)}, f32[128,128]{1,0:T(8,128)S(1)}, /*index=5*/f32[1,128]{1,0:T(1,128)}) custom-call(bf16[384,512]{1,0:T(8,128)(2,1)S(1)} %shard_map.69.near_own.refs_0_, ...), custom_call_target="tpu_custom_call" | custom-call | flops 65536 | bytes 65536 | tf_op jit(solution)/shard_map/pallas_call | solution.py:401
  42.2 1.1 %collective-permute-done.16.refs_3_ = bf16[128,512]{1,0:T(8,128)(2,1)S(1)} collective-permute-done((bf16[128,512]{1,0:T(8,128)(2,1)S(1)}, bf16[128,512]{1,0:T(8,128)(2,1)S(1)}, u32[]{:S(2)}, u32[]{:S(2)}) %collective-permute-start.16) | collective-permute-done | bytes 131104 | tf_op jit(solution)/shard_map/ppermute | solution.py:327
  43.3 0.5 %collective-permute-done.19.refs_5_ = bf16[128,512]{1,0:T(8,128)(2,1)S(1)} collective-permute-done((bf16[128,512]{1,0:T(8,128)(2,1)S(1)}, bf16[128,512]{1,0:T(8,128)(2,1)S(1)}, u32[]{:S(2)}, u32[]{:S(2)}) %collective-permute-start.19) | collective-permute-done | bytes 131104 | tf_op jit(solution)/shard_map/ppermute | solution.py:327
  43.8 1.0 %shard_map.81 = (f32[128,512]{1,0:T(8,128)}, f32[128,512]{1,0:T(8,128)}) custom-call(f32[128,512]{1,0:T(8,128)S(1)} %get-tuple-element.48.prog_base, f32[128,512]{1,0:T(8,128)S(1)} %get-tuple-element.49.trace_base, f32[128,512]{1,0:T(8,128)S(1)} %get-tuple-element.50.prog_unit, f32[128,512]{1,0:T(8,128)S(1)} %get-tuple-element.51.trace_unit, ...), custom_call_target="tpu_custom_call" | custom-call | flops 65536 | bytes 65536 | tf_op jit(solution)/shard_map/pallas_call | solution.py:408
  (31 shorter events, 0.8 us)
Async XLA Ops:
  2.8 10.7 %collective-permute-start.1 = (bf16[128,512]{1,0:T(8,128)(2,1)}, bf16[128,512]{1,0:T(8,128)(2,1)S(1)}, u32[]{:S(2)}, u32[]{:S(2)}) collective-permute-start(bf16[128,512]{1,0:T(8,128)(2,1)} %get-tuple-element.34.refs_0_), channel_id=1, source_target_pairs={{0,16},{1,17},{2,18},{3,19},{4,20},{5,21},{6,22},{7,23},{8,24},{9,... | collective-permute-start | bytes 393224 | tf_op jit(solution)/shard_map/ppermute | solution.py:327
  6.9 8.5 %collective-permute-start = (bf16[128,512]{1,0:T(8,128)(2,1)}, bf16[128,512]{1,0:T(8,128)(2,1)S(1)}, u32[]{:S(2)}, u32[]{:S(2)}) collective-permute-start(bf16[128,512]{1,0:T(8,128)(2,1)} %get-tuple-element.34.refs_0_), channel_id=1, source_target_pairs={{0,2},{1,3},{2,0},{3,1},{4,6},{5,7},{6,4},{7,5},{8,10},{9,11},{10,... | collective-permute-start | bytes 393224 | tf_op jit(solution)/shard_map/ppermute | solution.py:327
  8.4 7.6 %collective-permute-start.4 = (bf16[136,512]{1,0:T(8,128)(2,1)}, bf16[136,512]{1,0:T(8,128)(2,1)S(1)}, u32[]{:S(2)}, u32[]{:S(2)}) collective-permute-start(bf16[136,512]{1,0:T(8,128)(2,1)} %get-tuple-element.36), channel_id=1, source_target_pairs={{0,4},{1,5},{2,6},{3,7},{4,0},{5,1},{6,2},{7,3},{8,12},{9,13},{10,... | collective-permute-start | bytes 417800 | tf_op jit(solution)/shard_map/ppermute | solution.py:327
  9.9 6.8 %collective-permute-start.5 = (bf16[136,512]{1,0:T(8,128)(2,1)}, bf16[136,512]{1,0:T(8,128)(2,1)S(1)}, u32[]{:S(2)}, u32[]{:S(2)}) collective-permute-start(bf16[136,512]{1,0:T(8,128)(2,1)} %get-tuple-element.37), channel_id=1, source_target_pairs={{0,8},{1,9},{2,10},{3,11},{4,12},{5,13},{6,14},{7,15},{8,0},{9,1},... | collective-permute-start | bytes 417800 | tf_op jit(solution)/shard_map/ppermute | solution.py:327
  11.5 3.7 %copy-start = (f32[128,512]{1,0:T(8,128)S(1)}, f32[128,512]{1,0:T(8,128)}, u32[]{:S(2)}) copy-start(f32[128,512]{1,0:T(8,128)} %refs_4_.1) | copy-start | bytes 786436
  11.5 3.7 %copy-start.1 = (f32[128,512]{1,0:T(8,128)S(1)}, f32[128,512]{1,0:T(8,128)}, u32[]{:S(2)}) copy-start(f32[128,512]{1,0:T(8,128)} %refs_5_.1) | copy-start | bytes 786436
  11.5 7.8 %collective-permute-start.6 = (bf16[136,512]{1,0:T(8,128)(2,1)}, bf16[136,512]{1,0:T(8,128)(2,1)S(1)}, u32[]{:S(2)}, u32[]{:S(2)}) collective-permute-start(bf16[136,512]{1,0:T(8,128)(2,1)} %get-tuple-element.38), channel_id=1, source_target_pairs={{0,12},{1,13},{2,14},{3,15},{4,8},{5,9},{6,10},{7,11},{8,4},{9,5},... | collective-permute-start | bytes 417800 | tf_op jit(solution)/shard_map/ppermute | solution.py:327
  13.5 2.4 %copy-start.3 = (bf16[128,512]{1,0:T(8,128)(2,1)S(1)}, bf16[128,512]{1,0:T(8,128)(2,1)}, u32[]{:S(2)}) copy-start(bf16[128,512]{1,0:T(8,128)(2,1)} %get-tuple-element.34.refs_0_) | copy-start | bytes 393220
  13.5 6.5 %collective-permute-start.8 = (bf16[128,512]{1,0:T(8,128)(2,1)S(1)}, bf16[128,512]{1,0:T(8,128)(2,1)S(1)}, u32[]{:S(2)}, u32[]{:S(2)}) collective-permute-start(bf16[128,512]{1,0:T(8,128)(2,1)S(1)} %shard_map.68.refs_2_.refs_0_), channel_id=1, source_target_pairs={{0,2},{1,3},{2,0},{3,1},{4,6},{5,7},{6,4},{7,5},{8,10},{9,11},{10,... | collective-permute-start | bytes 393224 | tf_op jit(solution)/shard_map/ppermute | solution.py:327
  15.4 4.0 %copy-start.2 = (bf16[136,512]{1,0:T(8,128)(2,1)S(1)}, bf16[136,512]{1,0:T(8,128)(2,1)}, u32[]{:S(2)}) copy-start(bf16[136,512]{1,0:T(8,128)(2,1)} %get-tuple-element.35.refs_0_) | copy-start | bytes 417796
  15.4 14.1 %collective-permute-start.3 = (bf16[384,512]{1,0:T(8,128)(2,1)S(1)}, bf16[384,512]{1,0:T(8,128)(2,1)S(1)}, u32[]{:S(2)}, u32[]{:S(2)}) collective-permute-start(bf16[384,512]{1,0:T(8,128)(2,1)S(1)} %shard_map.70.own_ref), channel_id=1, source_target_pairs={{0,2},{1,3},{2,0},{3,1},{4,6},{5,7},{6,4},{7,5},{8,10},{9,11},{10,... | collective-permute-start | bytes 1179656 | tf_op jit(solution)/shard_map/ppermute | solution.py:327
  16.0 4.2 %collective-permute-start.2 = (bf16[384,512]{1,0:T(8,128)(2,1)S(1)}, bf16[384,512]{1,0:T(8,128)(2,1)S(1)}, u32[]{:S(2)}, u32[]{:S(2)}) collective-permute-start(bf16[384,512]{1,0:T(8,128)(2,1)S(1)} %shard_map.69.near_own.refs_0_), channel_id=1, source_target_pairs={{0,1},{1,0},{2,3},{3,2},{4,5},{5,4},{6,7},{7,6},{8,9},{9,8},{10,11... | collective-permute-start | bytes 1179656 | tf_op jit(solution)/shard_map/ppermute | solution.py:327
  19.4 2.0 %collective-permute-start.7 = (bf16[544,512]{1,0:T(8,128)(2,1)S(1)}, bf16[544,512]{1,0:T(8,128)(2,1)S(1)}, u32[]{:S(2)}, u32[]{:S(2)}) collective-permute-start(bf16[544,512]{1,0:T(8,128)(2,1)S(1)} %shard_map.71.own_ref.own_stack), channel_id=1, source_target_pairs={{0,1},{1,0},{2,3},{3,2},{4,5},{5,4},{6,7},{7,6},{8,9},{9,8},{10,11... | collective-permute-start | bytes 1671176 | tf_op jit(solution)/shard_map/ppermute | solution.py:327
  20.1 2.4 %collective-permute-start.9 = (bf16[128,512]{1,0:T(8,128)(2,1)S(1)}, bf16[128,512]{1,0:T(8,128)(2,1)S(1)}, u32[]{:S(2)}, u32[]{:S(2)}) collective-permute-start(bf16[128,512]{1,0:T(8,128)(2,1)S(1)} %shard_map.73.far_own), channel_id=1, source_target_pairs={{0,1},{1,0},{2,3},{3,2},{4,5},{5,4},{6,7},{7,6},{8,9},{9,8},{10,11... | collective-permute-start | bytes 393224 | tf_op jit(solution)/shard_map/ppermute | solution.py:327
  23.0 4.8 %collective-permute-start.12 = (f32[1,1024]{1,0:T(1,128)S(1)}, f32[1,1024]{1,0:T(1,128)S(1)}, u32[]{:S(2)}, u32[]{:S(2)}) collective-permute-start(f32[1,1024]{1,0:T(1,128)S(1)} %get-tuple-element.43._.refs_0_), channel_id=1, source_target_pairs={{0,4},{1,5},{2,6},{3,7},{4,0},{5,1},{6,2},{7,3},{8,12},{9,13},{10,... | collective-permute-start | bytes 12296 | tf_op jit(solution)/shard_map/ppermute | solution.py:327
  24.5 3.6 %collective-permute-start.11 = (f32[1,1024]{1,0:T(1,128)S(1)}, f32[1,1024]{1,0:T(1,128)S(1)}, u32[]{:S(2)}, u32[]{:S(2)}) collective-permute-start(f32[1,1024]{1,0:T(1,128)S(1)} %get-tuple-element.43._.refs_0_), channel_id=1, source_target_pairs={{0,8},{1,9},{2,10},{3,11},{4,12},{5,13},{6,14},{7,15},{8,0},{9,1},... | collective-permute-start | bytes 12296 | tf_op jit(solution)/shard_map/ppermute | solution.py:327
  24.5 4.5 %collective-permute-start.10 = (f32[1,1024]{1,0:T(1,128)S(1)}, f32[1,1024]{1,0:T(1,128)S(1)}, u32[]{:S(2)}, u32[]{:S(2)}) collective-permute-start(f32[1,1024]{1,0:T(1,128)S(1)} %get-tuple-element.43._.refs_0_), channel_id=1, source_target_pairs={{0,12},{1,13},{2,14},{3,15},{4,8},{5,9},{6,10},{7,11},{8,4},{9,5},... | collective-permute-start | bytes 12296 | tf_op jit(solution)/shard_map/ppermute | solution.py:327
  29.5 9.3 %collective-permute-start.13 = (bf16[768,512]{1,0:T(8,128)(2,1)S(1)}, bf16[768,512]{1,0:T(8,128)(2,1)S(1)}, u32[]{:S(2)}, u32[]{:S(2)}) collective-permute-start(bf16[768,512]{1,0:T(8,128)(2,1)S(1)} %shard_map.77.refs_2_), channel_id=1, source_target_pairs={{0,1},{1,0},{2,3},{3,2},{4,5},{5,4},{6,7},{7,6},{8,9},{9,8},{10,11... | collective-permute-start | bytes 2359304 | tf_op jit(solution)/shard_map/ppermute | solution.py:327
  29.6 5.9 %collective-permute-start.17 = (bf16[128,512]{1,0:T(8,128)(2,1)S(1)}, bf16[128,512]{1,0:T(8,128)(2,1)S(1)}, u32[]{:S(2)}, u32[]{:S(2)}) collective-permute-start(bf16[128,512]{1,0:T(8,128)(2,1)S(1)} %get-tuple-element.58), channel_id=1, source_target_pairs={{0,2},{1,3},{2,0},{3,1},{4,6},{5,7},{6,4},{7,5},{8,10},{9,11},{10,... | collective-permute-start | bytes 393224 | tf_op jit(solution)/shard_map/ppermute | solution.py:327
  30.9 11.3 %collective-permute-start.14 = (bf16[128,512]{1,0:T(8,128)(2,1)S(1)}, bf16[128,512]{1,0:T(8,128)(2,1)S(1)}, u32[]{:S(2)}, u32[]{:S(2)}) collective-permute-start(bf16[128,512]{1,0:T(8,128)(2,1)S(1)} %get-tuple-element.54), channel_id=1, source_target_pairs={{0,4},{1,5},{2,6},{3,7},{4,0},{5,1},{6,2},{7,3},{8,12},{9,13},{10,... | collective-permute-start | bytes 393224 | tf_op jit(solution)/shard_map/ppermute | solution.py:327
  31.7 10.5 %collective-permute-start.15 = (bf16[128,512]{1,0:T(8,128)(2,1)S(1)}, bf16[128,512]{1,0:T(8,128)(2,1)S(1)}, u32[]{:S(2)}, u32[]{:S(2)}) collective-permute-start(bf16[128,512]{1,0:T(8,128)(2,1)S(1)} %get-tuple-element.55), channel_id=1, source_target_pairs={{0,8},{1,9},{2,10},{3,11},{4,12},{5,13},{6,14},{7,15},{8,0},{9,1},... | collective-permute-start | bytes 393224 | tf_op jit(solution)/shard_map/ppermute | solution.py:327
  32.8 10.5 %collective-permute-start.16 = (bf16[128,512]{1,0:T(8,128)(2,1)S(1)}, bf16[128,512]{1,0:T(8,128)(2,1)S(1)}, u32[]{:S(2)}, u32[]{:S(2)}) collective-permute-start(bf16[128,512]{1,0:T(8,128)(2,1)S(1)} %get-tuple-element.56), channel_id=1, source_target_pairs={{0,12},{1,13},{2,14},{3,15},{4,8},{5,9},{6,10},{7,11},{8,4},{9,5},... | collective-permute-start | bytes 393224 | tf_op jit(solution)/shard_map/ppermute | solution.py:327
  35.6 7.7 %collective-permute-start.18 = (bf16[128,512]{1,0:T(8,128)(2,1)S(1)}, bf16[128,512]{1,0:T(8,128)(2,1)S(1)}, u32[]{:S(2)}, u32[]{:S(2)}) collective-permute-start(bf16[128,512]{1,0:T(8,128)(2,1)S(1)} %get-tuple-element.60), channel_id=1, source_target_pairs={{0,16},{1,17},{2,18},{3,19},{4,20},{5,21},{6,22},{7,23},{8,24},{9,... | collective-permute-start | bytes 393224 | tf_op jit(solution)/shard_map/ppermute | solution.py:327
  38.9 5.0 %collective-permute-start.19 = (bf16[128,512]{1,0:T(8,128)(2,1)S(1)}, bf16[128,512]{1,0:T(8,128)(2,1)S(1)}, u32[]{:S(2)}, u32[]{:S(2)}) collective-permute-start(bf16[128,512]{1,0:T(8,128)(2,1)S(1)} %get-tuple-element.61), channel_id=1, source_target_pairs={{0,2},{1,3},{2,0},{3,1},{4,6},{5,7},{6,4},{7,5},{8,10},{9,11},{10,... | collective-permute-start | bytes 393224 | tf_op jit(solution)/shard_map/ppermute | solution.py:327

commit v6 on v5

--- a/solution.py
+++ b/solution.py
@@ -12,6 +12,7 @@
 LOW = jnp.bfloat16
 F32 = jnp.float32
 ROWS = 128
+MORE = 16
 AHEAD = 2 * 10**9
 NEAR = 10**8
 FAR = 5*10**9
@@ -101,11 +102,12 @@
     pick_ref[...] = picks
     plane = own_plane(planes)
     rest = jnp.zeros((8, feat - 2 * ROWS), F32)
+    blank = jnp.zeros((MORE - 8, feat), F32)
     for k, msg_ref in enumerate(msg_refs):
         at = pl.multiple_of(8 * (plane ^ k), 8)
         aux = jnp.concatenate([pick_ref[pl.ds(at, 8), :], pos_tile, rest], axis=1)
         msg_ref[0:ROWS, :] = prog_high
-        msg_ref[ROWS:, :] = aux.astype(LOW)
+        msg_ref[ROWS:, :] = jnp.concatenate([aux, blank], axis=0).astype(LOW)
 
 
 def group_parts(prog_ref, trace_ref, *refs):
@@ -117,7 +119,7 @@
     msgs, out_ref = refs[:planes], refs[planes]
     for k, msg in enumerate(msgs):
         out_ref[k * ROWS : (k + 1) * ROWS, :] = msg[0:ROWS, :]
-    aux = jnp.concatenate([msg[ROWS:, :].astype(F32) for msg in msgs], axis=0)
+    aux = jnp.concatenate([msg[ROWS:, :].astype(F32)[0:8, :] for msg in msgs], axis=0)
     out_ref[planes * ROWS :, :] = aux.astype(LOW)
 
 
@@ -336,7 +338,7 @@
     index = hard_owner.shape[::-1]
     *sent, high = call(
         functools.partial(prepare, planes),
-        [((rows + 8, feat), LOW)] * planes + [(shape, LOW)],
+        [((rows + MORE, feat), LOW)] * planes + [(shape, LOW)],
         10 * block,
         20 * block,
         [

time: 45 us -> 45.2 us (level)
  waiting for transfers between devices: 9.68 us -> 10.3 us
  starting transfers between devices: 24.5 us -> 24 us
    ppermute x20, waiting for transfers between devices: 9.68 us -> 10.3 us  [flipped(): return lax.ppermute(value, both, [(i, i ^ bits) for i in range(size)])]
    ppermute x20, starting transfers between devices: 24.5 us -> 24 us  [flipped(): return lax.ppermute(value, both, [(i, i ^ bits) for i in range(size)])]
  transfers between devices with their start and end apart: 20 -> 20, of which waited for: 10 -> 11; matrix products, arithmetic and copies ran while one was open for 0% -> 0% of each run, Pallas kernels for 15% -> 15%
where the time goes in v6:
time: 45.2 us; the launch traced here: 45 us
  starting transfers between devices  24 us (53%)
  waiting for transfers between devices  10.3 us (23%)
  Pallas kernels  9.84 us (22%)
  between operations  0.81 us (2%)
    ppermute x20, starting transfers between devices, flipped(): return lax.ppermute(value, both, [(i, i ^ bits) for i in range(size)])  24 us
    ppermute x20, waiting for transfers between devices, flipped(): return lax.ppermute(value, both, [(i, i ^ bits) for i in range(size)])  10.3 us
    pallas_call x1, Pallas kernels, on_device(): call(functools.partial(prepare, planes), [((rows + MORE, feat), LOW)] * p...  2.17 us
    pallas_call x1, Pallas kernels, on_device(): call(group_terms, [(shape, F32)] * 4 + [((rows, rows), F32), ((1, rows),...  2 us
    pallas_call x1, Pallas kernels, on_device(): call(functools.partial(program_terms, planes), [((8, rows), F32), (shape,...  1.27 us
    pallas_call x1, Pallas kernels, on_device(): call(functools.partial(score_near, planes), lists, NEAR, 0)  1.08 us
    pallas_call x1, Pallas kernels, on_device(): call(functools.partial(finish, planes), [(shape, F32)] * 2, block, block)  1.03 us
    pallas_call x1, Pallas kernels, on_device(): call(functools.partial(near_terms, planes), [(shape, F32), (shape, LOW),...  0.97 us
  transfers between devices with their start and end apart: 20, of which 11 were waited for; matrix products, arithmetic and copies ran while one was open for 0% of the time, Pallas kernels for 15%

profile of v6, /device:TPU:0, one launch (start us, length us, event | category | flops | bytes accessed | tf_op | source)
XLA Modules:
  0.0 45.0 jit_solution(2926136737178293772)
XLA Ops:
  0.6 2.2 %shard_map.67 = (bf16[144,512]{1,0:T(8,128)(2,1)}, bf16[144,512]{1,0:T(8,128)(2,1)}, bf16[144,512]{1,0:T(8,128)(2,1)}, bf16[144,512]{1,0:T(8,128)(2,1)}, bf16[128,512]{1,0:T(8,128)(2,1)}) custom-call(f32[128,512]{1,0:T(8,128)} %refs_4_.1, f32[128,512]{1,0:T(8,128)} %refs_5_.1, s32[16,128]{1,0:T(8,128)} %bitcast.3, s32[16,128]{1,0:T(8,128)} %bitcast.4), custom_call_target="tpu_custom_call" | custom-call | flops 655360 | bytes 1310720 | tf_op jit(solution)/shard_map/pallas_call | solution.py:339
  2.8 4.1 %collective-permute-start.1 = (bf16[128,512]{1,0:T(8,128)(2,1)}, bf16[128,512]{1,0:T(8,128)(2,1)S(1)}, u32[]{:S(2)}, u32[]{:S(2)}) collective-permute-start(bf16[128,512]{1,0:T(8,128)(2,1)} %get-tuple-element.34.refs_0_), channel_id=1, source_target_pairs={{0,16},{1,17},{2,18},{3,19},{4,20},{5,21},{6,22},{7,23},{8,24},{9,... | collective-permute-start | bytes 393224 | tf_op jit(solution)/shard_map/ppermute | solution.py:329
  6.9 1.5 %collective-permute-start = (bf16[128,512]{1,0:T(8,128)(2,1)}, bf16[128,512]{1,0:T(8,128)(2,1)S(1)}, u32[]{:S(2)}, u32[]{:S(2)}) collective-permute-start(bf16[128,512]{1,0:T(8,128)(2,1)} %get-tuple-element.34.refs_0_), channel_id=1, source_target_pairs={{0,2},{1,3},{2,0},{3,1},{4,6},{5,7},{6,4},{7,5},{8,10},{9,11},{10,... | collective-permute-start | bytes 393224 | tf_op jit(solution)/shard_map/ppermute | solution.py:329
  8.4 1.5 %collective-permute-start.4 = (bf16[144,512]{1,0:T(8,128)(2,1)}, bf16[144,512]{1,0:T(8,128)(2,1)S(1)}, u32[]{:S(2)}, u32[]{:S(2)}) collective-permute-start(bf16[144,512]{1,0:T(8,128)(2,1)} %get-tuple-element.36), channel_id=1, source_target_pairs={{0,4},{1,5},{2,6},{3,7},{4,0},{5,1},{6,2},{7,3},{8,12},{9,13},{10,... | collective-permute-start | bytes 442376 | tf_op jit(solution)/shard_map/ppermute | solution.py:329
  9.9 1.6 %collective-permute-start.5 = (bf16[144,512]{1,0:T(8,128)(2,1)}, bf16[144,512]{1,0:T(8,128)(2,1)S(1)}, u32[]{:S(2)}, u32[]{:S(2)}) collective-permute-start(bf16[144,512]{1,0:T(8,128)(2,1)} %get-tuple-element.37), channel_id=1, source_target_pairs={{0,8},{1,9},{2,10},{3,11},{4,12},{5,13},{6,14},{7,15},{8,0},{9,1},... | collective-permute-start | bytes 442376 | tf_op jit(solution)/shard_map/ppermute | solution.py:329
  11.5 0.4 collective-permute-start.6
  11.9 1.6 %collective-permute-done.1.refs_0_ = bf16[128,512]{1,0:T(8,128)(2,1)S(1)} collective-permute-done((bf16[128,512]{1,0:T(8,128)(2,1)}, bf16[128,512]{1,0:T(8,128)(2,1)S(1)}, u32[]{:S(2)}, u32[]{:S(2)}) %collective-permute-start.1) | collective-permute-done | bytes 131104 | tf_op jit(solution)/shard_map/ppermute | solution.py:329
  13.6 1.6 %collective-permute-start.8 = (bf16[128,512]{1,0:T(8,128)(2,1)S(1)}, bf16[128,512]{1,0:T(8,128)(2,1)S(1)}, u32[]{:S(2)}, u32[]{:S(2)}) collective-permute-start(bf16[128,512]{1,0:T(8,128)(2,1)S(1)} %shard_map.68.refs_2_.refs_0_), channel_id=1, source_target_pairs={{0,2},{1,3},{2,0},{3,1},{4,6},{5,7},{6,4},{7,5},{8,10},{9,11},{10,... | collective-permute-start | bytes 393224 | tf_op jit(solution)/shard_map/ppermute | solution.py:329
  15.4 0.5 %collective-permute-start.3 = (bf16[384,512]{1,0:T(8,128)(2,1)S(1)}, bf16[384,512]{1,0:T(8,128)(2,1)S(1)}, u32[]{:S(2)}, u32[]{:S(2)}) collective-permute-start(bf16[384,512]{1,0:T(8,128)(2,1)S(1)} %shard_map.70.own_ref), channel_id=1, source_target_pairs={{0,2},{1,3},{2,0},{3,1},{4,6},{5,7},{6,4},{7,5},{8,10},{9,11},{10,... | collective-permute-start | bytes 1179656 | tf_op jit(solution)/shard_map/ppermute | solution.py:329
  16.1 0.9 %collective-permute-done.5.refs_2_ = bf16[144,512]{1,0:T(8,128)(2,1)S(1)} collective-permute-done((bf16[144,512]{1,0:T(8,128)(2,1)}, bf16[144,512]{1,0:T(8,128)(2,1)S(1)}, u32[]{:S(2)}, u32[]{:S(2)}) %collective-permute-start.5) | collective-permute-done | bytes 147488 | tf_op jit(solution)/shard_map/ppermute | solution.py:329
  16.9 2.8 %collective-permute-done.6.refs_3_ = bf16[144,512]{1,0:T(8,128)(2,1)S(1)} collective-permute-done((bf16[144,512]{1,0:T(8,128)(2,1)}, bf16[144,512]{1,0:T(8,128)(2,1)S(1)}, u32[]{:S(2)}, u32[]{:S(2)}) %collective-permute-start.6) | collective-permute-done | bytes 147488 | tf_op jit(solution)/shard_map/ppermute | solution.py:329
  20.1 0.3 collective-permute-start.9
  20.4 1.4 %collective-permute-done.7.other_ref.other_stack = bf16[544,512]{1,0:T(8,128)(2,1)S(1)} collective-permute-done((bf16[544,512]{1,0:T(8,128)(2,1)S(1)}, bf16[544,512]{1,0:T(8,128)(2,1)S(1)}, u32[]{:S(2)}, u32[]{:S(2)}) %collective-permute-start.7) | collective-permute-done | bytes 557088 | tf_op jit(solution)/shard_map/ppermute | solution.py:329
  21.7 1.1 %shard_map.72 = (f32[8,1024]{1,0:T(8,128)S(1)}, f32[8,1024]{1,0:T(8,128)S(1)}, f32[1,1024]{1,0:T(1,128)S(1)}) custom-call(bf16[544,512]{1,0:T(8,128)(2,1)S(1)} %shard_map.71.own_ref.own_stack, bf16[544,512]{1,0:T(8,128)(2,1)S(1)} %collective-permute-done.7.other_ref.other_stack, bf16[384,512]{1,0:T(8,128)(2,1)S(1)} %shard_map.69.near_own.refs_0_, ...), custom_call_target="tpu_custom_call" | custom-call | flops 100000000 | tf_op jit(solution)/shard_map/pallas_call | solution.py:373
  22.8 0.5 %shard_map.74 = (f32[8,1024]{1,0:T(8,128)S(1)}, f32[1,1024]{1,0:T(1,128)S(1)}) custom-call(f32[8,1024]{1,0:T(8,128)S(1)} %get-tuple-element.39.exp_in, f32[8,1024]{1,0:T(8,128)S(1)} %get-tuple-element.40.pick_ref, bf16[544,512]{1,0:T(8,128)(2,1)S(1)} %shard_map.71.own_ref.own_stack, bf16[544,512]{1,0:T(8,128)(2,1)S(1)} %collective-permute-done.7.other_ref.other_stack, ...), custom_call_target="tpu_custom_call" | custom-call | flops 300000000 | tf_op jit(solution)/shard_map/pallas_call | solution.py:376
  23.3 1.5 %collective-permute-start.12 = (f32[1,1024]{1,0:T(1,128)S(1)}, f32[1,1024]{1,0:T(1,128)S(1)}, u32[]{:S(2)}, u32[]{:S(2)}) collective-permute-start(f32[1,1024]{1,0:T(1,128)S(1)} %get-tuple-element.43._.refs_0_), channel_id=1, source_target_pairs={{0,4},{1,5},{2,6},{3,7},{4,0},{5,1},{6,2},{7,3},{8,12},{9,13},{10,... | collective-permute-start | bytes 12296 | tf_op jit(solution)/shard_map/ppermute | solution.py:329
  24.9 2.0 %collective-permute-start.10 = (f32[1,1024]{1,0:T(1,128)S(1)}, f32[1,1024]{1,0:T(1,128)S(1)}, u32[]{:S(2)}, u32[]{:S(2)}) collective-permute-start(f32[1,1024]{1,0:T(1,128)S(1)} %get-tuple-element.43._.refs_0_), channel_id=1, source_target_pairs={{0,12},{1,13},{2,14},{3,15},{4,8},{5,9},{6,10},{7,11},{8,4},{9,5},... | collective-permute-start | bytes 12296 | tf_op jit(solution)/shard_map/ppermute | solution.py:329
  26.9 1.3 %shard_map.75 = (f32[8,128]{1,0:T(8,128)S(1)}, f32[128,512]{1,0:T(8,128)S(1)}, bf16[128,512]{1,0:T(8,128)(2,1)S(1)}, bf16[128,512]{1,0:T(8,128)(2,1)S(1)}, bf16[128,512]{1,0:T(8,128)(2,1)S(1)}) custom-call(f32[8,1024]{1,0:T(8,128)S(1)} %get-tuple-element.41.exp_ref, f32[8,1024]{1,0:T(8,128)S(1)} %get-tuple-element.40.pick_ref, ...), custom_call_target="tpu_custom_call" | custom-call | flops 2000000000 | tf_op jit(solution)/shard_map/pallas_call | solution.py:381
  28.5 0.9 %collective-permute-done.10.refs_1_ = f32[1,1024]{1,0:T(1,128)S(1)} collective-permute-done((f32[1,1024]{1,0:T(1,128)S(1)}, f32[1,1024]{1,0:T(1,128)S(1)}, u32[]{:S(2)}, u32[]{:S(2)}) %collective-permute-start.10) | collective-permute-done | bytes 4128 | tf_op jit(solution)/shard_map/ppermute | solution.py:329
  29.4 0.5 %shard_map.76 = (f32[1,128]{1,0:T(1,128)S(1)}, f32[8,1024]{1,0:T(8,128)S(1)}, bf16[128,512]{1,0:T(8,128)(2,1)S(1)}) custom-call(f32[8,1024]{1,0:T(8,128)S(1)} %get-tuple-element.41.exp_ref, f32[8,1024]{1,0:T(8,128)S(1)} %get-tuple-element.40.pick_ref, f32[1,1024]{1,0:T(1,128)S(1)} %get-tuple-element.42.pos_ref, ...), custom_call_target="tpu_custom_call" | custom-call | tf_op jit(solution)/shard_map/pallas_call | solution.py:387
  30.0 0.9 %collective-permute-start.17 = (bf16[128,512]{1,0:T(8,128)(2,1)S(1)}, bf16[128,512]{1,0:T(8,128)(2,1)S(1)}, u32[]{:S(2)}, u32[]{:S(2)}) collective-permute-start(bf16[128,512]{1,0:T(8,128)(2,1)S(1)} %get-tuple-element.58), channel_id=1, source_target_pairs={{0,2},{1,3},{2,0},{3,1},{4,6},{5,7},{6,4},{7,5},{8,10},{9,11},{10,... | collective-permute-start | bytes 393224 | tf_op jit(solution)/shard_map/ppermute | solution.py:329
  30.9 1.1 %collective-permute-start.14 = (bf16[128,512]{1,0:T(8,128)(2,1)S(1)}, bf16[128,512]{1,0:T(8,128)(2,1)S(1)}, u32[]{:S(2)}, u32[]{:S(2)}) collective-permute-start(bf16[128,512]{1,0:T(8,128)(2,1)S(1)} %get-tuple-element.54), channel_id=1, source_target_pairs={{0,4},{1,5},{2,6},{3,7},{4,0},{5,1},{6,2},{7,3},{8,12},{9,13},{10,... | collective-permute-start | bytes 393224 | tf_op jit(solution)/shard_map/ppermute | solution.py:329
  32.1 1.1 %collective-permute-start.15 = (bf16[128,512]{1,0:T(8,128)(2,1)S(1)}, bf16[128,512]{1,0:T(8,128)(2,1)S(1)}, u32[]{:S(2)}, u32[]{:S(2)}) collective-permute-start(bf16[128,512]{1,0:T(8,128)(2,1)S(1)} %get-tuple-element.55), channel_id=1, source_target_pairs={{0,8},{1,9},{2,10},{3,11},{4,12},{5,13},{6,14},{7,15},{8,0},{9,1},... | collective-permute-start | bytes 393224 | tf_op jit(solution)/shard_map/ppermute | solution.py:329
  33.2 1.2 %collective-permute-start.16 = (bf16[128,512]{1,0:T(8,128)(2,1)S(1)}, bf16[128,512]{1,0:T(8,128)(2,1)S(1)}, u32[]{:S(2)}, u32[]{:S(2)}) collective-permute-start(bf16[128,512]{1,0:T(8,128)(2,1)S(1)} %get-tuple-element.56), channel_id=1, source_target_pairs={{0,12},{1,13},{2,14},{3,15},{4,8},{5,9},{6,10},{7,11},{8,4},{9,5},... | collective-permute-start | bytes 393224 | tf_op jit(solution)/shard_map/ppermute | solution.py:329
  34.4 1.0 %shard_map.78 = (f32[128,512]{1,0:T(8,128)S(1)}, bf16[128,512]{1,0:T(8,128)(2,1)S(1)}, f32[128,512]{1,0:T(8,128)S(1)}) custom-call(f32[8,1024]{1,0:T(8,128)S(1)} %get-tuple-element.46.weight_ref, f32[8,1024]{1,0:T(8,128)S(1)} %get-tuple-element.40.pick_ref, bf16[544,512]{1,0:T(8,128)(2,1)S(1)} %shard_map.71.own_ref.own_stack, ...), custom_call_target="tpu_custom_call" | custom-call | flops 805306368 | bytes 2097152 | tf_op jit(solution)/shard_map/pallas_call | solution.py:390
  35.4 0.5 %collective-permute-done.17.other_ref = bf16[128,512]{1,0:T(8,128)(2,1)S(1)} collective-permute-done((bf16[128,512]{1,0:T(8,128)(2,1)S(1)}, bf16[128,512]{1,0:T(8,128)(2,1)S(1)}, u32[]{:S(2)}, u32[]{:S(2)}) %collective-permute-start.17) | collective-permute-done | bytes 131104 | tf_op jit(solution)/shard_map/ppermute | solution.py:329
  35.9 3.1 %collective-permute-start.18 = (bf16[128,512]{1,0:T(8,128)(2,1)S(1)}, bf16[128,512]{1,0:T(8,128)(2,1)S(1)}, u32[]{:S(2)}, u32[]{:S(2)}) collective-permute-start(bf16[128,512]{1,0:T(8,128)(2,1)S(1)} %get-tuple-element.60), channel_id=1, source_target_pairs={{0,16},{1,17},{2,18},{3,19},{4,20},{5,21},{6,22},{7,23},{8,24},{9,... | collective-permute-start | bytes 393224 | tf_op jit(solution)/shard_map/ppermute | solution.py:329
  39.0 1.2 %collective-permute-start.19 = (bf16[128,512]{1,0:T(8,128)(2,1)S(1)}, bf16[128,512]{1,0:T(8,128)(2,1)S(1)}, u32[]{:S(2)}, u32[]{:S(2)}) collective-permute-start(bf16[128,512]{1,0:T(8,128)(2,1)S(1)} %get-tuple-element.61), channel_id=1, source_target_pairs={{0,2},{1,3},{2,0},{3,1},{4,6},{5,7},{6,4},{7,5},{8,10},{9,11},{10,... | collective-permute-start | bytes 393224 | tf_op jit(solution)/shard_map/ppermute | solution.py:329
  40.2 2.0 %shard_map.79 = (f32[128,512]{1,0:T(8,128)S(1)}, f32[128,512]{1,0:T(8,128)S(1)}, f32[128,512]{1,0:T(8,128)S(1)}, f32[128,512]{1,0:T(8,128)S(1)}, f32[128,128]{1,0:T(8,128)S(1)}, /*index=5*/f32[1,128]{1,0:T(1,128)}) custom-call(bf16[384,512]{1,0:T(8,128)(2,1)S(1)} %shard_map.69.near_own.refs_0_, ...), custom_call_target="tpu_custom_call" | custom-call | flops 65536 | bytes 65536 | tf_op jit(solution)/shard_map/pallas_call | solution.py:403
  42.2 1.1 %collective-permute-done.16.refs_3_ = bf16[128,512]{1,0:T(8,128)(2,1)S(1)} collective-permute-done((bf16[128,512]{1,0:T(8,128)(2,1)S(1)}, bf16[128,512]{1,0:T(8,128)(2,1)S(1)}, u32[]{:S(2)}, u32[]{:S(2)}) %collective-permute-start.16) | collective-permute-done | bytes 131104 | tf_op jit(solution)/shard_map/ppermute | solution.py:329
  43.5 0.5 %collective-permute-done.19.refs_5_ = bf16[128,512]{1,0:T(8,128)(2,1)S(1)} collective-permute-done((bf16[128,512]{1,0:T(8,128)(2,1)S(1)}, bf16[128,512]{1,0:T(8,128)(2,1)S(1)}, u32[]{:S(2)}, u32[]{:S(2)}) %collective-permute-start.19) | collective-permute-done | bytes 131104 | tf_op jit(solution)/shard_map/ppermute | solution.py:329
  44.0 1.0 %shard_map.81 = (f32[128,512]{1,0:T(8,128)}, f32[128,512]{1,0:T(8,128)}) custom-call(f32[128,512]{1,0:T(8,128)S(1)} %get-tuple-element.48.prog_base, f32[128,512]{1,0:T(8,128)S(1)} %get-tuple-element.49.trace_base, f32[128,512]{1,0:T(8,128)S(1)} %get-tuple-element.50.prog_unit, f32[128,512]{1,0:T(8,128)S(1)} %get-tuple-element.51.trace_unit, ...), custom_call_target="tpu_custom_call" | custom-call | flops 65536 | bytes 65536 | tf_op jit(solution)/shard_map/pallas_call | solution.py:410
  (31 shorter events, 1.3 us)
Async XLA Ops:
  2.8 10.7 %collective-permute-start.1 = (bf16[128,512]{1,0:T(8,128)(2,1)}, bf16[128,512]{1,0:T(8,128)(2,1)S(1)}, u32[]{:S(2)}, u32[]{:S(2)}) collective-permute-start(bf16[128,512]{1,0:T(8,128)(2,1)} %get-tuple-element.34.refs_0_), channel_id=1, source_target_pairs={{0,16},{1,17},{2,18},{3,19},{4,20},{5,21},{6,22},{7,23},{8,24},{9,... | collective-permute-start | bytes 393224 | tf_op jit(solution)/shard_map/ppermute | solution.py:329
  6.9 8.5 %collective-permute-start = (bf16[128,512]{1,0:T(8,128)(2,1)}, bf16[128,512]{1,0:T(8,128)(2,1)S(1)}, u32[]{:S(2)}, u32[]{:S(2)}) collective-permute-start(bf16[128,512]{1,0:T(8,128)(2,1)} %get-tuple-element.34.refs_0_), channel_id=1, source_target_pairs={{0,2},{1,3},{2,0},{3,1},{4,6},{5,7},{6,4},{7,5},{8,10},{9,11},{10,... | collective-permute-start | bytes 393224 | tf_op jit(solution)/shard_map/ppermute | solution.py:329
  8.4 7.6 %collective-permute-start.4 = (bf16[144,512]{1,0:T(8,128)(2,1)}, bf16[144,512]{1,0:T(8,128)(2,1)S(1)}, u32[]{:S(2)}, u32[]{:S(2)}) collective-permute-start(bf16[144,512]{1,0:T(8,128)(2,1)} %get-tuple-element.36), channel_id=1, source_target_pairs={{0,4},{1,5},{2,6},{3,7},{4,0},{5,1},{6,2},{7,3},{8,12},{9,13},{10,... | collective-permute-start | bytes 442376 | tf_op jit(solution)/shard_map/ppermute | solution.py:329
  9.9 7.0 %collective-permute-start.5 = (bf16[144,512]{1,0:T(8,128)(2,1)}, bf16[144,512]{1,0:T(8,128)(2,1)S(1)}, u32[]{:S(2)}, u32[]{:S(2)}) collective-permute-start(bf16[144,512]{1,0:T(8,128)(2,1)} %get-tuple-element.37), channel_id=1, source_target_pairs={{0,8},{1,9},{2,10},{3,11},{4,12},{5,13},{6,14},{7,15},{8,0},{9,1},... | collective-permute-start | bytes 442376 | tf_op jit(solution)/shard_map/ppermute | solution.py:329
  11.5 3.7 %copy-start = (f32[128,512]{1,0:T(8,128)S(1)}, f32[128,512]{1,0:T(8,128)}, u32[]{:S(2)}) copy-start(f32[128,512]{1,0:T(8,128)} %refs_4_.1) | copy-start | bytes 786436
  11.5 3.7 %copy-start.1 = (f32[128,512]{1,0:T(8,128)S(1)}, f32[128,512]{1,0:T(8,128)}, u32[]{:S(2)}) copy-start(f32[128,512]{1,0:T(8,128)} %refs_5_.1) | copy-start | bytes 786436
  11.5 8.2 %collective-permute-start.6 = (bf16[144,512]{1,0:T(8,128)(2,1)}, bf16[144,512]{1,0:T(8,128)(2,1)S(1)}, u32[]{:S(2)}, u32[]{:S(2)}) collective-permute-start(bf16[144,512]{1,0:T(8,128)(2,1)} %get-tuple-element.38), channel_id=1, source_target_pairs={{0,12},{1,13},{2,14},{3,15},{4,8},{5,9},{6,10},{7,11},{8,4},{9,5},... | collective-permute-start | bytes 442376 | tf_op jit(solution)/shard_map/ppermute | solution.py:329
  13.5 2.4 %copy-start.3 = (bf16[128,512]{1,0:T(8,128)(2,1)S(1)}, bf16[128,512]{1,0:T(8,128)(2,1)}, u32[]{:S(2)}) copy-start(bf16[128,512]{1,0:T(8,128)(2,1)} %get-tuple-element.34.refs_0_) | copy-start | bytes 393220
  13.6 6.5 %collective-permute-start.8 = (bf16[128,512]{1,0:T(8,128)(2,1)S(1)}, bf16[128,512]{1,0:T(8,128)(2,1)S(1)}, u32[]{:S(2)}, u32[]{:S(2)}) collective-permute-start(bf16[128,512]{1,0:T(8,128)(2,1)S(1)} %shard_map.68.refs_2_.refs_0_), channel_id=1, source_target_pairs={{0,2},{1,3},{2,0},{3,1},{4,6},{5,7},{6,4},{7,5},{8,10},{9,11},{10,... | collective-permute-start | bytes 393224 | tf_op jit(solution)/shard_map/ppermute | solution.py:329
  15.4 4.3 %copy-start.2 = (bf16[144,512]{1,0:T(8,128)(2,1)S(1)}, bf16[144,512]{1,0:T(8,128)(2,1)}, u32[]{:S(2)}) copy-start(bf16[144,512]{1,0:T(8,128)(2,1)} %get-tuple-element.35.refs_0_) | copy-start | bytes 442372
  15.4 14.4 %collective-permute-start.3 = (bf16[384,512]{1,0:T(8,128)(2,1)S(1)}, bf16[384,512]{1,0:T(8,128)(2,1)S(1)}, u32[]{:S(2)}, u32[]{:S(2)}) collective-permute-start(bf16[384,512]{1,0:T(8,128)(2,1)S(1)} %shard_map.70.own_ref), channel_id=1, source_target_pairs={{0,2},{1,3},{2,0},{3,1},{4,6},{5,7},{6,4},{7,5},{8,10},{9,11},{10,... | collective-permute-start | bytes 1179656 | tf_op jit(solution)/shard_map/ppermute | solution.py:329
  16.0 4.4 %collective-permute-start.2 = (bf16[384,512]{1,0:T(8,128)(2,1)S(1)}, bf16[384,512]{1,0:T(8,128)(2,1)S(1)}, u32[]{:S(2)}, u32[]{:S(2)}) collective-permute-start(bf16[384,512]{1,0:T(8,128)(2,1)S(1)} %shard_map.69.near_own.refs_0_), channel_id=1, source_target_pairs={{0,1},{1,0},{2,3},{3,2},{4,5},{5,4},{6,7},{7,6},{8,9},{9,8},{10,11... | collective-permute-start | bytes 1179656 | tf_op jit(solution)/shard_map/ppermute | solution.py:329
  19.7 2.0 %collective-permute-start.7 = (bf16[544,512]{1,0:T(8,128)(2,1)S(1)}, bf16[544,512]{1,0:T(8,128)(2,1)S(1)}, u32[]{:S(2)}, u32[]{:S(2)}) collective-permute-start(bf16[544,512]{1,0:T(8,128)(2,1)S(1)} %shard_map.71.own_ref.own_stack), channel_id=1, source_target_pairs={{0,1},{1,0},{2,3},{3,2},{4,5},{5,4},{6,7},{7,6},{8,9},{9,8},{10,11... | collective-permute-start | bytes 1671176 | tf_op jit(solution)/shard_map/ppermute | solution.py:329
  20.1 2.8 %collective-permute-start.9 = (bf16[128,512]{1,0:T(8,128)(2,1)S(1)}, bf16[128,512]{1,0:T(8,128)(2,1)S(1)}, u32[]{:S(2)}, u32[]{:S(2)}) collective-permute-start(bf16[128,512]{1,0:T(8,128)(2,1)S(1)} %shard_map.73.far_own), channel_id=1, source_target_pairs={{0,1},{1,0},{2,3},{3,2},{4,5},{5,4},{6,7},{7,6},{8,9},{9,8},{10,11... | collective-permute-start | bytes 393224 | tf_op jit(solution)/shard_map/ppermute | solution.py:329
  23.3 4.8 %collective-permute-start.12 = (f32[1,1024]{1,0:T(1,128)S(1)}, f32[1,1024]{1,0:T(1,128)S(1)}, u32[]{:S(2)}, u32[]{:S(2)}) collective-permute-start(f32[1,1024]{1,0:T(1,128)S(1)} %get-tuple-element.43._.refs_0_), channel_id=1, source_target_pairs={{0,4},{1,5},{2,6},{3,7},{4,0},{5,1},{6,2},{7,3},{8,12},{9,13},{10,... | collective-permute-start | bytes 12296 | tf_op jit(solution)/shard_map/ppermute | solution.py:329
  24.9 3.6 %collective-permute-start.11 = (f32[1,1024]{1,0:T(1,128)S(1)}, f32[1,1024]{1,0:T(1,128)S(1)}, u32[]{:S(2)}, u32[]{:S(2)}) collective-permute-start(f32[1,1024]{1,0:T(1,128)S(1)} %get-tuple-element.43._.refs_0_), channel_id=1, source_target_pairs={{0,8},{1,9},{2,10},{3,11},{4,12},{5,13},{6,14},{7,15},{8,0},{9,1},... | collective-permute-start | bytes 12296 | tf_op jit(solution)/shard_map/ppermute | solution.py:329
  24.9 4.5 %collective-permute-start.10 = (f32[1,1024]{1,0:T(1,128)S(1)}, f32[1,1024]{1,0:T(1,128)S(1)}, u32[]{:S(2)}, u32[]{:S(2)}) collective-permute-start(f32[1,1024]{1,0:T(1,128)S(1)} %get-tuple-element.43._.refs_0_), channel_id=1, source_target_pairs={{0,12},{1,13},{2,14},{3,15},{4,8},{5,9},{6,10},{7,11},{8,4},{9,5},... | collective-permute-start | bytes 12296 | tf_op jit(solution)/shard_map/ppermute | solution.py:329
  29.9 9.1 %collective-permute-start.13 = (bf16[768,512]{1,0:T(8,128)(2,1)S(1)}, bf16[768,512]{1,0:T(8,128)(2,1)S(1)}, u32[]{:S(2)}, u32[]{:S(2)}) collective-permute-start(bf16[768,512]{1,0:T(8,128)(2,1)S(1)} %shard_map.77.refs_2_), channel_id=1, source_target_pairs={{0,1},{1,0},{2,3},{3,2},{4,5},{5,4},{6,7},{7,6},{8,9},{9,8},{10,11... | collective-permute-start | bytes 2359304 | tf_op jit(solution)/shard_map/ppermute | solution.py:329
  30.0 5.9 %collective-permute-start.17 = (bf16[128,512]{1,0:T(8,128)(2,1)S(1)}, bf16[128,512]{1,0:T(8,128)(2,1)S(1)}, u32[]{:S(2)}, u32[]{:S(2)}) collective-permute-start(bf16[128,512]{1,0:T(8,128)(2,1)S(1)} %get-tuple-element.58), channel_id=1, source_target_pairs={{0,2},{1,3},{2,0},{3,1},{4,6},{5,7},{6,4},{7,5},{8,10},{9,11},{10,... | collective-permute-start | bytes 393224 | tf_op jit(solution)/shard_map/ppermute | solution.py:329
  30.9 11.3 %collective-permute-start.14 = (bf16[128,512]{1,0:T(8,128)(2,1)S(1)}, bf16[128,512]{1,0:T(8,128)(2,1)S(1)}, u32[]{:S(2)}, u32[]{:S(2)}) collective-permute-start(bf16[128,512]{1,0:T(8,128)(2,1)S(1)} %get-tuple-element.54), channel_id=1, source_target_pairs={{0,4},{1,5},{2,6},{3,7},{4,0},{5,1},{6,2},{7,3},{8,12},{9,13},{10,... | collective-permute-start | bytes 393224 | tf_op jit(solution)/shard_map/ppermute | solution.py:329
  32.1 10.2 %collective-permute-start.15 = (bf16[128,512]{1,0:T(8,128)(2,1)S(1)}, bf16[128,512]{1,0:T(8,128)(2,1)S(1)}, u32[]{:S(2)}, u32[]{:S(2)}) collective-permute-start(bf16[128,512]{1,0:T(8,128)(2,1)S(1)} %get-tuple-element.55), channel_id=1, source_target_pairs={{0,8},{1,9},{2,10},{3,11},{4,12},{5,13},{6,14},{7,15},{8,0},{9,1},... | collective-permute-start | bytes 393224 | tf_op jit(solution)/shard_map/ppermute | solution.py:329
  33.2 10.1 %collective-permute-start.16 = (bf16[128,512]{1,0:T(8,128)(2,1)S(1)}, bf16[128,512]{1,0:T(8,128)(2,1)S(1)}, u32[]{:S(2)}, u32[]{:S(2)}) collective-permute-start(bf16[128,512]{1,0:T(8,128)(2,1)S(1)} %get-tuple-element.56), channel_id=1, source_target_pairs={{0,12},{1,13},{2,14},{3,15},{4,8},{5,9},{6,10},{7,11},{8,4},{9,5},... | collective-permute-start | bytes 393224 | tf_op jit(solution)/shard_map/ppermute | solution.py:329
  35.9 7.6 %collective-permute-start.18 = (bf16[128,512]{1,0:T(8,128)(2,1)S(1)}, bf16[128,512]{1,0:T(8,128)(2,1)S(1)}, u32[]{:S(2)}, u32[]{:S(2)}) collective-permute-start(bf16[128,512]{1,0:T(8,128)(2,1)S(1)} %get-tuple-element.60), channel_id=1, source_target_pairs={{0,16},{1,17},{2,18},{3,19},{4,20},{5,21},{6,22},{7,23},{8,24},{9,... | collective-permute-start | bytes 393224 | tf_op jit(solution)/shard_map/ppermute | solution.py:329
  39.0 5.0 %collective-permute-start.19 = (bf16[128,512]{1,0:T(8,128)(2,1)S(1)}, bf16[128,512]{1,0:T(8,128)(2,1)S(1)}, u32[]{:S(2)}, u32[]{:S(2)}) collective-permute-start(bf16[128,512]{1,0:T(8,128)(2,1)S(1)} %get-tuple-element.61), channel_id=1, source_target_pairs={{0,2},{1,3},{2,0},{3,1},{4,6},{5,7},{6,4},{7,5},{8,10},{9,11},{10,... | collective-permute-start | bytes 393224 | tf_op jit(solution)/shard_map/ppermute | solution.py:329

commit v7 on v6

--- a/solution.py
+++ b/solution.py
@@ -376,7 +376,7 @@
     exps, sums = call(functools.partial(score_far, planes), lists[1:], LAST, 0)(
         exps, picks, *stacks, far, other_far
     )
-    all_sums = [sums] + [to_plane(sums, k) for k in far_first]
+    all_sums = [sums] + [to_plane(sums, k) for k in [2] + [k for k in far_first if k != 2]]
 
     mark, prog_own, *prog_parts = call(
         functools.partial(program_terms, planes),

time: 45.2 us -> 44.2 us (0.978)
  starting transfers between devices: 24 us -> 22.8 us
    ppermute x20, starting transfers between devices: 24 us -> 22.8 us  [flipped(): return lax.ppermute(value, both, [(i, i ^ bits) for i in range(size)])]
  transfers between devices with their start and end apart: 20 -> 20, of which waited for: 11 -> 10; matrix products, arithmetic and copies ran while one was open for 0% -> 0% of each run, Pallas kernels for 15% -> 15%
where the time goes in v7:
time: 44.2 us; the launch traced here: 44.1 us
  starting transfers between devices  22.8 us (52%)
  waiting for transfers between devices  10.6 us (24%)
  Pallas kernels  9.85 us (22%)
  between operations  0.81 us (2%)
    ppermute x20, starting transfers between devices, flipped(): return lax.ppermute(value, both, [(i, i ^ bits) for i in range(size)])  22.8 us
    ppermute x20, waiting for transfers between devices, flipped(): return lax.ppermute(value, both, [(i, i ^ bits) for i in range(size)])  10.6 us
    pallas_call x1, Pallas kernels, on_device(): call(functools.partial(prepare, planes), [((rows + MORE, feat), LOW)] * p...  2.17 us
    pallas_call x1, Pallas kernels, on_device(): call(group_terms, [(shape, F32)] * 4 + [((rows, rows), F32), ((1, rows),...  2.01 us
    pallas_call x1, Pallas kernels, on_device(): call(functools.partial(program_terms, planes), [((8, rows), F32), (shape,...  1.27 us
    pallas_call x1, Pallas kernels, on_device(): call(functools.partial(score_near, planes), lists, NEAR, 0)  1.08 us
    pallas_call x1, Pallas kernels, on_device(): call(functools.partial(finish, planes), [(shape, F32)] * 2, block, block)  1.03 us
    pallas_call x1, Pallas kernels, on_device(): call(functools.partial(near_terms, planes), [(shape, F32), (shape, LOW),...  0.97 us
  transfers between devices with their start and end apart: 20, of which 10 were waited for; matrix products, arithmetic and copies ran while one was open for 0% of the time, Pallas kernels for 15%

profile of v7, /device:TPU:0, one launch (start us, length us, event | category | flops | bytes accessed | tf_op | source)
XLA Modules:
  0.0 44.1 jit_solution(16051110311323040167)
XLA Ops:
  0.6 2.2 %shard_map.67 = (bf16[144,512]{1,0:T(8,128)(2,1)}, bf16[144,512]{1,0:T(8,128)(2,1)}, bf16[144,512]{1,0:T(8,128)(2,1)}, bf16[144,512]{1,0:T(8,128)(2,1)}, bf16[128,512]{1,0:T(8,128)(2,1)}) custom-call(f32[128,512]{1,0:T(8,128)} %refs_4_.1, f32[128,512]{1,0:T(8,128)} %refs_5_.1, s32[16,128]{1,0:T(8,128)} %bitcast.3, s32[16,128]{1,0:T(8,128)} %bitcast.4), custom_call_target="tpu_custom_call" | custom-call | flops 655360 | bytes 1310720 | tf_op jit(solution)/shard_map/pallas_call | solution.py:339
  2.8 4.1 %collective-permute-start.1 = (bf16[128,512]{1,0:T(8,128)(2,1)}, bf16[128,512]{1,0:T(8,128)(2,1)S(1)}, u32[]{:S(2)}, u32[]{:S(2)}) collective-permute-start(bf16[128,512]{1,0:T(8,128)(2,1)} %get-tuple-element.34.refs_0_), channel_id=1, source_target_pairs={{0,16},{1,17},{2,18},{3,19},{4,20},{5,21},{6,22},{7,23},{8,24},{9,... | collective-permute-start | bytes 393224 | tf_op jit(solution)/shard_map/ppermute | solution.py:329
  6.9 1.5 %collective-permute-start = (bf16[128,512]{1,0:T(8,128)(2,1)}, bf16[128,512]{1,0:T(8,128)(2,1)S(1)}, u32[]{:S(2)}, u32[]{:S(2)}) collective-permute-start(bf16[128,512]{1,0:T(8,128)(2,1)} %get-tuple-element.34.refs_0_), channel_id=1, source_target_pairs={{0,2},{1,3},{2,0},{3,1},{4,6},{5,7},{6,4},{7,5},{8,10},{9,11},{10,... | collective-permute-start | bytes 393224 | tf_op jit(solution)/shard_map/ppermute | solution.py:329
  8.4 1.5 %collective-permute-start.4 = (bf16[144,512]{1,0:T(8,128)(2,1)}, bf16[144,512]{1,0:T(8,128)(2,1)S(1)}, u32[]{:S(2)}, u32[]{:S(2)}) collective-permute-start(bf16[144,512]{1,0:T(8,128)(2,1)} %get-tuple-element.36), channel_id=1, source_target_pairs={{0,4},{1,5},{2,6},{3,7},{4,0},{5,1},{6,2},{7,3},{8,12},{9,13},{10,... | collective-permute-start | bytes 442376 | tf_op jit(solution)/shard_map/ppermute | solution.py:329
  9.9 1.6 %collective-permute-start.5 = (bf16[144,512]{1,0:T(8,128)(2,1)}, bf16[144,512]{1,0:T(8,128)(2,1)S(1)}, u32[]{:S(2)}, u32[]{:S(2)}) collective-permute-start(bf16[144,512]{1,0:T(8,128)(2,1)} %get-tuple-element.37), channel_id=1, source_target_pairs={{0,8},{1,9},{2,10},{3,11},{4,12},{5,13},{6,14},{7,15},{8,0},{9,1},... | collective-permute-start | bytes 442376 | tf_op jit(solution)/shard_map/ppermute | solution.py:329
  11.5 0.4 collective-permute-start.6
  11.9 1.6 %collective-permute-done.1.refs_0_ = bf16[128,512]{1,0:T(8,128)(2,1)S(1)} collective-permute-done((bf16[128,512]{1,0:T(8,128)(2,1)}, bf16[128,512]{1,0:T(8,128)(2,1)S(1)}, u32[]{:S(2)}, u32[]{:S(2)}) %collective-permute-start.1) | collective-permute-done | bytes 131104 | tf_op jit(solution)/shard_map/ppermute | solution.py:329
  13.6 1.6 %collective-permute-start.8 = (bf16[128,512]{1,0:T(8,128)(2,1)S(1)}, bf16[128,512]{1,0:T(8,128)(2,1)S(1)}, u32[]{:S(2)}, u32[]{:S(2)}) collective-permute-start(bf16[128,512]{1,0:T(8,128)(2,1)S(1)} %shard_map.68.refs_2_.refs_0_), channel_id=1, source_target_pairs={{0,2},{1,3},{2,0},{3,1},{4,6},{5,7},{6,4},{7,5},{8,10},{9,11},{10,... | collective-permute-start | bytes 393224 | tf_op jit(solution)/shard_map/ppermute | solution.py:329
  15.4 0.5 %collective-permute-start.3 = (bf16[384,512]{1,0:T(8,128)(2,1)S(1)}, bf16[384,512]{1,0:T(8,128)(2,1)S(1)}, u32[]{:S(2)}, u32[]{:S(2)}) collective-permute-start(bf16[384,512]{1,0:T(8,128)(2,1)S(1)} %shard_map.70.own_ref), channel_id=1, source_target_pairs={{0,2},{1,3},{2,0},{3,1},{4,6},{5,7},{6,4},{7,5},{8,10},{9,11},{10,... | collective-permute-start | bytes 1179656 | tf_op jit(solution)/shard_map/ppermute | solution.py:329
  16.1 0.9 %collective-permute-done.5.refs_2_ = bf16[144,512]{1,0:T(8,128)(2,1)S(1)} collective-permute-done((bf16[144,512]{1,0:T(8,128)(2,1)}, bf16[144,512]{1,0:T(8,128)(2,1)S(1)}, u32[]{:S(2)}, u32[]{:S(2)}) %collective-permute-start.5) | collective-permute-done | bytes 147488 | tf_op jit(solution)/shard_map/ppermute | solution.py:329
  16.9 2.8 %collective-permute-done.6.refs_3_ = bf16[144,512]{1,0:T(8,128)(2,1)S(1)} collective-permute-done((bf16[144,512]{1,0:T(8,128)(2,1)}, bf16[144,512]{1,0:T(8,128)(2,1)S(1)}, u32[]{:S(2)}, u32[]{:S(2)}) %collective-permute-start.6) | collective-permute-done | bytes 147488 | tf_op jit(solution)/shard_map/ppermute | solution.py:329
  20.1 0.3 collective-permute-start.9
  20.4 1.4 %collective-permute-done.7.other_ref.other_stack = bf16[544,512]{1,0:T(8,128)(2,1)S(1)} collective-permute-done((bf16[544,512]{1,0:T(8,128)(2,1)S(1)}, bf16[544,512]{1,0:T(8,128)(2,1)S(1)}, u32[]{:S(2)}, u32[]{:S(2)}) %collective-permute-start.7) | collective-permute-done | bytes 557088 | tf_op jit(solution)/shard_map/ppermute | solution.py:329
  21.7 1.1 %shard_map.72 = (f32[8,1024]{1,0:T(8,128)S(1)}, f32[8,1024]{1,0:T(8,128)S(1)}, f32[1,1024]{1,0:T(1,128)S(1)}) custom-call(bf16[544,512]{1,0:T(8,128)(2,1)S(1)} %shard_map.71.own_ref.own_stack, bf16[544,512]{1,0:T(8,128)(2,1)S(1)} %collective-permute-done.7.other_ref.other_stack, bf16[384,512]{1,0:T(8,128)(2,1)S(1)} %shard_map.69.near_own.refs_0_, ...), custom_call_target="tpu_custom_call" | custom-call | flops 100000000 | tf_op jit(solution)/shard_map/pallas_call | solution.py:373
  22.8 0.5 %shard_map.74 = (f32[8,1024]{1,0:T(8,128)S(1)}, f32[1,1024]{1,0:T(1,128)S(1)}) custom-call(f32[8,1024]{1,0:T(8,128)S(1)} %get-tuple-element.39.exp_in, f32[8,1024]{1,0:T(8,128)S(1)} %get-tuple-element.40.pick_ref, bf16[544,512]{1,0:T(8,128)(2,1)S(1)} %shard_map.71.own_ref.own_stack, bf16[544,512]{1,0:T(8,128)(2,1)S(1)} %collective-permute-done.7.other_ref.other_stack, ...), custom_call_target="tpu_custom_call" | custom-call | flops 300000000 | tf_op jit(solution)/shard_map/pallas_call | solution.py:376
  23.3 1.5 %collective-permute-start.12 = (f32[1,1024]{1,0:T(1,128)S(1)}, f32[1,1024]{1,0:T(1,128)S(1)}, u32[]{:S(2)}, u32[]{:S(2)}) collective-permute-start(f32[1,1024]{1,0:T(1,128)S(1)} %get-tuple-element.43._.refs_0_), channel_id=1, source_target_pairs={{0,4},{1,5},{2,6},{3,7},{4,0},{5,1},{6,2},{7,3},{8,12},{9,13},{10,... | collective-permute-start | bytes 12296 | tf_op jit(solution)/shard_map/ppermute | solution.py:329
  24.9 2.0 %collective-permute-start.10 = (f32[1,1024]{1,0:T(1,128)S(1)}, f32[1,1024]{1,0:T(1,128)S(1)}, u32[]{:S(2)}, u32[]{:S(2)}) collective-permute-start(f32[1,1024]{1,0:T(1,128)S(1)} %get-tuple-element.43._.refs_0_), channel_id=1, source_target_pairs={{0,8},{1,9},{2,10},{3,11},{4,12},{5,13},{6,14},{7,15},{8,0},{9,1},... | collective-permute-start | bytes 12296 | tf_op jit(solution)/shard_map/ppermute | solution.py:329
  26.9 1.3 %shard_map.75 = (f32[8,128]{1,0:T(8,128)S(1)}, f32[128,512]{1,0:T(8,128)S(1)}, bf16[128,512]{1,0:T(8,128)(2,1)S(1)}, bf16[128,512]{1,0:T(8,128)(2,1)S(1)}, bf16[128,512]{1,0:T(8,128)(2,1)S(1)}) custom-call(f32[8,1024]{1,0:T(8,128)S(1)} %get-tuple-element.41.exp_ref, f32[8,1024]{1,0:T(8,128)S(1)} %get-tuple-element.40.pick_ref, ...), custom_call_target="tpu_custom_call" | custom-call | flops 2000000000 | tf_op jit(solution)/shard_map/pallas_call | solution.py:381
  28.2 1.2 %collective-permute-done.11.refs_2_ = f32[1,1024]{1,0:T(1,128)S(1)} collective-permute-done((f32[1,1024]{1,0:T(1,128)S(1)}, f32[1,1024]{1,0:T(1,128)S(1)}, u32[]{:S(2)}, u32[]{:S(2)}) %collective-permute-start.11) | collective-permute-done | bytes 4128 | tf_op jit(solution)/shard_map/ppermute | solution.py:329
  29.4 0.5 %shard_map.76 = (f32[1,128]{1,0:T(1,128)S(1)}, f32[8,1024]{1,0:T(8,128)S(1)}, bf16[128,512]{1,0:T(8,128)(2,1)S(1)}) custom-call(f32[8,1024]{1,0:T(8,128)S(1)} %get-tuple-element.41.exp_ref, f32[8,1024]{1,0:T(8,128)S(1)} %get-tuple-element.40.pick_ref, f32[1,1024]{1,0:T(1,128)S(1)} %get-tuple-element.42.pos_ref, ...), custom_call_target="tpu_custom_call" | custom-call | tf_op jit(solution)/shard_map/pallas_call | solution.py:387
  30.0 0.6 %collective-permute-start.17 = (bf16[128,512]{1,0:T(8,128)(2,1)S(1)}, bf16[128,512]{1,0:T(8,128)(2,1)S(1)}, u32[]{:S(2)}, u32[]{:S(2)}) collective-permute-start(bf16[128,512]{1,0:T(8,128)(2,1)S(1)} %get-tuple-element.58), channel_id=1, source_target_pairs={{0,2},{1,3},{2,0},{3,1},{4,6},{5,7},{6,4},{7,5},{8,10},{9,11},{10,... | collective-permute-start | bytes 393224 | tf_op jit(solution)/shard_map/ppermute | solution.py:329
  30.6 0.9 %collective-permute-start.14 = (bf16[128,512]{1,0:T(8,128)(2,1)S(1)}, bf16[128,512]{1,0:T(8,128)(2,1)S(1)}, u32[]{:S(2)}, u32[]{:S(2)}) collective-permute-start(bf16[128,512]{1,0:T(8,128)(2,1)S(1)} %get-tuple-element.54), channel_id=1, source_target_pairs={{0,4},{1,5},{2,6},{3,7},{4,0},{5,1},{6,2},{7,3},{8,12},{9,13},{10,... | collective-permute-start | bytes 393224 | tf_op jit(solution)/shard_map/ppermute | solution.py:329
  31.5 1.7 %collective-permute-start.15 = (bf16[128,512]{1,0:T(8,128)(2,1)S(1)}, bf16[128,512]{1,0:T(8,128)(2,1)S(1)}, u32[]{:S(2)}, u32[]{:S(2)}) collective-permute-start(bf16[128,512]{1,0:T(8,128)(2,1)S(1)} %get-tuple-element.55), channel_id=1, source_target_pairs={{0,8},{1,9},{2,10},{3,11},{4,12},{5,13},{6,14},{7,15},{8,0},{9,1},... | collective-permute-start | bytes 393224 | tf_op jit(solution)/shard_map/ppermute | solution.py:329
  33.2 0.9 %collective-permute-start.16 = (bf16[128,512]{1,0:T(8,128)(2,1)S(1)}, bf16[128,512]{1,0:T(8,128)(2,1)S(1)}, u32[]{:S(2)}, u32[]{:S(2)}) collective-permute-start(bf16[128,512]{1,0:T(8,128)(2,1)S(1)} %get-tuple-element.56), channel_id=1, source_target_pairs={{0,12},{1,13},{2,14},{3,15},{4,8},{5,9},{6,10},{7,11},{8,4},{9,5},... | collective-permute-start | bytes 393224 | tf_op jit(solution)/shard_map/ppermute | solution.py:329
  34.1 1.0 %shard_map.78 = (f32[128,512]{1,0:T(8,128)S(1)}, bf16[128,512]{1,0:T(8,128)(2,1)S(1)}, f32[128,512]{1,0:T(8,128)S(1)}) custom-call(f32[8,1024]{1,0:T(8,128)S(1)} %get-tuple-element.46.weight_ref, f32[8,1024]{1,0:T(8,128)S(1)} %get-tuple-element.40.pick_ref, bf16[544,512]{1,0:T(8,128)(2,1)S(1)} %shard_map.71.own_ref.own_stack, ...), custom_call_target="tpu_custom_call" | custom-call | flops 805306368 | bytes 2097152 | tf_op jit(solution)/shard_map/pallas_call | solution.py:390
  35.1 0.8 %collective-permute-done.17.other_ref = bf16[128,512]{1,0:T(8,128)(2,1)S(1)} collective-permute-done((bf16[128,512]{1,0:T(8,128)(2,1)S(1)}, bf16[128,512]{1,0:T(8,128)(2,1)S(1)}, u32[]{:S(2)}, u32[]{:S(2)}) %collective-permute-start.17) | collective-permute-done | bytes 131104 | tf_op jit(solution)/shard_map/ppermute | solution.py:329
  35.9 2.2 %collective-permute-start.18 = (bf16[128,512]{1,0:T(8,128)(2,1)S(1)}, bf16[128,512]{1,0:T(8,128)(2,1)S(1)}, u32[]{:S(2)}, u32[]{:S(2)}) collective-permute-start(bf16[128,512]{1,0:T(8,128)(2,1)S(1)} %get-tuple-element.60), channel_id=1, source_target_pairs={{0,16},{1,17},{2,18},{3,19},{4,20},{5,21},{6,22},{7,23},{8,24},{9,... | collective-permute-start | bytes 393224 | tf_op jit(solution)/shard_map/ppermute | solution.py:329
  38.1 1.2 %collective-permute-start.19 = (bf16[128,512]{1,0:T(8,128)(2,1)S(1)}, bf16[128,512]{1,0:T(8,128)(2,1)S(1)}, u32[]{:S(2)}, u32[]{:S(2)}) collective-permute-start(bf16[128,512]{1,0:T(8,128)(2,1)S(1)} %get-tuple-element.61), channel_id=1, source_target_pairs={{0,2},{1,3},{2,0},{3,1},{4,6},{5,7},{6,4},{7,5},{8,10},{9,11},{10,... | collective-permute-start | bytes 393224 | tf_op jit(solution)/shard_map/ppermute | solution.py:329
  39.3 2.0 %shard_map.79 = (f32[128,512]{1,0:T(8,128)S(1)}, f32[128,512]{1,0:T(8,128)S(1)}, f32[128,512]{1,0:T(8,128)S(1)}, f32[128,512]{1,0:T(8,128)S(1)}, f32[128,128]{1,0:T(8,128)S(1)}, /*index=5*/f32[1,128]{1,0:T(1,128)}) custom-call(bf16[384,512]{1,0:T(8,128)(2,1)S(1)} %shard_map.69.near_own.refs_0_, ...), custom_call_target="tpu_custom_call" | custom-call | flops 65536 | bytes 65536 | tf_op jit(solution)/shard_map/pallas_call | solution.py:403
  41.3 1.2 %collective-permute-done.16.refs_3_ = bf16[128,512]{1,0:T(8,128)(2,1)S(1)} collective-permute-done((bf16[128,512]{1,0:T(8,128)(2,1)S(1)}, bf16[128,512]{1,0:T(8,128)(2,1)S(1)}, u32[]{:S(2)}, u32[]{:S(2)}) %collective-permute-start.16) | collective-permute-done | bytes 131104 | tf_op jit(solution)/shard_map/ppermute | solution.py:329
  42.7 0.3 collective-permute-done.19.refs_5_
  43.1 1.0 %shard_map.81 = (f32[128,512]{1,0:T(8,128)}, f32[128,512]{1,0:T(8,128)}) custom-call(f32[128,512]{1,0:T(8,128)S(1)} %get-tuple-element.48.prog_base, f32[128,512]{1,0:T(8,128)S(1)} %get-tuple-element.49.trace_base, f32[128,512]{1,0:T(8,128)S(1)} %get-tuple-element.50.prog_unit, f32[128,512]{1,0:T(8,128)S(1)} %get-tuple-element.51.trace_unit, ...), custom_call_target="tpu_custom_call" | custom-call | flops 65536 | bytes 65536 | tf_op jit(solution)/shard_map/pallas_call | solution.py:410
  (31 shorter events, 1.1 us)
Async XLA Ops:
  2.8 10.7 %collective-permute-start.1 = (bf16[128,512]{1,0:T(8,128)(2,1)}, bf16[128,512]{1,0:T(8,128)(2,1)S(1)}, u32[]{:S(2)}, u32[]{:S(2)}) collective-permute-start(bf16[128,512]{1,0:T(8,128)(2,1)} %get-tuple-element.34.refs_0_), channel_id=1, source_target_pairs={{0,16},{1,17},{2,18},{3,19},{4,20},{5,21},{6,22},{7,23},{8,24},{9,... | collective-permute-start | bytes 393224 | tf_op jit(solution)/shard_map/ppermute | solution.py:329
  6.9 8.5 %collective-permute-start = (bf16[128,512]{1,0:T(8,128)(2,1)}, bf16[128,512]{1,0:T(8,128)(2,1)S(1)}, u32[]{:S(2)}, u32[]{:S(2)}) collective-permute-start(bf16[128,512]{1,0:T(8,128)(2,1)} %get-tuple-element.34.refs_0_), channel_id=1, source_target_pairs={{0,2},{1,3},{2,0},{3,1},{4,6},{5,7},{6,4},{7,5},{8,10},{9,11},{10,... | collective-permute-start | bytes 393224 | tf_op jit(solution)/shard_map/ppermute | solution.py:329
  8.4 7.6 %collective-permute-start.4 = (bf16[144,512]{1,0:T(8,128)(2,1)}, bf16[144,512]{1,0:T(8,128)(2,1)S(1)}, u32[]{:S(2)}, u32[]{:S(2)}) collective-permute-start(bf16[144,512]{1,0:T(8,128)(2,1)} %get-tuple-element.36), channel_id=1, source_target_pairs={{0,4},{1,5},{2,6},{3,7},{4,0},{5,1},{6,2},{7,3},{8,12},{9,13},{10,... | collective-permute-start | bytes 442376 | tf_op jit(solution)/shard_map/ppermute | solution.py:329
  9.9 7.0 %collective-permute-start.5 = (bf16[144,512]{1,0:T(8,128)(2,1)}, bf16[144,512]{1,0:T(8,128)(2,1)S(1)}, u32[]{:S(2)}, u32[]{:S(2)}) collective-permute-start(bf16[144,512]{1,0:T(8,128)(2,1)} %get-tuple-element.37), channel_id=1, source_target_pairs={{0,8},{1,9},{2,10},{3,11},{4,12},{5,13},{6,14},{7,15},{8,0},{9,1},... | collective-permute-start | bytes 442376 | tf_op jit(solution)/shard_map/ppermute | solution.py:329
  11.5 3.7 %copy-start = (f32[128,512]{1,0:T(8,128)S(1)}, f32[128,512]{1,0:T(8,128)}, u32[]{:S(2)}) copy-start(f32[128,512]{1,0:T(8,128)} %refs_4_.1) | copy-start | bytes 786436
  11.5 3.7 %copy-start.1 = (f32[128,512]{1,0:T(8,128)S(1)}, f32[128,512]{1,0:T(8,128)}, u32[]{:S(2)}) copy-start(f32[128,512]{1,0:T(8,128)} %refs_5_.1) | copy-start | bytes 786436
  11.5 8.2 %collective-permute-start.6 = (bf16[144,512]{1,0:T(8,128)(2,1)}, bf16[144,512]{1,0:T(8,128)(2,1)S(1)}, u32[]{:S(2)}, u32[]{:S(2)}) collective-permute-start(bf16[144,512]{1,0:T(8,128)(2,1)} %get-tuple-element.38), channel_id=1, source_target_pairs={{0,12},{1,13},{2,14},{3,15},{4,8},{5,9},{6,10},{7,11},{8,4},{9,5},... | collective-permute-start | bytes 442376 | tf_op jit(solution)/shard_map/ppermute | solution.py:329
  13.5 2.4 %copy-start.3 = (bf16[128,512]{1,0:T(8,128)(2,1)S(1)}, bf16[128,512]{1,0:T(8,128)(2,1)}, u32[]{:S(2)}) copy-start(bf16[128,512]{1,0:T(8,128)(2,1)} %get-tuple-element.34.refs_0_) | copy-start | bytes 393220
  13.6 6.5 %collective-permute-start.8 = (bf16[128,512]{1,0:T(8,128)(2,1)S(1)}, bf16[128,512]{1,0:T(8,128)(2,1)S(1)}, u32[]{:S(2)}, u32[]{:S(2)}) collective-permute-start(bf16[128,512]{1,0:T(8,128)(2,1)S(1)} %shard_map.68.refs_2_.refs_0_), channel_id=1, source_target_pairs={{0,2},{1,3},{2,0},{3,1},{4,6},{5,7},{6,4},{7,5},{8,10},{9,11},{10,... | collective-permute-start | bytes 393224 | tf_op jit(solution)/shard_map/ppermute | solution.py:329
  15.4 4.3 %copy-start.2 = (bf16[144,512]{1,0:T(8,128)(2,1)S(1)}, bf16[144,512]{1,0:T(8,128)(2,1)}, u32[]{:S(2)}) copy-start(bf16[144,512]{1,0:T(8,128)(2,1)} %get-tuple-element.35.refs_0_) | copy-start | bytes 442372
  15.4 14.4 %collective-permute-start.3 = (bf16[384,512]{1,0:T(8,128)(2,1)S(1)}, bf16[384,512]{1,0:T(8,128)(2,1)S(1)}, u32[]{:S(2)}, u32[]{:S(2)}) collective-permute-start(bf16[384,512]{1,0:T(8,128)(2,1)S(1)} %shard_map.70.own_ref), channel_id=1, source_target_pairs={{0,2},{1,3},{2,0},{3,1},{4,6},{5,7},{6,4},{7,5},{8,10},{9,11},{10,... | collective-permute-start | bytes 1179656 | tf_op jit(solution)/shard_map/ppermute | solution.py:329
  16.0 4.4 %collective-permute-start.2 = (bf16[384,512]{1,0:T(8,128)(2,1)S(1)}, bf16[384,512]{1,0:T(8,128)(2,1)S(1)}, u32[]{:S(2)}, u32[]{:S(2)}) collective-permute-start(bf16[384,512]{1,0:T(8,128)(2,1)S(1)} %shard_map.69.near_own.refs_0_), channel_id=1, source_target_pairs={{0,1},{1,0},{2,3},{3,2},{4,5},{5,4},{6,7},{7,6},{8,9},{9,8},{10,11... | collective-permute-start | bytes 1179656 | tf_op jit(solution)/shard_map/ppermute | solution.py:329
  19.7 2.0 %collective-permute-start.7 = (bf16[544,512]{1,0:T(8,128)(2,1)S(1)}, bf16[544,512]{1,0:T(8,128)(2,1)S(1)}, u32[]{:S(2)}, u32[]{:S(2)}) collective-permute-start(bf16[544,512]{1,0:T(8,128)(2,1)S(1)} %shard_map.71.own_ref.own_stack), channel_id=1, source_target_pairs={{0,1},{1,0},{2,3},{3,2},{4,5},{5,4},{6,7},{7,6},{8,9},{9,8},{10,11... | collective-permute-start | bytes 1671176 | tf_op jit(solution)/shard_map/ppermute | solution.py:329
  20.1 2.8 %collective-permute-start.9 = (bf16[128,512]{1,0:T(8,128)(2,1)S(1)}, bf16[128,512]{1,0:T(8,128)(2,1)S(1)}, u32[]{:S(2)}, u32[]{:S(2)}) collective-permute-start(bf16[128,512]{1,0:T(8,128)(2,1)S(1)} %shard_map.73.far_own), channel_id=1, source_target_pairs={{0,1},{1,0},{2,3},{3,2},{4,5},{5,4},{6,7},{7,6},{8,9},{9,8},{10,11... | collective-permute-start | bytes 393224 | tf_op jit(solution)/shard_map/ppermute | solution.py:329
  23.3 4.8 %collective-permute-start.12 = (f32[1,1024]{1,0:T(1,128)S(1)}, f32[1,1024]{1,0:T(1,128)S(1)}, u32[]{:S(2)}, u32[]{:S(2)}) collective-permute-start(f32[1,1024]{1,0:T(1,128)S(1)} %get-tuple-element.43._.refs_0_), channel_id=1, source_target_pairs={{0,4},{1,5},{2,6},{3,7},{4,0},{5,1},{6,2},{7,3},{8,12},{9,13},{10,... | collective-permute-start | bytes 12296 | tf_op jit(solution)/shard_map/ppermute | solution.py:329
  24.9 4.5 %collective-permute-start.11 = (f32[1,1024]{1,0:T(1,128)S(1)}, f32[1,1024]{1,0:T(1,128)S(1)}, u32[]{:S(2)}, u32[]{:S(2)}) collective-permute-start(f32[1,1024]{1,0:T(1,128)S(1)} %get-tuple-element.43._.refs_0_), channel_id=1, source_target_pairs={{0,12},{1,13},{2,14},{3,15},{4,8},{5,9},{6,10},{7,11},{8,4},{9,5},... | collective-permute-start | bytes 12296 | tf_op jit(solution)/shard_map/ppermute | solution.py:329
  24.9 4.5 %collective-permute-start.10 = (f32[1,1024]{1,0:T(1,128)S(1)}, f32[1,1024]{1,0:T(1,128)S(1)}, u32[]{:S(2)}, u32[]{:S(2)}) collective-permute-start(f32[1,1024]{1,0:T(1,128)S(1)} %get-tuple-element.43._.refs_0_), channel_id=1, source_target_pairs={{0,8},{1,9},{2,10},{3,11},{4,12},{5,13},{6,14},{7,15},{8,0},{9,1},... | collective-permute-start | bytes 12296 | tf_op jit(solution)/shard_map/ppermute | solution.py:329
  29.9 8.2 %collective-permute-start.13 = (bf16[768,512]{1,0:T(8,128)(2,1)S(1)}, bf16[768,512]{1,0:T(8,128)(2,1)S(1)}, u32[]{:S(2)}, u32[]{:S(2)}) collective-permute-start(bf16[768,512]{1,0:T(8,128)(2,1)S(1)} %shard_map.77.refs_2_), channel_id=1, source_target_pairs={{0,1},{1,0},{2,3},{3,2},{4,5},{5,4},{6,7},{7,6},{8,9},{9,8},{10,11... | collective-permute-start | bytes 2359304 | tf_op jit(solution)/shard_map/ppermute | solution.py:329
  30.0 5.9 %collective-permute-start.17 = (bf16[128,512]{1,0:T(8,128)(2,1)S(1)}, bf16[128,512]{1,0:T(8,128)(2,1)S(1)}, u32[]{:S(2)}, u32[]{:S(2)}) collective-permute-start(bf16[128,512]{1,0:T(8,128)(2,1)S(1)} %get-tuple-element.58), channel_id=1, source_target_pairs={{0,2},{1,3},{2,0},{3,1},{4,6},{5,7},{6,4},{7,5},{8,10},{9,11},{10,... | collective-permute-start | bytes 393224 | tf_op jit(solution)/shard_map/ppermute | solution.py:329
  30.6 10.7 %collective-permute-start.14 = (bf16[128,512]{1,0:T(8,128)(2,1)S(1)}, bf16[128,512]{1,0:T(8,128)(2,1)S(1)}, u32[]{:S(2)}, u32[]{:S(2)}) collective-permute-start(bf16[128,512]{1,0:T(8,128)(2,1)S(1)} %get-tuple-element.54), channel_id=1, source_target_pairs={{0,4},{1,5},{2,6},{3,7},{4,0},{5,1},{6,2},{7,3},{8,12},{9,13},{10,... | collective-permute-start | bytes 393224 | tf_op jit(solution)/shard_map/ppermute | solution.py:329
  31.5 9.8 %collective-permute-start.15 = (bf16[128,512]{1,0:T(8,128)(2,1)S(1)}, bf16[128,512]{1,0:T(8,128)(2,1)S(1)}, u32[]{:S(2)}, u32[]{:S(2)}) collective-permute-start(bf16[128,512]{1,0:T(8,128)(2,1)S(1)} %get-tuple-element.55), channel_id=1, source_target_pairs={{0,8},{1,9},{2,10},{3,11},{4,12},{5,13},{6,14},{7,15},{8,0},{9,1},... | collective-permute-start | bytes 393224 | tf_op jit(solution)/shard_map/ppermute | solution.py:329
  33.2 9.2 %collective-permute-start.16 = (bf16[128,512]{1,0:T(8,128)(2,1)S(1)}, bf16[128,512]{1,0:T(8,128)(2,1)S(1)}, u32[]{:S(2)}, u32[]{:S(2)}) collective-permute-start(bf16[128,512]{1,0:T(8,128)(2,1)S(1)} %get-tuple-element.56), channel_id=1, source_target_pairs={{0,12},{1,13},{2,14},{3,15},{4,8},{5,9},{6,10},{7,11},{8,4},{9,5},... | collective-permute-start | bytes 393224 | tf_op jit(solution)/shard_map/ppermute | solution.py:329
  35.9 6.8 %collective-permute-start.18 = (bf16[128,512]{1,0:T(8,128)(2,1)S(1)}, bf16[128,512]{1,0:T(8,128)(2,1)S(1)}, u32[]{:S(2)}, u32[]{:S(2)}) collective-permute-start(bf16[128,512]{1,0:T(8,128)(2,1)S(1)} %get-tuple-element.60), channel_id=1, source_target_pairs={{0,16},{1,17},{2,18},{3,19},{4,20},{5,21},{6,22},{7,23},{8,24},{9,... | collective-permute-start | bytes 393224 | tf_op jit(solution)/shard_map/ppermute | solution.py:329
  38.1 5.0 %collective-permute-start.19 = (bf16[128,512]{1,0:T(8,128)(2,1)S(1)}, bf16[128,512]{1,0:T(8,128)(2,1)S(1)}, u32[]{:S(2)}, u32[]{:S(2)}) collective-permute-start(bf16[128,512]{1,0:T(8,128)(2,1)S(1)} %get-tuple-element.61), channel_id=1, source_target_pairs={{0,2},{1,3},{2,0},{3,1},{4,6},{5,7},{6,4},{7,5},{8,10},{9,11},{10,... | collective-permute-start | bytes 393224 | tf_op jit(solution)/shard_map/ppermute | solution.py:329

commit v8 on v7

--- a/solution.py
+++ b/solution.py
@@ -287,7 +287,9 @@
 
 
 def finish(planes, prog_base, trace_base, prog_unit, trace_unit, size_ref, *refs):
-    progs, traces, (prog_out, trace_out) = refs[:planes], refs[planes : planes + 2], refs[planes + 2 :]
+    progs, traces, refs = refs[:planes], refs[planes : planes + 2], refs[planes + 2 :]
+    results, made, sems = refs[:2], refs[2:4], refs[4]
+    copies = [pltpu.make_async_copy(made[i], results[i], sems.at[i]) for i in range(2)]
     back = trace_base[...]
     for one in traces:
         back = back + one[...].astype(F32)
@@ -295,20 +297,21 @@
     for one in progs[1:]:
         hard = hard + one[...].astype(F32)
     direction = prog_base[...] + size_ref[:, 2:3] * hard
-    for unit, towards, length, out in (
-        (prog_unit[...], direction, size_ref[:, 0:1], prog_out),
-        (trace_unit[...], back, size_ref[:, 1:2], trace_out),
-    ):
+    for i, (unit, towards) in enumerate(((prog_unit[...], direction), (trace_unit[...], back))):
         along = jnp.sum(unit * towards, axis=-1, keepdims=True)
-        out[...] = (towards - unit * along) / length
-
-
-def call(body, outs, flops, moved, scratch=(), in_specs=None, limit=VMEM_LIMIT):
+        made[i][...] = (towards - unit * along) / size_ref[:, i : i + 1]
+        copies[i].start()
+    for copy in copies:
+        copy.wait()
+
+
+def call(body, outs, flops, moved, scratch=(), in_specs=None, limit=VMEM_LIMIT, out_specs=None):
     return pl.pallas_call(
         body,
         out_shape=[jax.ShapeDtypeStruct(shape, dtype) for shape, dtype in outs],
         scratch_shapes=list(scratch),
         **({"in_specs": in_specs} if in_specs else {}),
+        **({"out_specs": out_specs} if out_specs else {}),
         compiler_params=pltpu.CompilerParams(vmem_limit_bytes=limit),
         cost_estimate=pl.CostEstimate(flops=flops, bytes_accessed=moved, transcendentals=0),
     )
@@ -399,7 +402,7 @@
     trace_back = [flipped(for_h, h_bit), flipped(part_x, x_bit)]
 
     groups = call(joined, [((6 * rows, feat), LOW)], JOIN, 0)(group, group_x, total)[0]
-    prog_back = [to_plane(part, k) for k, part in enumerate(prog_parts, 1)]
+    prog_back = [to_plane(prog_parts[k - 1], k) for k in [1] + far_first[:-1]]
     *bases, loss = call(
         group_terms,
         [(shape, F32)] * 4 + [((rows, rows), F32), ((1, rows), F32)],
@@ -408,7 +411,14 @@
     )(near, other_near, groups, flipped(groups, 1), programs, traces, total, trace_own)
 
     grad_programs, grad_traces = call(
-        functools.partial(finish, planes), [(shape, F32)] * 2, block, block
+        functools.partial(finish, planes),
+        [(shape, F32)] * 2,
+        block,
+        block,
+        [pltpu.VMEM(shape, F32), pltpu.VMEM(shape, F32), pltpu.SemaphoreType.DMA((2,))],
+        None,
+        VMEM_LIMIT,
+        [hbm] * 2,
     )(*bases, prog_own, *prog_back, *trace_back)
     return grad_programs, grad_traces, loss.reshape(rows)
 

time: 44.2 us -> 44.3 us (level)
  transfers between devices with their start and end apart: 20 -> 20, of which waited for: 10 -> 8; matrix products, arithmetic and copies ran while one was open for 0% -> 0% of each run, Pallas kernels for 15% -> 15%
where the time goes in v8:
time: 44.3 us; the launch traced here: 44.1 us
  starting transfers between devices  22.8 us (51%)
  waiting for transfers between devices  10.6 us (24%)
  Pallas kernels  9.87 us (22%)
  between operations  0.81 us (2%)
    ppermute x20, starting transfers between devices, flipped(): return lax.ppermute(value, both, [(i, i ^ bits) for i in range(size)])  22.8 us
    ppermute x20, waiting for transfers between devices, flipped(): return lax.ppermute(value, both, [(i, i ^ bits) for i in range(size)])  10.6 us
    pallas_call x1, Pallas kernels, on_device(): call(functools.partial(prepare, planes), [((rows + MORE, feat), LOW)] * p...  2.17 us
    pallas_call x1, Pallas kernels, on_device(): call(group_terms, [(shape, F32)] * 4 + [((rows, rows), F32), ((1, rows),...  2.01 us
    pallas_call x1, Pallas kernels, on_device(): call(functools.partial(program_terms, planes), [((8, rows), F32), (shape,...  1.27 us
    pallas_call x1, Pallas kernels, on_device(): call(functools.partial(score_near, planes), lists, NEAR, 0)  1.08 us
    pallas_call x1, Pallas kernels, on_device(): call(functools.partial(finish, planes), [(shape, F32)] * 2, block, block,...  1.05 us
    pallas_call x1, Pallas kernels, on_device(): call(functools.partial(near_terms, planes), [(shape, F32), (shape, LOW),...  0.97 us
  transfers between devices with their start and end apart: 20, of which 8 were waited for; matrix products, arithmetic and copies ran while one was open for 0% of the time, Pallas kernels for 15%

profile of v8, /device:TPU:0, one launch (start us, length us, event | category | flops | bytes accessed | tf_op | source)
XLA Modules:
  0.0 44.1 jit_solution(2568867121800699459)
XLA Ops:
  0.6 2.2 %shard_map.67 = (bf16[144,512]{1,0:T(8,128)(2,1)}, bf16[144,512]{1,0:T(8,128)(2,1)}, bf16[144,512]{1,0:T(8,128)(2,1)}, bf16[144,512]{1,0:T(8,128)(2,1)}, bf16[128,512]{1,0:T(8,128)(2,1)}) custom-call(f32[128,512]{1,0:T(8,128)} %refs_4_.1, f32[128,512]{1,0:T(8,128)} %refs_5_.1, s32[16,128]{1,0:T(8,128)} %bitcast.3, s32[16,128]{1,0:T(8,128)} %bitcast.4), custom_call_target="tpu_custom_call" | custom-call | flops 655360 | bytes 1310720 | tf_op jit(solution)/shard_map/pallas_call | solution.py:342
  2.8 4.1 %collective-permute-start.1 = (bf16[128,512]{1,0:T(8,128)(2,1)}, bf16[128,512]{1,0:T(8,128)(2,1)S(1)}, u32[]{:S(2)}, u32[]{:S(2)}) collective-permute-start(bf16[128,512]{1,0:T(8,128)(2,1)} %get-tuple-element.34.refs_0_), channel_id=1, source_target_pairs={{0,16},{1,17},{2,18},{3,19},{4,20},{5,21},{6,22},{7,23},{8,24},{9,... | collective-permute-start | bytes 393224 | tf_op jit(solution)/shard_map/ppermute | solution.py:332
  6.9 1.5 %collective-permute-start = (bf16[128,512]{1,0:T(8,128)(2,1)}, bf16[128,512]{1,0:T(8,128)(2,1)S(1)}, u32[]{:S(2)}, u32[]{:S(2)}) collective-permute-start(bf16[128,512]{1,0:T(8,128)(2,1)} %get-tuple-element.34.refs_0_), channel_id=1, source_target_pairs={{0,2},{1,3},{2,0},{3,1},{4,6},{5,7},{6,4},{7,5},{8,10},{9,11},{10,... | collective-permute-start | bytes 393224 | tf_op jit(solution)/shard_map/ppermute | solution.py:332
  8.4 1.5 %collective-permute-start.4 = (bf16[144,512]{1,0:T(8,128)(2,1)}, bf16[144,512]{1,0:T(8,128)(2,1)S(1)}, u32[]{:S(2)}, u32[]{:S(2)}) collective-permute-start(bf16[144,512]{1,0:T(8,128)(2,1)} %get-tuple-element.36), channel_id=1, source_target_pairs={{0,4},{1,5},{2,6},{3,7},{4,0},{5,1},{6,2},{7,3},{8,12},{9,13},{10,... | collective-permute-start | bytes 442376 | tf_op jit(solution)/shard_map/ppermute | solution.py:332
  9.9 1.6 %collective-permute-start.5 = (bf16[144,512]{1,0:T(8,128)(2,1)}, bf16[144,512]{1,0:T(8,128)(2,1)S(1)}, u32[]{:S(2)}, u32[]{:S(2)}) collective-permute-start(bf16[144,512]{1,0:T(8,128)(2,1)} %get-tuple-element.37), channel_id=1, source_target_pairs={{0,8},{1,9},{2,10},{3,11},{4,12},{5,13},{6,14},{7,15},{8,0},{9,1},... | collective-permute-start | bytes 442376 | tf_op jit(solution)/shard_map/ppermute | solution.py:332
  11.5 0.4 collective-permute-start.6
  11.9 1.6 %collective-permute-done.1.refs_0_ = bf16[128,512]{1,0:T(8,128)(2,1)S(1)} collective-permute-done((bf16[128,512]{1,0:T(8,128)(2,1)}, bf16[128,512]{1,0:T(8,128)(2,1)S(1)}, u32[]{:S(2)}, u32[]{:S(2)}) %collective-permute-start.1) | collective-permute-done | bytes 131104 | tf_op jit(solution)/shard_map/ppermute | solution.py:332
  13.6 1.6 %collective-permute-start.8 = (bf16[128,512]{1,0:T(8,128)(2,1)S(1)}, bf16[128,512]{1,0:T(8,128)(2,1)S(1)}, u32[]{:S(2)}, u32[]{:S(2)}) collective-permute-start(bf16[128,512]{1,0:T(8,128)(2,1)S(1)} %shard_map.68.refs_2_.refs_0_), channel_id=1, source_target_pairs={{0,2},{1,3},{2,0},{3,1},{4,6},{5,7},{6,4},{7,5},{8,10},{9,11},{10,... | collective-permute-start | bytes 393224 | tf_op jit(solution)/shard_map/ppermute | solution.py:332
  15.4 0.5 %collective-permute-start.3 = (bf16[384,512]{1,0:T(8,128)(2,1)S(1)}, bf16[384,512]{1,0:T(8,128)(2,1)S(1)}, u32[]{:S(2)}, u32[]{:S(2)}) collective-permute-start(bf16[384,512]{1,0:T(8,128)(2,1)S(1)} %shard_map.70.own_ref), channel_id=1, source_target_pairs={{0,2},{1,3},{2,0},{3,1},{4,6},{5,7},{6,4},{7,5},{8,10},{9,11},{10,... | collective-permute-start | bytes 1179656 | tf_op jit(solution)/shard_map/ppermute | solution.py:332
  16.1 0.9 %collective-permute-done.5.refs_2_ = bf16[144,512]{1,0:T(8,128)(2,1)S(1)} collective-permute-done((bf16[144,512]{1,0:T(8,128)(2,1)}, bf16[144,512]{1,0:T(8,128)(2,1)S(1)}, u32[]{:S(2)}, u32[]{:S(2)}) %collective-permute-start.5) | collective-permute-done | bytes 147488 | tf_op jit(solution)/shard_map/ppermute | solution.py:332
  16.9 2.8 %collective-permute-done.6.refs_3_ = bf16[144,512]{1,0:T(8,128)(2,1)S(1)} collective-permute-done((bf16[144,512]{1,0:T(8,128)(2,1)}, bf16[144,512]{1,0:T(8,128)(2,1)S(1)}, u32[]{:S(2)}, u32[]{:S(2)}) %collective-permute-start.6) | collective-permute-done | bytes 147488 | tf_op jit(solution)/shard_map/ppermute | solution.py:332
  19.8 0.3 collective-permute-done.8.refs_0_
  20.1 0.3 collective-permute-start.9
  20.4 1.4 %collective-permute-done.7.other_ref.other_stack = bf16[544,512]{1,0:T(8,128)(2,1)S(1)} collective-permute-done((bf16[544,512]{1,0:T(8,128)(2,1)S(1)}, bf16[544,512]{1,0:T(8,128)(2,1)S(1)}, u32[]{:S(2)}, u32[]{:S(2)}) %collective-permute-start.7) | collective-permute-done | bytes 557088 | tf_op jit(solution)/shard_map/ppermute | solution.py:332
  21.7 1.1 %shard_map.72 = (f32[8,1024]{1,0:T(8,128)S(1)}, f32[8,1024]{1,0:T(8,128)S(1)}, f32[1,1024]{1,0:T(1,128)S(1)}) custom-call(bf16[544,512]{1,0:T(8,128)(2,1)S(1)} %shard_map.71.own_ref.own_stack, bf16[544,512]{1,0:T(8,128)(2,1)S(1)} %collective-permute-done.7.other_ref.other_stack, bf16[384,512]{1,0:T(8,128)(2,1)S(1)} %shard_map.69.near_own.refs_0_, ...), custom_call_target="tpu_custom_call" | custom-call | flops 100000000 | tf_op jit(solution)/shard_map/pallas_call | solution.py:376
  22.8 0.5 %shard_map.74 = (f32[8,1024]{1,0:T(8,128)S(1)}, f32[1,1024]{1,0:T(1,128)S(1)}) custom-call(f32[8,1024]{1,0:T(8,128)S(1)} %get-tuple-element.39.exp_in, f32[8,1024]{1,0:T(8,128)S(1)} %get-tuple-element.40.pick_ref, bf16[544,512]{1,0:T(8,128)(2,1)S(1)} %shard_map.71.own_ref.own_stack, bf16[544,512]{1,0:T(8,128)(2,1)S(1)} %collective-permute-done.7.other_ref.other_stack, ...), custom_call_target="tpu_custom_call" | custom-call | flops 300000000 | tf_op jit(solution)/shard_map/pallas_call | solution.py:379
  23.3 1.5 %collective-permute-start.12 = (f32[1,1024]{1,0:T(1,128)S(1)}, f32[1,1024]{1,0:T(1,128)S(1)}, u32[]{:S(2)}, u32[]{:S(2)}) collective-permute-start(f32[1,1024]{1,0:T(1,128)S(1)} %get-tuple-element.43._.refs_0_), channel_id=1, source_target_pairs={{0,4},{1,5},{2,6},{3,7},{4,0},{5,1},{6,2},{7,3},{8,12},{9,13},{10,... | collective-permute-start | bytes 12296 | tf_op jit(solution)/shard_map/ppermute | solution.py:332
  24.9 2.0 %collective-permute-start.10 = (f32[1,1024]{1,0:T(1,128)S(1)}, f32[1,1024]{1,0:T(1,128)S(1)}, u32[]{:S(2)}, u32[]{:S(2)}) collective-permute-start(f32[1,1024]{1,0:T(1,128)S(1)} %get-tuple-element.43._.refs_0_), channel_id=1, source_target_pairs={{0,8},{1,9},{2,10},{3,11},{4,12},{5,13},{6,14},{7,15},{8,0},{9,1},... | collective-permute-start | bytes 12296 | tf_op jit(solution)/shard_map/ppermute | solution.py:332
  26.9 1.3 %shard_map.75 = (f32[8,128]{1,0:T(8,128)S(1)}, f32[128,512]{1,0:T(8,128)S(1)}, bf16[128,512]{1,0:T(8,128)(2,1)S(1)}, bf16[128,512]{1,0:T(8,128)(2,1)S(1)}, bf16[128,512]{1,0:T(8,128)(2,1)S(1)}) custom-call(f32[8,1024]{1,0:T(8,128)S(1)} %get-tuple-element.41.exp_ref, f32[8,1024]{1,0:T(8,128)S(1)} %get-tuple-element.40.pick_ref, ...), custom_call_target="tpu_custom_call" | custom-call | flops 2000000000 | tf_op jit(solution)/shard_map/pallas_call | solution.py:384
  28.2 1.2 %collective-permute-done.11.refs_2_ = f32[1,1024]{1,0:T(1,128)S(1)} collective-permute-done((f32[1,1024]{1,0:T(1,128)S(1)}, f32[1,1024]{1,0:T(1,128)S(1)}, u32[]{:S(2)}, u32[]{:S(2)}) %collective-permute-start.11) | collective-permute-done | bytes 4128 | tf_op jit(solution)/shard_map/ppermute | solution.py:332
  29.4 0.5 %shard_map.76 = (f32[1,128]{1,0:T(1,128)S(1)}, f32[8,1024]{1,0:T(8,128)S(1)}, bf16[128,512]{1,0:T(8,128)(2,1)S(1)}) custom-call(f32[8,1024]{1,0:T(8,128)S(1)} %get-tuple-element.41.exp_ref, f32[8,1024]{1,0:T(8,128)S(1)} %get-tuple-element.40.pick_ref, f32[1,1024]{1,0:T(1,128)S(1)} %get-tuple-element.42.pos_ref, ...), custom_call_target="tpu_custom_call" | custom-call | tf_op jit(solution)/shard_map/pallas_call | solution.py:390
  30.0 0.6 %collective-permute-start.17 = (bf16[128,512]{1,0:T(8,128)(2,1)S(1)}, bf16[128,512]{1,0:T(8,128)(2,1)S(1)}, u32[]{:S(2)}, u32[]{:S(2)}) collective-permute-start(bf16[128,512]{1,0:T(8,128)(2,1)S(1)} %get-tuple-element.58), channel_id=1, source_target_pairs={{0,2},{1,3},{2,0},{3,1},{4,6},{5,7},{6,4},{7,5},{8,10},{9,11},{10,... | collective-permute-start | bytes 393224 | tf_op jit(solution)/shard_map/ppermute | solution.py:332
  30.6 0.9 %collective-permute-start.14 = (bf16[128,512]{1,0:T(8,128)(2,1)S(1)}, bf16[128,512]{1,0:T(8,128)(2,1)S(1)}, u32[]{:S(2)}, u32[]{:S(2)}) collective-permute-start(bf16[128,512]{1,0:T(8,128)(2,1)S(1)} %get-tuple-element.54), channel_id=1, source_target_pairs={{0,4},{1,5},{2,6},{3,7},{4,0},{5,1},{6,2},{7,3},{8,12},{9,13},{10,... | collective-permute-start | bytes 393224 | tf_op jit(solution)/shard_map/ppermute | solution.py:332
  31.5 1.7 %collective-permute-start.15 = (bf16[128,512]{1,0:T(8,128)(2,1)S(1)}, bf16[128,512]{1,0:T(8,128)(2,1)S(1)}, u32[]{:S(2)}, u32[]{:S(2)}) collective-permute-start(bf16[128,512]{1,0:T(8,128)(2,1)S(1)} %get-tuple-element.55), channel_id=1, source_target_pairs={{0,12},{1,13},{2,14},{3,15},{4,8},{5,9},{6,10},{7,11},{8,4},{9,5},... | collective-permute-start | bytes 393224 | tf_op jit(solution)/shard_map/ppermute | solution.py:332
  33.2 0.9 %collective-permute-start.16 = (bf16[128,512]{1,0:T(8,128)(2,1)S(1)}, bf16[128,512]{1,0:T(8,128)(2,1)S(1)}, u32[]{:S(2)}, u32[]{:S(2)}) collective-permute-start(bf16[128,512]{1,0:T(8,128)(2,1)S(1)} %get-tuple-element.56), channel_id=1, source_target_pairs={{0,8},{1,9},{2,10},{3,11},{4,12},{5,13},{6,14},{7,15},{8,0},{9,1},... | collective-permute-start | bytes 393224 | tf_op jit(solution)/shard_map/ppermute | solution.py:332
  34.1 1.0 %shard_map.78 = (f32[128,512]{1,0:T(8,128)S(1)}, bf16[128,512]{1,0:T(8,128)(2,1)S(1)}, f32[128,512]{1,0:T(8,128)S(1)}) custom-call(f32[8,1024]{1,0:T(8,128)S(1)} %get-tuple-element.46.weight_ref, f32[8,1024]{1,0:T(8,128)S(1)} %get-tuple-element.40.pick_ref, bf16[544,512]{1,0:T(8,128)(2,1)S(1)} %shard_map.71.own_ref.own_stack, ...), custom_call_target="tpu_custom_call" | custom-call | flops 805306368 | bytes 2097152 | tf_op jit(solution)/shard_map/pallas_call | solution.py:393
  35.1 0.8 %collective-permute-done.17.other_ref = bf16[128,512]{1,0:T(8,128)(2,1)S(1)} collective-permute-done((bf16[128,512]{1,0:T(8,128)(2,1)S(1)}, bf16[128,512]{1,0:T(8,128)(2,1)S(1)}, u32[]{:S(2)}, u32[]{:S(2)}) %collective-permute-start.17) | collective-permute-done | bytes 131104 | tf_op jit(solution)/shard_map/ppermute | solution.py:332
  35.9 2.2 %collective-permute-start.18 = (bf16[128,512]{1,0:T(8,128)(2,1)S(1)}, bf16[128,512]{1,0:T(8,128)(2,1)S(1)}, u32[]{:S(2)}, u32[]{:S(2)}) collective-permute-start(bf16[128,512]{1,0:T(8,128)(2,1)S(1)} %get-tuple-element.60), channel_id=1, source_target_pairs={{0,16},{1,17},{2,18},{3,19},{4,20},{5,21},{6,22},{7,23},{8,24},{9,... | collective-permute-start | bytes 393224 | tf_op jit(solution)/shard_map/ppermute | solution.py:332
  38.1 1.2 %collective-permute-start.19 = (bf16[128,512]{1,0:T(8,128)(2,1)S(1)}, bf16[128,512]{1,0:T(8,128)(2,1)S(1)}, u32[]{:S(2)}, u32[]{:S(2)}) collective-permute-start(bf16[128,512]{1,0:T(8,128)(2,1)S(1)} %get-tuple-element.61), channel_id=1, source_target_pairs={{0,2},{1,3},{2,0},{3,1},{4,6},{5,7},{6,4},{7,5},{8,10},{9,11},{10,... | collective-permute-start | bytes 393224 | tf_op jit(solution)/shard_map/ppermute | solution.py:332
  39.3 2.0 %shard_map.79 = (f32[128,512]{1,0:T(8,128)S(1)}, f32[128,512]{1,0:T(8,128)S(1)}, f32[128,512]{1,0:T(8,128)S(1)}, f32[128,512]{1,0:T(8,128)S(1)}, f32[128,128]{1,0:T(8,128)S(1)}, /*index=5*/f32[1,128]{1,0:T(1,128)}) custom-call(bf16[384,512]{1,0:T(8,128)(2,1)S(1)} %shard_map.69.near_own.refs_0_, ...), custom_call_target="tpu_custom_call" | custom-call | flops 65536 | bytes 65536 | tf_op jit(solution)/shard_map/pallas_call | solution.py:406
  41.3 1.8 %collective-permute-done.16.refs_3_ = bf16[128,512]{1,0:T(8,128)(2,1)S(1)} collective-permute-done((bf16[128,512]{1,0:T(8,128)(2,1)S(1)}, bf16[128,512]{1,0:T(8,128)(2,1)S(1)}, u32[]{:S(2)}, u32[]{:S(2)}) %collective-permute-start.16) | collective-permute-done | bytes 131104 | tf_op jit(solution)/shard_map/ppermute | solution.py:332
  43.1 1.0 %shard_map.81 = (f32[128,512]{1,0:T(8,128)}, f32[128,512]{1,0:T(8,128)}) custom-call(f32[128,512]{1,0:T(8,128)S(1)} %get-tuple-element.48.prog_base, f32[128,512]{1,0:T(8,128)S(1)} %get-tuple-element.49.trace_base, f32[128,512]{1,0:T(8,128)S(1)} %get-tuple-element.50.prog_unit, f32[128,512]{1,0:T(8,128)S(1)} %get-tuple-element.51.trace_unit, ...), custom_call_target="tpu_custom_call" | custom-call | flops 65536 | bytes 65536 | tf_op jit(solution)/shard_map/pallas_call | solution.py:413
  (31 shorter events, 0.6 us)
Async XLA Ops:
  2.8 10.7 %collective-permute-start.1 = (bf16[128,512]{1,0:T(8,128)(2,1)}, bf16[128,512]{1,0:T(8,128)(2,1)S(1)}, u32[]{:S(2)}, u32[]{:S(2)}) collective-permute-start(bf16[128,512]{1,0:T(8,128)(2,1)} %get-tuple-element.34.refs_0_), channel_id=1, source_target_pairs={{0,16},{1,17},{2,18},{3,19},{4,20},{5,21},{6,22},{7,23},{8,24},{9,... | collective-permute-start | bytes 393224 | tf_op jit(solution)/shard_map/ppermute | solution.py:332
  6.9 8.5 %collective-permute-start = (bf16[128,512]{1,0:T(8,128)(2,1)}, bf16[128,512]{1,0:T(8,128)(2,1)S(1)}, u32[]{:S(2)}, u32[]{:S(2)}) collective-permute-start(bf16[128,512]{1,0:T(8,128)(2,1)} %get-tuple-element.34.refs_0_), channel_id=1, source_target_pairs={{0,2},{1,3},{2,0},{3,1},{4,6},{5,7},{6,4},{7,5},{8,10},{9,11},{10,... | collective-permute-start | bytes 393224 | tf_op jit(solution)/shard_map/ppermute | solution.py:332
  8.4 7.6 %collective-permute-start.4 = (bf16[144,512]{1,0:T(8,128)(2,1)}, bf16[144,512]{1,0:T(8,128)(2,1)S(1)}, u32[]{:S(2)}, u32[]{:S(2)}) collective-permute-start(bf16[144,512]{1,0:T(8,128)(2,1)} %get-tuple-element.36), channel_id=1, source_target_pairs={{0,4},{1,5},{2,6},{3,7},{4,0},{5,1},{6,2},{7,3},{8,12},{9,13},{10,... | collective-permute-start | bytes 442376 | tf_op jit(solution)/shard_map/ppermute | solution.py:332
  9.9 7.0 %collective-permute-start.5 = (bf16[144,512]{1,0:T(8,128)(2,1)}, bf16[144,512]{1,0:T(8,128)(2,1)S(1)}, u32[]{:S(2)}, u32[]{:S(2)}) collective-permute-start(bf16[144,512]{1,0:T(8,128)(2,1)} %get-tuple-element.37), channel_id=1, source_target_pairs={{0,8},{1,9},{2,10},{3,11},{4,12},{5,13},{6,14},{7,15},{8,0},{9,1},... | collective-permute-start | bytes 442376 | tf_op jit(solution)/shard_map/ppermute | solution.py:332
  11.5 3.7 %copy-start = (f32[128,512]{1,0:T(8,128)S(1)}, f32[128,512]{1,0:T(8,128)}, u32[]{:S(2)}) copy-start(f32[128,512]{1,0:T(8,128)} %refs_4_.1) | copy-start | bytes 786436
  11.5 3.7 %copy-start.1 = (f32[128,512]{1,0:T(8,128)S(1)}, f32[128,512]{1,0:T(8,128)}, u32[]{:S(2)}) copy-start(f32[128,512]{1,0:T(8,128)} %refs_5_.1) | copy-start | bytes 786436
  11.5 8.2 %collective-permute-start.6 = (bf16[144,512]{1,0:T(8,128)(2,1)}, bf16[144,512]{1,0:T(8,128)(2,1)S(1)}, u32[]{:S(2)}, u32[]{:S(2)}) collective-permute-start(bf16[144,512]{1,0:T(8,128)(2,1)} %get-tuple-element.38), channel_id=1, source_target_pairs={{0,12},{1,13},{2,14},{3,15},{4,8},{5,9},{6,10},{7,11},{8,4},{9,5},... | collective-permute-start | bytes 442376 | tf_op jit(solution)/shard_map/ppermute | solution.py:332
  13.5 2.4 %copy-start.3 = (bf16[128,512]{1,0:T(8,128)(2,1)S(1)}, bf16[128,512]{1,0:T(8,128)(2,1)}, u32[]{:S(2)}) copy-start(bf16[128,512]{1,0:T(8,128)(2,1)} %get-tuple-element.34.refs_0_) | copy-start | bytes 393220
  13.6 6.5 %collective-permute-start.8 = (bf16[128,512]{1,0:T(8,128)(2,1)S(1)}, bf16[128,512]{1,0:T(8,128)(2,1)S(1)}, u32[]{:S(2)}, u32[]{:S(2)}) collective-permute-start(bf16[128,512]{1,0:T(8,128)(2,1)S(1)} %shard_map.68.refs_2_.refs_0_), channel_id=1, source_target_pairs={{0,2},{1,3},{2,0},{3,1},{4,6},{5,7},{6,4},{7,5},{8,10},{9,11},{10,... | collective-permute-start | bytes 393224 | tf_op jit(solution)/shard_map/ppermute | solution.py:332
  15.4 4.3 %copy-start.2 = (bf16[144,512]{1,0:T(8,128)(2,1)S(1)}, bf16[144,512]{1,0:T(8,128)(2,1)}, u32[]{:S(2)}) copy-start(bf16[144,512]{1,0:T(8,128)(2,1)} %get-tuple-element.35.refs_0_) | copy-start | bytes 442372
  15.4 14.4 %collective-permute-start.3 = (bf16[384,512]{1,0:T(8,128)(2,1)S(1)}, bf16[384,512]{1,0:T(8,128)(2,1)S(1)}, u32[]{:S(2)}, u32[]{:S(2)}) collective-permute-start(bf16[384,512]{1,0:T(8,128)(2,1)S(1)} %shard_map.70.own_ref), channel_id=1, source_target_pairs={{0,2},{1,3},{2,0},{3,1},{4,6},{5,7},{6,4},{7,5},{8,10},{9,11},{10,... | collective-permute-start | bytes 1179656 | tf_op jit(solution)/shard_map/ppermute | solution.py:332
  16.0 4.4 %collective-permute-start.2 = (bf16[384,512]{1,0:T(8,128)(2,1)S(1)}, bf16[384,512]{1,0:T(8,128)(2,1)S(1)}, u32[]{:S(2)}, u32[]{:S(2)}) collective-permute-start(bf16[384,512]{1,0:T(8,128)(2,1)S(1)} %shard_map.69.near_own.refs_0_), channel_id=1, source_target_pairs={{0,1},{1,0},{2,3},{3,2},{4,5},{5,4},{6,7},{7,6},{8,9},{9,8},{10,11... | collective-permute-start | bytes 1179656 | tf_op jit(solution)/shard_map/ppermute | solution.py:332
  19.7 2.0 %collective-permute-start.7 = (bf16[544,512]{1,0:T(8,128)(2,1)S(1)}, bf16[544,512]{1,0:T(8,128)(2,1)S(1)}, u32[]{:S(2)}, u32[]{:S(2)}) collective-permute-start(bf16[544,512]{1,0:T(8,128)(2,1)S(1)} %shard_map.71.own_ref.own_stack), channel_id=1, source_target_pairs={{0,1},{1,0},{2,3},{3,2},{4,5},{5,4},{6,7},{7,6},{8,9},{9,8},{10,11... | collective-permute-start | bytes 1671176 | tf_op jit(solution)/shard_map/ppermute | solution.py:332
  20.1 2.8 %collective-permute-start.9 = (bf16[128,512]{1,0:T(8,128)(2,1)S(1)}, bf16[128,512]{1,0:T(8,128)(2,1)S(1)}, u32[]{:S(2)}, u32[]{:S(2)}) collective-permute-start(bf16[128,512]{1,0:T(8,128)(2,1)S(1)} %shard_map.73.far_own), channel_id=1, source_target_pairs={{0,1},{1,0},{2,3},{3,2},{4,5},{5,4},{6,7},{7,6},{8,9},{9,8},{10,11... | collective-permute-start | bytes 393224 | tf_op jit(solution)/shard_map/ppermute | solution.py:332
  23.3 4.8 %collective-permute-start.12 = (f32[1,1024]{1,0:T(1,128)S(1)}, f32[1,1024]{1,0:T(1,128)S(1)}, u32[]{:S(2)}, u32[]{:S(2)}) collective-permute-start(f32[1,1024]{1,0:T(1,128)S(1)} %get-tuple-element.43._.refs_0_), channel_id=1, source_target_pairs={{0,4},{1,5},{2,6},{3,7},{4,0},{5,1},{6,2},{7,3},{8,12},{9,13},{10,... | collective-permute-start | bytes 12296 | tf_op jit(solution)/shard_map/ppermute | solution.py:332
  24.9 4.5 %collective-permute-start.11 = (f32[1,1024]{1,0:T(1,128)S(1)}, f32[1,1024]{1,0:T(1,128)S(1)}, u32[]{:S(2)}, u32[]{:S(2)}) collective-permute-start(f32[1,1024]{1,0:T(1,128)S(1)} %get-tuple-element.43._.refs_0_), channel_id=1, source_target_pairs={{0,12},{1,13},{2,14},{3,15},{4,8},{5,9},{6,10},{7,11},{8,4},{9,5},... | collective-permute-start | bytes 12296 | tf_op jit(solution)/shard_map/ppermute | solution.py:332
  24.9 4.5 %collective-permute-start.10 = (f32[1,1024]{1,0:T(1,128)S(1)}, f32[1,1024]{1,0:T(1,128)S(1)}, u32[]{:S(2)}, u32[]{:S(2)}) collective-permute-start(f32[1,1024]{1,0:T(1,128)S(1)} %get-tuple-element.43._.refs_0_), channel_id=1, source_target_pairs={{0,8},{1,9},{2,10},{3,11},{4,12},{5,13},{6,14},{7,15},{8,0},{9,1},... | collective-permute-start | bytes 12296 | tf_op jit(solution)/shard_map/ppermute | solution.py:332
  29.9 8.2 %collective-permute-start.13 = (bf16[768,512]{1,0:T(8,128)(2,1)S(1)}, bf16[768,512]{1,0:T(8,128)(2,1)S(1)}, u32[]{:S(2)}, u32[]{:S(2)}) collective-permute-start(bf16[768,512]{1,0:T(8,128)(2,1)S(1)} %shard_map.77.refs_2_), channel_id=1, source_target_pairs={{0,1},{1,0},{2,3},{3,2},{4,5},{5,4},{6,7},{7,6},{8,9},{9,8},{10,11... | collective-permute-start | bytes 2359304 | tf_op jit(solution)/shard_map/ppermute | solution.py:332
  30.0 5.9 %collective-permute-start.17 = (bf16[128,512]{1,0:T(8,128)(2,1)S(1)}, bf16[128,512]{1,0:T(8,128)(2,1)S(1)}, u32[]{:S(2)}, u32[]{:S(2)}) collective-permute-start(bf16[128,512]{1,0:T(8,128)(2,1)S(1)} %get-tuple-element.58), channel_id=1, source_target_pairs={{0,2},{1,3},{2,0},{3,1},{4,6},{5,7},{6,4},{7,5},{8,10},{9,11},{10,... | collective-permute-start | bytes 393224 | tf_op jit(solution)/shard_map/ppermute | solution.py:332
  30.6 10.7 %collective-permute-start.14 = (bf16[128,512]{1,0:T(8,128)(2,1)S(1)}, bf16[128,512]{1,0:T(8,128)(2,1)S(1)}, u32[]{:S(2)}, u32[]{:S(2)}) collective-permute-start(bf16[128,512]{1,0:T(8,128)(2,1)S(1)} %get-tuple-element.54), channel_id=1, source_target_pairs={{0,4},{1,5},{2,6},{3,7},{4,0},{5,1},{6,2},{7,3},{8,12},{9,13},{10,... | collective-permute-start | bytes 393224 | tf_op jit(solution)/shard_map/ppermute | solution.py:332
  31.5 9.8 %collective-permute-start.15 = (bf16[128,512]{1,0:T(8,128)(2,1)S(1)}, bf16[128,512]{1,0:T(8,128)(2,1)S(1)}, u32[]{:S(2)}, u32[]{:S(2)}) collective-permute-start(bf16[128,512]{1,0:T(8,128)(2,1)S(1)} %get-tuple-element.55), channel_id=1, source_target_pairs={{0,12},{1,13},{2,14},{3,15},{4,8},{5,9},{6,10},{7,11},{8,4},{9,5},... | collective-permute-start | bytes 393224 | tf_op jit(solution)/shard_map/ppermute | solution.py:332
  33.2 9.9 %collective-permute-start.16 = (bf16[128,512]{1,0:T(8,128)(2,1)S(1)}, bf16[128,512]{1,0:T(8,128)(2,1)S(1)}, u32[]{:S(2)}, u32[]{:S(2)}) collective-permute-start(bf16[128,512]{1,0:T(8,128)(2,1)S(1)} %get-tuple-element.56), channel_id=1, source_target_pairs={{0,8},{1,9},{2,10},{3,11},{4,12},{5,13},{6,14},{7,15},{8,0},{9,1},... | collective-permute-start | bytes 393224 | tf_op jit(solution)/shard_map/ppermute | solution.py:332
  35.9 7.1 %collective-permute-start.18 = (bf16[128,512]{1,0:T(8,128)(2,1)S(1)}, bf16[128,512]{1,0:T(8,128)(2,1)S(1)}, u32[]{:S(2)}, u32[]{:S(2)}) collective-permute-start(bf16[128,512]{1,0:T(8,128)(2,1)S(1)} %get-tuple-element.60), channel_id=1, source_target_pairs={{0,16},{1,17},{2,18},{3,19},{4,20},{5,21},{6,22},{7,23},{8,24},{9,... | collective-permute-start | bytes 393224 | tf_op jit(solution)/shard_map/ppermute | solution.py:332
  38.1 5.0 %collective-permute-start.19 = (bf16[128,512]{1,0:T(8,128)(2,1)S(1)}, bf16[128,512]{1,0:T(8,128)(2,1)S(1)}, u32[]{:S(2)}, u32[]{:S(2)}) collective-permute-start(bf16[128,512]{1,0:T(8,128)(2,1)S(1)} %get-tuple-element.61), channel_id=1, source_target_pairs={{0,2},{1,3},{2,0},{3,1},{4,6},{5,7},{6,4},{7,5},{8,10},{9,11},{10,... | collective-permute-start | bytes 393224 | tf_op jit(solution)/shard_map/ppermute | solution.py:332

commit v9 on v7

--- a/solution.py
+++ b/solution.py
@@ -214,15 +214,20 @@
 def far_terms(planes, exp_ref, pick_ref, pos_ref, own_stack, other_stack, _, *refs):
     sums, (total_ref, weight_ref, far_ref) = refs[:planes], refs[planes:]
     plane, core = own_plane(planes), own_core()
+    parts, pairs = [], []
+    for b in range(2 * planes):
+        lane = block_lane(planes, b, plane, core)
+        part = sums[0][:, pl.ds(lane, ROWS)]
+        for one in sums[1:]:
+            part = part + one[:, pl.ds(lane, ROWS)]
+        parts.append(part)
+        pairs.append(pos_ref[:, b * ROWS : (b + 1) * ROWS])
+    total = jnp.exp(jnp.concatenate(pairs, axis=0)) + jnp.concatenate(parts, axis=0)
+    total_ref[...] = total[0:1, :]
+    scale = SCALE / total
     for b in range(2 * planes):
         lanes = slice(b * ROWS, (b + 1) * ROWS)
-        lane = block_lane(planes, b, plane, core)
-        total = jnp.exp(pos_ref[:, lanes])
-        for one in sums:
-            total = total + one[:, pl.ds(lane, ROWS)]
-        if b == 0:
-            total_ref[...] = total
-        weight_ref[:, lanes] = exp_ref[:, lanes] * (SCALE / total)
+        weight_ref[:, lanes] = exp_ref[:, lanes] * scale[b : b + 1, :]
     far_ref[...] = weighted(planes, weight_ref, pick_ref, own_stack, other_stack, (3,)).astype(LOW)
 
 

time: 44.2 us -> 44.3 us (level)
  no operation moved by 1% of the time
where the time goes in v9:
time: 44.3 us; the launch traced here: 44.1 us
  starting transfers between devices  22.8 us (51%)
  waiting for transfers between devices  10.7 us (24%)
  Pallas kernels  9.88 us (22%)
  between operations  0.81 us (2%)
    ppermute x20, starting transfers between devices, flipped(): return lax.ppermute(value, both, [(i, i ^ bits) for i in range(size)])  22.8 us
    ppermute x20, waiting for transfers between devices, flipped(): return lax.ppermute(value, both, [(i, i ^ bits) for i in range(size)])  10.7 us
    pallas_call x1, Pallas kernels, on_device(): call(functools.partial(prepare, planes), [((rows + MORE, feat), LOW)] * p...  2.17 us
    pallas_call x1, Pallas kernels, on_device(): call(group_terms, [(shape, F32)] * 4 + [((rows, rows), F32), ((1, rows),...  2 us
    pallas_call x1, Pallas kernels, on_device(): call(functools.partial(program_terms, planes), [((8, rows), F32), (shape,...  1.27 us
    pallas_call x1, Pallas kernels, on_device(): call(functools.partial(score_near, planes), lists, NEAR, 0)  1.08 us
    pallas_call x1, Pallas kernels, on_device(): call(functools.partial(finish, planes), [(shape, F32)] * 2, block, block)  1.03 us
    pallas_call x1, Pallas kernels, on_device(): call(functools.partial(near_terms, planes), [(shape, F32), (shape, LOW),...  0.97 us
  transfers between devices with their start and end apart: 20, of which 10 were waited for; matrix products, arithmetic and copies ran while one was open for 0% of the time, Pallas kernels for 15%

profile of v9, /device:TPU:0, one launch (start us, length us, event | category | flops | bytes accessed | tf_op | source)
XLA Modules:
  0.0 44.1 jit_solution(4500335403838421369)
XLA Ops:
  0.6 2.2 %shard_map.67 = (bf16[144,512]{1,0:T(8,128)(2,1)}, bf16[144,512]{1,0:T(8,128)(2,1)}, bf16[144,512]{1,0:T(8,128)(2,1)}, bf16[144,512]{1,0:T(8,128)(2,1)}, bf16[128,512]{1,0:T(8,128)(2,1)}) custom-call(f32[128,512]{1,0:T(8,128)} %refs_4_.1, f32[128,512]{1,0:T(8,128)} %refs_5_.1, s32[16,128]{1,0:T(8,128)} %bitcast.3, s32[16,128]{1,0:T(8,128)} %bitcast.4), custom_call_target="tpu_custom_call" | custom-call | flops 655360 | bytes 1310720 | tf_op jit(solution)/shard_map/pallas_call | solution.py:344
  2.8 4.1 %collective-permute-start.1 = (bf16[128,512]{1,0:T(8,128)(2,1)}, bf16[128,512]{1,0:T(8,128)(2,1)S(1)}, u32[]{:S(2)}, u32[]{:S(2)}) collective-permute-start(bf16[128,512]{1,0:T(8,128)(2,1)} %get-tuple-element.34.refs_0_), channel_id=1, source_target_pairs={{0,16},{1,17},{2,18},{3,19},{4,20},{5,21},{6,22},{7,23},{8,24},{9,... | collective-permute-start | bytes 393224 | tf_op jit(solution)/shard_map/ppermute | solution.py:334
  6.9 1.5 %collective-permute-start = (bf16[128,512]{1,0:T(8,128)(2,1)}, bf16[128,512]{1,0:T(8,128)(2,1)S(1)}, u32[]{:S(2)}, u32[]{:S(2)}) collective-permute-start(bf16[128,512]{1,0:T(8,128)(2,1)} %get-tuple-element.34.refs_0_), channel_id=1, source_target_pairs={{0,2},{1,3},{2,0},{3,1},{4,6},{5,7},{6,4},{7,5},{8,10},{9,11},{10,... | collective-permute-start | bytes 393224 | tf_op jit(solution)/shard_map/ppermute | solution.py:334
  8.4 1.5 %collective-permute-start.4 = (bf16[144,512]{1,0:T(8,128)(2,1)}, bf16[144,512]{1,0:T(8,128)(2,1)S(1)}, u32[]{:S(2)}, u32[]{:S(2)}) collective-permute-start(bf16[144,512]{1,0:T(8,128)(2,1)} %get-tuple-element.36), channel_id=1, source_target_pairs={{0,4},{1,5},{2,6},{3,7},{4,0},{5,1},{6,2},{7,3},{8,12},{9,13},{10,... | collective-permute-start | bytes 442376 | tf_op jit(solution)/shard_map/ppermute | solution.py:334
  9.9 1.6 %collective-permute-start.5 = (bf16[144,512]{1,0:T(8,128)(2,1)}, bf16[144,512]{1,0:T(8,128)(2,1)S(1)}, u32[]{:S(2)}, u32[]{:S(2)}) collective-permute-start(bf16[144,512]{1,0:T(8,128)(2,1)} %get-tuple-element.37), channel_id=1, source_target_pairs={{0,8},{1,9},{2,10},{3,11},{4,12},{5,13},{6,14},{7,15},{8,0},{9,1},... | collective-permute-start | bytes 442376 | tf_op jit(solution)/shard_map/ppermute | solution.py:334
  11.5 0.4 collective-permute-start.6
  11.9 1.6 %collective-permute-done.1.refs_0_ = bf16[128,512]{1,0:T(8,128)(2,1)S(1)} collective-permute-done((bf16[128,512]{1,0:T(8,128)(2,1)}, bf16[128,512]{1,0:T(8,128)(2,1)S(1)}, u32[]{:S(2)}, u32[]{:S(2)}) %collective-permute-start.1) | collective-permute-done | bytes 131104 | tf_op jit(solution)/shard_map/ppermute | solution.py:334
  13.6 1.6 %collective-permute-start.8 = (bf16[128,512]{1,0:T(8,128)(2,1)S(1)}, bf16[128,512]{1,0:T(8,128)(2,1)S(1)}, u32[]{:S(2)}, u32[]{:S(2)}) collective-permute-start(bf16[128,512]{1,0:T(8,128)(2,1)S(1)} %shard_map.68.refs_2_.refs_0_), channel_id=1, source_target_pairs={{0,2},{1,3},{2,0},{3,1},{4,6},{5,7},{6,4},{7,5},{8,10},{9,11},{10,... | collective-permute-start | bytes 393224 | tf_op jit(solution)/shard_map/ppermute | solution.py:334
  15.4 0.5 %collective-permute-start.3 = (bf16[384,512]{1,0:T(8,128)(2,1)S(1)}, bf16[384,512]{1,0:T(8,128)(2,1)S(1)}, u32[]{:S(2)}, u32[]{:S(2)}) collective-permute-start(bf16[384,512]{1,0:T(8,128)(2,1)S(1)} %shard_map.70.own_ref), channel_id=1, source_target_pairs={{0,2},{1,3},{2,0},{3,1},{4,6},{5,7},{6,4},{7,5},{8,10},{9,11},{10,... | collective-permute-start | bytes 1179656 | tf_op jit(solution)/shard_map/ppermute | solution.py:334
  16.1 0.9 %collective-permute-done.5.refs_2_ = bf16[144,512]{1,0:T(8,128)(2,1)S(1)} collective-permute-done((bf16[144,512]{1,0:T(8,128)(2,1)}, bf16[144,512]{1,0:T(8,128)(2,1)S(1)}, u32[]{:S(2)}, u32[]{:S(2)}) %collective-permute-start.5) | collective-permute-done | bytes 147488 | tf_op jit(solution)/shard_map/ppermute | solution.py:334
  16.9 2.8 %collective-permute-done.6.refs_3_ = bf16[144,512]{1,0:T(8,128)(2,1)S(1)} collective-permute-done((bf16[144,512]{1,0:T(8,128)(2,1)}, bf16[144,512]{1,0:T(8,128)(2,1)S(1)}, u32[]{:S(2)}, u32[]{:S(2)}) %collective-permute-start.6) | collective-permute-done | bytes 147488 | tf_op jit(solution)/shard_map/ppermute | solution.py:334
  20.1 0.3 collective-permute-start.9
  20.4 1.4 %collective-permute-done.7.other_ref.other_stack = bf16[544,512]{1,0:T(8,128)(2,1)S(1)} collective-permute-done((bf16[544,512]{1,0:T(8,128)(2,1)S(1)}, bf16[544,512]{1,0:T(8,128)(2,1)S(1)}, u32[]{:S(2)}, u32[]{:S(2)}) %collective-permute-start.7) | collective-permute-done | bytes 557088 | tf_op jit(solution)/shard_map/ppermute | solution.py:334
  21.7 1.1 %shard_map.72 = (f32[8,1024]{1,0:T(8,128)S(1)}, f32[8,1024]{1,0:T(8,128)S(1)}, f32[1,1024]{1,0:T(1,128)S(1)}) custom-call(bf16[544,512]{1,0:T(8,128)(2,1)S(1)} %shard_map.71.own_ref.own_stack, bf16[544,512]{1,0:T(8,128)(2,1)S(1)} %collective-permute-done.7.other_ref.other_stack, bf16[384,512]{1,0:T(8,128)(2,1)S(1)} %shard_map.69.near_own.refs_0_, ...), custom_call_target="tpu_custom_call" | custom-call | flops 100000000 | tf_op jit(solution)/shard_map/pallas_call | solution.py:378
  22.8 0.5 %shard_map.74 = (f32[8,1024]{1,0:T(8,128)S(1)}, f32[1,1024]{1,0:T(1,128)S(1)}) custom-call(f32[8,1024]{1,0:T(8,128)S(1)} %get-tuple-element.39.exp_in, f32[8,1024]{1,0:T(8,128)S(1)} %get-tuple-element.40.pick_ref, bf16[544,512]{1,0:T(8,128)(2,1)S(1)} %shard_map.71.own_ref.own_stack, bf16[544,512]{1,0:T(8,128)(2,1)S(1)} %collective-permute-done.7.other_ref.other_stack, ...), custom_call_target="tpu_custom_call" | custom-call | flops 300000000 | tf_op jit(solution)/shard_map/pallas_call | solution.py:381
  23.3 1.5 %collective-permute-start.12 = (f32[1,1024]{1,0:T(1,128)S(1)}, f32[1,1024]{1,0:T(1,128)S(1)}, u32[]{:S(2)}, u32[]{:S(2)}) collective-permute-start(f32[1,1024]{1,0:T(1,128)S(1)} %get-tuple-element.43._.refs_0_), channel_id=1, source_target_pairs={{0,4},{1,5},{2,6},{3,7},{4,0},{5,1},{6,2},{7,3},{8,12},{9,13},{10,... | collective-permute-start | bytes 12296 | tf_op jit(solution)/shard_map/ppermute | solution.py:334
  24.9 2.0 %collective-permute-start.10 = (f32[1,1024]{1,0:T(1,128)S(1)}, f32[1,1024]{1,0:T(1,128)S(1)}, u32[]{:S(2)}, u32[]{:S(2)}) collective-permute-start(f32[1,1024]{1,0:T(1,128)S(1)} %get-tuple-element.43._.refs_0_), channel_id=1, source_target_pairs={{0,8},{1,9},{2,10},{3,11},{4,12},{5,13},{6,14},{7,15},{8,0},{9,1},... | collective-permute-start | bytes 12296 | tf_op jit(solution)/shard_map/ppermute | solution.py:334
  26.9 1.3 %shard_map.75 = (f32[8,128]{1,0:T(8,128)S(1)}, f32[128,512]{1,0:T(8,128)S(1)}, bf16[128,512]{1,0:T(8,128)(2,1)S(1)}, bf16[128,512]{1,0:T(8,128)(2,1)S(1)}, bf16[128,512]{1,0:T(8,128)(2,1)S(1)}) custom-call(f32[8,1024]{1,0:T(8,128)S(1)} %get-tuple-element.41.exp_ref, f32[8,1024]{1,0:T(8,128)S(1)} %get-tuple-element.40.pick_ref, ...), custom_call_target="tpu_custom_call" | custom-call | flops 2000000000 | tf_op jit(solution)/shard_map/pallas_call | solution.py:386
  28.2 1.2 %collective-permute-done.11.refs_2_ = f32[1,1024]{1,0:T(1,128)S(1)} collective-permute-done((f32[1,1024]{1,0:T(1,128)S(1)}, f32[1,1024]{1,0:T(1,128)S(1)}, u32[]{:S(2)}, u32[]{:S(2)}) %collective-permute-start.11) | collective-permute-done | bytes 4128 | tf_op jit(solution)/shard_map/ppermute | solution.py:334
  29.4 0.5 %shard_map.76 = (f32[1,128]{1,0:T(1,128)S(1)}, f32[8,1024]{1,0:T(8,128)S(1)}, bf16[128,512]{1,0:T(8,128)(2,1)S(1)}) custom-call(f32[8,1024]{1,0:T(8,128)S(1)} %get-tuple-element.41.exp_ref, f32[8,1024]{1,0:T(8,128)S(1)} %get-tuple-element.40.pick_ref, f32[1,1024]{1,0:T(1,128)S(1)} %get-tuple-element.42.pos_ref, ...), custom_call_target="tpu_custom_call" | custom-call | tf_op jit(solution)/shard_map/pallas_call | solution.py:392
  30.0 0.6 %collective-permute-start.17 = (bf16[128,512]{1,0:T(8,128)(2,1)S(1)}, bf16[128,512]{1,0:T(8,128)(2,1)S(1)}, u32[]{:S(2)}, u32[]{:S(2)}) collective-permute-start(bf16[128,512]{1,0:T(8,128)(2,1)S(1)} %get-tuple-element.58), channel_id=1, source_target_pairs={{0,2},{1,3},{2,0},{3,1},{4,6},{5,7},{6,4},{7,5},{8,10},{9,11},{10,... | collective-permute-start | bytes 393224 | tf_op jit(solution)/shard_map/ppermute | solution.py:334
  30.6 0.9 %collective-permute-start.14 = (bf16[128,512]{1,0:T(8,128)(2,1)S(1)}, bf16[128,512]{1,0:T(8,128)(2,1)S(1)}, u32[]{:S(2)}, u32[]{:S(2)}) collective-permute-start(bf16[128,512]{1,0:T(8,128)(2,1)S(1)} %get-tuple-element.54), channel_id=1, source_target_pairs={{0,4},{1,5},{2,6},{3,7},{4,0},{5,1},{6,2},{7,3},{8,12},{9,13},{10,... | collective-permute-start | bytes 393224 | tf_op jit(solution)/shard_map/ppermute | solution.py:334
  31.5 1.7 %collective-permute-start.15 = (bf16[128,512]{1,0:T(8,128)(2,1)S(1)}, bf16[128,512]{1,0:T(8,128)(2,1)S(1)}, u32[]{:S(2)}, u32[]{:S(2)}) collective-permute-start(bf16[128,512]{1,0:T(8,128)(2,1)S(1)} %get-tuple-element.55), channel_id=1, source_target_pairs={{0,8},{1,9},{2,10},{3,11},{4,12},{5,13},{6,14},{7,15},{8,0},{9,1},... | collective-permute-start | bytes 393224 | tf_op jit(solution)/shard_map/ppermute | solution.py:334
  33.3 0.9 %collective-permute-start.16 = (bf16[128,512]{1,0:T(8,128)(2,1)S(1)}, bf16[128,512]{1,0:T(8,128)(2,1)S(1)}, u32[]{:S(2)}, u32[]{:S(2)}) collective-permute-start(bf16[128,512]{1,0:T(8,128)(2,1)S(1)} %get-tuple-element.56), channel_id=1, source_target_pairs={{0,12},{1,13},{2,14},{3,15},{4,8},{5,9},{6,10},{7,11},{8,4},{9,5},... | collective-permute-start | bytes 393224 | tf_op jit(solution)/shard_map/ppermute | solution.py:334
  34.1 1.0 %shard_map.78 = (f32[128,512]{1,0:T(8,128)S(1)}, bf16[128,512]{1,0:T(8,128)(2,1)S(1)}, f32[128,512]{1,0:T(8,128)S(1)}) custom-call(f32[8,1024]{1,0:T(8,128)S(1)} %get-tuple-element.46.weight_ref, f32[8,1024]{1,0:T(8,128)S(1)} %get-tuple-element.40.pick_ref, bf16[544,512]{1,0:T(8,128)(2,1)S(1)} %shard_map.71.own_ref.own_stack, ...), custom_call_target="tpu_custom_call" | custom-call | flops 805306368 | bytes 2097152 | tf_op jit(solution)/shard_map/pallas_call | solution.py:395
  35.1 0.8 %collective-permute-done.17.other_ref = bf16[128,512]{1,0:T(8,128)(2,1)S(1)} collective-permute-done((bf16[128,512]{1,0:T(8,128)(2,1)S(1)}, bf16[128,512]{1,0:T(8,128)(2,1)S(1)}, u32[]{:S(2)}, u32[]{:S(2)}) %collective-permute-start.17) | collective-permute-done | bytes 131104 | tf_op jit(solution)/shard_map/ppermute | solution.py:334
  36.0 2.2 %collective-permute-start.18 = (bf16[128,512]{1,0:T(8,128)(2,1)S(1)}, bf16[128,512]{1,0:T(8,128)(2,1)S(1)}, u32[]{:S(2)}, u32[]{:S(2)}) collective-permute-start(bf16[128,512]{1,0:T(8,128)(2,1)S(1)} %get-tuple-element.60), channel_id=1, source_target_pairs={{0,16},{1,17},{2,18},{3,19},{4,20},{5,21},{6,22},{7,23},{8,24},{9,... | collective-permute-start | bytes 393224 | tf_op jit(solution)/shard_map/ppermute | solution.py:334
  38.1 1.2 %collective-permute-start.19 = (bf16[128,512]{1,0:T(8,128)(2,1)S(1)}, bf16[128,512]{1,0:T(8,128)(2,1)S(1)}, u32[]{:S(2)}, u32[]{:S(2)}) collective-permute-start(bf16[128,512]{1,0:T(8,128)(2,1)S(1)} %get-tuple-element.61), channel_id=1, source_target_pairs={{0,2},{1,3},{2,0},{3,1},{4,6},{5,7},{6,4},{7,5},{8,10},{9,11},{10,... | collective-permute-start | bytes 393224 | tf_op jit(solution)/shard_map/ppermute | solution.py:334
  39.3 2.0 %shard_map.79 = (f32[128,512]{1,0:T(8,128)S(1)}, f32[128,512]{1,0:T(8,128)S(1)}, f32[128,512]{1,0:T(8,128)S(1)}, f32[128,512]{1,0:T(8,128)S(1)}, f32[128,128]{1,0:T(8,128)S(1)}, /*index=5*/f32[1,128]{1,0:T(1,128)}) custom-call(bf16[384,512]{1,0:T(8,128)(2,1)S(1)} %shard_map.69.near_own.refs_0_, ...), custom_call_target="tpu_custom_call" | custom-call | flops 65536 | bytes 65536 | tf_op jit(solution)/shard_map/pallas_call | solution.py:408
  41.3 1.2 %collective-permute-done.16.refs_3_ = bf16[128,512]{1,0:T(8,128)(2,1)S(1)} collective-permute-done((bf16[128,512]{1,0:T(8,128)(2,1)S(1)}, bf16[128,512]{1,0:T(8,128)(2,1)S(1)}, u32[]{:S(2)}, u32[]{:S(2)}) %collective-permute-start.16) | collective-permute-done | bytes 131104 | tf_op jit(solution)/shard_map/ppermute | solution.py:334
  42.8 0.3 collective-permute-done.19.refs_5_
  43.1 1.0 %shard_map.81 = (f32[128,512]{1,0:T(8,128)}, f32[128,512]{1,0:T(8,128)}) custom-call(f32[128,512]{1,0:T(8,128)S(1)} %get-tuple-element.48.prog_base, f32[128,512]{1,0:T(8,128)S(1)} %get-tuple-element.49.trace_base, f32[128,512]{1,0:T(8,128)S(1)} %get-tuple-element.50.prog_unit, f32[128,512]{1,0:T(8,128)S(1)} %get-tuple-element.51.trace_unit, ...), custom_call_target="tpu_custom_call" | custom-call | flops 65536 | bytes 65536 | tf_op jit(solution)/shard_map/pallas_call | solution.py:415
  (31 shorter events, 1.2 us)
Async XLA Ops:
  2.8 10.7 %collective-permute-start.1 = (bf16[128,512]{1,0:T(8,128)(2,1)}, bf16[128,512]{1,0:T(8,128)(2,1)S(1)}, u32[]{:S(2)}, u32[]{:S(2)}) collective-permute-start(bf16[128,512]{1,0:T(8,128)(2,1)} %get-tuple-element.34.refs_0_), channel_id=1, source_target_pairs={{0,16},{1,17},{2,18},{3,19},{4,20},{5,21},{6,22},{7,23},{8,24},{9,... | collective-permute-start | bytes 393224 | tf_op jit(solution)/shard_map/ppermute | solution.py:334
  6.9 8.5 %collective-permute-start = (bf16[128,512]{1,0:T(8,128)(2,1)}, bf16[128,512]{1,0:T(8,128)(2,1)S(1)}, u32[]{:S(2)}, u32[]{:S(2)}) collective-permute-start(bf16[128,512]{1,0:T(8,128)(2,1)} %get-tuple-element.34.refs_0_), channel_id=1, source_target_pairs={{0,2},{1,3},{2,0},{3,1},{4,6},{5,7},{6,4},{7,5},{8,10},{9,11},{10,... | collective-permute-start | bytes 393224 | tf_op jit(solution)/shard_map/ppermute | solution.py:334
  8.4 7.6 %collective-permute-start.4 = (bf16[144,512]{1,0:T(8,128)(2,1)}, bf16[144,512]{1,0:T(8,128)(2,1)S(1)}, u32[]{:S(2)}, u32[]{:S(2)}) collective-permute-start(bf16[144,512]{1,0:T(8,128)(2,1)} %get-tuple-element.36), channel_id=1, source_target_pairs={{0,4},{1,5},{2,6},{3,7},{4,0},{5,1},{6,2},{7,3},{8,12},{9,13},{10,... | collective-permute-start | bytes 442376 | tf_op jit(solution)/shard_map/ppermute | solution.py:334
  9.9 7.0 %collective-permute-start.5 = (bf16[144,512]{1,0:T(8,128)(2,1)}, bf16[144,512]{1,0:T(8,128)(2,1)S(1)}, u32[]{:S(2)}, u32[]{:S(2)}) collective-permute-start(bf16[144,512]{1,0:T(8,128)(2,1)} %get-tuple-element.37), channel_id=1, source_target_pairs={{0,8},{1,9},{2,10},{3,11},{4,12},{5,13},{6,14},{7,15},{8,0},{9,1},... | collective-permute-start | bytes 442376 | tf_op jit(solution)/shard_map/ppermute | solution.py:334
  11.5 3.7 %copy-start = (f32[128,512]{1,0:T(8,128)S(1)}, f32[128,512]{1,0:T(8,128)}, u32[]{:S(2)}) copy-start(f32[128,512]{1,0:T(8,128)} %refs_4_.1) | copy-start | bytes 786436
  11.5 3.7 %copy-start.1 = (f32[128,512]{1,0:T(8,128)S(1)}, f32[128,512]{1,0:T(8,128)}, u32[]{:S(2)}) copy-start(f32[128,512]{1,0:T(8,128)} %refs_5_.1) | copy-start | bytes 786436
  11.5 8.2 %collective-permute-start.6 = (bf16[144,512]{1,0:T(8,128)(2,1)}, bf16[144,512]{1,0:T(8,128)(2,1)S(1)}, u32[]{:S(2)}, u32[]{:S(2)}) collective-permute-start(bf16[144,512]{1,0:T(8,128)(2,1)} %get-tuple-element.38), channel_id=1, source_target_pairs={{0,12},{1,13},{2,14},{3,15},{4,8},{5,9},{6,10},{7,11},{8,4},{9,5},... | collective-permute-start | bytes 442376 | tf_op jit(solution)/shard_map/ppermute | solution.py:334
  13.5 2.4 %copy-start.3 = (bf16[128,512]{1,0:T(8,128)(2,1)S(1)}, bf16[128,512]{1,0:T(8,128)(2,1)}, u32[]{:S(2)}) copy-start(bf16[128,512]{1,0:T(8,128)(2,1)} %get-tuple-element.34.refs_0_) | copy-start | bytes 393220
  13.6 6.5 %collective-permute-start.8 = (bf16[128,512]{1,0:T(8,128)(2,1)S(1)}, bf16[128,512]{1,0:T(8,128)(2,1)S(1)}, u32[]{:S(2)}, u32[]{:S(2)}) collective-permute-start(bf16[128,512]{1,0:T(8,128)(2,1)S(1)} %shard_map.68.refs_2_.refs_0_), channel_id=1, source_target_pairs={{0,2},{1,3},{2,0},{3,1},{4,6},{5,7},{6,4},{7,5},{8,10},{9,11},{10,... | collective-permute-start | bytes 393224 | tf_op jit(solution)/shard_map/ppermute | solution.py:334
  15.4 4.3 %copy-start.2 = (bf16[144,512]{1,0:T(8,128)(2,1)S(1)}, bf16[144,512]{1,0:T(8,128)(2,1)}, u32[]{:S(2)}) copy-start(bf16[144,512]{1,0:T(8,128)(2,1)} %get-tuple-element.35.refs_0_) | copy-start | bytes 442372
  15.4 14.5 %collective-permute-start.3 = (bf16[384,512]{1,0:T(8,128)(2,1)S(1)}, bf16[384,512]{1,0:T(8,128)(2,1)S(1)}, u32[]{:S(2)}, u32[]{:S(2)}) collective-permute-start(bf16[384,512]{1,0:T(8,128)(2,1)S(1)} %shard_map.70.own_ref), channel_id=1, source_target_pairs={{0,2},{1,3},{2,0},{3,1},{4,6},{5,7},{6,4},{7,5},{8,10},{9,11},{10,... | collective-permute-start | bytes 1179656 | tf_op jit(solution)/shard_map/ppermute | solution.py:334
  16.0 4.4 %collective-permute-start.2 = (bf16[384,512]{1,0:T(8,128)(2,1)S(1)}, bf16[384,512]{1,0:T(8,128)(2,1)S(1)}, u32[]{:S(2)}, u32[]{:S(2)}) collective-permute-start(bf16[384,512]{1,0:T(8,128)(2,1)S(1)} %shard_map.69.near_own.refs_0_), channel_id=1, source_target_pairs={{0,1},{1,0},{2,3},{3,2},{4,5},{5,4},{6,7},{7,6},{8,9},{9,8},{10,11... | collective-permute-start | bytes 1179656 | tf_op jit(solution)/shard_map/ppermute | solution.py:334
  19.7 2.0 %collective-permute-start.7 = (bf16[544,512]{1,0:T(8,128)(2,1)S(1)}, bf16[544,512]{1,0:T(8,128)(2,1)S(1)}, u32[]{:S(2)}, u32[]{:S(2)}) collective-permute-start(bf16[544,512]{1,0:T(8,128)(2,1)S(1)} %shard_map.71.own_ref.own_stack), channel_id=1, source_target_pairs={{0,1},{1,0},{2,3},{3,2},{4,5},{5,4},{6,7},{7,6},{8,9},{9,8},{10,11... | collective-permute-start | bytes 1671176 | tf_op jit(solution)/shard_map/ppermute | solution.py:334
  20.1 2.8 %collective-permute-start.9 = (bf16[128,512]{1,0:T(8,128)(2,1)S(1)}, bf16[128,512]{1,0:T(8,128)(2,1)S(1)}, u32[]{:S(2)}, u32[]{:S(2)}) collective-permute-start(bf16[128,512]{1,0:T(8,128)(2,1)S(1)} %shard_map.73.far_own), channel_id=1, source_target_pairs={{0,1},{1,0},{2,3},{3,2},{4,5},{5,4},{6,7},{7,6},{8,9},{9,8},{10,11... | collective-permute-start | bytes 393224 | tf_op jit(solution)/shard_map/ppermute | solution.py:334
  23.3 4.8 %collective-permute-start.12 = (f32[1,1024]{1,0:T(1,128)S(1)}, f32[1,1024]{1,0:T(1,128)S(1)}, u32[]{:S(2)}, u32[]{:S(2)}) collective-permute-start(f32[1,1024]{1,0:T(1,128)S(1)} %get-tuple-element.43._.refs_0_), channel_id=1, source_target_pairs={{0,4},{1,5},{2,6},{3,7},{4,0},{5,1},{6,2},{7,3},{8,12},{9,13},{10,... | collective-permute-start | bytes 12296 | tf_op jit(solution)/shard_map/ppermute | solution.py:334
  24.9 4.5 %collective-permute-start.11 = (f32[1,1024]{1,0:T(1,128)S(1)}, f32[1,1024]{1,0:T(1,128)S(1)}, u32[]{:S(2)}, u32[]{:S(2)}) collective-permute-start(f32[1,1024]{1,0:T(1,128)S(1)} %get-tuple-element.43._.refs_0_), channel_id=1, source_target_pairs={{0,12},{1,13},{2,14},{3,15},{4,8},{5,9},{6,10},{7,11},{8,4},{9,5},... | collective-permute-start | bytes 12296 | tf_op jit(solution)/shard_map/ppermute | solution.py:334
  24.9 4.5 %collective-permute-start.10 = (f32[1,1024]{1,0:T(1,128)S(1)}, f32[1,1024]{1,0:T(1,128)S(1)}, u32[]{:S(2)}, u32[]{:S(2)}) collective-permute-start(f32[1,1024]{1,0:T(1,128)S(1)} %get-tuple-element.43._.refs_0_), channel_id=1, source_target_pairs={{0,8},{1,9},{2,10},{3,11},{4,12},{5,13},{6,14},{7,15},{8,0},{9,1},... | collective-permute-start | bytes 12296 | tf_op jit(solution)/shard_map/ppermute | solution.py:334
  29.9 8.2 %collective-permute-start.13 = (bf16[768,512]{1,0:T(8,128)(2,1)S(1)}, bf16[768,512]{1,0:T(8,128)(2,1)S(1)}, u32[]{:S(2)}, u32[]{:S(2)}) collective-permute-start(bf16[768,512]{1,0:T(8,128)(2,1)S(1)} %shard_map.77.refs_2_), channel_id=1, source_target_pairs={{0,1},{1,0},{2,3},{3,2},{4,5},{5,4},{6,7},{7,6},{8,9},{9,8},{10,11... | collective-permute-start | bytes 2359304 | tf_op jit(solution)/shard_map/ppermute | solution.py:334
  30.0 5.9 %collective-permute-start.17 = (bf16[128,512]{1,0:T(8,128)(2,1)S(1)}, bf16[128,512]{1,0:T(8,128)(2,1)S(1)}, u32[]{:S(2)}, u32[]{:S(2)}) collective-permute-start(bf16[128,512]{1,0:T(8,128)(2,1)S(1)} %get-tuple-element.58), channel_id=1, source_target_pairs={{0,2},{1,3},{2,0},{3,1},{4,6},{5,7},{6,4},{7,5},{8,10},{9,11},{10,... | collective-permute-start | bytes 393224 | tf_op jit(solution)/shard_map/ppermute | solution.py:334
  30.6 10.7 %collective-permute-start.14 = (bf16[128,512]{1,0:T(8,128)(2,1)S(1)}, bf16[128,512]{1,0:T(8,128)(2,1)S(1)}, u32[]{:S(2)}, u32[]{:S(2)}) collective-permute-start(bf16[128,512]{1,0:T(8,128)(2,1)S(1)} %get-tuple-element.54), channel_id=1, source_target_pairs={{0,4},{1,5},{2,6},{3,7},{4,0},{5,1},{6,2},{7,3},{8,12},{9,13},{10,... | collective-permute-start | bytes 393224 | tf_op jit(solution)/shard_map/ppermute | solution.py:334
  31.5 9.8 %collective-permute-start.15 = (bf16[128,512]{1,0:T(8,128)(2,1)S(1)}, bf16[128,512]{1,0:T(8,128)(2,1)S(1)}, u32[]{:S(2)}, u32[]{:S(2)}) collective-permute-start(bf16[128,512]{1,0:T(8,128)(2,1)S(1)} %get-tuple-element.55), channel_id=1, source_target_pairs={{0,8},{1,9},{2,10},{3,11},{4,12},{5,13},{6,14},{7,15},{8,0},{9,1},... | collective-permute-start | bytes 393224 | tf_op jit(solution)/shard_map/ppermute | solution.py:334
  33.3 9.2 %collective-permute-start.16 = (bf16[128,512]{1,0:T(8,128)(2,1)S(1)}, bf16[128,512]{1,0:T(8,128)(2,1)S(1)}, u32[]{:S(2)}, u32[]{:S(2)}) collective-permute-start(bf16[128,512]{1,0:T(8,128)(2,1)S(1)} %get-tuple-element.56), channel_id=1, source_target_pairs={{0,12},{1,13},{2,14},{3,15},{4,8},{5,9},{6,10},{7,11},{8,4},{9,5},... | collective-permute-start | bytes 393224 | tf_op jit(solution)/shard_map/ppermute | solution.py:334
  36.0 6.8 %collective-permute-start.18 = (bf16[128,512]{1,0:T(8,128)(2,1)S(1)}, bf16[128,512]{1,0:T(8,128)(2,1)S(1)}, u32[]{:S(2)}, u32[]{:S(2)}) collective-permute-start(bf16[128,512]{1,0:T(8,128)(2,1)S(1)} %get-tuple-element.60), channel_id=1, source_target_pairs={{0,16},{1,17},{2,18},{3,19},{4,20},{5,21},{6,22},{7,23},{8,24},{9,... | collective-permute-start | bytes 393224 | tf_op jit(solution)/shard_map/ppermute | solution.py:334
  38.1 5.0 %collective-permute-start.19 = (bf16[128,512]{1,0:T(8,128)(2,1)S(1)}, bf16[128,512]{1,0:T(8,128)(2,1)S(1)}, u32[]{:S(2)}, u32[]{:S(2)}) collective-permute-start(bf16[128,512]{1,0:T(8,128)(2,1)S(1)} %get-tuple-element.61), channel_id=1, source_target_pairs={{0,2},{1,3},{2,0},{3,1},{4,6},{5,7},{6,4},{7,5},{8,10},{9,11},{10,... | collective-permute-start | bytes 393224 | tf_op jit(solution)/shard_map/ppermute | solution.py:334

commit v10 on v7

--- a/solution.py
+++ b/solution.py
@@ -116,7 +116,7 @@
 
 
 def stack_programs(planes, *refs):
-    msgs, out_ref = refs[:planes], refs[planes]
+    msgs, out_ref = (refs[0], *refs[planes - 1 : 0 : -1]), refs[planes]
     for k, msg in enumerate(msgs):
         out_ref[k * ROWS : (k + 1) * ROWS, :] = msg[0:ROWS, :]
     aux = jnp.concatenate([msg[ROWS:, :].astype(F32)[0:8, :] for msg in msgs], axis=0)
@@ -357,7 +357,7 @@
     arrived = [to_plane(sent[k], k) for k in far_first]
     stack = call(
         functools.partial(stack_programs, planes), [((side + 8 * planes, feat), LOW)], STACK, 0
-    )(sent[0], *arrived[::-1])[0]
+    )(sent[0], *arrived)[0]
     high_h = call(stack_traces, [(shape, LOW)], HALF, 0)(high_h)[0]
     high_x, far = flipped(high, x_bit), flipped(high_h, x_bit)
     far = call(stack_traces, [(shape, LOW)], FAR, 0)(far)[0]

time: 44.2 us -> 44.1 us (level)
  waiting for transfers between devices: 10.6 us -> 9.32 us
  starting transfers between devices: 22.8 us -> 23.9 us
    ppermute x20, waiting for transfers between devices: 10.6 us -> 9.32 us  [flipped(): return lax.ppermute(value, both, [(i, i ^ bits) for i in range(size)])]
    ppermute x20, starting transfers between devices: 22.8 us -> 23.9 us  [flipped(): return lax.ppermute(value, both, [(i, i ^ bits) for i in range(size)])]
where the time goes in v10:
time: 44.1 us; the launch traced here: 43.9 us
  starting transfers between devices  23.9 us (54%)
  Pallas kernels  9.84 us (22%)
  waiting for transfers between devices  9.32 us (21%)
  between operations  0.81 us (2%)
    ppermute x20, starting transfers between devices, flipped(): return lax.ppermute(value, both, [(i, i ^ bits) for i in range(size)])  23.9 us
    ppermute x20, waiting for transfers between devices, flipped(): return lax.ppermute(value, both, [(i, i ^ bits) for i in range(size)])  9.32 us
    pallas_call x1, Pallas kernels, on_device(): call(functools.partial(prepare, planes), [((rows + MORE, feat), LOW)] * p...  2.17 us
    pallas_call x1, Pallas kernels, on_device(): call(group_terms, [(shape, F32)] * 4 + [((rows, rows), F32), ((1, rows),...  2 us
    pallas_call x1, Pallas kernels, on_device(): call(functools.partial(program_terms, planes), [((8, rows), F32), (shape,...  1.27 us
    pallas_call x1, Pallas kernels, on_device(): call(functools.partial(score_near, planes), lists, NEAR, 0)  1.07 us
    pallas_call x1, Pallas kernels, on_device(): call(functools.partial(finish, planes), [(shape, F32)] * 2, block, block)  1.03 us
    pallas_call x1, Pallas kernels, on_device(): call(functools.partial(near_terms, planes), [(shape, F32), (shape, LOW),...  0.97 us
  transfers between devices with their start and end apart: 20, of which 10 were waited for; matrix products, arithmetic and copies ran while one was open for 0% of the time, Pallas kernels for 15%

profile of v10, /device:TPU:0, one launch (start us, length us, event | category | flops | bytes accessed | tf_op | source)
XLA Modules:
  0.0 43.9 jit_solution(38813431962017280)
XLA Ops:
  0.6 2.2 %shard_map.67 = (bf16[144,512]{1,0:T(8,128)(2,1)}, bf16[144,512]{1,0:T(8,128)(2,1)}, bf16[144,512]{1,0:T(8,128)(2,1)}, bf16[144,512]{1,0:T(8,128)(2,1)}, bf16[128,512]{1,0:T(8,128)(2,1)}) custom-call(f32[128,512]{1,0:T(8,128)} %refs_4_.1, f32[128,512]{1,0:T(8,128)} %refs_5_.1, s32[16,128]{1,0:T(8,128)} %bitcast.3, s32[16,128]{1,0:T(8,128)} %bitcast.4), custom_call_target="tpu_custom_call" | custom-call | flops 655360 | bytes 1310720 | tf_op jit(solution)/shard_map/pallas_call | solution.py:339
  2.8 4.1 %collective-permute-start.1 = (bf16[128,512]{1,0:T(8,128)(2,1)}, bf16[128,512]{1,0:T(8,128)(2,1)S(1)}, u32[]{:S(2)}, u32[]{:S(2)}) collective-permute-start(bf16[128,512]{1,0:T(8,128)(2,1)} %get-tuple-element.34.refs_0_), channel_id=1, source_target_pairs={{0,16},{1,17},{2,18},{3,19},{4,20},{5,21},{6,22},{7,23},{8,24},{9,... | collective-permute-start | bytes 393224 | tf_op jit(solution)/shard_map/ppermute | solution.py:329
  6.9 1.5 %collective-permute-start = (bf16[128,512]{1,0:T(8,128)(2,1)}, bf16[128,512]{1,0:T(8,128)(2,1)S(1)}, u32[]{:S(2)}, u32[]{:S(2)}) collective-permute-start(bf16[128,512]{1,0:T(8,128)(2,1)} %get-tuple-element.34.refs_0_), channel_id=1, source_target_pairs={{0,2},{1,3},{2,0},{3,1},{4,6},{5,7},{6,4},{7,5},{8,10},{9,11},{10,... | collective-permute-start | bytes 393224 | tf_op jit(solution)/shard_map/ppermute | solution.py:329
  8.4 2.5 %collective-permute-start.4 = (bf16[144,512]{1,0:T(8,128)(2,1)}, bf16[144,512]{1,0:T(8,128)(2,1)S(1)}, u32[]{:S(2)}, u32[]{:S(2)}) collective-permute-start(bf16[144,512]{1,0:T(8,128)(2,1)} %get-tuple-element.36), channel_id=1, source_target_pairs={{0,12},{1,13},{2,14},{3,15},{4,8},{5,9},{6,10},{7,11},{8,4},{9,5},... | collective-permute-start | bytes 442376 | tf_op jit(solution)/shard_map/ppermute | solution.py:329
  10.9 0.4 %collective-permute-start.5 = (bf16[144,512]{1,0:T(8,128)(2,1)}, bf16[144,512]{1,0:T(8,128)(2,1)S(1)}, u32[]{:S(2)}, u32[]{:S(2)}) collective-permute-start(bf16[144,512]{1,0:T(8,128)(2,1)} %get-tuple-element.37), channel_id=1, source_target_pairs={{0,8},{1,9},{2,10},{3,11},{4,12},{5,13},{6,14},{7,15},{8,0},{9,1},... | collective-permute-start | bytes 442376 | tf_op jit(solution)/shard_map/ppermute | solution.py:329
  11.4 0.5 %collective-permute-start.6 = (bf16[144,512]{1,0:T(8,128)(2,1)}, bf16[144,512]{1,0:T(8,128)(2,1)S(1)}, u32[]{:S(2)}, u32[]{:S(2)}) collective-permute-start(bf16[144,512]{1,0:T(8,128)(2,1)} %get-tuple-element.38), channel_id=1, source_target_pairs={{0,4},{1,5},{2,6},{3,7},{4,0},{5,1},{6,2},{7,3},{8,12},{9,13},{10,... | collective-permute-start | bytes 442376 | tf_op jit(solution)/shard_map/ppermute | solution.py:329
  11.9 1.6 %collective-permute-done.1.refs_0_ = bf16[128,512]{1,0:T(8,128)(2,1)S(1)} collective-permute-done((bf16[128,512]{1,0:T(8,128)(2,1)}, bf16[128,512]{1,0:T(8,128)(2,1)S(1)}, u32[]{:S(2)}, u32[]{:S(2)}) %collective-permute-start.1) | collective-permute-done | bytes 131104 | tf_op jit(solution)/shard_map/ppermute | solution.py:329
  13.6 1.6 %collective-permute-start.8 = (bf16[128,512]{1,0:T(8,128)(2,1)S(1)}, bf16[128,512]{1,0:T(8,128)(2,1)S(1)}, u32[]{:S(2)}, u32[]{:S(2)}) collective-permute-start(bf16[128,512]{1,0:T(8,128)(2,1)S(1)} %shard_map.68.refs_2_.refs_0_), channel_id=1, source_target_pairs={{0,2},{1,3},{2,0},{3,1},{4,6},{5,7},{6,4},{7,5},{8,10},{9,11},{10,... | collective-permute-start | bytes 393224 | tf_op jit(solution)/shard_map/ppermute | solution.py:329
  15.4 0.5 %collective-permute-start.3 = (bf16[384,512]{1,0:T(8,128)(2,1)S(1)}, bf16[384,512]{1,0:T(8,128)(2,1)S(1)}, u32[]{:S(2)}, u32[]{:S(2)}) collective-permute-start(bf16[384,512]{1,0:T(8,128)(2,1)S(1)} %shard_map.70.own_ref), channel_id=1, source_target_pairs={{0,2},{1,3},{2,0},{3,1},{4,6},{5,7},{6,4},{7,5},{8,10},{9,11},{10,... | collective-permute-start | bytes 1179656 | tf_op jit(solution)/shard_map/ppermute | solution.py:329
  16.0 1.3 %collective-permute-done.4.refs_1_ = bf16[144,512]{1,0:T(8,128)(2,1)S(1)} collective-permute-done((bf16[144,512]{1,0:T(8,128)(2,1)}, bf16[144,512]{1,0:T(8,128)(2,1)S(1)}, u32[]{:S(2)}, u32[]{:S(2)}) %collective-permute-start.4) | collective-permute-done | bytes 147488 | tf_op jit(solution)/shard_map/ppermute | solution.py:329
  17.3 2.1 %collective-permute-done.5.refs_2_ = bf16[144,512]{1,0:T(8,128)(2,1)S(1)} collective-permute-done((bf16[144,512]{1,0:T(8,128)(2,1)}, bf16[144,512]{1,0:T(8,128)(2,1)S(1)}, u32[]{:S(2)}, u32[]{:S(2)}) %collective-permute-start.5) | collective-permute-done | bytes 147488 | tf_op jit(solution)/shard_map/ppermute | solution.py:329
  19.5 0.5 %collective-permute-done.8.refs_0_ = bf16[128,512]{1,0:T(8,128)(2,1)S(1)} collective-permute-done((bf16[128,512]{1,0:T(8,128)(2,1)S(1)}, bf16[128,512]{1,0:T(8,128)(2,1)S(1)}, u32[]{:S(2)}, u32[]{:S(2)}) %collective-permute-start.8) | collective-permute-done | bytes 131104 | tf_op jit(solution)/shard_map/ppermute | solution.py:329
  20.2 1.3 %collective-permute-done.7.other_ref.other_stack = bf16[544,512]{1,0:T(8,128)(2,1)S(1)} collective-permute-done((bf16[544,512]{1,0:T(8,128)(2,1)S(1)}, bf16[544,512]{1,0:T(8,128)(2,1)S(1)}, u32[]{:S(2)}, u32[]{:S(2)}) %collective-permute-start.7) | collective-permute-done | bytes 557088 | tf_op jit(solution)/shard_map/ppermute | solution.py:329
  21.5 1.1 %shard_map.72 = (f32[8,1024]{1,0:T(8,128)S(1)}, f32[8,1024]{1,0:T(8,128)S(1)}, f32[1,1024]{1,0:T(1,128)S(1)}) custom-call(bf16[544,512]{1,0:T(8,128)(2,1)S(1)} %shard_map.71.own_ref.own_stack, bf16[544,512]{1,0:T(8,128)(2,1)S(1)} %collective-permute-done.7.other_ref.other_stack, bf16[384,512]{1,0:T(8,128)(2,1)S(1)} %shard_map.69.near_own.refs_0_, ...), custom_call_target="tpu_custom_call" | custom-call | flops 100000000 | tf_op jit(solution)/shard_map/pallas_call | solution.py:373
  22.6 0.5 %shard_map.74 = (f32[8,1024]{1,0:T(8,128)S(1)}, f32[1,1024]{1,0:T(1,128)S(1)}) custom-call(f32[8,1024]{1,0:T(8,128)S(1)} %get-tuple-element.39.exp_in, f32[8,1024]{1,0:T(8,128)S(1)} %get-tuple-element.40.pick_ref, bf16[544,512]{1,0:T(8,128)(2,1)S(1)} %shard_map.71.own_ref.own_stack, bf16[544,512]{1,0:T(8,128)(2,1)S(1)} %collective-permute-done.7.other_ref.other_stack, ...), custom_call_target="tpu_custom_call" | custom-call | flops 300000000 | tf_op jit(solution)/shard_map/pallas_call | solution.py:376
  23.1 0.6 %collective-permute-start.12 = (f32[1,1024]{1,0:T(1,128)S(1)}, f32[1,1024]{1,0:T(1,128)S(1)}, u32[]{:S(2)}, u32[]{:S(2)}) collective-permute-start(f32[1,1024]{1,0:T(1,128)S(1)} %get-tuple-element.43._.refs_0_), channel_id=1, source_target_pairs={{0,4},{1,5},{2,6},{3,7},{4,0},{5,1},{6,2},{7,3},{8,12},{9,13},{10,... | collective-permute-start | bytes 12296 | tf_op jit(solution)/shard_map/ppermute | solution.py:329
  23.7 1.2 %collective-permute-start.11 = (f32[1,1024]{1,0:T(1,128)S(1)}, f32[1,1024]{1,0:T(1,128)S(1)}, u32[]{:S(2)}, u32[]{:S(2)}) collective-permute-start(f32[1,1024]{1,0:T(1,128)S(1)} %get-tuple-element.43._.refs_0_), channel_id=1, source_target_pairs={{0,12},{1,13},{2,14},{3,15},{4,8},{5,9},{6,10},{7,11},{8,4},{9,5},... | collective-permute-start | bytes 12296 | tf_op jit(solution)/shard_map/ppermute | solution.py:329
  24.9 1.8 %collective-permute-start.10 = (f32[1,1024]{1,0:T(1,128)S(1)}, f32[1,1024]{1,0:T(1,128)S(1)}, u32[]{:S(2)}, u32[]{:S(2)}) collective-permute-start(f32[1,1024]{1,0:T(1,128)S(1)} %get-tuple-element.43._.refs_0_), channel_id=1, source_target_pairs={{0,8},{1,9},{2,10},{3,11},{4,12},{5,13},{6,14},{7,15},{8,0},{9,1},... | collective-permute-start | bytes 12296 | tf_op jit(solution)/shard_map/ppermute | solution.py:329
  26.6 1.3 %shard_map.75 = (f32[8,128]{1,0:T(8,128)S(1)}, f32[128,512]{1,0:T(8,128)S(1)}, bf16[128,512]{1,0:T(8,128)(2,1)S(1)}, bf16[128,512]{1,0:T(8,128)(2,1)S(1)}, bf16[128,512]{1,0:T(8,128)(2,1)S(1)}) custom-call(f32[8,1024]{1,0:T(8,128)S(1)} %get-tuple-element.41.exp_ref, f32[8,1024]{1,0:T(8,128)S(1)} %get-tuple-element.40.pick_ref, ...), custom_call_target="tpu_custom_call" | custom-call | flops 2000000000 | tf_op jit(solution)/shard_map/pallas_call | solution.py:381
  28.2 0.3 collective-permute-done.10.refs_1_
  28.5 0.5 %shard_map.76 = (f32[1,128]{1,0:T(1,128)S(1)}, f32[8,1024]{1,0:T(8,128)S(1)}, bf16[128,512]{1,0:T(8,128)(2,1)S(1)}) custom-call(f32[8,1024]{1,0:T(8,128)S(1)} %get-tuple-element.41.exp_ref, f32[8,1024]{1,0:T(8,128)S(1)} %get-tuple-element.40.pick_ref, f32[1,1024]{1,0:T(1,128)S(1)} %get-tuple-element.42.pos_ref, ...), custom_call_target="tpu_custom_call" | custom-call | tf_op jit(solution)/shard_map/pallas_call | solution.py:387
  29.1 1.2 %collective-permute-start.17 = (bf16[128,512]{1,0:T(8,128)(2,1)S(1)}, bf16[128,512]{1,0:T(8,128)(2,1)S(1)}, u32[]{:S(2)}, u32[]{:S(2)}) collective-permute-start(bf16[128,512]{1,0:T(8,128)(2,1)S(1)} %get-tuple-element.58), channel_id=1, source_target_pairs={{0,2},{1,3},{2,0},{3,1},{4,6},{5,7},{6,4},{7,5},{8,10},{9,11},{10,... | collective-permute-start | bytes 393224 | tf_op jit(solution)/shard_map/ppermute | solution.py:329
  30.3 1.2 %collective-permute-start.14 = (bf16[128,512]{1,0:T(8,128)(2,1)S(1)}, bf16[128,512]{1,0:T(8,128)(2,1)S(1)}, u32[]{:S(2)}, u32[]{:S(2)}) collective-permute-start(bf16[128,512]{1,0:T(8,128)(2,1)S(1)} %get-tuple-element.54), channel_id=1, source_target_pairs={{0,4},{1,5},{2,6},{3,7},{4,0},{5,1},{6,2},{7,3},{8,12},{9,13},{10,... | collective-permute-start | bytes 393224 | tf_op jit(solution)/shard_map/ppermute | solution.py:329
  31.5 1.4 %collective-permute-start.15 = (bf16[128,512]{1,0:T(8,128)(2,1)S(1)}, bf16[128,512]{1,0:T(8,128)(2,1)S(1)}, u32[]{:S(2)}, u32[]{:S(2)}) collective-permute-start(bf16[128,512]{1,0:T(8,128)(2,1)S(1)} %get-tuple-element.55), channel_id=1, source_target_pairs={{0,8},{1,9},{2,10},{3,11},{4,12},{5,13},{6,14},{7,15},{8,0},{9,1},... | collective-permute-start | bytes 393224 | tf_op jit(solution)/shard_map/ppermute | solution.py:329
  32.9 0.9 %collective-permute-start.16 = (bf16[128,512]{1,0:T(8,128)(2,1)S(1)}, bf16[128,512]{1,0:T(8,128)(2,1)S(1)}, u32[]{:S(2)}, u32[]{:S(2)}) collective-permute-start(bf16[128,512]{1,0:T(8,128)(2,1)S(1)} %get-tuple-element.56), channel_id=1, source_target_pairs={{0,12},{1,13},{2,14},{3,15},{4,8},{5,9},{6,10},{7,11},{8,4},{9,5},... | collective-permute-start | bytes 393224 | tf_op jit(solution)/shard_map/ppermute | solution.py:329
  33.8 1.0 %shard_map.78 = (f32[128,512]{1,0:T(8,128)S(1)}, bf16[128,512]{1,0:T(8,128)(2,1)S(1)}, f32[128,512]{1,0:T(8,128)S(1)}) custom-call(f32[8,1024]{1,0:T(8,128)S(1)} %get-tuple-element.46.weight_ref, f32[8,1024]{1,0:T(8,128)S(1)} %get-tuple-element.40.pick_ref, bf16[544,512]{1,0:T(8,128)(2,1)S(1)} %shard_map.71.own_ref.own_stack, ...), custom_call_target="tpu_custom_call" | custom-call | flops 805306368 | bytes 2097152 | tf_op jit(solution)/shard_map/pallas_call | solution.py:390
  35.0 2.9 %collective-permute-start.18 = (bf16[128,512]{1,0:T(8,128)(2,1)S(1)}, bf16[128,512]{1,0:T(8,128)(2,1)S(1)}, u32[]{:S(2)}, u32[]{:S(2)}) collective-permute-start(bf16[128,512]{1,0:T(8,128)(2,1)S(1)} %get-tuple-element.60), channel_id=1, source_target_pairs={{0,16},{1,17},{2,18},{3,19},{4,20},{5,21},{6,22},{7,23},{8,24},{9,... | collective-permute-start | bytes 393224 | tf_op jit(solution)/shard_map/ppermute | solution.py:329
  37.9 1.4 %collective-permute-start.19 = (bf16[128,512]{1,0:T(8,128)(2,1)S(1)}, bf16[128,512]{1,0:T(8,128)(2,1)S(1)}, u32[]{:S(2)}, u32[]{:S(2)}) collective-permute-start(bf16[128,512]{1,0:T(8,128)(2,1)S(1)} %get-tuple-element.61), channel_id=1, source_target_pairs={{0,2},{1,3},{2,0},{3,1},{4,6},{5,7},{6,4},{7,5},{8,10},{9,11},{10,... | collective-permute-start | bytes 393224 | tf_op jit(solution)/shard_map/ppermute | solution.py:329
  39.3 2.0 %shard_map.79 = (f32[128,512]{1,0:T(8,128)S(1)}, f32[128,512]{1,0:T(8,128)S(1)}, f32[128,512]{1,0:T(8,128)S(1)}, f32[128,512]{1,0:T(8,128)S(1)}, f32[128,128]{1,0:T(8,128)S(1)}, /*index=5*/f32[1,128]{1,0:T(1,128)}) custom-call(bf16[384,512]{1,0:T(8,128)(2,1)S(1)} %shard_map.69.near_own.refs_0_, ...), custom_call_target="tpu_custom_call" | custom-call | flops 65536 | bytes 65536 | tf_op jit(solution)/shard_map/pallas_call | solution.py:403
  41.3 1.1 %collective-permute-done.16.refs_3_ = bf16[128,512]{1,0:T(8,128)(2,1)S(1)} collective-permute-done((bf16[128,512]{1,0:T(8,128)(2,1)S(1)}, bf16[128,512]{1,0:T(8,128)(2,1)S(1)}, u32[]{:S(2)}, u32[]{:S(2)}) %collective-permute-start.16) | collective-permute-done | bytes 131104 | tf_op jit(solution)/shard_map/ppermute | solution.py:329
  42.3 0.5 %collective-permute-done.19.refs_5_ = bf16[128,512]{1,0:T(8,128)(2,1)S(1)} collective-permute-done((bf16[128,512]{1,0:T(8,128)(2,1)S(1)}, bf16[128,512]{1,0:T(8,128)(2,1)S(1)}, u32[]{:S(2)}, u32[]{:S(2)}) %collective-permute-start.19) | collective-permute-done | bytes 131104 | tf_op jit(solution)/shard_map/ppermute | solution.py:329
  42.9 1.0 %shard_map.81 = (f32[128,512]{1,0:T(8,128)}, f32[128,512]{1,0:T(8,128)}) custom-call(f32[128,512]{1,0:T(8,128)S(1)} %get-tuple-element.48.prog_base, f32[128,512]{1,0:T(8,128)S(1)} %get-tuple-element.49.trace_base, f32[128,512]{1,0:T(8,128)S(1)} %get-tuple-element.50.prog_unit, f32[128,512]{1,0:T(8,128)S(1)} %get-tuple-element.51.trace_unit, ...), custom_call_target="tpu_custom_call" | custom-call | flops 65536 | bytes 65536 | tf_op jit(solution)/shard_map/pallas_call | solution.py:410
  (31 shorter events, 1.1 us)
Async XLA Ops:
  2.8 10.7 %collective-permute-start.1 = (bf16[128,512]{1,0:T(8,128)(2,1)}, bf16[128,512]{1,0:T(8,128)(2,1)S(1)}, u32[]{:S(2)}, u32[]{:S(2)}) collective-permute-start(bf16[128,512]{1,0:T(8,128)(2,1)} %get-tuple-element.34.refs_0_), channel_id=1, source_target_pairs={{0,16},{1,17},{2,18},{3,19},{4,20},{5,21},{6,22},{7,23},{8,24},{9,... | collective-permute-start | bytes 393224 | tf_op jit(solution)/shard_map/ppermute | solution.py:329
  6.9 8.5 %collective-permute-start = (bf16[128,512]{1,0:T(8,128)(2,1)}, bf16[128,512]{1,0:T(8,128)(2,1)S(1)}, u32[]{:S(2)}, u32[]{:S(2)}) collective-permute-start(bf16[128,512]{1,0:T(8,128)(2,1)} %get-tuple-element.34.refs_0_), channel_id=1, source_target_pairs={{0,2},{1,3},{2,0},{3,1},{4,6},{5,7},{6,4},{7,5},{8,10},{9,11},{10,... | collective-permute-start | bytes 393224 | tf_op jit(solution)/shard_map/ppermute | solution.py:329
  8.4 8.9 %collective-permute-start.4 = (bf16[144,512]{1,0:T(8,128)(2,1)}, bf16[144,512]{1,0:T(8,128)(2,1)S(1)}, u32[]{:S(2)}, u32[]{:S(2)}) collective-permute-start(bf16[144,512]{1,0:T(8,128)(2,1)} %get-tuple-element.36), channel_id=1, source_target_pairs={{0,12},{1,13},{2,14},{3,15},{4,8},{5,9},{6,10},{7,11},{8,4},{9,5},... | collective-permute-start | bytes 442376 | tf_op jit(solution)/shard_map/ppermute | solution.py:329
  10.9 8.5 %collective-permute-start.5 = (bf16[144,512]{1,0:T(8,128)(2,1)}, bf16[144,512]{1,0:T(8,128)(2,1)S(1)}, u32[]{:S(2)}, u32[]{:S(2)}) collective-permute-start(bf16[144,512]{1,0:T(8,128)(2,1)} %get-tuple-element.37), channel_id=1, source_target_pairs={{0,8},{1,9},{2,10},{3,11},{4,12},{5,13},{6,14},{7,15},{8,0},{9,1},... | collective-permute-start | bytes 442376 | tf_op jit(solution)/shard_map/ppermute | solution.py:329
  11.4 3.8 %copy-start = (f32[128,512]{1,0:T(8,128)S(1)}, f32[128,512]{1,0:T(8,128)}, u32[]{:S(2)}) copy-start(f32[128,512]{1,0:T(8,128)} %refs_4_.1) | copy-start | bytes 786436
  11.4 3.8 %copy-start.1 = (f32[128,512]{1,0:T(8,128)S(1)}, f32[128,512]{1,0:T(8,128)}, u32[]{:S(2)}) copy-start(f32[128,512]{1,0:T(8,128)} %refs_5_.1) | copy-start | bytes 786436
  11.4 8.0 %collective-permute-start.6 = (bf16[144,512]{1,0:T(8,128)(2,1)}, bf16[144,512]{1,0:T(8,128)(2,1)S(1)}, u32[]{:S(2)}, u32[]{:S(2)}) collective-permute-start(bf16[144,512]{1,0:T(8,128)(2,1)} %get-tuple-element.38), channel_id=1, source_target_pairs={{0,4},{1,5},{2,6},{3,7},{4,0},{5,1},{6,2},{7,3},{8,12},{9,13},{10,... | collective-permute-start | bytes 442376 | tf_op jit(solution)/shard_map/ppermute | solution.py:329
  13.5 2.4 %copy-start.3 = (bf16[128,512]{1,0:T(8,128)(2,1)S(1)}, bf16[128,512]{1,0:T(8,128)(2,1)}, u32[]{:S(2)}) copy-start(bf16[128,512]{1,0:T(8,128)(2,1)} %get-tuple-element.34.refs_0_) | copy-start | bytes 393220
  13.6 6.5 %collective-permute-start.8 = (bf16[128,512]{1,0:T(8,128)(2,1)S(1)}, bf16[128,512]{1,0:T(8,128)(2,1)S(1)}, u32[]{:S(2)}, u32[]{:S(2)}) collective-permute-start(bf16[128,512]{1,0:T(8,128)(2,1)S(1)} %shard_map.68.refs_2_.refs_0_), channel_id=1, source_target_pairs={{0,2},{1,3},{2,0},{3,1},{4,6},{5,7},{6,4},{7,5},{8,10},{9,11},{10,... | collective-permute-start | bytes 393224 | tf_op jit(solution)/shard_map/ppermute | solution.py:329
  15.4 4.0 %copy-start.2 = (bf16[144,512]{1,0:T(8,128)(2,1)S(1)}, bf16[144,512]{1,0:T(8,128)(2,1)}, u32[]{:S(2)}) copy-start(bf16[144,512]{1,0:T(8,128)(2,1)} %get-tuple-element.35.refs_0_) | copy-start | bytes 442372
  15.4 13.6 %collective-permute-start.3 = (bf16[384,512]{1,0:T(8,128)(2,1)S(1)}, bf16[384,512]{1,0:T(8,128)(2,1)S(1)}, u32[]{:S(2)}, u32[]{:S(2)}) collective-permute-start(bf16[384,512]{1,0:T(8,128)(2,1)S(1)} %shard_map.70.own_ref), channel_id=1, source_target_pairs={{0,2},{1,3},{2,0},{3,1},{4,6},{5,7},{6,4},{7,5},{8,10},{9,11},{10,... | collective-permute-start | bytes 1179656 | tf_op jit(solution)/shard_map/ppermute | solution.py:329
  17.3 2.8 %collective-permute-start.2 = (bf16[384,512]{1,0:T(8,128)(2,1)S(1)}, bf16[384,512]{1,0:T(8,128)(2,1)S(1)}, u32[]{:S(2)}, u32[]{:S(2)}) collective-permute-start(bf16[384,512]{1,0:T(8,128)(2,1)S(1)} %shard_map.69.near_own.refs_0_), channel_id=1, source_target_pairs={{0,1},{1,0},{2,3},{3,2},{4,5},{5,4},{6,7},{7,6},{8,9},{9,8},{10,11... | collective-permute-start | bytes 1179656 | tf_op jit(solution)/shard_map/ppermute | solution.py:329
  19.5 2.0 %collective-permute-start.7 = (bf16[544,512]{1,0:T(8,128)(2,1)S(1)}, bf16[544,512]{1,0:T(8,128)(2,1)S(1)}, u32[]{:S(2)}, u32[]{:S(2)}) collective-permute-start(bf16[544,512]{1,0:T(8,128)(2,1)S(1)} %shard_map.71.own_ref.own_stack), channel_id=1, source_target_pairs={{0,1},{1,0},{2,3},{3,2},{4,5},{5,4},{6,7},{7,6},{8,9},{9,8},{10,11... | collective-permute-start | bytes 1671176 | tf_op jit(solution)/shard_map/ppermute | solution.py:329
  20.1 2.5 %collective-permute-start.9 = (bf16[128,512]{1,0:T(8,128)(2,1)S(1)}, bf16[128,512]{1,0:T(8,128)(2,1)S(1)}, u32[]{:S(2)}, u32[]{:S(2)}) collective-permute-start(bf16[128,512]{1,0:T(8,128)(2,1)S(1)} %shard_map.73.far_own), channel_id=1, source_target_pairs={{0,1},{1,0},{2,3},{3,2},{4,5},{5,4},{6,7},{7,6},{8,9},{9,8},{10,11... | collective-permute-start | bytes 393224 | tf_op jit(solution)/shard_map/ppermute | solution.py:329
  23.1 4.8 %collective-permute-start.12 = (f32[1,1024]{1,0:T(1,128)S(1)}, f32[1,1024]{1,0:T(1,128)S(1)}, u32[]{:S(2)}, u32[]{:S(2)}) collective-permute-start(f32[1,1024]{1,0:T(1,128)S(1)} %get-tuple-element.43._.refs_0_), channel_id=1, source_target_pairs={{0,4},{1,5},{2,6},{3,7},{4,0},{5,1},{6,2},{7,3},{8,12},{9,13},{10,... | collective-permute-start | bytes 12296 | tf_op jit(solution)/shard_map/ppermute | solution.py:329
  23.7 4.5 %collective-permute-start.11 = (f32[1,1024]{1,0:T(1,128)S(1)}, f32[1,1024]{1,0:T(1,128)S(1)}, u32[]{:S(2)}, u32[]{:S(2)}) collective-permute-start(f32[1,1024]{1,0:T(1,128)S(1)} %get-tuple-element.43._.refs_0_), channel_id=1, source_target_pairs={{0,12},{1,13},{2,14},{3,15},{4,8},{5,9},{6,10},{7,11},{8,4},{9,5},... | collective-permute-start | bytes 12296 | tf_op jit(solution)/shard_map/ppermute | solution.py:329
  24.9 3.6 %collective-permute-start.10 = (f32[1,1024]{1,0:T(1,128)S(1)}, f32[1,1024]{1,0:T(1,128)S(1)}, u32[]{:S(2)}, u32[]{:S(2)}) collective-permute-start(f32[1,1024]{1,0:T(1,128)S(1)} %get-tuple-element.43._.refs_0_), channel_id=1, source_target_pairs={{0,8},{1,9},{2,10},{3,11},{4,12},{5,13},{6,14},{7,15},{8,0},{9,1},... | collective-permute-start | bytes 12296 | tf_op jit(solution)/shard_map/ppermute | solution.py:329
  29.0 8.9 %collective-permute-start.13 = (bf16[768,512]{1,0:T(8,128)(2,1)S(1)}, bf16[768,512]{1,0:T(8,128)(2,1)S(1)}, u32[]{:S(2)}, u32[]{:S(2)}) collective-permute-start(bf16[768,512]{1,0:T(8,128)(2,1)S(1)} %shard_map.77.refs_2_), channel_id=1, source_target_pairs={{0,1},{1,0},{2,3},{3,2},{4,5},{5,4},{6,7},{7,6},{8,9},{9,8},{10,11... | collective-permute-start | bytes 2359304 | tf_op jit(solution)/shard_map/ppermute | solution.py:329
  29.1 5.9 %collective-permute-start.17 = (bf16[128,512]{1,0:T(8,128)(2,1)S(1)}, bf16[128,512]{1,0:T(8,128)(2,1)S(1)}, u32[]{:S(2)}, u32[]{:S(2)}) collective-permute-start(bf16[128,512]{1,0:T(8,128)(2,1)S(1)} %get-tuple-element.58), channel_id=1, source_target_pairs={{0,2},{1,3},{2,0},{3,1},{4,6},{5,7},{6,4},{7,5},{8,10},{9,11},{10,... | collective-permute-start | bytes 393224 | tf_op jit(solution)/shard_map/ppermute | solution.py:329
  30.3 11.0 %collective-permute-start.14 = (bf16[128,512]{1,0:T(8,128)(2,1)S(1)}, bf16[128,512]{1,0:T(8,128)(2,1)S(1)}, u32[]{:S(2)}, u32[]{:S(2)}) collective-permute-start(bf16[128,512]{1,0:T(8,128)(2,1)S(1)} %get-tuple-element.54), channel_id=1, source_target_pairs={{0,4},{1,5},{2,6},{3,7},{4,0},{5,1},{6,2},{7,3},{8,12},{9,13},{10,... | collective-permute-start | bytes 393224 | tf_op jit(solution)/shard_map/ppermute | solution.py:329
  31.5 9.8 %collective-permute-start.15 = (bf16[128,512]{1,0:T(8,128)(2,1)S(1)}, bf16[128,512]{1,0:T(8,128)(2,1)S(1)}, u32[]{:S(2)}, u32[]{:S(2)}) collective-permute-start(bf16[128,512]{1,0:T(8,128)(2,1)S(1)} %get-tuple-element.55), channel_id=1, source_target_pairs={{0,8},{1,9},{2,10},{3,11},{4,12},{5,13},{6,14},{7,15},{8,0},{9,1},... | collective-permute-start | bytes 393224 | tf_op jit(solution)/shard_map/ppermute | solution.py:329
  32.9 9.4 %collective-permute-start.16 = (bf16[128,512]{1,0:T(8,128)(2,1)S(1)}, bf16[128,512]{1,0:T(8,128)(2,1)S(1)}, u32[]{:S(2)}, u32[]{:S(2)}) collective-permute-start(bf16[128,512]{1,0:T(8,128)(2,1)S(1)} %get-tuple-element.56), channel_id=1, source_target_pairs={{0,12},{1,13},{2,14},{3,15},{4,8},{5,9},{6,10},{7,11},{8,4},{9,5},... | collective-permute-start | bytes 393224 | tf_op jit(solution)/shard_map/ppermute | solution.py:329
  35.0 7.3 %collective-permute-start.18 = (bf16[128,512]{1,0:T(8,128)(2,1)S(1)}, bf16[128,512]{1,0:T(8,128)(2,1)S(1)}, u32[]{:S(2)}, u32[]{:S(2)}) collective-permute-start(bf16[128,512]{1,0:T(8,128)(2,1)S(1)} %get-tuple-element.60), channel_id=1, source_target_pairs={{0,16},{1,17},{2,18},{3,19},{4,20},{5,21},{6,22},{7,23},{8,24},{9,... | collective-permute-start | bytes 393224 | tf_op jit(solution)/shard_map/ppermute | solution.py:329
  37.9 5.0 %collective-permute-start.19 = (bf16[128,512]{1,0:T(8,128)(2,1)S(1)}, bf16[128,512]{1,0:T(8,128)(2,1)S(1)}, u32[]{:S(2)}, u32[]{:S(2)}) collective-permute-start(bf16[128,512]{1,0:T(8,128)(2,1)S(1)} %get-tuple-element.61), channel_id=1, source_target_pairs={{0,2},{1,3},{2,0},{3,1},{4,6},{5,7},{6,4},{7,5},{8,10},{9,11},{10,... | collective-permute-start | bytes 393224 | tf_op jit(solution)/shard_map/ppermute | solution.py:329
